TPU v7x, 128 devices: a whole 4x4x4 slice. The times are simulated.
128 devices in a mesh: dp: 32 (over y, z, core), mp: 4 (over x).
Axes of the slice: x: 4, y: 4, z: 4, core: 2. Of those that a mesh axis runs over, the one named last changes fastest.
Arguments:
- latents: bfloat16 [32768, 1536], P('dp', 'mp'), may hold values from -6 to 6
- targets: bfloat16 [32768, 1536], P('dp', 'mp'), may hold values from -6 to 6
- tok_count: int32 [32], P('dp'), may hold values from 64 to 256, as said below
- caption_states: bfloat16 [32, 128, 4096], P('dp', None, 'mp'), may hold values from -6 to 6
- cap_len: int32 [32], P('dp'), may hold values from 16 to 128, as said below
- owner: int32 [32], replicated, may hold values from 0 to 31, each once
- ctx_w: bfloat16 [4096, 1536], P('mp'), may hold values from -0.09375 to 0.09375
- mod_w: bfloat16 [1536, 3, 1536], P(None, None, 'mp'), may hold values from -0.15625 to 0.15625
- in_w: bfloat16 [1536, 6144], P(None, 'mp'), may hold values from -0.15625 to 0.15625
- out_w: bfloat16 [1536, 6144], P(None, 'mp'), may hold values from -0.078125 to 0.078125
- noise_in: float32 [1536, 6144], P('dp', 'mp'), may hold values from -6 to 6
- noise_out: float32 [1536, 6144], P('dp', 'mp'), may hold values from -6 to 6
Outputs:
- grad_in: float32 [1536, 6144], P('dp', 'mp')
- grad_out: float32 [1536, 6144], P('dp', 'mp')
Inputs may be any that keep to these rules, and one draw needn't show every extreme that they name: `tok_count`: one example has all 256 tokens live. `cap_len`: one caption fills all 128 slots. `owner`: every learner slot appears exactly once.
All inputs are finite; a program needn't handle non-finite values.
Results may differ from a plain program's by a relative error of at most 0.0043.
Values may be sent and summed in bfloat16 or wider, within the bound.
No kernel may reach another device: no remote copies, remote signals or barrier semaphores. Data moves between devices by JAX's collectives and lax.ppermute only.
A program may use at most 128 MiB of HBM per device.

v0:
```python
import math

import jax
import jax.numpy as jnp
from jax import lax
from jax.sharding import PartitionSpec as P

D = 1536
FF = 6144
DRAWS = 4


def gelu_tanh(values):
    return jax.nn.gelu(values, approximate=True)


def contract_rows(left, right):
    return lax.dot_general(
        left, right, (((0,), (0,)), ((), ())), preferred_element_type=jnp.float32
    )


def local(
    latents,
    targets,
    tok_count,
    caption_states,
    cap_len,
    owner,
    ctx_w,
    mod_w,
    in_w,
    out_w,
    noise_in,
    noise_out,
):
    per_device = tok_count.shape[0]
    dp_size = lax.axis_size("dp")
    row_total = latents.shape[0]
    example_rows = row_total // per_device
    token_span = example_rows // DRAWS
    positions = jnp.arange(caption_states.shape[1])
    keep_mask = (positions[None, :] < cap_len[:, None]).astype(jnp.bfloat16)
    summed = jnp.einsum("ec,ecf->ef", keep_mask, caption_states, preferred_element_type=jnp.float32)
    pooled = (summed / cap_len[:, None].astype(jnp.float32)).astype(jnp.bfloat16)
    context = lax.psum(jnp.dot(pooled, ctx_w, preferred_element_type=jnp.float32), "mp")
    conditioning = context * lax.rsqrt(jnp.mean(context * context, 1, keepdims=True) + 1e-06)
    activated = jax.nn.silu(conditioning).astype(jnp.bfloat16)
    everyone = lax.all_gather(activated, "dp", axis=0, tiled=True)
    slot_ids = lax.axis_index("dp") * per_device + jnp.arange(per_device)
    picker = (owner[None, :] == slot_ids[:, None]).astype(jnp.bfloat16)
    chosen = jnp.dot(picker, everyone, preferred_element_type=jnp.float32).astype(jnp.bfloat16)
    modulation = jnp.einsum("ed,dkf->ekf", chosen, mod_w, preferred_element_type=jnp.float32)
    local_rows = latents.astype(jnp.float32).reshape(per_device, example_rows, -1)
    totals = lax.psum((jnp.sum(local_rows, 2), jnp.sum(local_rows * local_rows, 2)), "mp")
    center = totals[0][:, :, None] / D
    spread = totals[1][:, :, None] / D - center * center
    normed = (local_rows - center) * lax.rsqrt(spread + 1e-06)
    shaped = (normed * (1.0 + modulation[:, 1:2, :]) + modulation[:, 0:1, :]).astype(jnp.bfloat16)
    modded = lax.all_gather(shaped.reshape(row_total, -1), "mp", axis=1, tiled=True)
    gate = modulation[:, 2:3, :]
    pre = jnp.dot(modded, in_w, preferred_element_type=jnp.float32)
    hidden_full, gelu_back = jax.vjp(gelu_tanh, pre)
    hidden = hidden_full.astype(jnp.bfloat16)
    partial_out = lax.dot_general(
        hidden, out_w, (((1,), (1,)), ((), ())), preferred_element_type=jnp.float32
    )
    branch = lax.psum_scatter(partial_out, "mp", scatter_dimension=1, tiled=True).reshape(
        per_device, example_rows, -1
    )
    output = local_rows + gate * branch
    live = ((jnp.arange(example_rows) % token_span)[None, :] < tok_count[:, None]).astype(
        jnp.float32
    )[:, :, None]
    factor = (2.0 / (D * DRAWS * tok_count.astype(jnp.float32)))[:, None, None]
    tgt_rows = targets.astype(jnp.float32).reshape(per_device, example_rows, -1)
    delta = (output - tgt_rows) * live * factor
    back_local = (gate * delta).astype(jnp.bfloat16).reshape(row_total, -1)
    back_full = lax.all_gather(back_local, "mp", axis=1, tiled=True)
    hidden_grad = jnp.dot(back_full, out_w, preferred_element_type=jnp.float32)
    pre_grad = gelu_back(hidden_grad)[0].astype(jnp.bfloat16)
    root = math.sqrt(2.0 * D * FF)
    grad_first = contract_rows(modded, pre_grad)
    grad_second = contract_rows(back_full, hidden)
    squares = [jnp.sum(grad_first * grad_first) + jnp.sum(grad_second * grad_second)]
    norms = jnp.sqrt(lax.psum(jnp.stack(squares), "mp"))
    units = root / (norms + 0.01)
    total_first = units[0] * grad_first
    total_second = units[0] * grad_second
    summed_first, summed_second = (
        lax.psum_scatter(total_first, "dp", scatter_dimension=0, tiled=True),
        lax.psum_scatter(total_second, "dp", scatter_dimension=0, tiled=True),
    )
    examples = per_device * dp_size
    return ((summed_first + noise_in) / examples, (summed_second + noise_out) / examples)


def solution(mesh):
    placed = (
        P("dp", "mp"),
        P("dp", "mp"),
        P("dp"),
        P("dp", None, "mp"),
        P("dp"),
        P(),
        P("mp", None),
        P(None, None, "mp"),
        P(None, "mp"),
        P(None, "mp"),
        P("dp", "mp"),
        P("dp", "mp"),
    )
    return jax.shard_map(
        local, mesh=mesh, in_specs=placed, out_specs=(P("dp", "mp"), P("dp", "mp")), check_vma=False
    )
```

profile of v0, /device:TPU:0, one launch (start us, length us, event | category | flops | bytes accessed | tf_op | source)
XLA Modules:
  0.0 481.7 jit_solution(10472138555647282612)
XLA Ops:
  7.2 0.0 copy-start
  7.2 0.0 all-gather.4.cloned.1.call-start
  8.0 1.3 fusion.19
  9.3 2.1 convert_reduce_fusion
  11.4 2.4 fusion.49
  13.8 18.2 %all-reduce = (f32[1,1536]{1,0:T(1,128)S(1)}, f32[1,1024]{1,0:T(1,128)}, f32[1,1024]{1,0:T(1,128)}) all-reduce(f32[1,1536]{1,0:T(1,128)S(1)} %fusion.49, f32[1,1024]{1,0:T(1,128)} %bitcast.57, f32[1,1024]{1,0:T(1,128)} %bitcast.56), channel_id=1, replica_groups=mesh['dp'=32,'mp'=4] {'mp'}, use_global_device_ids=true, to_apply=%region_4.5 | all-reduce | flops 3584 | bytes 28672 | tf_op jit(solution)/shard_map/psum | solution.py:46
  32.0 0.7 multiply_reduce_fusion.2
  33.5 26.2 %all-gather = bf16[32,1,1536]{2,1,0:T(2,128)(2,1)S(1)} all-gather(bf16[1,1,1536]{2,1,0:T(2,128)(2,1)S(1)} %convert_bitcast_fusion), channel_id=1, replica_groups=mesh['dp'=32,'mp'=4] {'dp'}, dimensions={0}, use_global_device_ids=true | all-gather | bytes 101376 | tf_op jit(solution)/shard_map/all_gather | solution.py:49
  59.7 0.8 convolution_reduce_fusion
  60.5 0.0 copy-done
  60.5 0.6 fusion.50
  61.1 0.7 broadcast_multiply_fusion.2
  61.9 2.4 fusion.12
  64.3 0.0 all-gather.4.cloned.1.call-update
  64.3 0.0 reduce-scatter.4.cloned.1.call-start
  64.4 36.5 %all-gather.4.cloned.1.call-done = bf16[1024,1536]{1,0:T(8,128)(2,1)} async-done(((bf16[1024,384]{1,0:T(8,128)(2,1)}), bf16[1024,1536]{1,0:T(8,128)(2,1)}) %all-gather.4.cloned.1.call-update) | async-done | bytes 3145744 | tf_op jit(solution)/shard_map/all_gather | solution.py:60
  100.9 7.8 %fusion.51 = f32[1024,1536]{1,0:T(8,128)S(1)} fusion(bf16[1024,1536]{1,0:T(8,128)(2,1)} %all-gather.4.cloned.1.call-done, bf16[1536,1536]{1,0:T(8,128)(2,1)} %param.20), kind=kOutput, calls=%fused_computation.75 | convolution fusion | flops 4831838208 | bytes 14155776 | tf_op jit(solution)/shard_map/dot_general | solution.py:62
  108.7 0.0 copy-start.5
  108.7 2.6 copy-done.5
  111.3 9.7 %fusion.46 = f32[1024,1536]{1,0:T(8,128)} fusion(bf16[1536,1536]{1,0:T(8,128)(2,1)} %param.21, f32[1024,1536]{1,0:T(8,128)S(1)} %fusion.51), kind=kOutput, calls=%fused_computation.71 | convolution fusion | flops 4845993984 | bytes 17301504 | tf_op jit(solution)/shard_map/dot_general | solution.py:65
  121.1 0.0 copy-start.2
  121.1 0.0 copy-start.3
  121.1 0.0 reduce-scatter.4.cloned.1.call-update
  121.1 0.0 all-gather.6.cloned.1.call-start
  122.0 63.4 %reduce-scatter.4.cloned.1.call-done = f32[1024,384]{1,0:T(8,128)} async-done(((f32[1024,1536]{1,0:T(8,128)}), f32[1024,384]{1,0:T(8,128)}) %reduce-scatter.4.cloned.1.call-update) | async-done | bytes 1572880 | tf_op jit(solution)/shard_map/reduce_scatter | solution.py:68
  185.4 0.0 copy-done.2
  185.4 0.0 copy-done.3
  185.4 2.8 fusion.18
  188.2 0.0 all-gather.6.cloned.1.call-update
  188.2 0.2 reduce-scatter.6.cloned.1.call-start
  188.4 39.2 %all-gather.6.cloned.1.call-done = bf16[1024,1536]{1,0:T(8,128)(2,1)} async-done(((bf16[1024,384]{1,0:T(8,128)(2,1)}), bf16[1024,1536]{1,0:T(8,128)(2,1)}) %all-gather.6.cloned.1.call-update) | async-done | bytes 3145744 | tf_op jit(solution)/shard_map/all_gather | solution.py:79
  227.6 0.0 copy-start.4
  227.6 20.6 %multiply_reduce_fusion.1 = (f32[]{:T(128)}, f32[1536,1536]{1,0:T(8,128)}) fusion(bf16[1024,1536]{1,0:T(8,128)(2,1)} %all-gather.4.cloned.1.call-done, f32[1024,1536]{1,0:T(8,128)} %copy-done.5, bf16[1024,1536]{1,0:T(8,128)(2,1)} %all-gather.6.cloned.1.call-done, bf16[1536,1536]{1,0:T(8,128)(2,1)} %param.21), kind=kOutput, calls=%fused_computation.1 | convolution fusion | flops 9699852288 | bytes 26738692 | tf_op jit(solution)/shard_map/dot_general | solution.py:18
  248.3 0.0 copy-done.4
  248.3 10.7 %multiply_reduce_fusion = (f32[]{:T(128)}, f32[1536,1536]{1,0:T(8,128)}) fusion(bf16[1024,1536]{1,0:T(8,128)(2,1)S(1)} %copy-done.4, f32[1024,1536]{1,0:T(8,128)} %copy-done.5), kind=kOutput, calls=%fused_computation | convolution fusion | flops 4850712576 | bytes 18874372 | tf_op jit(solution)/shard_map/dot_general | solution.py:18
  260.3 9.7 %psum.31 = f32[1]{0:T(128)} all-reduce(f32[1]{0:T(128)} %bitcast.15), channel_id=1, replica_groups=mesh['dp'=32,'mp'=4] {'mp'}, use_global_device_ids=true, to_apply=%region_9.10 | all-reduce | flops 1 | bytes 8 | tf_op jit(solution)/shard_map/psum | solution.py:86
  270.7 8.4 %broadcast_multiply_fusion.1 = f32[1536,1536]{1,0:T(8,128)} fusion(f32[1536,1536]{1,0:T(8,128)} %get-tuple-element.11, f32[]{:T(128)} %bitcast.16), kind=kLoop, calls=%fused_computation.13 | loop fusion | flops 2359296 | bytes 18874372 | tf_op jit(solution)/shard_map/mul | solution.py:88
  279.2 0.0 reduce-scatter.6.cloned.1.call-update
  279.2 0.0 reduce-scatter.8.cloned.1.call-start
  279.3 0.0 copy-start.1
  279.3 8.5 %broadcast_multiply_fusion = f32[1536,1536]{1,0:T(8,128)} fusion(f32[1536,1536]{1,0:T(8,128)} %get-tuple-element.13, f32[]{:T(128)} %bitcast.16), kind=kLoop, calls=%fused_computation.12 | loop fusion | flops 2359296 | bytes 18874372 | tf_op jit(solution)/shard_map/mul | solution.py:89
  287.8 0.0 reduce-scatter.8.cloned.1.call-update
  287.8 86.6 %reduce-scatter.6.cloned.1.call-done = f32[48,1536]{1,0:T(8,128)} async-done(((f32[1536,1536]{1,0:T(8,128)}), f32[48,1536]{1,0:T(8,128)}) %reduce-scatter.6.cloned.1.call-update) | async-done | bytes 294928 | tf_op jit(solution)/shard_map/reduce_scatter | solution.py:91
  374.4 1.8 add_multiply_fusion.1
  376.2 97.2 %reduce-scatter.8.cloned.1.call-done = f32[48,1536]{1,0:T(8,128)} async-done(((f32[1536,1536]{1,0:T(8,128)}), f32[48,1536]{1,0:T(8,128)}) %reduce-scatter.8.cloned.1.call-update) | async-done | bytes 294928 | tf_op jit(solution)/shard_map/reduce_scatter | solution.py:92
  473.4 1.8 add_multiply_fusion
  475.2 0.0 copy-done.1
  (7 shorter events, 0.1 us)
Async XLA Ops:
  7.2 53.4 %copy-start = (bf16[1536,3,384]{2,0,1:T(8,128)(2,1)S(1)}, bf16[1536,3,384]{2,0,1:T(8,128)(2,1)}, u32[]{:S(2)}) copy-start(bf16[1536,3,384]{2,0,1:T(8,128)(2,1)} %param.19) | copy-start | bytes 10616836
  7.2 93.7 %all-gather.4.cloned.1.call-start = ((), (), s32[]{:S(2)}) async-start(), calls=%async_computation.3 | async-start | bytes 3932160 | tf_op jit(solution)/shard_map/all_gather | solution.py:60
  64.3 121.1 %reduce-scatter.4.cloned.1.call-start = ((), (), s32[]{:S(2)}) async-start(), calls=%async_computation.4 | async-start | bytes 7864320 | tf_op jit(solution)/shard_map/reduce_scatter | solution.py:68
  108.7 2.6 copy-start.5
  121.1 64.3 %copy-start.2 = (bf16[1024,384]{1,0:T(8,128)(2,1)S(1)}, bf16[1024,384]{1,0:T(8,128)(2,1)}, u32[]{:S(2)}) copy-start(bf16[1024,384]{1,0:T(8,128)(2,1)} %param.12) | copy-start | bytes 2359300
  121.1 64.3 %copy-start.3 = (bf16[1024,384]{1,0:T(8,128)(2,1)S(1)}, bf16[1024,384]{1,0:T(8,128)(2,1)}, u32[]{:S(2)}) copy-start(bf16[1024,384]{1,0:T(8,128)(2,1)} %param.13) | copy-start | bytes 2359300
  121.1 106.5 %all-gather.6.cloned.1.call-start = ((), (), s32[]{:S(2)}) async-start(), calls=%async_computation.5 | async-start | bytes 3932160 | tf_op jit(solution)/shard_map/all_gather | solution.py:79
  188.2 186.2 %reduce-scatter.6.cloned.1.call-start = ((), (), s32[]{:S(2)}) async-start(), calls=%async_computation.6 | async-start | bytes 9732096 | tf_op jit(solution)/shard_map/reduce_scatter | solution.py:91
  227.6 20.6 %copy-start.4 = (bf16[1024,1536]{1,0:T(8,128)(2,1)S(1)}, bf16[1024,1536]{1,0:T(8,128)(2,1)}, u32[]{:S(2)}) copy-start(bf16[1024,1536]{1,0:T(8,128)(2,1)} %all-gather.6.cloned.1.call-done) | copy-start | bytes 9437188
  279.2 194.1 %reduce-scatter.8.cloned.1.call-start = ((), (), s32[]{:S(2)}) async-start(), calls=%async_computation.7 | async-start | bytes 9732096 | tf_op jit(solution)/shard_map/reduce_scatter | solution.py:92
  279.3 195.9 %copy-start.1 = (bf16[1536,3,384]{2,0,1:T(8,128)(2,1)S(1)}, bf16[1536,3,384]{2,0,1:T(8,128)(2,1)}, u32[]{:S(2)}) copy-start(bf16[1536,3,384]{2,0,1:T(8,128)(2,1)} %param.19) | copy-start | bytes 10616836
Sparse Core Ops, SparseCore 0:
  64.4 36.4 all-gather.3
  121.2 64.1 reduce-scatter.3
  188.3 39.2 all-gather.5
  279.3 95.0 reduce-scatter.5
  378.5 94.8 reduce-scatter.7
where the time goes:
time: 482 us
  waiting for transfers between devices  323 us (67%)
  blocking collectives  54.1 us (11%)
  matrix products  54 us (11%)
  other arithmetic  29.3 us (6%)
  between operations  18.2 us (4%)
    reduce_scatter x1, waiting for transfers between devices, local(): lax.psum_scatter(total_second, 'dp', scatter_dimension=0, tiled=True)  97.2 us
    reduce_scatter x1, waiting for transfers between devices, local(): lax.psum_scatter(total_first, 'dp', scatter_dimension=0, tiled=True)  86.6 us
    reduce_scatter x1, waiting for transfers between devices, local(): lax.psum_scatter(partial_out, 'mp', scatter_dimension=1, tiled=True)  63.4 us
    all_gather x1, waiting for transfers between devices, local(): back_full = lax.all_gather(back_local, 'mp', axis=1, tiled=True)  39.2 us
    all_gather x1, waiting for transfers between devices, local(): lax.all_gather(shaped.reshape(row_total, -1), 'mp', axis=1, tiled=True)  36.5 us
    dot_general x2, matrix products, contract_rows(): lax.dot_general(left, right, (((0,), (0,)), ((), ())), preferred_element_...  31.4 us
    all_gather x1, blocking collectives, local(): everyone = lax.all_gather(activated, 'dp', axis=0, tiled=True)  26.2 us
    psum x1, blocking collectives, local(): lax.psum(jnp.dot(pooled, ctx_w, preferred_element_type=jnp.float32), 'mp')  18.2 us
  transfers between devices with their start and end apart: 5, of which 5 were waited for; matrix products, arithmetic and copies ran while one was open for 2% of the time, Pallas kernels for 0%

commit v1 on v0

v1 whole, which is shorter than its diff:
```python
import math

import jax
import jax.numpy as jnp
from jax import lax
from jax.experimental import pallas as pl
from jax.experimental.pallas import tpu as pltpu
from jax.sharding import PartitionSpec as P

D = 1536
FF = 6144
DRAWS = 4
BF = jnp.bfloat16
F32 = jnp.float32
RING = 4
PART = D // RING
WIDE = 512
VMEM_LIMIT = 32 * 1024 * 1024
C1 = math.sqrt(2.0 / math.pi)
C2 = 0.044715


def dot(left, right):
    return jnp.dot(left, right, preferred_element_type=F32)


def sign(core, way):
    return way if core == 0 else -way


def by_x(value, way):
    pairs = []
    for dp in range(32):
        for x in range(RING):
            pairs.append((dp * RING + x, dp * RING + (x + sign(dp % 2, way)) % RING))
    return lax.ppermute(value, ("dp", "mp"), pairs)


def by_dp(value, target):
    pairs = []
    for y in range(RING):
        for z in range(RING):
            for c in range(2):
                ty, tz, tc = target(y, z, c)
                pairs.append(((y * RING + z) * 2 + c, ((ty % RING) * RING + tz % RING) * 2 + tc))
    return lax.ppermute(value, "dp", pairs)


def by_turns(value, way, first):
    return by_dp(
        value,
        lambda y, z, c: (y + way, z, c) if (c == 0) == first else (y, z + way, c),
    )


def by_core(value):
    return by_dp(value, lambda y, z, c: (y, z, 1 - c))


def swap_x(value, kind):
    other = [x ^ 1 for x in range(RING)] if kind == 0 else [3 - x for x in range(RING)]
    return lax.ppermute(value, "mp", list(enumerate(other)))


def params():
    return pltpu.CompilerParams(vmem_limit_bytes=VMEM_LIMIT)


def shaped(shape, dtype=BF):
    return jax.ShapeDtypeStruct(shape, dtype)


def cost(flops, size, special=0):
    return pl.CostEstimate(flops=flops, bytes_accessed=size, transcendentals=special)


def in_hbm(value):
    return pltpu.with_memory_space_constraint(value, pltpu.HBM)


def whole(shape):
    return pl.BlockSpec(shape, lambda s, *_: (0, 0))


def columns(rows, width):
    return pl.BlockSpec((rows, width), lambda s, *_: (0, s))


def call(kernel, grid, in_specs, out_specs, out_shape, scratch, estimate, name, aliases={}):
    return pl.pallas_call(
        kernel,
        grid_spec=pltpu.PrefetchScalarGridSpec(
            num_scalar_prefetch=1,
            grid=(grid,),
            in_specs=in_specs,
            out_specs=out_specs,
            scratch_shapes=scratch,
        ),
        out_shape=out_shape,
        input_output_aliases=aliases,
        compiler_params=params(),
        cost_estimate=estimate,
        name=name,
    )


def forward_kernel(at, x0, x1, x2, x3, m0, m1, m2, in_w, modded_o, hidden, pre, mods, modded):
    step = pl.program_id(0)

    @pl.when(step == 0)
    def _():
        for place, ref, row in ((0, m0, 0), (1, m1, 0), (2, m2, 0), (3, m2, 3)):
            mods[:, pl.ds(pl.multiple_of(at[place], 128), PART)] = ref[row : row + 2]
        total = 0.0
        squares = 0.0
        for ref in (x0, x1, x2, x3):
            value = ref[...].astype(F32)
            total = total + jnp.sum(value, 1, keepdims=True)
            squares = squares + jnp.sum(value * value, 1, keepdims=True)
        center = total / D
        scale = lax.rsqrt(squares / D - center * center + 1e-06)
        for k, ref in enumerate((x0, x1, x2, x3)):
            cols = pl.ds(pl.multiple_of(at[8 + k] * PART, 128), PART)
            normed = (ref[...].astype(F32) - center) * scale
            modded[:, cols] = (normed * (1.0 + mods[1:2, cols]) + mods[0:1, cols]).astype(BF)

    modded_o[...] = modded[:, pl.ds(pl.multiple_of(step * WIDE, 128), WIDE)]
    value = dot(modded[...], in_w[...])
    pre[...] = value
    bent = jnp.tanh(value * (C1 + (C1 * C2) * (value * value)))
    hidden[...] = ((0.5 * value) * (1.0 + bent)).astype(BF)


def forward(chunk, at, blocks, mods, in_w):
    rows, ff = blocks[0].shape[0] // 2, in_w.shape[1]
    piece = pl.BlockSpec((rows, PART), lambda s, *_: (chunk, 0))
    return call(
        forward_kernel,
        ff // WIDE,
        [piece] * 4
        + [whole((3, PART)), whole((3, PART)), whole((6, PART)), columns(D, WIDE)],
        [columns(rows, WIDE)] * 3,
        [shaped((rows, D)), shaped((rows, ff)), shaped((rows, ff), F32)],
        [pltpu.VMEM((2, D), F32), pltpu.VMEM((rows, D), BF)],
        cost(2 * rows * D * ff, 12 * 10**6, rows * ff),
        "forward",
    )(at, *[in_hbm(b) for b in blocks], *mods, in_hbm(in_w))


def split_rows(at, turned, keep, send):
    mine = at[4]
    for z in range(RING):
        keep[z * 48 : (z + 1) * 48] = turned[pl.ds(pl.multiple_of(z * 96 + mine, 16), 48)]
        send[z * 48 : (z + 1) * 48] = turned[pl.ds(pl.multiple_of(z * 96 + 48 - mine, 16), 48)]


def turn_kernel(at, top, low, keep, send, turned):
    turned[:, : top.shape[0]] = top[...].T
    turned[:, top.shape[0] :] = low[...].T
    split_rows(at, turned, keep, send)


def turn(at, top, low):
    rows = top.shape[0]
    out = pl.BlockSpec((PART // 2, 2 * rows), lambda s, *_: (s, 0))
    return call(
        turn_kernel,
        RING,
        [columns(rows, PART)] * 2,
        [out, out],
        [shaped((D // 2, 2 * rows))] * 2,
        [pltpu.VMEM((PART, 2 * rows), BF)],
        cost(2 * rows * D, 8 * rows * D),
        "turn",
    )(at, top, low)


def backward_kernel(at, b0, b1, b2, b3, out_w, slope, grad, back):
    @pl.when(pl.program_id(0) == 0)
    def _():
        for k, ref in enumerate((b0, b1, b2, b3)):
            back[:, pl.ds(pl.multiple_of(at[8 + k] * PART, 128), PART)] = ref[...]

    grad[...] = (dot(back[...], out_w[...]) * slope[...].astype(F32)).astype(BF)


def backward(at, blocks, out_w, slope):
    rows, ff = slope.shape
    return call(
        backward_kernel,
        ff // WIDE,
        [whole((rows, PART))] * 4 + [columns(D, WIDE), columns(rows, WIDE)],
        columns(rows, WIDE),
        shaped((rows, ff)),
        [pltpu.VMEM((rows, D), BF)],
        cost(2 * rows * D * ff, 14 * 10**6),
        "backward",
    )(at, *blocks, out_w, slope)


def rows_kernel(count, at, *refs):
    tops, lows = refs[:count], refs[count : 2 * count]
    right0, right1 = refs[2 * count : 2 * count + 2]
    keep, send, square, turned = refs[-4:]
    rows = right0.shape[0]
    for k in range(count):

        @pl.when(pl.program_id(0) == k)
        def _():
            turned[:, :rows] = tops[k][...].T
            turned[:, rows:] = lows[k][...].T

    mine = at[4]
    for n in range(right0.shape[1] // 512):
        cols = slice(n * 512, (n + 1) * 512)
        value = dot(turned[:, :rows], right0[:, cols]) + dot(turned[:, rows:], right1[:, cols])
        piece = jnp.sum(value * value, 0, keepdims=True)

        @pl.when(pl.program_id(0) == 0)
        def _():
            square[:, cols] = piece

        @pl.when(pl.program_id(0) > 0)
        def _():
            square[:, cols] += piece

        for z in range(RING):
            low = value[z * 96 : z * 96 + 48].astype(BF)
            high = value[z * 96 + 48 : (z + 1) * 96].astype(BF)
            at_rows = slice(z * 48, (z + 1) * 48)
            keep[at_rows, cols] = jnp.where(mine == 0, low, high)
            send[at_rows, cols] = jnp.where(mine == 0, high, low)


def rows_grad(at, places, tops, lows, rights, before):
    rows, ff = rights[0].shape
    count = len(tops)
    first = places[0]
    step = places[1] - first if count > 1 else 0
    out = pl.BlockSpec((PART // 2, ff), lambda s, a: (a[8 + first + s * step], 0))
    return call(
        lambda *refs: rows_kernel(count, *refs),
        count,
        [whole((rows, PART))] * (2 * count)
        + [whole((rows, ff))] * 2
        + [pl.BlockSpec(memory_space=pl.ANY)] * len(before),
        [out, out, whole((1, ff))],
        [shaped((D // 2, ff))] * 2 + [shaped((1, ff), F32)],
        [pltpu.VMEM((PART, 2 * rows), BF)],
        cost(4 * rows * PART * ff * count, 5 * 10**6 * count),
        "rows_grad",
        {2 * count + 3 + n: n for n in range(len(before))},
    )(at, *tops, *lows, *rights, *before)


def weight_kernel(at, keep_l, send_l, right0, right1, q0, q1, q2, keep, send, square, sums):
    rows = right0.shape[0]
    keep_v = dot(keep_l[:, :rows], right0[...]) + dot(keep_l[:, rows:], right1[...])
    send_v = dot(send_l[:, :rows], right0[...]) + dot(send_l[:, rows:], right1[...])
    keep[...] = keep_v.astype(BF)
    send[...] = send_v.astype(BF)
    piece = jnp.sum(keep_v * keep_v, 0, keepdims=True) + jnp.sum(send_v * send_v, 0, keepdims=True)
    step = pl.program_id(0)

    @pl.when(step == 0)
    def _():
        sums[...] = piece

    @pl.when(step > 0)
    def _():
        sums[...] += piece

    @pl.when(step == pl.num_programs(0) - 1)
    def _():
        rest = q0[...] + q1[...] + q2[...]
        total = jnp.sum(sums[...], 1, keepdims=True) + jnp.sum(rest, 1, keepdims=True)
        square[...] = jnp.broadcast_to(total, square.shape)


def weight_grad(at, keep_l, send_l, rights, squares):
    rows, ff = rights[0].shape
    width = 512
    return call(
        weight_kernel,
        ff // width,
        [whole((D // 2, 2 * rows))] * 2 + [columns(rows, width)] * 2 + [whole((1, ff))] * 3,
        [columns(D // 2, width)] * 2 + [whole((1, 128))],
        [shaped((D // 2, ff))] * 2 + [shaped((1, 128), F32)],
        [pltpu.VMEM((1, width), F32)],
        cost(4 * rows * D * ff, 11 * 10**6),
        "weight_grad",
    )(at, keep_l, send_l, *rights, *squares)


def scaled(kept, got, u0, u1):
    return kept[...].astype(F32) * u0[0:1, 0:1] + got[...].astype(F32) * u1[0:1, 0:1]


def far_kernel(at, u0, u1, k1, k2, g1, g2, far1, far2):
    far1[0] = scaled(k1, g1, u0, u1).astype(BF)
    far2[0] = scaled(k2, g2, u0, u1).astype(BF)


def near_kernel(at, u0, u1, k1, k2, k3, k4, g1, g2, g3, g4, own, ahead2, behind1):
    own[0, 0] = scaled(k1, g1, u0, u1)
    own[0, 1] = scaled(k2, g2, u0, u1)
    behind1[0] = scaled(k3, g3, u0, u1).astype(BF)
    ahead2[0] = scaled(k4, g4, u0, u1).astype(BF)


def relay_kernel(at, u0, u1, k1, k2, g1, g2, up, down, ahead1, behind2):
    ahead1[0] = (scaled(k1, g1, u0, u1) + up[0].astype(F32)).astype(BF)
    behind2[0] = (scaled(k2, g2, u0, u1) + down[0].astype(F32)).astype(BF)


def close_kernel(at, own, up1, down1, up2, down2, out):
    out[0, 0] = (own[0, 0] + up1[0].astype(F32) + down1[0].astype(F32)).astype(BF)
    out[0, 1] = (own[0, 1] + up2[0].astype(F32) + down2[0].astype(F32)).astype(BF)


def ring_stage(at, u0, u1, first, second, move):
    ff = first[0].shape[1]
    block = lambda k: pl.BlockSpec((48, ff), lambda s, a: (a[12 + k] + s * a[5], 0))
    one = pl.BlockSpec((1, 48, ff), lambda s, *_: (s, 0, 0))
    both = pl.BlockSpec((1, 2, 48, ff), lambda s, *_: (s, 0, 0, 0))
    single = shaped((RING, 48, ff))
    unit = [whole((1, 128))] * 2
    size = RING * 48 * ff
    far1, far2 = call(
        far_kernel,
        RING,
        unit + [block(2)] * 4,
        [one, one],
        [single] * 2,
        [],
        cost(6 * size, 12 * size),
        "far",
    )(at, u0, u1, first[0], second[0], first[1], second[1])
    far1, far2 = move(far1, 1), move(far2, -1)
    order = [block(0), block(0), block(3), block(1)]
    own, ahead2, behind1 = call(
        near_kernel,
        RING,
        unit + order * 2,
        [both, one, one],
        [shaped((RING, 2, 48, ff), F32), single, single],
        [],
        cost(12 * size, 28 * size),
        "near",
    )(
        at, u0, u1, first[0], second[0], first[0], second[0],
        first[1], second[1], first[1], second[1],
    )
    up2, down1 = move(ahead2, 1), move(behind1, -1)
    ahead1, behind2 = call(
        relay_kernel,
        RING,
        unit + [block(1), block(3)] * 2 + [one, one],
        [one, one],
        [single] * 2,
        [],
        cost(8 * size, 16 * size),
        "relay",
    )(at, u0, u1, first[0], second[0], first[1], second[1], far1, far2)
    up1, down2 = move(ahead1, 1), move(behind2, -1)
    return call(
        close_kernel,
        RING,
        [both] + [one] * 4,
        both,
        shaped((RING, 2, 48, ff)),
        [],
        cost(4 * size, 20 * size),
        "close",
    )(at, own, up1, down1, up2, down2)


def local(
    latents,
    targets,
    tok_count,
    caption_states,
    cap_len,
    owner,
    ctx_w,
    mod_w,
    in_w,
    out_w,
    noise_in,
    noise_out,
):
    rows = latents.shape[0]
    token_span = rows // DRAWS
    me_x = lax.axis_index("mp")
    me_dp = lax.axis_index("dp")
    me_y, me_z, me_c = me_dp // 8, (me_dp // 2) % 4, me_dp % 2
    way = 1 - 2 * me_c

    ahead = [(me_x + k * way) % RING for k in range(RING)]
    swapped = [me_x, me_x ^ 1, 3 - me_x, (3 - me_x) ^ 1]
    me_one = jnp.where(me_c == 0, me_y, me_z)
    stride = jnp.where(me_c == 0, 4, 1)
    at = jnp.stack(
        [b * PART for b in swapped]
        + [me_c * 48, jnp.where(me_c == 0, 1, 4), me_c * 0, me_c * 0]
        + ahead
        + [((me_one + k) % RING) * stride for k in range(RING)]
    ).astype(jnp.int32)
    outs = [lax.dynamic_slice_in_dim(out_w, b * PART, PART, 0) for b in ahead]

    positions = jnp.arange(caption_states.shape[1])
    keep_mask = (positions[None, :] < cap_len[:, None]).astype(BF)
    summed = jnp.einsum("ec,ecf->ef", keep_mask, caption_states, preferred_element_type=F32)
    pooled = (summed / cap_len[:, None].astype(F32)).astype(BF).astype(F32)
    everywhere = jnp.broadcast_to(pooled.reshape(1, 8, -1), (32, 8, pooled.shape[1] // 8))
    received = lax.all_to_all(everywhere, "dp", 0, 0, tiled=True)

    behind, next_ahead = by_x(latents, 1), by_x(latents, -1)
    half = rows // 2
    received, behind, next_ahead, at, outs = lax.optimization_barrier(
        (received, behind, next_ahead, at, outs)
    )
    far = by_x(behind, 1)
    wanted = (owner == me_dp)[:, None, None]
    mine = jnp.sum(jnp.where(wanted, received, 0.0), 0).reshape(1, -1).astype(BF)

    context = dot(mine, ctx_w)
    context = context + swap_x(context, 0)
    swapped_context, far = lax.optimization_barrier((swap_x(context, 1), far))
    context = context + swapped_context
    conditioning = context * lax.rsqrt(jnp.mean(context * context, 1, keepdims=True) + 1e-06)
    chosen = jax.nn.silu(conditioning).astype(BF)
    modulation = jnp.einsum("ed,dkf->ekf", chosen, mod_w, preferred_element_type=F32)[0]
    gate = modulation[2:3]
    own_mods = modulation
    pair_mods = swap_x(own_mods, 0)
    far_mods = swap_x(jnp.concatenate([own_mods, pair_mods], 0), 1)
    mods = (own_mods, pair_mods, far_mods)

    count = tok_count[0]
    factor = 2.0 / (D * DRAWS * count.astype(F32))

    def slope_of(pre):
        square = pre * pre
        bent = jnp.tanh(pre * (C1 + (C1 * C2) * square))
        half = 0.5 * (1.0 + bent)
        return half + (0.5 * pre) * (1.0 - bent * bent) * (C1 + (3.0 * C1 * C2) * square)

    def project(hidden, j):
        return lax.dot_general(
            hidden, outs[j], (((1,), (1,)), ((), ())), preferred_element_type=F32
        )

    def leave(k, own, up, down):
        at_rows = slice(k * half, (k + 1) * half)
        output = latents[at_rows].astype(F32) + gate * (
            own + up.astype(F32) + down.astype(F32)
        )
        live = (jnp.arange(k * half, (k + 1) * half) % token_span < count).astype(F32)[:, None]
        delta = (output - targets[at_rows].astype(F32)) * live * factor
        return (gate * delta).astype(BF)

    latent_blocks = (latents, next_ahead, far, behind)
    modded0, hidden0, pre0 = forward(0, at, latent_blocks, mods, in_w)
    far0, down0 = project(hidden0, 2).astype(BF), project(hidden0, 3).astype(BF)
    far0 = by_x(far0, 1)
    at_next, down0 = lax.optimization_barrier((at, down0))
    down0 = by_x(down0, -1)
    up0, own0 = lax.optimization_barrier((project(hidden0, 1), project(hidden0, 0)))
    modded1, hidden1, pre1 = forward(1, at_next, latent_blocks, mods, in_w)
    hidden1, far0, down0 = lax.optimization_barrier((hidden1, far0, down0))
    up0 = by_x((up0 + far0.astype(F32)).astype(BF), 1)
    far1, up1 = project(hidden1, 2).astype(BF), project(hidden1, 1).astype(BF)
    far1, up1, hidden1, at_late, pre0, pre1 = lax.optimization_barrier(
        (far1, up1, hidden1, at, pre0, pre1)
    )
    far1, up1 = by_x(far1, -1), by_x(up1, 1)
    down1, own1 = lax.optimization_barrier((project(hidden1, 3), project(hidden1, 0)))
    back0 = leave(0, own0, up0, down0)
    behind0, ahead0 = by_x(back0, 1), by_x(back0, -1)
    down1 = by_x((down1 + far1.astype(F32)).astype(BF), -1)
    slope0, slope1 = slope_of(pre0).astype(BF), slope_of(pre1).astype(BF)
    mod_keep, mod_send = turn(at_late, modded0, modded1)
    down1, slope0, slope1, mod_keep, mod_send, behind0, ahead0 = lax.optimization_barrier(
        (down1, slope0, slope1, mod_keep, mod_send, behind0, ahead0)
    )
    back1 = leave(1, own1, up1, down1)
    far0 = by_x(behind0, 1)
    behind1, ahead1 = by_x(back1, 1), by_x(back1, -1)
    far1 = by_x(ahead1, -1)

    rights = (hidden0, hidden1)
    *second, square_a = rows_grad(at, (0,), (back0,), (back1,), rights, ())
    grad0 = backward(at, (back0, ahead0, far0, behind0), out_w, slope0)
    *second, square_b = rows_grad(
        at, (1, 3), (ahead0, behind0), (ahead1, behind1), rights, tuple(second)
    )
    grad1 = backward(at, (back1, ahead1, far1, behind1), out_w, slope1)
    *second, square_c = rows_grad(at, (2,), (far0,), (far1,), rights, tuple(second))
    keep2, send2 = second
    got2 = by_core(send2)
    keep1, send1, square = weight_grad(
        at, mod_keep, mod_send, (grad0, grad1), (square_a, square_b, square_c)
    )
    got1 = by_core(send1)
    square = square + swap_x(square, 0)
    square = square + swap_x(square, 1)
    root = math.sqrt(2.0 * D * FF)
    unit = root / (jnp.sqrt(square) + 0.01)

    value = ring_stage(
        at, unit, by_core(unit), (keep1, got1), (keep2, got2), lambda v, w: by_turns(v, w, True)
    )
    groups = [[(y * RING + z) * 2 for z in range(RING)] for y in range(RING)]
    groups += [[(y * RING + z) * 2 + 1 for y in range(RING)] for z in range(RING)]
    got = lax.all_to_all(value, "dp", 0, 0, axis_index_groups=groups, tiled=True)
    value = jnp.sum(got.astype(F32), 0)
    return (value[0] + noise_in) / 32.0, (value[1] + noise_out) / 32.0


def solution(mesh):
    placed = (
        P("dp", "mp"),
        P("dp", "mp"),
        P("dp"),
        P("dp", None, "mp"),
        P("dp"),
        P(),
        P("mp", None),
        P(None, None, "mp"),
        P(None, "mp"),
        P(None, "mp"),
        P("dp", "mp"),
        P("dp", "mp"),
    )
    return jax.shard_map(
        local, mesh=mesh, in_specs=placed, out_specs=(P("dp", "mp"), P("dp", "mp")), check_vma=False
    )
```

time: 482 us -> 194 us (0.40)
  waiting for transfers between devices: 323 us -> 53.1 us
  starting transfers between devices: 0.39 us -> 48.4 us
  Pallas kernels: 0 us -> 47.7 us
  matrix products: 54 us -> 12 us
  blocking collectives: 54.1 us -> 16.9 us
  other arithmetic: 29.3 us -> 6.79 us
  between operations: 18.2 us -> 3.23 us
    reduce_scatter x3 -> x0, waiting for transfers between devices: 247 us -> none  [the longest x1 97.2 us: local(): lax.psum_scatter(total_second, 'dp', scatter_dimension=0, tiled=True)]
    all_gather x2 -> x0, waiting for transfers between devices: 75.7 us -> none  [the longest x1 39.2 us: local(): back_full = lax.all_gather(back_local, 'mp', axis=1, tiled=True)]
    ppermute x0 -> x30, waiting for transfers between devices: none -> 50.1 us  [the longest x6 18.8 us: swap_x(): return lax.ppermute(value, 'mp', list(enumerate(other)))]
    pallas_call x0 -> x13, Pallas kernels: none -> 47.7 us  [the longest x2 15.8 us: forward(): call(forward_kernel, ff // WIDE, [piece] * 4 + [whole((3, PART)), whole((...]
    dot_general x7 -> x10, matrix products: 52.7 us -> 10.9 us  [the longest x8 7.91 us: project(): lax.dot_general(hidden, outs[j], (((1,), (1,)), ((), ())), preferred_elem...]
    ppermute x0 -> x30, starting transfers between devices: none -> 39.8 us  [the longest x15 21 us: by_x(): return lax.ppermute(value, ('dp', 'mp'), pairs)]
    psum x2 -> x0, blocking collectives: 27.9 us -> none  [the longest x1 18.2 us: local(): lax.psum(jnp.dot(pooled, ctx_w, preferred_element_type=jnp.float32), 'mp')]
    all_gather x1 -> x0, blocking collectives: 26.2 us -> none  [local(): everyone = lax.all_gather(activated, 'dp', axis=0, tiled=True)]
  transfers between devices with their start and end apart: 5 -> 31, of which waited for: 5 -> 18; matrix products, arithmetic and copies ran while one was open for 2% -> 9% of each run, Pallas kernels for 0% -> 13%
where the time goes in v1:
time: 194 us
  waiting for transfers between devices  53.1 us (27%)
  starting transfers between devices  48.4 us (25%)
  Pallas kernels  47.7 us (25%)
  blocking collectives  16.9 us (9%)
  matrix products  12 us (6%)
  other arithmetic  6.79 us (4%)
  local copies, waits for them, and re-layouts  5.89 us (3%)
  between operations  3.23 us (2%)
    ppermute x15, starting transfers between devices, by_x(): return lax.ppermute(value, ('dp', 'mp'), pairs)  21 us
    ppermute x6, waiting for transfers between devices, swap_x(): return lax.ppermute(value, 'mp', list(enumerate(other)))  18.8 us
    ppermute x15, waiting for transfers between devices, by_x(): return lax.ppermute(value, ('dp', 'mp'), pairs)  18.2 us
    all_to_all x1, blocking collectives, local(): lax.all_to_all(value, 'dp', 0, 0, axis_index_groups=groups, tiled=True)  16.9 us
    pallas_call x2, Pallas kernels, forward(): call(forward_kernel, ff // WIDE, [piece] * 4 + [whole((3, PART)), whole((...  15.8 us
    ppermute x9, waiting for transfers between devices, by_dp(): return lax.ppermute(value, 'dp', pairs)  13.2 us
    ppermute x6, starting transfers between devices, swap_x(): return lax.ppermute(value, 'mp', list(enumerate(other)))  9.43 us
    ppermute x9, starting transfers between devices, by_dp(): return lax.ppermute(value, 'dp', pairs)  9.41 us
  transfers between devices with their start and end apart: 31, of which 18 were waited for; matrix products, arithmetic and copies ran while one was open for 9% of the time, Pallas kernels for 13%

profile of v1, /device:TPU:0, one launch (start us, length us, event | category | flops | bytes accessed | tf_op | source)
XLA Modules:
  0.0 194.0 jit_solution(14633234345888329219)
XLA Ops:
  0.6 1.6 collective-permute-start
  2.3 1.7 collective-permute-start.1
  6.4 8.5 %all-to-all-start = ((f32[32,8,128]{2,1,0:T(8,128)}), f32[32,8,128]{2,1,0:T(8,128)}, u32[]{:S(2)}, u32[]{:S(2)}) async-start(f32[32,8,128]{2,1,0:T(8,128)} %broadcast_in_dim.31), calls=%async_computation | async-start | bytes 262144 | tf_op jit(solution)/shard_map/all_to_all | solution.py:416
  15.1 4.6 %constant_dynamic-slice_fusion = (bf16[384,1536]{1,0:T(8,128)(2,1)}, bf16[384,1536]{1,0:T(8,128)(2,1)}, bf16[384,1536]{1,0:T(8,128)(2,1)}, bf16[384,1536]{1,0:T(8,128)(2,1)}) fusion(bf16[1536,1536]{1,0:T(8,128)(2,1)} %out_w.3, s32[]{:T(128)S(6)} %select_n.112, s32[]{:T(128)S(6)} %select_n.111, s32[]{:T(128)S(6)} %select_n.110, s32[]{:T(128)S(6)} %select_n.109), kind=kLoop, calls=%fused_computation.51 | loop fusion | bytes 9437200 | tf_op jit(solution)/shard_map/dynamic_slice | solution.py:409
  19.7 3.0 %all-to-all-done = f32[32,8,128]{2,1,0:T(8,128)} async-done(((f32[32,8,128]{2,1,0:T(8,128)}), f32[32,8,128]{2,1,0:T(8,128)}, u32[]{:S(2)}, u32[]{:S(2)}) %all-to-all-start) | async-done | bytes 131104 | tf_op jit(solution)/shard_map/all_to_all | solution.py:416
  24.1 2.4 %fusion.27 = f32[1,1536]{1,0:T(1,128)S(1)} fusion(bf16[1024,1]{0,1:T(2,128)(2,1)S(1)} %reshape.95, bf16[1024,1536]{1,0:T(8,128)(2,1)} %param.18), kind=kOutput, calls=%fused_computation.60 | convolution fusion | flops 3145728 | bytes 3153920 | tf_op jit(solution)/shard_map/dot_general | solution.py:24
  26.5 1.5 collective-permute-start.2
  28.7 4.3 %collective-permute-done.2 = f32[1,1536]{1,0:T(1,128)S(1)} collective-permute-done((f32[1,1536]{1,0:T(1,128)S(1)}, f32[1,1536]{1,0:T(1,128)S(1)}, u32[]{:S(2)}, u32[]{:S(2)}) %collective-permute-start.2) | collective-permute-done | bytes 6176 | tf_op jit(solution)/shard_map/ppermute | solution.py:62
  33.0 3.9 %collective-permute-start.3 = (f32[1,1536]{1,0:T(1,128)S(1)}, f32[1,1536]{1,0:T(1,128)S(1)}, u32[]{:S(2)}, u32[]{:S(2)}) collective-permute-start(f32[1,1536]{1,0:T(1,128)S(1)} %add.191), channel_id=1, source_target_pairs={{0,3},{1,2},{2,1},{3,0},{4,7},{5,6},{6,5},{7,4},{8,11},{9,10},{10,... | collective-permute-start | bytes 18440 | tf_op jit(solution)/shard_map/ppermute | solution.py:62
  36.9 1.6 collective-permute-done.3
  41.4 2.9 %collective-permute-done.5.m1 = f32[3,384]{1,0:T(4,128)S(1)} collective-permute-done((f32[3,384]{1,0:T(4,128)S(1)}, f32[3,384]{1,0:T(4,128)S(1)}, u32[]{:S(2)}, u32[]{:S(2)}) %collective-permute-start.5) | collective-permute-done | bytes 4640 | tf_op jit(solution)/shard_map/ppermute | solution.py:62
  44.3 3.3 %collective-permute-start.6 = (f32[6,384]{1,0:T(8,128)S(1)}, f32[6,384]{1,0:T(8,128)S(1)}, u32[]{:S(2)}, u32[]{:S(2)}) collective-permute-start(f32[6,384]{1,0:T(8,128)S(1)} %pad_maximum_fusion), channel_id=1, source_target_pairs={{0,3},{1,2},{2,1},{3,0},{4,7},{5,6},{6,5},{7,4},{8,11},{9,10},{10,... | collective-permute-start | bytes 27656 | tf_op jit(solution)/shard_map/ppermute | solution.py:62
  47.7 1.6 collective-permute-done.6.m2
  49.3 7.9 %forward.2 = (bf16[512,1536]{1,0:T(8,128)(2,1)S(1)}, bf16[512,1536]{1,0:T(8,128)(2,1)S(1)}, f32[512,1536]{1,0:T(8,128)S(1)}) custom-call(s32[16]{0:T(128)S(1)} %stack.59.at.refs_0_, bf16[1024,384]{1,0:T(8,128)(2,1)} %x0.3, bf16[1024,384]{1,0:T(8,128)(2,1)} %collective-permute-done.1.x1, bf16[1024,384]{1,0:T(8,128)(2,1)} %copy-done.10, ...), custom_call_target="tpu_custom_call" | custom-call | flops 2415919104 | bytes 12000000 | tf_op jit(solution)/shard_map/forward/pallas_call | solution.py:137
  59.6 3.5 %collective-permute-start.8 = (bf16[512,384]{1,0:T(8,128)(2,1)S(1)}, bf16[512,384]{1,0:T(8,128)(2,1)S(1)}, u32[]{:S(2)}, u32[]{:S(2)}) collective-permute-start(bf16[512,384]{1,0:T(8,128)(2,1)S(1)} %convolution_convert_fusion.3), channel_id=1, source_target_pairs={{0,3},{1,0},{2,1},{3,2},{4,5},{5,6},{6,7},{7,4},{8,11},{9,8},{10,9... | collective-permute-start | bytes 1179656 | tf_op jit(solution)/shard_map/ppermute | solution.py:36
  65.1 7.9 %forward.3 = (bf16[512,1536]{1,0:T(8,128)(2,1)S(1)}, bf16[512,1536]{1,0:T(8,128)(2,1)S(1)}, f32[512,1536]{1,0:T(8,128)S(1)}) custom-call(s32[16]{0:T(128)S(1)} %stack.59.at.refs_0_, bf16[1024,384]{1,0:T(8,128)(2,1)} %x0.3, bf16[1024,384]{1,0:T(8,128)(2,1)} %collective-permute-done.1.x1, bf16[1024,384]{1,0:T(8,128)(2,1)} %copy-done.10, ...), custom_call_target="tpu_custom_call" | custom-call | flops 2415919104 | bytes 12000000 | tf_op jit(solution)/shard_map/forward/pallas_call | solution.py:137
  76.1 3.3 %collective-permute-start.9 = (bf16[512,384]{1,0:T(8,128)(2,1)S(1)}, bf16[512,384]{1,0:T(8,128)(2,1)S(1)}, u32[]{:S(2)}, u32[]{:S(2)}) collective-permute-start(bf16[512,384]{1,0:T(8,128)(2,1)S(1)} %convolution_convert_fusion.1), channel_id=1, source_target_pairs={{0,3},{1,0},{2,1},{3,2},{4,5},{5,6},{6,7},{7,4},{8,11},{9,8},{10,9... | collective-permute-start | bytes 1179656 | tf_op jit(solution)/shard_map/ppermute | solution.py:36
  80.5 6.0 %collective-permute-done.11 = bf16[512,384]{1,0:T(8,128)(2,1)S(1)} collective-permute-done((bf16[512,384]{1,0:T(8,128)(2,1)S(1)}, bf16[512,384]{1,0:T(8,128)(2,1)S(1)}, u32[]{:S(2)}, u32[]{:S(2)}) %collective-permute-start.11) | collective-permute-done | bytes 393248 | tf_op jit(solution)/shard_map/ppermute | solution.py:36
  86.9 3.2 %collective-permute-start.13 = (bf16[512,384]{1,0:T(8,128)(2,1)S(1)}, bf16[512,384]{1,0:T(8,128)(2,1)S(1)}, u32[]{:S(2)}, u32[]{:S(2)}) collective-permute-start(bf16[512,384]{1,0:T(8,128)(2,1)S(1)} %multiply_convert_fusion.1.b0.refs_1_), channel_id=1, source_target_pairs={{0,3},{1,0},{2,1},{3,2},{4,5},{5,6},{6,7},{7,4},{8,11},{9,8},{10,9... | collective-permute-start | bytes 1179656 | tf_op jit(solution)/shard_map/ppermute | solution.py:36
  90.2 2.7 %collective-permute-start.10 = (bf16[512,384]{1,0:T(8,128)(2,1)S(1)}, bf16[512,384]{1,0:T(8,128)(2,1)S(1)}, u32[]{:S(2)}, u32[]{:S(2)}) collective-permute-start(bf16[512,384]{1,0:T(8,128)(2,1)S(1)} %add_convert_fusion.3), channel_id=1, source_target_pairs={{0,3},{1,0},{2,1},{3,2},{4,5},{5,6},{6,7},{7,4},{8,11},{9,8},{10,9... | collective-permute-start | bytes 1179656 | tf_op jit(solution)/shard_map/ppermute | solution.py:36
  92.8 3.2 %add_convert_fusion = (bf16[512,1536]{1,0:T(8,128)(2,1)S(1)}, bf16[512,1536]{1,0:T(8,128)(2,1)S(1)}) fusion(f32[512,1536]{1,0:T(8,128)S(1)} %get-tuple-element.82, f32[512,1536]{1,0:T(8,128)S(1)} %get-tuple-element.81), kind=kLoop, calls=%fused_computation | loop fusion | flops 23592960 | bytes 9437184 | tf_op jit(solution)/shard_map/convert_element_type | solution.py:482
  96.0 2.2 %turn.1 = (bf16[768,1024]{1,0:T(8,128)(2,1)S(1)}, bf16[768,1024]{1,0:T(8,128)(2,1)S(1)}) custom-call(s32[16]{0:T(128)S(1)} %stack.59.at.refs_0_, bf16[512,1536]{1,0:T(8,128)(2,1)S(1)} %get-tuple-element.84.top, bf16[512,1536]{1,0:T(8,128)(2,1)S(1)} %get-tuple-element.85.low), custom_call_target="tpu_custom_call" | custom-call | flops 1572864 | bytes 6291456 | tf_op jit(solution)/shard_map/turn/pallas_call | solution.py:166
  98.3 1.4 collective-permute-done.10
  99.6 2.5 %collective-permute-done.12.b3.refs_2_ = bf16[512,384]{1,0:T(8,128)(2,1)S(1)} collective-permute-done((bf16[512,384]{1,0:T(8,128)(2,1)S(1)}, bf16[512,384]{1,0:T(8,128)(2,1)S(1)}, u32[]{:S(2)}, u32[]{:S(2)}) %collective-permute-start.12) | collective-permute-done | bytes 393248 | tf_op jit(solution)/shard_map/ppermute | solution.py:36
  102.5 1.3 collective-permute-start.16
  104.6 2.0 %rows_grad.3 = (bf16[768,1536]{1,0:T(8,128)(2,1)S(1)}, bf16[768,1536]{1,0:T(8,128)(2,1)S(1)}, f32[1,1536]{1,0:T(1,128)S(1)}) custom-call(s32[16]{0:T(128)S(1)} %stack.59.at.refs_0_, bf16[512,384]{1,0:T(8,128)(2,1)S(1)} %multiply_convert_fusion.1.b0.refs_1_, bf16[512,384]{1,0:T(8,128)(2,1)S(1)} %multiply_convert_fusion.b0.refs_2_, ...), custom_call_target="tpu_custom_call" | custom-call | flops 1207959552 | bytes 5000000 | tf_op jit(solution)/shard_map/rows_grad/pallas_call | solution.py:241
  106.6 8.0 %collective-permute-done.16.b1.refs_3_ = bf16[512,384]{1,0:T(8,128)(2,1)S(1)} collective-permute-done((bf16[512,384]{1,0:T(8,128)(2,1)S(1)}, bf16[512,384]{1,0:T(8,128)(2,1)S(1)}, u32[]{:S(2)}, u32[]{:S(2)}) %collective-permute-start.16) | collective-permute-done | bytes 393248 | tf_op jit(solution)/shard_map/ppermute | solution.py:36
  114.6 2.3 %collective-permute-start.17 = (bf16[512,384]{1,0:T(8,128)(2,1)S(1)}, bf16[512,384]{1,0:T(8,128)(2,1)S(1)}, u32[]{:S(2)}, u32[]{:S(2)}) collective-permute-start(bf16[512,384]{1,0:T(8,128)(2,1)S(1)} %collective-permute-done.16.b1.refs_3_), channel_id=1, source_target_pairs={{0,3},{1,0},{2,1},{3,2},{4,5},{5,6},{6,7},{7,4},{8,11},{9,8},{10,9... | collective-permute-start | bytes 1179656 | tf_op jit(solution)/shard_map/ppermute | solution.py:36
  117.0 4.2 %backward.2.right0 = bf16[512,1536]{1,0:T(8,128)(2,1)S(1)} custom-call(s32[16]{0:T(128)S(1)} %stack.59.at.refs_0_, bf16[512,384]{1,0:T(8,128)(2,1)S(1)} %multiply_convert_fusion.1.b0.refs_1_, bf16[512,384]{1,0:T(8,128)(2,1)S(1)} %collective-permute-done.13.b1.refs_1_, bf16[512,384]{1,0:T(8,128)(2,1)S(1)} %collective-permute-done.14.b2.refs_1_, ...), custom_call_target="tpu_custom_call" | custom-call | flops 2415919104 | bytes 14000000 | tf_op jit(solution)/shard_map/backward/pallas_call | solution.py:189
  121.4 4.8 %rows_grad.4 = (bf16[768,1536]{1,0:T(8,128)(2,1)S(1)}, bf16[768,1536]{1,0:T(8,128)(2,1)S(1)}, f32[1,1536]{1,0:T(1,128)S(1)}) custom-call(s32[16]{0:T(128)S(1)} %stack.59.at.refs_0_, bf16[512,384]{1,0:T(8,128)(2,1)S(1)} %collective-permute-done.13.b1.refs_1_, ...), custom_call_target="tpu_custom_call", output_to_operand_aliasing={{0}: (7, {}), {1}: (8, {})} | custom-call | flops 2415919104 | bytes 10000000 | tf_op jit(solution)/shard_map/rows_grad/pallas_call | solution.py:241
  126.3 4.2 %backward.3.right1 = bf16[512,1536]{1,0:T(8,128)(2,1)S(1)} custom-call(s32[16]{0:T(128)S(1)} %stack.59.at.refs_0_, bf16[512,384]{1,0:T(8,128)(2,1)S(1)} %multiply_convert_fusion.b0.refs_2_, bf16[512,384]{1,0:T(8,128)(2,1)S(1)} %collective-permute-done.16.b1.refs_3_, bf16[512,384]{1,0:T(8,128)(2,1)S(1)} %collective-permute-done.17.b2.refs_2_, ...), custom_call_target="tpu_custom_call" | custom-call | flops 2415919104 | bytes 14000000 | tf_op jit(solution)/shard_map/backward/pallas_call | solution.py:189
  130.4 2.0 %rows_grad.5 = (bf16[768,1536]{1,0:T(8,128)(2,1)S(1)}, bf16[768,1536]{1,0:T(8,128)(2,1)S(1)}, f32[1,1536]{1,0:T(1,128)S(1)}) custom-call(s32[16]{0:T(128)S(1)} %stack.59.at.refs_0_, bf16[512,384]{1,0:T(8,128)(2,1)S(1)} %collective-permute-done.14.b2.refs_1_, ...), custom_call_target="tpu_custom_call", output_to_operand_aliasing={{0}: (5, {}), {1}: (6, {})} | custom-call | flops 1207959552 | bytes 5000000 | tf_op jit(solution)/shard_map/rows_grad/pallas_call | solution.py:241
  132.4 6.7 %weight_grad.1 = (bf16[768,1536]{1,0:T(8,128)(2,1)S(1)}, bf16[768,1536]{1,0:T(8,128)(2,1)S(1)}, f32[1,128]{1,0:T(1,128)S(1)}) custom-call(s32[16]{0:T(128)S(1)} %stack.59.at.refs_0_, bf16[768,1024]{1,0:T(8,128)(2,1)S(1)} %get-tuple-element.92.keep_l, bf16[768,1024]{1,0:T(8,128)(2,1)S(1)} %get-tuple-element.93.send_l, bf16[512,1536]{1,0:T(8,128)(2,1)S(1)} %backward.2.right0, ...), custom_call_target="tpu_custom_call" | custom-call | flops 4831838208 | bytes 11000000 | tf_op jit(solution)/shard_map/weight_grad/pallas_call | solution.py:283
  139.7 3.5 %collective-permute-done.19 = f32[1,128]{1,0:T(1,128)S(1)} collective-permute-done((f32[1,128]{1,0:T(1,128)S(1)}, f32[1,128]{1,0:T(1,128)S(1)}, u32[]{:S(2)}, u32[]{:S(2)}) %collective-permute-start.19) | collective-permute-done | bytes 544 | tf_op jit(solution)/shard_map/ppermute | solution.py:62
  143.2 4.7 %collective-permute-done.20 = f32[1,128]{1,0:T(1,128)S(1)} collective-permute-done((f32[1,128]{1,0:T(1,128)S(1)}, f32[1,128]{1,0:T(1,128)S(1)}, u32[]{:S(2)}, u32[]{:S(2)}) %collective-permute-start.20) | collective-permute-done | bytes 544 | tf_op jit(solution)/shard_map/ppermute | solution.py:62
  148.1 1.1 collective-permute-done.21.u1
  149.2 1.4 far.1
  150.6 1.3 collective-permute-start.24
  151.9 2.0 %collective-permute-start.25 = (bf16[4,48,1536]{2,1,0:T(8,128)(2,1)S(1)}, bf16[4,48,1536]{2,1,0:T(8,128)(2,1)S(1)}, u32[]{:S(2)}, u32[]{:S(2)}) collective-permute-start(bf16[4,48,1536]{2,1,0:T(8,128)(2,1)S(1)} %get-tuple-element.115), channel_id=1, source_target_pairs={{0,96},{4,28},{8,104},{12,4},{16,112},{20,12},{24,120},{28,20},{32... | collective-permute-start | bytes 1769480 | tf_op jit(solution)/shard_map/ppermute | solution.py:46
  153.9 1.9 near.1
  155.8 1.6 collective-permute-start.27
  157.9 3.8 %collective-permute-done.24.up = bf16[4,48,1536]{2,1,0:T(8,128)(2,1)S(1)} collective-permute-done((bf16[4,48,1536]{2,1,0:T(8,128)(2,1)S(1)}, bf16[4,48,1536]{2,1,0:T(8,128)(2,1)S(1)}, u32[]{:S(2)}, u32[]{:S(2)}) %collective-permute-start.24) | collective-permute-done | bytes 589856 | tf_op jit(solution)/shard_map/ppermute | solution.py:46
  161.8 1.6 relay.1
  163.5 1.6 collective-permute-start.26
  165.1 1.7 collective-permute-start.29
  166.8 1.3 collective-permute-done.27.down1
  168.5 6.3 %collective-permute-done.26.up1 = bf16[4,48,1536]{2,1,0:T(8,128)(2,1)S(1)} collective-permute-done((bf16[4,48,1536]{2,1,0:T(8,128)(2,1)S(1)}, bf16[4,48,1536]{2,1,0:T(8,128)(2,1)S(1)}, u32[]{:S(2)}, u32[]{:S(2)}) %collective-permute-start.26) | collective-permute-done | bytes 589856 | tf_op jit(solution)/shard_map/ppermute | solution.py:46
  176.0 16.9 %all_to_all.10 = bf16[4,2,48,1536]{3,2,1,0:T(8,128)(2,1)S(1)} all-to-all(bf16[4,2,48,1536]{3,2,1,0:T(8,128)(2,1)S(1)} %close.1), channel_id=1, replica_groups={{0,8,16,24},{32,40,48,56},{64,72,80,88},{96,104,112,120},{4,36,68,100},..., dimensions={0} | all-to-all | bytes 2359296 | tf_op jit(solution)/shard_map/all_to_all | solution.py:516
  (92 shorter events, 19.7 us)
Async XLA Ops:
  0.6 39.4 %copy-start = (bf16[1536,3,384]{2,0,1:T(8,128)(2,1)S(1)}, bf16[1536,3,384]{2,0,1:T(8,128)(2,1)}, u32[]{:S(2)}) copy-start(bf16[1536,3,384]{2,0,1:T(8,128)(2,1)} %param.19) | copy-start | bytes 10616836
  0.6 22.1 %collective-permute-start = (bf16[1024,384]{1,0:T(8,128)(2,1)}, bf16[1024,384]{1,0:T(8,128)(2,1)}, u32[]{:S(2)}, u32[]{:S(2)}) collective-permute-start(bf16[1024,384]{1,0:T(8,128)(2,1)} %x0.3), channel_id=1, source_target_pairs={{0,1},{1,2},{2,3},{3,0},{4,7},{5,4},{6,5},{7,6},{8,9},{9,10},{10,1... | collective-permute-start | bytes 2359304 | tf_op jit(solution)/shard_map/ppermute | solution.py:36
  2.3 20.5 %collective-permute-start.1 = (bf16[1024,384]{1,0:T(8,128)(2,1)}, bf16[1024,384]{1,0:T(8,128)(2,1)}, u32[]{:S(2)}, u32[]{:S(2)}) collective-permute-start(bf16[1024,384]{1,0:T(8,128)(2,1)} %x0.3), channel_id=1, source_target_pairs={{0,3},{1,0},{2,1},{3,2},{4,5},{5,6},{6,7},{7,4},{8,11},{9,8},{10,9... | collective-permute-start | bytes 2359304 | tf_op jit(solution)/shard_map/ppermute | solution.py:36
  6.4 16.4 %all-to-all-start = ((f32[32,8,128]{2,1,0:T(8,128)}), f32[32,8,128]{2,1,0:T(8,128)}, u32[]{:S(2)}, u32[]{:S(2)}) async-start(f32[32,8,128]{2,1,0:T(8,128)} %broadcast_in_dim.31), calls=%async_computation | async-start | bytes 262144 | tf_op jit(solution)/shard_map/all_to_all | solution.py:416
  15.0 8.0 %copy-start.11 = (s32[32]{0:T(128)S(1)}, s32[32]{0:T(128)}, u32[]{:S(2)}) copy-start(s32[32]{0:T(128)} %param.17) | copy-start | bytes 388
  22.8 15.7 %collective-permute-start.4 = (bf16[1024,384]{1,0:T(8,128)(2,1)}, bf16[1024,384]{1,0:T(8,128)(2,1)S(1)}, u32[]{:S(2)}, u32[]{:S(2)}) collective-permute-start(bf16[1024,384]{1,0:T(8,128)(2,1)} %collective-permute-done.x3), channel_id=1, source_target_pairs={{0,1},{1,2},{2,3},{3,0},{4,7},{5,4},{6,5},{7,6},{8,9},{9,10},{10,1... | collective-permute-start | bytes 2359304 | tf_op jit(solution)/shard_map/ppermute | solution.py:36
  26.5 6.5 %collective-permute-start.2 = (f32[1,1536]{1,0:T(1,128)S(1)}, f32[1,1536]{1,0:T(1,128)S(1)}, u32[]{:S(2)}, u32[]{:S(2)}) collective-permute-start(f32[1,1536]{1,0:T(1,128)S(1)} %fusion.27), channel_id=1, source_target_pairs={{0,1},{1,0},{2,3},{3,2},{4,5},{5,4},{6,7},{7,6},{8,9},{9,8},{10,11... | collective-permute-start | bytes 18440 | tf_op jit(solution)/shard_map/ppermute | solution.py:62
  33.0 5.5 %collective-permute-start.3 = (f32[1,1536]{1,0:T(1,128)S(1)}, f32[1,1536]{1,0:T(1,128)S(1)}, u32[]{:S(2)}, u32[]{:S(2)}) collective-permute-start(f32[1,1536]{1,0:T(1,128)S(1)} %add.191), channel_id=1, source_target_pairs={{0,3},{1,2},{2,1},{3,0},{4,7},{5,6},{6,5},{7,4},{8,11},{9,10},{10,... | collective-permute-start | bytes 18440 | tf_op jit(solution)/shard_map/ppermute | solution.py:62
  38.5 0.9 copy-start.10
  40.6 3.7 %collective-permute-start.5 = (f32[3,384]{1,0:T(4,128)S(1)}, f32[3,384]{1,0:T(4,128)S(1)}, u32[]{:S(2)}, u32[]{:S(2)}) collective-permute-start(f32[3,384]{1,0:T(4,128)S(1)} %bitcast.74), channel_id=1, source_target_pairs={{0,1},{1,0},{2,3},{3,2},{4,5},{5,4},{6,7},{7,6},{8,9},{9,8},{10,11... | collective-permute-start | bytes 13832 | tf_op jit(solution)/shard_map/ppermute | solution.py:62
  44.3 5.0 %collective-permute-start.6 = (f32[6,384]{1,0:T(8,128)S(1)}, f32[6,384]{1,0:T(8,128)S(1)}, u32[]{:S(2)}, u32[]{:S(2)}) collective-permute-start(f32[6,384]{1,0:T(8,128)S(1)} %pad_maximum_fusion), channel_id=1, source_target_pairs={{0,3},{1,2},{2,1},{3,0},{4,7},{5,6},{6,5},{7,4},{8,11},{9,10},{10,... | collective-permute-start | bytes 27656 | tf_op jit(solution)/shard_map/ppermute | solution.py:62
  47.6 9.6 %copy-start.3 = (bf16[384,1536]{1,0:T(8,128)(2,1)S(1)}, bf16[384,1536]{1,0:T(8,128)(2,1)}, u32[]{:S(2)}) copy-start(bf16[384,1536]{1,0:T(8,128)(2,1)} %get-tuple-element.68) | copy-start | bytes 3538948
  57.2 1.3 copy-start.5
  58.5 4.6 %copy-start.4 = (bf16[384,1536]{1,0:T(8,128)(2,1)S(1)}, bf16[384,1536]{1,0:T(8,128)(2,1)}, u32[]{:S(2)}) copy-start(bf16[384,1536]{1,0:T(8,128)(2,1)} %get-tuple-element.74) | copy-start | bytes 3538948
  59.5 4.6 %copy-start.2 = (bf16[384,1536]{1,0:T(8,128)(2,1)S(1)}, bf16[384,1536]{1,0:T(8,128)(2,1)}, u32[]{:S(2)}) copy-start(bf16[384,1536]{1,0:T(8,128)(2,1)} %get-tuple-element.78) | copy-start | bytes 3538948
  59.5 13.4 %collective-permute-start.7 = (bf16[512,384]{1,0:T(8,128)(2,1)S(1)}, bf16[512,384]{1,0:T(8,128)(2,1)S(1)}, u32[]{:S(2)}, u32[]{:S(2)}) collective-permute-start(bf16[512,384]{1,0:T(8,128)(2,1)S(1)} %convolution_convert_fusion.2), channel_id=1, source_target_pairs={{0,1},{1,2},{2,3},{3,0},{4,7},{5,4},{6,5},{7,6},{8,9},{9,10},{10,1... | collective-permute-start | bytes 1179656 | tf_op jit(solution)/shard_map/ppermute | solution.py:36
  59.6 13.4 %collective-permute-start.8 = (bf16[512,384]{1,0:T(8,128)(2,1)S(1)}, bf16[512,384]{1,0:T(8,128)(2,1)S(1)}, u32[]{:S(2)}, u32[]{:S(2)}) collective-permute-start(bf16[512,384]{1,0:T(8,128)(2,1)S(1)} %convolution_convert_fusion.3), channel_id=1, source_target_pairs={{0,3},{1,0},{2,1},{3,2},{4,5},{5,6},{6,7},{7,4},{8,11},{9,8},{10,9... | collective-permute-start | bytes 1179656 | tf_op jit(solution)/shard_map/ppermute | solution.py:36
  75.0 11.4 %collective-permute-start.11 = (bf16[512,384]{1,0:T(8,128)(2,1)S(1)}, bf16[512,384]{1,0:T(8,128)(2,1)S(1)}, u32[]{:S(2)}, u32[]{:S(2)}) collective-permute-start(bf16[512,384]{1,0:T(8,128)(2,1)S(1)} %add_convert_fusion.2), channel_id=1, source_target_pairs={{0,1},{1,2},{2,3},{3,0},{4,7},{5,4},{6,5},{7,6},{8,9},{9,10},{10,1... | collective-permute-start | bytes 1179656 | tf_op jit(solution)/shard_map/ppermute | solution.py:36
  76.1 10.3 %copy-start.6 = (bf16[1024,384]{1,0:T(8,128)(2,1)S(1)}, bf16[1024,384]{1,0:T(8,128)(2,1)}, u32[]{:S(2)}) copy-start(bf16[1024,384]{1,0:T(8,128)(2,1)} %x0.3) | copy-start | bytes 2359300
  76.1 10.3 %copy-start.7 = (bf16[1024,384]{1,0:T(8,128)(2,1)S(1)}, bf16[1024,384]{1,0:T(8,128)(2,1)}, u32[]{:S(2)}) copy-start(bf16[1024,384]{1,0:T(8,128)(2,1)} %param.13) | copy-start | bytes 2359300
  76.1 14.0 %collective-permute-start.9 = (bf16[512,384]{1,0:T(8,128)(2,1)S(1)}, bf16[512,384]{1,0:T(8,128)(2,1)S(1)}, u32[]{:S(2)}, u32[]{:S(2)}) collective-permute-start(bf16[512,384]{1,0:T(8,128)(2,1)S(1)} %convolution_convert_fusion.1), channel_id=1, source_target_pairs={{0,3},{1,0},{2,1},{3,2},{4,5},{5,6},{6,7},{7,4},{8,11},{9,8},{10,9... | collective-permute-start | bytes 1179656 | tf_op jit(solution)/shard_map/ppermute | solution.py:36
  80.4 21.7 %collective-permute-start.15 = (bf16[512,384]{1,0:T(8,128)(2,1)S(1)}, bf16[512,384]{1,0:T(8,128)(2,1)S(1)}, u32[]{:S(2)}, u32[]{:S(2)}) collective-permute-start(bf16[512,384]{1,0:T(8,128)(2,1)S(1)} %convolution_convert_fusion), channel_id=1, source_target_pairs={{0,1},{1,2},{2,3},{3,0},{4,7},{5,4},{6,5},{7,6},{8,9},{9,10},{10,1... | collective-permute-start | bytes 1179656 | tf_op jit(solution)/shard_map/ppermute | solution.py:36
  86.8 15.3 %collective-permute-start.12 = (bf16[512,384]{1,0:T(8,128)(2,1)S(1)}, bf16[512,384]{1,0:T(8,128)(2,1)S(1)}, u32[]{:S(2)}, u32[]{:S(2)}) collective-permute-start(bf16[512,384]{1,0:T(8,128)(2,1)S(1)} %multiply_convert_fusion.1.b0.refs_1_), channel_id=1, source_target_pairs={{0,1},{1,2},{2,3},{3,0},{4,7},{5,4},{6,5},{7,6},{8,9},{9,10},{10,1... | collective-permute-start | bytes 1179656 | tf_op jit(solution)/shard_map/ppermute | solution.py:36
  86.9 15.2 %collective-permute-start.13 = (bf16[512,384]{1,0:T(8,128)(2,1)S(1)}, bf16[512,384]{1,0:T(8,128)(2,1)S(1)}, u32[]{:S(2)}, u32[]{:S(2)}) collective-permute-start(bf16[512,384]{1,0:T(8,128)(2,1)S(1)} %multiply_convert_fusion.1.b0.refs_1_), channel_id=1, source_target_pairs={{0,3},{1,0},{2,1},{3,2},{4,5},{5,6},{6,7},{7,4},{8,11},{9,8},{10,9... | collective-permute-start | bytes 1179656 | tf_op jit(solution)/shard_map/ppermute | solution.py:36
  90.2 9.4 %collective-permute-start.10 = (bf16[512,384]{1,0:T(8,128)(2,1)S(1)}, bf16[512,384]{1,0:T(8,128)(2,1)S(1)}, u32[]{:S(2)}, u32[]{:S(2)}) collective-permute-start(bf16[512,384]{1,0:T(8,128)(2,1)S(1)} %add_convert_fusion.3), channel_id=1, source_target_pairs={{0,3},{1,0},{2,1},{3,2},{4,5},{5,6},{6,7},{7,4},{8,11},{9,8},{10,9... | collective-permute-start | bytes 1179656 | tf_op jit(solution)/shard_map/ppermute | solution.py:36
  92.8 24.1 %slice-start = ((s8[4718592]{0:T(1024)(128)(4,1)}), s8[4194304]{0:T(1024)(128)(4,1)S(1)}, s32[]{:S(2)}) async-start(s8[4718592]{0:T(1024)(128)(4,1)} %bitcast.72), calls=%async_computation.2 | async-start | bytes 8388608
  96.0 20.9 %slice-start.1 = ((s8[4718592]{0:T(1024)(128)(4,1)}), s8[524288]{0:T(1024)(128)(4,1)S(1)}, s32[]{:S(2)}) async-start(s8[4718592]{0:T(1024)(128)(4,1)} %bitcast.72), calls=%async_computation.3 | async-start | bytes 1048576
  102.5 12.1 %collective-permute-start.16 = (bf16[512,384]{1,0:T(8,128)(2,1)S(1)}, bf16[512,384]{1,0:T(8,128)(2,1)S(1)}, u32[]{:S(2)}, u32[]{:S(2)}) collective-permute-start(bf16[512,384]{1,0:T(8,128)(2,1)S(1)} %multiply_convert_fusion.b0.refs_2_), channel_id=1, source_target_pairs={{0,3},{1,0},{2,1},{3,2},{4,5},{5,6},{6,7},{7,4},{8,11},{9,8},{10,9... | collective-permute-start | bytes 1179656 | tf_op jit(solution)/shard_map/ppermute | solution.py:36
  103.7 13.2 %collective-permute-start.14 = (bf16[512,384]{1,0:T(8,128)(2,1)S(1)}, bf16[512,384]{1,0:T(8,128)(2,1)S(1)}, u32[]{:S(2)}, u32[]{:S(2)}) collective-permute-start(bf16[512,384]{1,0:T(8,128)(2,1)S(1)} %collective-permute-done.12.b3.refs_2_), channel_id=1, source_target_pairs={{0,1},{1,2},{2,3},{3,0},{4,7},{5,4},{6,5},{7,6},{8,9},{9,10},{10,1... | collective-permute-start | bytes 1179656 | tf_op jit(solution)/shard_map/ppermute | solution.py:36
  104.6 16.9 %collective-permute-start.18 = (bf16[512,384]{1,0:T(8,128)(2,1)S(1)}, bf16[512,384]{1,0:T(8,128)(2,1)S(1)}, u32[]{:S(2)}, u32[]{:S(2)}) collective-permute-start(bf16[512,384]{1,0:T(8,128)(2,1)S(1)} %multiply_convert_fusion.b0.refs_2_), channel_id=1, source_target_pairs={{0,1},{1,2},{2,3},{3,0},{4,7},{5,4},{6,5},{7,6},{8,9},{9,10},{10,1... | collective-permute-start | bytes 1179656 | tf_op jit(solution)/shard_map/ppermute | solution.py:36
  114.6 11.7 %collective-permute-start.17 = (bf16[512,384]{1,0:T(8,128)(2,1)S(1)}, bf16[512,384]{1,0:T(8,128)(2,1)S(1)}, u32[]{:S(2)}, u32[]{:S(2)}) collective-permute-start(bf16[512,384]{1,0:T(8,128)(2,1)S(1)} %collective-permute-done.16.b1.refs_3_), channel_id=1, source_target_pairs={{0,3},{1,0},{2,1},{3,2},{4,5},{5,6},{6,7},{7,4},{8,11},{9,8},{10,9... | collective-permute-start | bytes 1179656 | tf_op jit(solution)/shard_map/ppermute | solution.py:36
  139.1 10.1 %collective-permute-start.22 = (bf16[768,1536]{1,0:T(8,128)(2,1)S(1)}, bf16[768,1536]{1,0:T(8,128)(2,1)S(1)}, u32[]{:S(2)}, u32[]{:S(2)}) collective-permute-start(bf16[768,1536]{1,0:T(8,128)(2,1)S(1)} %get-tuple-element.111), channel_id=1, source_target_pairs={{0,4},{4,0},{8,12},{12,8},{16,20},{20,16},{24,28},{28,24},{32,36},... | collective-permute-start | bytes 7077896 | tf_op jit(solution)/shard_map/ppermute | solution.py:46
  139.2 10.0 %collective-permute-start.23 = (bf16[768,1536]{1,0:T(8,128)(2,1)S(1)}, bf16[768,1536]{1,0:T(8,128)(2,1)S(1)}, u32[]{:S(2)}, u32[]{:S(2)}) collective-permute-start(bf16[768,1536]{1,0:T(8,128)(2,1)S(1)} %get-tuple-element.112), channel_id=1, source_target_pairs={{0,4},{4,0},{8,12},{12,8},{16,20},{20,16},{24,28},{28,24},{32,36},... | collective-permute-start | bytes 7077896 | tf_op jit(solution)/shard_map/ppermute | solution.py:46
  139.7 3.5 %collective-permute-start.19 = (f32[1,128]{1,0:T(1,128)S(1)}, f32[1,128]{1,0:T(1,128)S(1)}, u32[]{:S(2)}, u32[]{:S(2)}) collective-permute-start(f32[1,128]{1,0:T(1,128)S(1)} %get-tuple-element.108), channel_id=1, source_target_pairs={{0,1},{1,0},{2,3},{3,2},{4,5},{5,4},{6,7},{7,6},{8,9},{9,8},{10,11... | collective-permute-start | bytes 1544 | tf_op jit(solution)/shard_map/ppermute | solution.py:62
  143.2 4.8 %collective-permute-start.20 = (f32[1,128]{1,0:T(1,128)S(1)}, f32[1,128]{1,0:T(1,128)S(1)}, u32[]{:S(2)}, u32[]{:S(2)}) collective-permute-start(f32[1,128]{1,0:T(1,128)S(1)} %add.215), channel_id=1, source_target_pairs={{0,3},{1,2},{2,1},{3,0},{4,7},{5,6},{6,5},{7,4},{8,11},{9,10},{10,... | collective-permute-start | bytes 1544 | tf_op jit(solution)/shard_map/ppermute | solution.py:62
  148.0 1.2 collective-permute-start.21
  150.6 11.2 %collective-permute-start.24 = (bf16[4,48,1536]{2,1,0:T(8,128)(2,1)S(1)}, bf16[4,48,1536]{2,1,0:T(8,128)(2,1)S(1)}, u32[]{:S(2)}, u32[]{:S(2)}) collective-permute-start(bf16[4,48,1536]{2,1,0:T(8,128)(2,1)S(1)} %get-tuple-element.114), channel_id=1, source_target_pairs={{0,32},{4,12},{8,40},{12,20},{16,48},{20,28},{24,56},{28,4},{32,64... | collective-permute-start | bytes 1769480 | tf_op jit(solution)/shard_map/ppermute | solution.py:46
  151.9 9.9 %collective-permute-start.25 = (bf16[4,48,1536]{2,1,0:T(8,128)(2,1)S(1)}, bf16[4,48,1536]{2,1,0:T(8,128)(2,1)S(1)}, u32[]{:S(2)}, u32[]{:S(2)}) collective-permute-start(bf16[4,48,1536]{2,1,0:T(8,128)(2,1)S(1)} %get-tuple-element.115), channel_id=1, source_target_pairs={{0,96},{4,28},{8,104},{12,4},{16,112},{20,12},{24,120},{28,20},{32... | collective-permute-start | bytes 1769480 | tf_op jit(solution)/shard_map/ppermute | solution.py:46
  155.8 12.3 %collective-permute-start.27 = (bf16[4,48,1536]{2,1,0:T(8,128)(2,1)S(1)}, bf16[4,48,1536]{2,1,0:T(8,128)(2,1)S(1)}, u32[]{:S(2)}, u32[]{:S(2)}) collective-permute-start(bf16[4,48,1536]{2,1,0:T(8,128)(2,1)S(1)} %get-tuple-element.117), channel_id=1, source_target_pairs={{0,96},{4,28},{8,104},{12,4},{16,112},{20,12},{24,120},{28,20},{32... | collective-permute-start | bytes 1769480 | tf_op jit(solution)/shard_map/ppermute | solution.py:46
  157.4 11.1 %collective-permute-start.28 = (bf16[4,48,1536]{2,1,0:T(8,128)(2,1)S(1)}, bf16[4,48,1536]{2,1,0:T(8,128)(2,1)S(1)}, u32[]{:S(2)}, u32[]{:S(2)}) collective-permute-start(bf16[4,48,1536]{2,1,0:T(8,128)(2,1)S(1)} %get-tuple-element.118), channel_id=1, source_target_pairs={{0,32},{4,12},{8,40},{12,20},{16,48},{20,28},{24,56},{28,4},{32,64... | collective-permute-start | bytes 1769480 | tf_op jit(solution)/shard_map/ppermute | solution.py:46
  163.5 11.4 %collective-permute-start.26 = (bf16[4,48,1536]{2,1,0:T(8,128)(2,1)S(1)}, bf16[4,48,1536]{2,1,0:T(8,128)(2,1)S(1)}, u32[]{:S(2)}, u32[]{:S(2)}) collective-permute-start(bf16[4,48,1536]{2,1,0:T(8,128)(2,1)S(1)} %get-tuple-element.116), channel_id=1, source_target_pairs={{0,32},{4,12},{8,40},{12,20},{16,48},{20,28},{24,56},{28,4},{32,64... | collective-permute-start | bytes 1769480 | tf_op jit(solution)/shard_map/ppermute | solution.py:46
  165.1 9.9 %collective-permute-start.29 = (bf16[4,48,1536]{2,1,0:T(8,128)(2,1)S(1)}, bf16[4,48,1536]{2,1,0:T(8,128)(2,1)S(1)}, u32[]{:S(2)}, u32[]{:S(2)}) collective-permute-start(bf16[4,48,1536]{2,1,0:T(8,128)(2,1)S(1)} %get-tuple-element.119), channel_id=1, source_target_pairs={{0,96},{4,28},{8,104},{12,4},{16,112},{20,12},{24,120},{28,20},{32... | collective-permute-start | bytes 1769480 | tf_op jit(solution)/shard_map/ppermute | solution.py:46
  176.0 17.1 %copy-start.8 = (f32[48,1536]{1,0:T(8,128)S(1)}, f32[48,1536]{1,0:T(8,128)}, u32[]{:S(2)}) copy-start(f32[48,1536]{1,0:T(8,128)} %param.23) | copy-start | bytes 884740
  176.0 17.1 %copy-start.9 = (f32[48,1536]{1,0:T(8,128)S(1)}, f32[48,1536]{1,0:T(8,128)}, u32[]{:S(2)}) copy-start(f32[48,1536]{1,0:T(8,128)} %param.22) | copy-start | bytes 884740
  176.0 18.0 %copy-start.1 = (bf16[1536,3,384]{2,0,1:T(8,128)(2,1)S(1)}, bf16[1536,3,384]{2,0,1:T(8,128)(2,1)}, u32[]{:S(2)}) copy-start(bf16[1536,3,384]{2,0,1:T(8,128)(2,1)} %param.19) | copy-start | bytes 10616836

commit v2 on v1

--- a/solution.py
+++ b/solution.py
@@ -175,27 +175,48 @@
     )(at, top, low)
 
 
-def backward_kernel(at, b0, b1, b2, b3, out_w, slope, grad, back):
+def early_kernel(at, b0, b1, b2, w0, w1, w2, out, back, weights):
     @pl.when(pl.program_id(0) == 0)
     def _():
-        for k, ref in enumerate((b0, b1, b2, b3)):
-            back[:, pl.ds(pl.multiple_of(at[8 + k] * PART, 128), PART)] = ref[...]
-
-    grad[...] = (dot(back[...], out_w[...]) * slope[...].astype(F32)).astype(BF)
-
-
-def backward(at, blocks, out_w, slope):
+        for k, ref in enumerate((b0, b1, b2)):
+            back[:, k * PART : (k + 1) * PART] = ref[...]
+
+    for k, ref in enumerate((w0, w1, w2)):
+        weights[k * PART : (k + 1) * PART] = ref[...]
+    out[...] = dot(back[...], weights[...])
+
+
+def backward_early(at, blocks, weights):
+    rows, ff = blocks[0].shape[0], weights[0].shape[1]
+    return call(
+        early_kernel,
+        ff // WIDE,
+        [whole((rows, PART))] * 3 + [columns(PART, WIDE)] * 3,
+        columns(rows, WIDE),
+        shaped((rows, ff), F32),
+        [pltpu.VMEM((rows, 3 * PART), BF), pltpu.VMEM((3 * PART, WIDE), BF)],
+        cost(6 * rows * PART * ff, 9 * 10**6),
+        "backward_early",
+    )(at, *blocks, *weights)
+
+
+def late_kernel(at, block, weights, partial, slope, grad):
+    value = partial[...] + dot(block[...], weights[...])
+    grad[...] = (value * slope[...].astype(F32)).astype(BF)
+
+
+def backward_late(at, block, weights, partial, slope):
     rows, ff = slope.shape
     return call(
-        backward_kernel,
+        late_kernel,
         ff // WIDE,
-        [whole((rows, PART))] * 4 + [columns(D, WIDE), columns(rows, WIDE)],
+        [whole((rows, PART)), columns(PART, WIDE), columns(rows, WIDE), columns(rows, WIDE)],
         columns(rows, WIDE),
         shaped((rows, ff)),
-        [pltpu.VMEM((rows, D), BF)],
-        cost(2 * rows * D * ff, 14 * 10**6),
-        "backward",
-    )(at, *blocks, out_w, slope)
+        [],
+        cost(2 * rows * PART * ff, 8 * 10**6),
+        "backward_late",
+    )(at, block, weights, partial, slope)
 
 
 def rows_kernel(count, at, *refs):
@@ -313,9 +334,16 @@
     behind2[0] = (scaled(k2, g2, u0, u1) + down[0].astype(F32)).astype(BF)
 
 
-def close_kernel(at, own, up1, down1, up2, down2, out):
-    out[0, 0] = (own[0, 0] + up1[0].astype(F32) + down1[0].astype(F32)).astype(BF)
-    out[0, 1] = (own[0, 1] + up2[0].astype(F32) + down2[0].astype(F32)).astype(BF)
+def close_kernel(at, own, up1, down1, up2, down2, own_o, ahead, far, behind):
+    first = own[0, 0] + up1[0].astype(F32) + down1[0].astype(F32)
+    second = own[0, 1] + up2[0].astype(F32) + down2[0].astype(F32)
+    step = pl.program_id(0)
+    for k, out in enumerate((far, ahead, behind, own_o)):
+
+        @pl.when(step == k)
+        def _():
+            out[0] = first.astype(out.dtype)
+            out[1] = second.astype(out.dtype)
 
 
 def ring_stage(at, u0, u1, first, second, move):
@@ -363,12 +391,14 @@
         "relay",
     )(at, u0, u1, first[0], second[0], first[1], second[1], far1, far2)
     up1, down2 = move(ahead1, 1), move(behind2, -1)
+    place = lambda s, a: a[16 + s]
     return call(
         close_kernel,
         RING,
-        [both] + [one] * 4,
-        both,
-        shaped((RING, 2, 48, ff)),
+        [pl.BlockSpec((1, 2, 48, ff), lambda s, a: (place(s, a), 0, 0, 0))]
+        + [pl.BlockSpec((1, 48, ff), lambda s, a: (place(s, a), 0, 0))] * 4,
+        [pl.BlockSpec((2, 48, ff), lambda s, *_: (0, 0, 0))] * 4,
+        [shaped((2, 48, ff), k) for k in (F32, BF, BF, BF)],
         [],
         cost(4 * size, 20 * size),
         "close",
@@ -399,12 +429,14 @@
     ahead = [(me_x + k * way) % RING for k in range(RING)]
     swapped = [me_x, me_x ^ 1, 3 - me_x, (3 - me_x) ^ 1]
     me_one = jnp.where(me_c == 0, me_y, me_z)
+    me_two = jnp.where(me_c == 0, me_z, me_y)
     stride = jnp.where(me_c == 0, 4, 1)
     at = jnp.stack(
         [b * PART for b in swapped]
         + [me_c * 48, jnp.where(me_c == 0, 1, 4), me_c * 0, me_c * 0]
         + ahead
         + [((me_one + k) % RING) * stride for k in range(RING)]
+        + [(me_two + k) % RING for k in (2, 1, 3, 0)]
     ).astype(jnp.int32)
     outs = [lax.dynamic_slice_in_dim(out_w, b * PART, PART, 0) for b in ahead]
 
@@ -417,15 +449,14 @@
 
     behind, next_ahead = by_x(latents, 1), by_x(latents, -1)
     half = rows // 2
-    received, behind, next_ahead, at, outs = lax.optimization_barrier(
-        (received, behind, next_ahead, at, outs)
-    )
+    received, behind, at, outs = lax.optimization_barrier((received, behind, at, outs))
     far = by_x(behind, 1)
     wanted = (owner == me_dp)[:, None, None]
     mine = jnp.sum(jnp.where(wanted, received, 0.0), 0).reshape(1, -1).astype(BF)
 
     context = dot(mine, ctx_w)
-    context = context + swap_x(context, 0)
+    swapped_context, next_ahead = lax.optimization_barrier((swap_x(context, 0), next_ahead))
+    context = context + swapped_context
     swapped_context, far = lax.optimization_barrier((swap_x(context, 1), far))
     context = context + swapped_context
     conditioning = context * lax.rsqrt(jnp.mean(context * context, 1, keepdims=True) + 1e-06)
@@ -466,14 +497,15 @@
     far0 = by_x(far0, 1)
     at_next, down0 = lax.optimization_barrier((at, down0))
     down0 = by_x(down0, -1)
-    up0, own0 = lax.optimization_barrier((project(hidden0, 1), project(hidden0, 0)))
+    up0 = lax.optimization_barrier(project(hidden0, 1))
     modded1, hidden1, pre1 = forward(1, at_next, latent_blocks, mods, in_w)
     hidden1, far0, down0 = lax.optimization_barrier((hidden1, far0, down0))
     up0 = by_x((up0 + far0.astype(F32)).astype(BF), 1)
     far1, up1 = project(hidden1, 2).astype(BF), project(hidden1, 1).astype(BF)
-    far1, up1, hidden1, at_late, pre0, pre1 = lax.optimization_barrier(
-        (far1, up1, hidden1, at, pre0, pre1)
-    )
+    far1, up1, hidden1, hidden0, at_late, pre0, pre1 = lax.optimization_barrier(
+        (far1, up1, hidden1, hidden0, at, pre0, pre1)
+    )
+    own0 = lax.optimization_barrier(project(hidden0, 0))
     far1, up1 = by_x(far1, -1), by_x(up1, 1)
     down1, own1 = lax.optimization_barrier((project(hidden1, 3), project(hidden1, 0)))
     back0 = leave(0, own0, up0, down0)
@@ -491,11 +523,13 @@
 
     rights = (hidden0, hidden1)
     *second, square_a = rows_grad(at, (0,), (back0,), (back1,), rights, ())
-    grad0 = backward(at, (back0, ahead0, far0, behind0), out_w, slope0)
+    early0 = backward_early(at, (back0, ahead0, behind0), (outs[0], outs[1], outs[3]))
+    early1 = backward_early(at, (back1, ahead1, behind1), (outs[0], outs[1], outs[3]))
+    grad0 = backward_late(at, far0, outs[2], early0, slope0)
     *second, square_b = rows_grad(
         at, (1, 3), (ahead0, behind0), (ahead1, behind1), rights, tuple(second)
     )
-    grad1 = backward(at, (back1, ahead1, far1, behind1), out_w, slope1)
+    grad1 = backward_late(at, far1, outs[2], early1, slope1)
     *second, square_c = rows_grad(at, (2,), (far0,), (far1,), rights, tuple(second))
     keep2, send2 = second
     got2 = by_core(send2)
@@ -508,13 +542,14 @@
     root = math.sqrt(2.0 * D * FF)
     unit = root / (jnp.sqrt(square) + 0.01)
 
-    value = ring_stage(
+    own, ahead, far, behind = ring_stage(
         at, unit, by_core(unit), (keep1, got1), (keep2, got2), lambda v, w: by_turns(v, w, True)
     )
-    groups = [[(y * RING + z) * 2 for z in range(RING)] for y in range(RING)]
-    groups += [[(y * RING + z) * 2 + 1 for y in range(RING)] for z in range(RING)]
-    got = lax.all_to_all(value, "dp", 0, 0, axis_index_groups=groups, tiled=True)
-    value = jnp.sum(got.astype(F32), 0)
+    value = own + (
+        by_turns(far, 2, False).astype(F32)
+        + by_turns(ahead, 1, False).astype(F32)
+        + by_turns(behind, -1, False).astype(F32)
+    )
     return (value[0] + noise_in) / 32.0, (value[1] + noise_out) / 32.0
 
 

time: 194 us -> 195 us (level)
  blocking collectives: 16.9 us -> 0 us
  waiting for transfers between devices: 53.1 us -> 60.1 us
  starting transfers between devices: 48.4 us -> 52.4 us
  Pallas kernels: 47.7 us -> 51.6 us
  local copies, waits for them, and re-layouts: 5.89 us -> 8.18 us
    all_to_all x1 -> x0, blocking collectives: 16.9 us -> none  [local(): lax.all_to_all(value, 'dp', 0, 0, axis_index_groups=groups, tiled=True)]
    ppermute x9 -> x12, waiting for transfers between devices: 13.2 us -> 22 us  [by_dp(): return lax.ppermute(value, 'dp', pairs)]
    ppermute x9 -> x12, starting transfers between devices: 9.41 us -> 14.6 us  [by_dp(): return lax.ppermute(value, 'dp', pairs)]
    pallas_call x3 -> x5, Pallas kernels: 9.36 us -> 13.3 us  [the longest x2 7.31 us: backward_early(): call(early_kernel, ff // WIDE, [whole((rows, PART))] * 3 + [columns(PART,...]
    unnamed x28 -> x24, local copies, waits for them, and re-layouts: 0.51 us -> 2.76 us
  transfers between devices with their start and end apart: 31 -> 34, of which waited for: 18 -> 19; matrix products, arithmetic and copies ran while one was open for 9% -> 8% of each run, Pallas kernels for 13% -> 16%
where the time goes in v2:
time: 195 us; the launch traced here: 194 us
  waiting for transfers between devices  60.1 us (31%)
  starting transfers between devices  52.4 us (27%)
  Pallas kernels  51.6 us (26%)
  matrix products  12 us (6%)
  local copies, waits for them, and re-layouts  8.18 us (4%)
  other arithmetic  6.74 us (3%)
  between operations  3.23 us (2%)
    ppermute x12, waiting for transfers between devices, by_dp(): return lax.ppermute(value, 'dp', pairs)  22 us
    ppermute x15, starting transfers between devices, by_x(): return lax.ppermute(value, ('dp', 'mp'), pairs)  19.9 us
    ppermute x6, waiting for transfers between devices, swap_x(): return lax.ppermute(value, 'mp', list(enumerate(other)))  18.7 us
    ppermute x15, waiting for transfers between devices, by_x(): return lax.ppermute(value, ('dp', 'mp'), pairs)  16.4 us
    pallas_call x2, Pallas kernels, forward(): call(forward_kernel, ff // WIDE, [piece] * 4 + [whole((3, PART)), whole((...  15.8 us
    ppermute x12, starting transfers between devices, by_dp(): return lax.ppermute(value, 'dp', pairs)  14.6 us
    ppermute x6, starting transfers between devices, swap_x(): return lax.ppermute(value, 'mp', list(enumerate(other)))  9.43 us
    pallas_call x3, Pallas kernels, rows_grad(): call(lambda *refs: rows_kernel(count, *refs), count, [whole((rows, PART))...  8.72 us
  transfers between devices with their start and end apart: 34, of which 19 were waited for; matrix products, arithmetic and copies ran while one was open for 8% of the time, Pallas kernels for 16%

profile of v2, /device:TPU:0, one launch (start us, length us, event | category | flops | bytes accessed | tf_op | source)
XLA Modules:
  0.0 194.2 jit_solution(13699653967576956876)
XLA Ops:
  0.6 1.6 collective-permute-start
  2.3 1.7 collective-permute-start.2
  6.4 8.5 %all-to-all-start = ((f32[32,8,128]{2,1,0:T(8,128)}), f32[32,8,128]{2,1,0:T(8,128)}, u32[]{:S(2)}, u32[]{:S(2)}) async-start(f32[32,8,128]{2,1,0:T(8,128)} %broadcast_in_dim.31), calls=%async_computation | async-start | bytes 262144 | tf_op jit(solution)/shard_map/all_to_all | solution.py:448
  15.1 4.6 %constant_dynamic-slice_fusion = (bf16[384,1536]{1,0:T(8,128)(2,1)}, bf16[384,1536]{1,0:T(8,128)(2,1)}, bf16[384,1536]{1,0:T(8,128)(2,1)}, bf16[384,1536]{1,0:T(8,128)(2,1)}) fusion(bf16[1536,1536]{1,0:T(8,128)(2,1)} %param.21, s32[]{:T(128)S(6)} %select_n.136, s32[]{:T(128)S(6)} %select_n.134, s32[]{:T(128)S(6)} %select_n.133, s32[]{:T(128)S(6)} %select_n.135), kind=kLoop, calls=%fused_computation.51 | loop fusion | bytes 9437200 | tf_op jit(solution)/shard_map/dynamic_slice | solution.py:441
  19.8 3.0 %all-to-all-done = f32[32,8,128]{2,1,0:T(8,128)} async-done(((f32[32,8,128]{2,1,0:T(8,128)}), f32[32,8,128]{2,1,0:T(8,128)}, u32[]{:S(2)}, u32[]{:S(2)}) %all-to-all-start) | async-done | bytes 131104 | tf_op jit(solution)/shard_map/all_to_all | solution.py:448
  24.1 2.4 %fusion.27 = f32[1,1536]{1,0:T(1,128)S(1)} fusion(bf16[1024,1]{0,1:T(2,128)(2,1)S(1)} %reshape.95, bf16[1024,1536]{1,0:T(8,128)(2,1)} %param.18), kind=kOutput, calls=%fused_computation.60 | convolution fusion | flops 3145728 | bytes 3153920 | tf_op jit(solution)/shard_map/dot_general | solution.py:24
  26.5 1.5 collective-permute-start.1
  28.7 4.3 %collective-permute-done.1 = f32[1,1536]{1,0:T(1,128)S(1)} collective-permute-done((f32[1,1536]{1,0:T(1,128)S(1)}, f32[1,1536]{1,0:T(1,128)S(1)}, u32[]{:S(2)}, u32[]{:S(2)}) %collective-permute-start.1) | collective-permute-done | bytes 6176 | tf_op jit(solution)/shard_map/ppermute | solution.py:62
  33.0 3.9 %collective-permute-start.3 = (f32[1,1536]{1,0:T(1,128)S(1)}, f32[1,1536]{1,0:T(1,128)S(1)}, u32[]{:S(2)}, u32[]{:S(2)}) collective-permute-start(f32[1,1536]{1,0:T(1,128)S(1)} %add.228), channel_id=1, source_target_pairs={{0,3},{1,2},{2,1},{3,0},{4,7},{5,6},{6,5},{7,4},{8,11},{9,10},{10,... | collective-permute-start | bytes 18440 | tf_op jit(solution)/shard_map/ppermute | solution.py:62
  36.8 1.6 collective-permute-done.3
  41.4 2.9 %collective-permute-done.5.m1 = f32[3,384]{1,0:T(4,128)S(1)} collective-permute-done((f32[3,384]{1,0:T(4,128)S(1)}, f32[3,384]{1,0:T(4,128)S(1)}, u32[]{:S(2)}, u32[]{:S(2)}) %collective-permute-start.5) | collective-permute-done | bytes 4640 | tf_op jit(solution)/shard_map/ppermute | solution.py:62
  44.3 3.3 %collective-permute-start.6 = (f32[6,384]{1,0:T(8,128)S(1)}, f32[6,384]{1,0:T(8,128)S(1)}, u32[]{:S(2)}, u32[]{:S(2)}) collective-permute-start(f32[6,384]{1,0:T(8,128)S(1)} %pad_maximum_fusion), channel_id=1, source_target_pairs={{0,3},{1,2},{2,1},{3,0},{4,7},{5,6},{6,5},{7,4},{8,11},{9,10},{10,... | collective-permute-start | bytes 27656 | tf_op jit(solution)/shard_map/ppermute | solution.py:62
  47.6 1.6 collective-permute-done.6.m2
  49.3 7.9 %forward.2 = (bf16[512,1536]{1,0:T(8,128)(2,1)S(1)}, bf16[512,1536]{1,0:T(8,128)(2,1)S(1)}, f32[512,1536]{1,0:T(8,128)S(1)}) custom-call(s32[20]{0:T(128)S(1)} %stack.75.at.refs_0_, bf16[1024,384]{1,0:T(8,128)(2,1)} %x0.3, bf16[1024,384]{1,0:T(8,128)(2,1)} %collective-permute-done.2.x1, bf16[1024,384]{1,0:T(8,128)(2,1)} %copy-done.10, ...), custom_call_target="tpu_custom_call" | custom-call | flops 2415919104 | bytes 12000000 | tf_op jit(solution)/shard_map/forward/pallas_call | solution.py:137
  59.5 3.5 %collective-permute-start.8 = (bf16[512,384]{1,0:T(8,128)(2,1)S(1)}, bf16[512,384]{1,0:T(8,128)(2,1)S(1)}, u32[]{:S(2)}, u32[]{:S(2)}) collective-permute-start(bf16[512,384]{1,0:T(8,128)(2,1)S(1)} %convolution_convert_fusion.3), channel_id=1, source_target_pairs={{0,3},{1,0},{2,1},{3,2},{4,5},{5,6},{6,7},{7,4},{8,11},{9,8},{10,9... | collective-permute-start | bytes 1179656 | tf_op jit(solution)/shard_map/ppermute | solution.py:36
  64.0 7.9 %forward.3 = (bf16[512,1536]{1,0:T(8,128)(2,1)S(1)}, bf16[512,1536]{1,0:T(8,128)(2,1)S(1)}, f32[512,1536]{1,0:T(8,128)S(1)}) custom-call(s32[20]{0:T(128)S(1)} %stack.75.at.refs_0_, bf16[1024,384]{1,0:T(8,128)(2,1)} %x0.3, bf16[1024,384]{1,0:T(8,128)(2,1)} %collective-permute-done.2.x1, bf16[1024,384]{1,0:T(8,128)(2,1)} %copy-done.10, ...), custom_call_target="tpu_custom_call" | custom-call | flops 2415919104 | bytes 12000000 | tf_op jit(solution)/shard_map/forward/pallas_call | solution.py:137
  77.2 2.2 %collective-permute-start.9 = (bf16[512,384]{1,0:T(8,128)(2,1)S(1)}, bf16[512,384]{1,0:T(8,128)(2,1)S(1)}, u32[]{:S(2)}, u32[]{:S(2)}) collective-permute-start(bf16[512,384]{1,0:T(8,128)(2,1)S(1)} %convolution_convert_fusion.1), channel_id=1, source_target_pairs={{0,3},{1,0},{2,1},{3,2},{4,5},{5,6},{6,7},{7,4},{8,11},{9,8},{10,9... | collective-permute-start | bytes 1179656 | tf_op jit(solution)/shard_map/ppermute | solution.py:36
  80.5 6.0 %collective-permute-done.11 = bf16[512,384]{1,0:T(8,128)(2,1)S(1)} collective-permute-done((bf16[512,384]{1,0:T(8,128)(2,1)S(1)}, bf16[512,384]{1,0:T(8,128)(2,1)S(1)}, u32[]{:S(2)}, u32[]{:S(2)}) %collective-permute-start.11) | collective-permute-done | bytes 393248 | tf_op jit(solution)/shard_map/ppermute | solution.py:36
  86.9 3.2 %collective-permute-start.13 = (bf16[512,384]{1,0:T(8,128)(2,1)S(1)}, bf16[512,384]{1,0:T(8,128)(2,1)S(1)}, u32[]{:S(2)}, u32[]{:S(2)}) collective-permute-start(bf16[512,384]{1,0:T(8,128)(2,1)S(1)} %multiply_convert_fusion.1.b0.refs_1_), channel_id=1, source_target_pairs={{0,3},{1,0},{2,1},{3,2},{4,5},{5,6},{6,7},{7,4},{8,11},{9,8},{10,9... | collective-permute-start | bytes 1179656 | tf_op jit(solution)/shard_map/ppermute | solution.py:36
  90.2 2.6 %collective-permute-start.10 = (bf16[512,384]{1,0:T(8,128)(2,1)S(1)}, bf16[512,384]{1,0:T(8,128)(2,1)S(1)}, u32[]{:S(2)}, u32[]{:S(2)}) collective-permute-start(bf16[512,384]{1,0:T(8,128)(2,1)S(1)} %add_convert_fusion.3), channel_id=1, source_target_pairs={{0,3},{1,0},{2,1},{3,2},{4,5},{5,6},{6,7},{7,4},{8,11},{9,8},{10,9... | collective-permute-start | bytes 1179656 | tf_op jit(solution)/shard_map/ppermute | solution.py:36
  92.8 3.2 %add_convert_fusion = (bf16[512,1536]{1,0:T(8,128)(2,1)S(1)}, bf16[512,1536]{1,0:T(8,128)(2,1)S(1)}) fusion(f32[512,1536]{1,0:T(8,128)S(1)} %get-tuple-element.87, f32[512,1536]{1,0:T(8,128)S(1)} %get-tuple-element.86), kind=kLoop, calls=%fused_computation | loop fusion | flops 23592960 | bytes 9437184 | tf_op jit(solution)/shard_map/convert_element_type | solution.py:514
  96.0 2.2 %turn.1 = (bf16[768,1024]{1,0:T(8,128)(2,1)S(1)}, bf16[768,1024]{1,0:T(8,128)(2,1)S(1)}) custom-call(s32[20]{0:T(128)S(1)} %stack.75.at.refs_0_, bf16[512,1536]{1,0:T(8,128)(2,1)S(1)} %get-tuple-element.89.top, bf16[512,1536]{1,0:T(8,128)(2,1)S(1)} %get-tuple-element.90.low), custom_call_target="tpu_custom_call" | custom-call | flops 1572864 | bytes 6291456 | tf_op jit(solution)/shard_map/turn/pallas_call | solution.py:166
  99.6 2.5 %collective-permute-done.12.b2.refs_2_ = bf16[512,384]{1,0:T(8,128)(2,1)S(1)} collective-permute-done((bf16[512,384]{1,0:T(8,128)(2,1)S(1)}, bf16[512,384]{1,0:T(8,128)(2,1)S(1)}, u32[]{:S(2)}, u32[]{:S(2)}) %collective-permute-start.12) | collective-permute-done | bytes 393248 | tf_op jit(solution)/shard_map/ppermute | solution.py:36
  104.6 2.0 %rows_grad.3 = (bf16[768,1536]{1,0:T(8,128)(2,1)S(1)}, bf16[768,1536]{1,0:T(8,128)(2,1)S(1)}, f32[1,1536]{1,0:T(1,128)S(1)}) custom-call(s32[20]{0:T(128)S(1)} %stack.75.at.refs_0_, bf16[512,384]{1,0:T(8,128)(2,1)S(1)} %multiply_convert_fusion.1.b0.refs_1_, bf16[512,384]{1,0:T(8,128)(2,1)S(1)} %multiply_convert_fusion.b0.refs_2_, ...), custom_call_target="tpu_custom_call" | custom-call | flops 1207959552 | bytes 5000000 | tf_op jit(solution)/shard_map/rows_grad/pallas_call | solution.py:262
  106.5 3.7 %backward_early.2.partial = f32[512,1536]{1,0:T(8,128)S(1)} custom-call(s32[20]{0:T(128)S(1)} %stack.75.at.refs_0_, bf16[512,384]{1,0:T(8,128)(2,1)S(1)} %multiply_convert_fusion.1.b0.refs_1_, bf16[512,384]{1,0:T(8,128)(2,1)S(1)} %collective-permute-done.13.b1.refs_1_, bf16[512,384]{1,0:T(8,128)(2,1)S(1)} %collective-permute-done.12.b2.refs_2_, ...), custom_call_target="tpu_custom_call" | custom-call | flops 1811939328 | bytes 9000000 | tf_op jit(solution)/shard_map/backward_early/pallas_call | solution.py:191
  110.2 4.4 %collective-permute-done.16.b1.refs_3_ = bf16[512,384]{1,0:T(8,128)(2,1)S(1)} collective-permute-done((bf16[512,384]{1,0:T(8,128)(2,1)S(1)}, bf16[512,384]{1,0:T(8,128)(2,1)S(1)}, u32[]{:S(2)}, u32[]{:S(2)}) %collective-permute-start.16) | collective-permute-done | bytes 393248 | tf_op jit(solution)/shard_map/ppermute | solution.py:36
  114.6 2.4 %collective-permute-start.17 = (bf16[512,384]{1,0:T(8,128)(2,1)S(1)}, bf16[512,384]{1,0:T(8,128)(2,1)S(1)}, u32[]{:S(2)}, u32[]{:S(2)}) collective-permute-start(bf16[512,384]{1,0:T(8,128)(2,1)S(1)} %collective-permute-done.16.b1.refs_3_), channel_id=1, source_target_pairs={{0,3},{1,0},{2,1},{3,2},{4,5},{5,6},{6,7},{7,4},{8,11},{9,8},{10,9... | collective-permute-start | bytes 1179656 | tf_op jit(solution)/shard_map/ppermute | solution.py:36
  116.9 2.4 %backward_late.2.right0 = bf16[512,1536]{1,0:T(8,128)(2,1)S(1)} custom-call(s32[20]{0:T(128)S(1)} %stack.75.at.refs_0_, bf16[512,384]{1,0:T(8,128)(2,1)S(1)} %collective-permute-done.14.block.refs_1_, bf16[384,1536]{1,0:T(8,128)(2,1)S(1)} %copy-done.2, f32[512,1536]{1,0:T(8,128)S(1)} %backward_early.2.partial, bf16[512,1536]{1,0:T(8,128)(2,1)S(1)} %get-tuple-element.100.slope), custom_call_target="tpu_custom_call" | custom-call | flops 603979776 | bytes 8000000 | tf_op jit(solution)/shard_map/backward_late/pallas_call | solution.py:210
  119.3 2.1 %collective-permute-done.18.b2.refs_4_ = bf16[512,384]{1,0:T(8,128)(2,1)S(1)} collective-permute-done((bf16[512,384]{1,0:T(8,128)(2,1)S(1)}, bf16[512,384]{1,0:T(8,128)(2,1)S(1)}, u32[]{:S(2)}, u32[]{:S(2)}) %collective-permute-start.18) | collective-permute-done | bytes 393248 | tf_op jit(solution)/shard_map/ppermute | solution.py:36
  121.4 3.7 %backward_early.3.partial = f32[512,1536]{1,0:T(8,128)S(1)} custom-call(s32[20]{0:T(128)S(1)} %stack.75.at.refs_0_, bf16[512,384]{1,0:T(8,128)(2,1)S(1)} %multiply_convert_fusion.b0.refs_2_, bf16[512,384]{1,0:T(8,128)(2,1)S(1)} %collective-permute-done.16.b1.refs_3_, bf16[512,384]{1,0:T(8,128)(2,1)S(1)} %collective-permute-done.18.b2.refs_4_, ...), custom_call_target="tpu_custom_call" | custom-call | flops 1811939328 | bytes 9000000 | tf_op jit(solution)/shard_map/backward_early/pallas_call | solution.py:191
  125.1 4.8 %rows_grad.4 = (bf16[768,1536]{1,0:T(8,128)(2,1)S(1)}, bf16[768,1536]{1,0:T(8,128)(2,1)S(1)}, f32[1,1536]{1,0:T(1,128)S(1)}) custom-call(s32[20]{0:T(128)S(1)} %stack.75.at.refs_0_, bf16[512,384]{1,0:T(8,128)(2,1)S(1)} %collective-permute-done.13.b1.refs_1_, ...), custom_call_target="tpu_custom_call", output_to_operand_aliasing={{0}: (7, {}), {1}: (8, {})} | custom-call | flops 2415919104 | bytes 10000000 | tf_op jit(solution)/shard_map/rows_grad/pallas_call | solution.py:262
  129.9 2.4 %backward_late.3.right1 = bf16[512,1536]{1,0:T(8,128)(2,1)S(1)} custom-call(s32[20]{0:T(128)S(1)} %stack.75.at.refs_0_, bf16[512,384]{1,0:T(8,128)(2,1)S(1)} %collective-permute-done.17.block.refs_2_, bf16[384,1536]{1,0:T(8,128)(2,1)S(1)} %copy-done.2, f32[512,1536]{1,0:T(8,128)S(1)} %backward_early.3.partial, bf16[512,1536]{1,0:T(8,128)(2,1)S(1)} %get-tuple-element.104.slope), custom_call_target="tpu_custom_call" | custom-call | flops 603979776 | bytes 8000000 | tf_op jit(solution)/shard_map/backward_late/pallas_call | solution.py:210
  132.3 2.0 %rows_grad.5 = (bf16[768,1536]{1,0:T(8,128)(2,1)S(1)}, bf16[768,1536]{1,0:T(8,128)(2,1)S(1)}, f32[1,1536]{1,0:T(1,128)S(1)}) custom-call(s32[20]{0:T(128)S(1)} %stack.75.at.refs_0_, bf16[512,384]{1,0:T(8,128)(2,1)S(1)} %collective-permute-done.14.block.refs_1_, ...), custom_call_target="tpu_custom_call", output_to_operand_aliasing={{0}: (5, {}), {1}: (6, {})} | custom-call | flops 1207959552 | bytes 5000000 | tf_op jit(solution)/shard_map/rows_grad/pallas_call | solution.py:262
  134.3 6.7 %weight_grad.1 = (bf16[768,1536]{1,0:T(8,128)(2,1)S(1)}, bf16[768,1536]{1,0:T(8,128)(2,1)S(1)}, f32[1,128]{1,0:T(1,128)S(1)}) custom-call(s32[20]{0:T(128)S(1)} %stack.75.at.refs_0_, bf16[768,1024]{1,0:T(8,128)(2,1)S(1)} %get-tuple-element.96.keep_l, bf16[768,1024]{1,0:T(8,128)(2,1)S(1)} %get-tuple-element.97.send_l, ...), custom_call_target="tpu_custom_call" | custom-call | flops 4831838208 | bytes 11000000 | tf_op jit(solution)/shard_map/weight_grad/pallas_call | solution.py:304
  141.6 3.5 %collective-permute-done.19 = f32[1,128]{1,0:T(1,128)S(1)} collective-permute-done((f32[1,128]{1,0:T(1,128)S(1)}, f32[1,128]{1,0:T(1,128)S(1)}, u32[]{:S(2)}, u32[]{:S(2)}) %collective-permute-start.19) | collective-permute-done | bytes 544 | tf_op jit(solution)/shard_map/ppermute | solution.py:62
  145.1 4.7 %collective-permute-done.20 = f32[1,128]{1,0:T(1,128)S(1)} collective-permute-done((f32[1,128]{1,0:T(1,128)S(1)}, f32[1,128]{1,0:T(1,128)S(1)}, u32[]{:S(2)}, u32[]{:S(2)}) %collective-permute-start.20) | collective-permute-done | bytes 544 | tf_op jit(solution)/shard_map/ppermute | solution.py:62
  151.1 1.4 far.1
  153.1 2.7 %collective-permute-start.25 = (bf16[4,48,1536]{2,1,0:T(8,128)(2,1)S(1)}, bf16[4,48,1536]{2,1,0:T(8,128)(2,1)S(1)}, u32[]{:S(2)}, u32[]{:S(2)}) collective-permute-start(bf16[4,48,1536]{2,1,0:T(8,128)(2,1)S(1)} %get-tuple-element.119), channel_id=1, source_target_pairs={{0,96},{4,28},{8,104},{12,4},{16,112},{20,12},{24,120},{28,20},{32... | collective-permute-start | bytes 1769480 | tf_op jit(solution)/shard_map/ppermute | solution.py:46
  155.8 1.9 near.1
  157.8 2.0 %collective-permute-start.28 = (bf16[4,48,1536]{2,1,0:T(8,128)(2,1)S(1)}, bf16[4,48,1536]{2,1,0:T(8,128)(2,1)S(1)}, u32[]{:S(2)}, u32[]{:S(2)}) collective-permute-start(bf16[4,48,1536]{2,1,0:T(8,128)(2,1)S(1)} %get-tuple-element.122), channel_id=1, source_target_pairs={{0,32},{4,12},{8,40},{12,20},{16,48},{20,28},{24,56},{28,4},{32,64... | collective-permute-start | bytes 1769480 | tf_op jit(solution)/shard_map/ppermute | solution.py:46
  159.8 3.8 %collective-permute-done.24.up = bf16[4,48,1536]{2,1,0:T(8,128)(2,1)S(1)} collective-permute-done((bf16[4,48,1536]{2,1,0:T(8,128)(2,1)S(1)}, bf16[4,48,1536]{2,1,0:T(8,128)(2,1)S(1)}, u32[]{:S(2)}, u32[]{:S(2)}) %collective-permute-start.24) | collective-permute-done | bytes 589856 | tf_op jit(solution)/shard_map/ppermute | solution.py:46
  163.7 1.6 relay.1
  165.4 3.3 %collective-permute-start.29 = (bf16[4,48,1536]{2,1,0:T(8,128)(2,1)S(1)}, bf16[4,48,1536]{2,1,0:T(8,128)(2,1)S(1)}, u32[]{:S(2)}, u32[]{:S(2)}) collective-permute-start(bf16[4,48,1536]{2,1,0:T(8,128)(2,1)S(1)} %get-tuple-element.123), channel_id=1, source_target_pairs={{0,96},{4,28},{8,104},{12,4},{16,112},{20,12},{24,120},{28,20},{32... | collective-permute-start | bytes 1769480 | tf_op jit(solution)/shard_map/ppermute | solution.py:46
  170.0 6.5 %collective-permute-done.26.up1 = bf16[4,48,1536]{2,1,0:T(8,128)(2,1)S(1)} collective-permute-done((bf16[4,48,1536]{2,1,0:T(8,128)(2,1)S(1)}, bf16[4,48,1536]{2,1,0:T(8,128)(2,1)S(1)}, u32[]{:S(2)}, u32[]{:S(2)}) %collective-permute-start.26) | collective-permute-done | bytes 589856 | tf_op jit(solution)/shard_map/ppermute | solution.py:46
  177.7 3.2 %collective-permute-start.32 = (bf16[2,48,1536]{2,1,0:T(8,128)(2,1)S(1)}, bf16[2,48,1536]{2,1,0:T(8,128)(2,1)S(1)}, u32[]{:S(2)}, u32[]{:S(2)}) collective-permute-start(bf16[2,48,1536]{2,1,0:T(8,128)(2,1)S(1)} %get-tuple-element.127), channel_id=1, source_target_pairs={{0,24},{4,100},{8,0},{12,108},{16,8},{20,116},{24,16},{28,124},{32... | collective-permute-start | bytes 884744 | tf_op jit(solution)/shard_map/ppermute | solution.py:46
  180.9 1.9 collective-permute-start.30
  182.8 2.4 %collective-permute-done.32 = bf16[2,48,1536]{2,1,0:T(8,128)(2,1)S(1)} collective-permute-done((bf16[2,48,1536]{2,1,0:T(8,128)(2,1)S(1)}, bf16[2,48,1536]{2,1,0:T(8,128)(2,1)S(1)}, u32[]{:S(2)}, u32[]{:S(2)}) %collective-permute-start.32) | collective-permute-done | bytes 294944 | tf_op jit(solution)/shard_map/ppermute | solution.py:46
  185.2 6.9 %collective-permute-done.31 = bf16[2,48,1536]{2,1,0:T(8,128)(2,1)S(1)} collective-permute-done((bf16[2,48,1536]{2,1,0:T(8,128)(2,1)S(1)}, bf16[2,48,1536]{2,1,0:T(8,128)(2,1)S(1)}, u32[]{:S(2)}, u32[]{:S(2)}) %collective-permute-start.31) | collective-permute-done | bytes 294944 | tf_op jit(solution)/shard_map/ppermute | solution.py:46
  (94 shorter events, 26.7 us)
Async XLA Ops:
  0.6 39.4 %copy-start = (bf16[1536,3,384]{2,0,1:T(8,128)(2,1)S(1)}, bf16[1536,3,384]{2,0,1:T(8,128)(2,1)}, u32[]{:S(2)}) copy-start(bf16[1536,3,384]{2,0,1:T(8,128)(2,1)} %param.19) | copy-start | bytes 10616836
  0.6 22.1 %collective-permute-start = (bf16[1024,384]{1,0:T(8,128)(2,1)}, bf16[1024,384]{1,0:T(8,128)(2,1)}, u32[]{:S(2)}, u32[]{:S(2)}) collective-permute-start(bf16[1024,384]{1,0:T(8,128)(2,1)} %x0.3), channel_id=1, source_target_pairs={{0,1},{1,2},{2,3},{3,0},{4,7},{5,4},{6,5},{7,6},{8,9},{9,10},{10,1... | collective-permute-start | bytes 2359304 | tf_op jit(solution)/shard_map/ppermute | solution.py:36
  2.3 26.4 %collective-permute-start.2 = (bf16[1024,384]{1,0:T(8,128)(2,1)}, bf16[1024,384]{1,0:T(8,128)(2,1)}, u32[]{:S(2)}, u32[]{:S(2)}) collective-permute-start(bf16[1024,384]{1,0:T(8,128)(2,1)} %x0.3), channel_id=1, source_target_pairs={{0,3},{1,0},{2,1},{3,2},{4,5},{5,6},{6,7},{7,4},{8,11},{9,8},{10,9... | collective-permute-start | bytes 2359304 | tf_op jit(solution)/shard_map/ppermute | solution.py:36
  6.4 16.4 %all-to-all-start = ((f32[32,8,128]{2,1,0:T(8,128)}), f32[32,8,128]{2,1,0:T(8,128)}, u32[]{:S(2)}, u32[]{:S(2)}) async-start(f32[32,8,128]{2,1,0:T(8,128)} %broadcast_in_dim.31), calls=%async_computation | async-start | bytes 262144 | tf_op jit(solution)/shard_map/all_to_all | solution.py:448
  15.0 8.0 %copy-start.11 = (s32[32]{0:T(128)S(1)}, s32[32]{0:T(128)}, u32[]{:S(2)}) copy-start(s32[32]{0:T(128)} %param.17) | copy-start | bytes 388
  22.8 15.7 %collective-permute-start.4 = (bf16[1024,384]{1,0:T(8,128)(2,1)}, bf16[1024,384]{1,0:T(8,128)(2,1)S(1)}, u32[]{:S(2)}, u32[]{:S(2)}) collective-permute-start(bf16[1024,384]{1,0:T(8,128)(2,1)} %collective-permute-done.x3), channel_id=1, source_target_pairs={{0,1},{1,2},{2,3},{3,0},{4,7},{5,4},{6,5},{7,6},{8,9},{9,10},{10,1... | collective-permute-start | bytes 2359304 | tf_op jit(solution)/shard_map/ppermute | solution.py:36
  26.5 6.5 %collective-permute-start.1 = (f32[1,1536]{1,0:T(1,128)S(1)}, f32[1,1536]{1,0:T(1,128)S(1)}, u32[]{:S(2)}, u32[]{:S(2)}) collective-permute-start(f32[1,1536]{1,0:T(1,128)S(1)} %fusion.27), channel_id=1, source_target_pairs={{0,1},{1,0},{2,3},{3,2},{4,5},{5,4},{6,7},{7,6},{8,9},{9,8},{10,11... | collective-permute-start | bytes 18440 | tf_op jit(solution)/shard_map/ppermute | solution.py:62
  33.0 5.5 %collective-permute-start.3 = (f32[1,1536]{1,0:T(1,128)S(1)}, f32[1,1536]{1,0:T(1,128)S(1)}, u32[]{:S(2)}, u32[]{:S(2)}) collective-permute-start(f32[1,1536]{1,0:T(1,128)S(1)} %add.228), channel_id=1, source_target_pairs={{0,3},{1,2},{2,1},{3,0},{4,7},{5,6},{6,5},{7,4},{8,11},{9,10},{10,... | collective-permute-start | bytes 18440 | tf_op jit(solution)/shard_map/ppermute | solution.py:62
  38.5 0.9 copy-start.10
  40.6 3.7 %collective-permute-start.5 = (f32[3,384]{1,0:T(4,128)S(1)}, f32[3,384]{1,0:T(4,128)S(1)}, u32[]{:S(2)}, u32[]{:S(2)}) collective-permute-start(f32[3,384]{1,0:T(4,128)S(1)} %bitcast.76), channel_id=1, source_target_pairs={{0,1},{1,0},{2,3},{3,2},{4,5},{5,4},{6,7},{7,6},{8,9},{9,8},{10,11... | collective-permute-start | bytes 13832 | tf_op jit(solution)/shard_map/ppermute | solution.py:62
  44.3 5.0 %collective-permute-start.6 = (f32[6,384]{1,0:T(8,128)S(1)}, f32[6,384]{1,0:T(8,128)S(1)}, u32[]{:S(2)}, u32[]{:S(2)}) collective-permute-start(f32[6,384]{1,0:T(8,128)S(1)} %pad_maximum_fusion), channel_id=1, source_target_pairs={{0,3},{1,2},{2,1},{3,0},{4,7},{5,6},{6,5},{7,4},{8,11},{9,10},{10,... | collective-permute-start | bytes 27656 | tf_op jit(solution)/shard_map/ppermute | solution.py:62
  47.6 9.6 %copy-start.3 = (bf16[384,1536]{1,0:T(8,128)(2,1)S(1)}, bf16[384,1536]{1,0:T(8,128)(2,1)}, u32[]{:S(2)}) copy-start(bf16[384,1536]{1,0:T(8,128)(2,1)} %get-tuple-element.73.w2) | copy-start | bytes 3538948
  57.2 1.3 copy-start.2
  58.5 4.6 %copy-start.4 = (bf16[384,1536]{1,0:T(8,128)(2,1)S(1)}, bf16[384,1536]{1,0:T(8,128)(2,1)}, u32[]{:S(2)}) copy-start(bf16[384,1536]{1,0:T(8,128)(2,1)} %get-tuple-element.79.w1) | copy-start | bytes 3538948
  59.5 12.4 %collective-permute-start.7 = (bf16[512,384]{1,0:T(8,128)(2,1)S(1)}, bf16[512,384]{1,0:T(8,128)(2,1)S(1)}, u32[]{:S(2)}, u32[]{:S(2)}) collective-permute-start(bf16[512,384]{1,0:T(8,128)(2,1)S(1)} %convolution_convert_fusion.2), channel_id=1, source_target_pairs={{0,1},{1,2},{2,3},{3,0},{4,7},{5,4},{6,5},{7,6},{8,9},{9,10},{10,1... | collective-permute-start | bytes 1179656 | tf_op jit(solution)/shard_map/ppermute | solution.py:36
  59.5 12.4 %collective-permute-start.8 = (bf16[512,384]{1,0:T(8,128)(2,1)S(1)}, bf16[512,384]{1,0:T(8,128)(2,1)S(1)}, u32[]{:S(2)}, u32[]{:S(2)}) collective-permute-start(bf16[512,384]{1,0:T(8,128)(2,1)S(1)} %convolution_convert_fusion.3), channel_id=1, source_target_pairs={{0,3},{1,0},{2,1},{3,2},{4,5},{5,6},{6,7},{7,4},{8,11},{9,8},{10,9... | collective-permute-start | bytes 1179656 | tf_op jit(solution)/shard_map/ppermute | solution.py:36
  74.9 1.3 copy-start.5
  75.0 11.4 %collective-permute-start.11 = (bf16[512,384]{1,0:T(8,128)(2,1)S(1)}, bf16[512,384]{1,0:T(8,128)(2,1)S(1)}, u32[]{:S(2)}, u32[]{:S(2)}) collective-permute-start(bf16[512,384]{1,0:T(8,128)(2,1)S(1)} %add_convert_fusion.2), channel_id=1, source_target_pairs={{0,1},{1,2},{2,3},{3,0},{4,7},{5,4},{6,5},{7,6},{8,9},{9,10},{10,1... | collective-permute-start | bytes 1179656 | tf_op jit(solution)/shard_map/ppermute | solution.py:36
  77.2 9.3 %copy-start.6 = (bf16[1024,384]{1,0:T(8,128)(2,1)S(1)}, bf16[1024,384]{1,0:T(8,128)(2,1)}, u32[]{:S(2)}) copy-start(bf16[1024,384]{1,0:T(8,128)(2,1)} %x0.3) | copy-start | bytes 2359300
  77.2 9.3 %copy-start.7 = (bf16[1024,384]{1,0:T(8,128)(2,1)S(1)}, bf16[1024,384]{1,0:T(8,128)(2,1)}, u32[]{:S(2)}) copy-start(bf16[1024,384]{1,0:T(8,128)(2,1)} %param.13) | copy-start | bytes 2359300
  77.2 12.9 %collective-permute-start.9 = (bf16[512,384]{1,0:T(8,128)(2,1)S(1)}, bf16[512,384]{1,0:T(8,128)(2,1)S(1)}, u32[]{:S(2)}, u32[]{:S(2)}) collective-permute-start(bf16[512,384]{1,0:T(8,128)(2,1)S(1)} %convolution_convert_fusion.1), channel_id=1, source_target_pairs={{0,3},{1,0},{2,1},{3,2},{4,5},{5,6},{6,7},{7,4},{8,11},{9,8},{10,9... | collective-permute-start | bytes 1179656 | tf_op jit(solution)/shard_map/ppermute | solution.py:36
  80.4 21.7 %collective-permute-start.15 = (bf16[512,384]{1,0:T(8,128)(2,1)S(1)}, bf16[512,384]{1,0:T(8,128)(2,1)S(1)}, u32[]{:S(2)}, u32[]{:S(2)}) collective-permute-start(bf16[512,384]{1,0:T(8,128)(2,1)S(1)} %convolution_convert_fusion), channel_id=1, source_target_pairs={{0,1},{1,2},{2,3},{3,0},{4,7},{5,4},{6,5},{7,6},{8,9},{9,10},{10,1... | collective-permute-start | bytes 1179656 | tf_op jit(solution)/shard_map/ppermute | solution.py:36
  86.8 15.3 %collective-permute-start.12 = (bf16[512,384]{1,0:T(8,128)(2,1)S(1)}, bf16[512,384]{1,0:T(8,128)(2,1)S(1)}, u32[]{:S(2)}, u32[]{:S(2)}) collective-permute-start(bf16[512,384]{1,0:T(8,128)(2,1)S(1)} %multiply_convert_fusion.1.b0.refs_1_), channel_id=1, source_target_pairs={{0,1},{1,2},{2,3},{3,0},{4,7},{5,4},{6,5},{7,6},{8,9},{9,10},{10,1... | collective-permute-start | bytes 1179656 | tf_op jit(solution)/shard_map/ppermute | solution.py:36
  86.9 15.2 %collective-permute-start.13 = (bf16[512,384]{1,0:T(8,128)(2,1)S(1)}, bf16[512,384]{1,0:T(8,128)(2,1)S(1)}, u32[]{:S(2)}, u32[]{:S(2)}) collective-permute-start(bf16[512,384]{1,0:T(8,128)(2,1)S(1)} %multiply_convert_fusion.1.b0.refs_1_), channel_id=1, source_target_pairs={{0,3},{1,0},{2,1},{3,2},{4,5},{5,6},{6,7},{7,4},{8,11},{9,8},{10,9... | collective-permute-start | bytes 1179656 | tf_op jit(solution)/shard_map/ppermute | solution.py:36
  90.2 9.4 %collective-permute-start.10 = (bf16[512,384]{1,0:T(8,128)(2,1)S(1)}, bf16[512,384]{1,0:T(8,128)(2,1)S(1)}, u32[]{:S(2)}, u32[]{:S(2)}) collective-permute-start(bf16[512,384]{1,0:T(8,128)(2,1)S(1)} %add_convert_fusion.3), channel_id=1, source_target_pairs={{0,3},{1,0},{2,1},{3,2},{4,5},{5,6},{6,7},{7,4},{8,11},{9,8},{10,9... | collective-permute-start | bytes 1179656 | tf_op jit(solution)/shard_map/ppermute | solution.py:36
  102.5 12.1 %collective-permute-start.16 = (bf16[512,384]{1,0:T(8,128)(2,1)S(1)}, bf16[512,384]{1,0:T(8,128)(2,1)S(1)}, u32[]{:S(2)}, u32[]{:S(2)}) collective-permute-start(bf16[512,384]{1,0:T(8,128)(2,1)S(1)} %multiply_convert_fusion.b0.refs_2_), channel_id=1, source_target_pairs={{0,3},{1,0},{2,1},{3,2},{4,5},{5,6},{6,7},{7,4},{8,11},{9,8},{10,9... | collective-permute-start | bytes 1179656 | tf_op jit(solution)/shard_map/ppermute | solution.py:36
  103.7 13.2 %collective-permute-start.14 = (bf16[512,384]{1,0:T(8,128)(2,1)S(1)}, bf16[512,384]{1,0:T(8,128)(2,1)S(1)}, u32[]{:S(2)}, u32[]{:S(2)}) collective-permute-start(bf16[512,384]{1,0:T(8,128)(2,1)S(1)} %collective-permute-done.12.b2.refs_2_), channel_id=1, source_target_pairs={{0,1},{1,2},{2,3},{3,0},{4,7},{5,4},{6,5},{7,6},{8,9},{9,10},{10,1... | collective-permute-start | bytes 1179656 | tf_op jit(solution)/shard_map/ppermute | solution.py:36
  104.5 16.9 %collective-permute-start.18 = (bf16[512,384]{1,0:T(8,128)(2,1)S(1)}, bf16[512,384]{1,0:T(8,128)(2,1)S(1)}, u32[]{:S(2)}, u32[]{:S(2)}) collective-permute-start(bf16[512,384]{1,0:T(8,128)(2,1)S(1)} %multiply_convert_fusion.b0.refs_2_), channel_id=1, source_target_pairs={{0,1},{1,2},{2,3},{3,0},{4,7},{5,4},{6,5},{7,6},{8,9},{9,10},{10,1... | collective-permute-start | bytes 1179656 | tf_op jit(solution)/shard_map/ppermute | solution.py:36
  114.6 15.3 %collective-permute-start.17 = (bf16[512,384]{1,0:T(8,128)(2,1)S(1)}, bf16[512,384]{1,0:T(8,128)(2,1)S(1)}, u32[]{:S(2)}, u32[]{:S(2)}) collective-permute-start(bf16[512,384]{1,0:T(8,128)(2,1)S(1)} %collective-permute-done.16.b1.refs_3_), channel_id=1, source_target_pairs={{0,3},{1,0},{2,1},{3,2},{4,5},{5,6},{6,7},{7,4},{8,11},{9,8},{10,9... | collective-permute-start | bytes 1179656 | tf_op jit(solution)/shard_map/ppermute | solution.py:36
  141.0 10.1 %collective-permute-start.22 = (bf16[768,1536]{1,0:T(8,128)(2,1)S(1)}, bf16[768,1536]{1,0:T(8,128)(2,1)S(1)}, u32[]{:S(2)}, u32[]{:S(2)}) collective-permute-start(bf16[768,1536]{1,0:T(8,128)(2,1)S(1)} %get-tuple-element.115), channel_id=1, source_target_pairs={{0,4},{4,0},{8,12},{12,8},{16,20},{20,16},{24,28},{28,24},{32,36},... | collective-permute-start | bytes 7077896 | tf_op jit(solution)/shard_map/ppermute | solution.py:46
  141.1 10.0 %collective-permute-start.23 = (bf16[768,1536]{1,0:T(8,128)(2,1)S(1)}, bf16[768,1536]{1,0:T(8,128)(2,1)S(1)}, u32[]{:S(2)}, u32[]{:S(2)}) collective-permute-start(bf16[768,1536]{1,0:T(8,128)(2,1)S(1)} %get-tuple-element.116), channel_id=1, source_target_pairs={{0,4},{4,0},{8,12},{12,8},{16,20},{20,16},{24,28},{28,24},{32,36},... | collective-permute-start | bytes 7077896 | tf_op jit(solution)/shard_map/ppermute | solution.py:46
  141.6 3.5 %collective-permute-start.19 = (f32[1,128]{1,0:T(1,128)S(1)}, f32[1,128]{1,0:T(1,128)S(1)}, u32[]{:S(2)}, u32[]{:S(2)}) collective-permute-start(f32[1,128]{1,0:T(1,128)S(1)} %get-tuple-element.112), channel_id=1, source_target_pairs={{0,1},{1,0},{2,3},{3,2},{4,5},{5,4},{6,7},{7,6},{8,9},{9,8},{10,11... | collective-permute-start | bytes 1544 | tf_op jit(solution)/shard_map/ppermute | solution.py:62
  145.1 4.8 %collective-permute-start.20 = (f32[1,128]{1,0:T(1,128)S(1)}, f32[1,128]{1,0:T(1,128)S(1)}, u32[]{:S(2)}, u32[]{:S(2)}) collective-permute-start(f32[1,128]{1,0:T(1,128)S(1)} %add.252), channel_id=1, source_target_pairs={{0,3},{1,2},{2,1},{3,0},{4,7},{5,6},{6,5},{7,4},{8,11},{9,10},{10,... | collective-permute-start | bytes 1544 | tf_op jit(solution)/shard_map/ppermute | solution.py:62
  149.9 1.2 collective-permute-start.21
  152.5 11.2 %collective-permute-start.24 = (bf16[4,48,1536]{2,1,0:T(8,128)(2,1)S(1)}, bf16[4,48,1536]{2,1,0:T(8,128)(2,1)S(1)}, u32[]{:S(2)}, u32[]{:S(2)}) collective-permute-start(bf16[4,48,1536]{2,1,0:T(8,128)(2,1)S(1)} %get-tuple-element.118), channel_id=1, source_target_pairs={{0,32},{4,12},{8,40},{12,20},{16,48},{20,28},{24,56},{28,4},{32,64... | collective-permute-start | bytes 1769480 | tf_op jit(solution)/shard_map/ppermute | solution.py:46
  153.1 10.5 %collective-permute-start.25 = (bf16[4,48,1536]{2,1,0:T(8,128)(2,1)S(1)}, bf16[4,48,1536]{2,1,0:T(8,128)(2,1)S(1)}, u32[]{:S(2)}, u32[]{:S(2)}) collective-permute-start(bf16[4,48,1536]{2,1,0:T(8,128)(2,1)S(1)} %get-tuple-element.119), channel_id=1, source_target_pairs={{0,96},{4,28},{8,104},{12,4},{16,112},{20,12},{24,120},{28,20},{32... | collective-permute-start | bytes 1769480 | tf_op jit(solution)/shard_map/ppermute | solution.py:46
  157.7 11.8 %collective-permute-start.27 = (bf16[4,48,1536]{2,1,0:T(8,128)(2,1)S(1)}, bf16[4,48,1536]{2,1,0:T(8,128)(2,1)S(1)}, u32[]{:S(2)}, u32[]{:S(2)}) collective-permute-start(bf16[4,48,1536]{2,1,0:T(8,128)(2,1)S(1)} %get-tuple-element.121), channel_id=1, source_target_pairs={{0,96},{4,28},{8,104},{12,4},{16,112},{20,12},{24,120},{28,20},{32... | collective-permute-start | bytes 1769480 | tf_op jit(solution)/shard_map/ppermute | solution.py:46
  157.8 12.2 %collective-permute-start.28 = (bf16[4,48,1536]{2,1,0:T(8,128)(2,1)S(1)}, bf16[4,48,1536]{2,1,0:T(8,128)(2,1)S(1)}, u32[]{:S(2)}, u32[]{:S(2)}) collective-permute-start(bf16[4,48,1536]{2,1,0:T(8,128)(2,1)S(1)} %get-tuple-element.122), channel_id=1, source_target_pairs={{0,32},{4,12},{8,40},{12,20},{16,48},{20,28},{24,56},{28,4},{32,64... | collective-permute-start | bytes 1769480 | tf_op jit(solution)/shard_map/ppermute | solution.py:46
  165.3 11.2 %collective-permute-start.26 = (bf16[4,48,1536]{2,1,0:T(8,128)(2,1)S(1)}, bf16[4,48,1536]{2,1,0:T(8,128)(2,1)S(1)}, u32[]{:S(2)}, u32[]{:S(2)}) collective-permute-start(bf16[4,48,1536]{2,1,0:T(8,128)(2,1)S(1)} %get-tuple-element.120), channel_id=1, source_target_pairs={{0,32},{4,12},{8,40},{12,20},{16,48},{20,28},{24,56},{28,4},{32,64... | collective-permute-start | bytes 1769480 | tf_op jit(solution)/shard_map/ppermute | solution.py:46
  165.4 11.0 %collective-permute-start.29 = (bf16[4,48,1536]{2,1,0:T(8,128)(2,1)S(1)}, bf16[4,48,1536]{2,1,0:T(8,128)(2,1)S(1)}, u32[]{:S(2)}, u32[]{:S(2)}) collective-permute-start(bf16[4,48,1536]{2,1,0:T(8,128)(2,1)S(1)} %get-tuple-element.123), channel_id=1, source_target_pairs={{0,96},{4,28},{8,104},{12,4},{16,112},{20,12},{24,120},{28,20},{32... | collective-permute-start | bytes 1769480 | tf_op jit(solution)/shard_map/ppermute | solution.py:46
  177.7 14.5 %copy-start.8 = (f32[48,1536]{1,0:T(8,128)S(1)}, f32[48,1536]{1,0:T(8,128)}, u32[]{:S(2)}) copy-start(f32[48,1536]{1,0:T(8,128)} %param.23) | copy-start | bytes 884740
  177.7 14.5 %copy-start.9 = (f32[48,1536]{1,0:T(8,128)S(1)}, f32[48,1536]{1,0:T(8,128)}, u32[]{:S(2)}) copy-start(f32[48,1536]{1,0:T(8,128)} %param.22) | copy-start | bytes 884740
  177.7 7.5 %collective-permute-start.32 = (bf16[2,48,1536]{2,1,0:T(8,128)(2,1)S(1)}, bf16[2,48,1536]{2,1,0:T(8,128)(2,1)S(1)}, u32[]{:S(2)}, u32[]{:S(2)}) collective-permute-start(bf16[2,48,1536]{2,1,0:T(8,128)(2,1)S(1)} %get-tuple-element.127), channel_id=1, source_target_pairs={{0,24},{4,100},{8,0},{12,108},{16,8},{20,116},{24,16},{28,124},{32... | collective-permute-start | bytes 884744 | tf_op jit(solution)/shard_map/ppermute | solution.py:46
  180.9 11.1 %collective-permute-start.31 = (bf16[2,48,1536]{2,1,0:T(8,128)(2,1)S(1)}, bf16[2,48,1536]{2,1,0:T(8,128)(2,1)S(1)}, u32[]{:S(2)}, u32[]{:S(2)}) collective-permute-start(bf16[2,48,1536]{2,1,0:T(8,128)(2,1)S(1)} %get-tuple-element.126), channel_id=1, source_target_pairs={{0,8},{4,36},{8,16},{12,44},{16,24},{20,52},{24,0},{28,60},{32,40}... | collective-permute-start | bytes 884744 | tf_op jit(solution)/shard_map/ppermute | solution.py:46
  180.9 11.1 %collective-permute-start.30 = (bf16[2,48,1536]{2,1,0:T(8,128)(2,1)S(1)}, bf16[2,48,1536]{2,1,0:T(8,128)(2,1)S(1)}, u32[]{:S(2)}, u32[]{:S(2)}) collective-permute-start(bf16[2,48,1536]{2,1,0:T(8,128)(2,1)S(1)} %get-tuple-element.125), channel_id=1, source_target_pairs={{0,16},{4,68},{8,24},{12,76},{16,0},{20,84},{24,8},{28,92},{32,48}... | collective-permute-start | bytes 884744 | tf_op jit(solution)/shard_map/ppermute | solution.py:46
  192.0 2.2 %copy-start.1 = (bf16[1536,3,384]{2,0,1:T(8,128)(2,1)S(1)}, bf16[1536,3,384]{2,0,1:T(8,128)(2,1)}, u32[]{:S(2)}) copy-start(bf16[1536,3,384]{2,0,1:T(8,128)(2,1)} %param.19) | copy-start | bytes 10616836

commit v3 on v1

--- a/solution.py
+++ b/solution.py
@@ -131,9 +131,9 @@
     hidden[...] = ((0.5 * value) * (1.0 + bent)).astype(BF)
 
 
-def forward(chunk, at, blocks, mods, in_w):
-    rows, ff = blocks[0].shape[0] // 2, in_w.shape[1]
-    piece = pl.BlockSpec((rows, PART), lambda s, *_: (chunk, 0))
+def forward(first, rows, at, blocks, mods, in_w):
+    ff = in_w.shape[1]
+    piece = pl.BlockSpec((rows, PART), lambda s, *_: (first // rows, 0))
     return call(
         forward_kernel,
         ff // WIDE,
@@ -161,16 +161,16 @@
 
 
 def turn(at, top, low):
-    rows = top.shape[0]
-    out = pl.BlockSpec((PART // 2, 2 * rows), lambda s, *_: (s, 0))
+    rows = top.shape[0] + low.shape[0]
+    out = pl.BlockSpec((PART // 2, rows), lambda s, *_: (s, 0))
     return call(
         turn_kernel,
         RING,
-        [columns(rows, PART)] * 2,
+        [columns(top.shape[0], PART), columns(low.shape[0], PART)],
         [out, out],
-        [shaped((D // 2, 2 * rows))] * 2,
-        [pltpu.VMEM((PART, 2 * rows), BF)],
-        cost(2 * rows * D, 8 * rows * D),
+        [shaped((D // 2, rows))] * 2,
+        [pltpu.VMEM((PART, rows), BF)],
+        cost(rows * D, 4 * rows * D),
         "turn",
     )(at, top, low)
 
@@ -233,7 +233,8 @@
 
 
 def rows_grad(at, places, tops, lows, rights, before):
-    rows, ff = rights[0].shape
+    ff = rights[0].shape[1]
+    rows = rights[0].shape[0] + rights[1].shape[0]
     count = len(tops)
     first = places[0]
     step = places[1] - first if count > 1 else 0
@@ -241,13 +242,12 @@
     return call(
         lambda *refs: rows_kernel(count, *refs),
         count,
-        [whole((rows, PART))] * (2 * count)
-        + [whole((rows, ff))] * 2
+        [whole(block.shape) for block in (*tops, *lows, *rights)]
         + [pl.BlockSpec(memory_space=pl.ANY)] * len(before),
         [out, out, whole((1, ff))],
         [shaped((D // 2, ff))] * 2 + [shaped((1, ff), F32)],
-        [pltpu.VMEM((PART, 2 * rows), BF)],
-        cost(4 * rows * PART * ff * count, 5 * 10**6 * count),
+        [pltpu.VMEM((PART, rows), BF)],
+        cost(2 * rows * PART * ff * count, 5 * 10**6 * count),
         "rows_grad",
         {2 * count + 3 + n: n for n in range(len(before))},
     )(at, *tops, *lows, *rights, *before)
@@ -278,16 +278,19 @@
 
 
 def weight_grad(at, keep_l, send_l, rights, squares):
-    rows, ff = rights[0].shape
+    ff = rights[0].shape[1]
+    rows = rights[0].shape[0] + rights[1].shape[0]
     width = 512
     return call(
         weight_kernel,
         ff // width,
-        [whole((D // 2, 2 * rows))] * 2 + [columns(rows, width)] * 2 + [whole((1, ff))] * 3,
+        [whole((D // 2, rows))] * 2
+        + [columns(right.shape[0], width) for right in rights]
+        + [whole((1, ff))] * 3,
         [columns(D // 2, width)] * 2 + [whole((1, 128))],
         [shaped((D // 2, ff))] * 2 + [shaped((1, 128), F32)],
         [pltpu.VMEM((1, width), F32)],
-        cost(4 * rows * D * ff, 11 * 10**6),
+        cost(2 * rows * D * ff, 11 * 10**6),
         "weight_grad",
     )(at, keep_l, send_l, *rights, *squares)
 
@@ -416,7 +419,7 @@
     received = lax.all_to_all(everywhere, "dp", 0, 0, tiled=True)
 
     behind, next_ahead = by_x(latents, 1), by_x(latents, -1)
-    half = rows // 2
+    cut = rows * 3 // 4
     received, behind, next_ahead, at, outs = lax.optimization_barrier(
         (received, behind, next_ahead, at, outs)
     )
@@ -451,32 +454,37 @@
             hidden, outs[j], (((1,), (1,)), ((), ())), preferred_element_type=F32
         )
 
-    def leave(k, own, up, down):
-        at_rows = slice(k * half, (k + 1) * half)
+    def leave(first, last, own, up, down):
+        at_rows = slice(first, last)
         output = latents[at_rows].astype(F32) + gate * (
             own + up.astype(F32) + down.astype(F32)
         )
-        live = (jnp.arange(k * half, (k + 1) * half) % token_span < count).astype(F32)[:, None]
+        live = (jnp.arange(first, last) % token_span < count).astype(F32)[:, None]
         delta = (output - targets[at_rows].astype(F32)) * live * factor
         return (gate * delta).astype(BF)
 
     latent_blocks = (latents, next_ahead, far, behind)
-    modded0, hidden0, pre0 = forward(0, at, latent_blocks, mods, in_w)
+    modded0, hidden0, pre0 = forward(0, cut, at, latent_blocks, mods, in_w)
     far0, down0 = project(hidden0, 2).astype(BF), project(hidden0, 3).astype(BF)
     far0 = by_x(far0, 1)
     at_next, down0 = lax.optimization_barrier((at, down0))
     down0 = by_x(down0, -1)
     up0, own0 = lax.optimization_barrier((project(hidden0, 1), project(hidden0, 0)))
-    modded1, hidden1, pre1 = forward(1, at_next, latent_blocks, mods, in_w)
+    modded1, hidden1, pre1 = forward(
+        cut, rows - cut, at_next, latent_blocks, mods, in_w
+    )
     hidden1, far0, down0 = lax.optimization_barrier((hidden1, far0, down0))
-    up0 = by_x((up0 + far0.astype(F32)).astype(BF), 1)
+    up0 = (up0 + far0.astype(F32)).astype(BF)
+    up0, hidden1 = lax.optimization_barrier((up0, hidden1))
+    up0 = by_x(up0, 1)
     far1, up1 = project(hidden1, 2).astype(BF), project(hidden1, 1).astype(BF)
     far1, up1, hidden1, at_late, pre0, pre1 = lax.optimization_barrier(
         (far1, up1, hidden1, at, pre0, pre1)
     )
     far1, up1 = by_x(far1, -1), by_x(up1, 1)
-    down1, own1 = lax.optimization_barrier((project(hidden1, 3), project(hidden1, 0)))
-    back0 = leave(0, own0, up0, down0)
+    back0 = leave(0, cut, own0, up0, down0)
+    hidden1_late, back0 = lax.optimization_barrier((hidden1, back0))
+    down1, own1 = project(hidden1_late, 3), project(hidden1_late, 0)
     behind0, ahead0 = by_x(back0, 1), by_x(back0, -1)
     down1 = by_x((down1 + far1.astype(F32)).astype(BF), -1)
     slope0, slope1 = slope_of(pre0).astype(BF), slope_of(pre1).astype(BF)
@@ -484,7 +492,7 @@
     down1, slope0, slope1, mod_keep, mod_send, behind0, ahead0 = lax.optimization_barrier(
         (down1, slope0, slope1, mod_keep, mod_send, behind0, ahead0)
     )
-    back1 = leave(1, own1, up1, down1)
+    back1 = leave(cut, rows, own1, up1, down1)
     far0 = by_x(behind0, 1)
     behind1, ahead1 = by_x(back1, 1), by_x(back1, -1)
     far1 = by_x(ahead1, -1)
@@ -492,10 +500,11 @@
     rights = (hidden0, hidden1)
     *second, square_a = rows_grad(at, (0,), (back0,), (back1,), rights, ())
     grad0 = backward(at, (back0, ahead0, far0, behind0), out_w, slope0)
+    at_last, grad0 = lax.optimization_barrier((at, grad0))
     *second, square_b = rows_grad(
-        at, (1, 3), (ahead0, behind0), (ahead1, behind1), rights, tuple(second)
-    )
-    grad1 = backward(at, (back1, ahead1, far1, behind1), out_w, slope1)
+        at_last, (1, 3), (ahead0, behind0), (ahead1, behind1), rights, tuple(second)
+    )
+    grad1 = backward(at_last, (back1, ahead1, far1, behind1), out_w, slope1)
     *second, square_c = rows_grad(at, (2,), (far0,), (far1,), rights, tuple(second))
     keep2, send2 = second
     got2 = by_core(send2)

time: 194 us -> 197 us (1.015)
  waiting for transfers between devices: 53.1 us -> 56.3 us
    ppermute x15, waiting for transfers between devices: 18.2 us -> 21.6 us  [by_x(): return lax.ppermute(value, ('dp', 'mp'), pairs)]
  transfers between devices with their start and end apart: 31 -> 31, of which waited for: 18 -> 19; matrix products, arithmetic and copies ran while one was open for 9% -> 10% of each run, Pallas kernels for 13% -> 12%
where the time goes in v3:
time: 197 us
  waiting for transfers between devices  56.3 us (29%)
  starting transfers between devices  48.3 us (25%)
  Pallas kernels  48.1 us (24%)
  blocking collectives  17 us (9%)
  matrix products  12.1 us (6%)
  other arithmetic  6.5 us (3%)
  local copies, waits for them, and re-layouts  5.47 us (3%)
  between operations  3.2 us (2%)
    ppermute x15, waiting for transfers between devices, by_x(): return lax.ppermute(value, ('dp', 'mp'), pairs)  21.6 us
    ppermute x15, starting transfers between devices, by_x(): return lax.ppermute(value, ('dp', 'mp'), pairs)  20.8 us
    ppermute x6, waiting for transfers between devices, swap_x(): return lax.ppermute(value, 'mp', list(enumerate(other)))  18.8 us
    all_to_all x1, blocking collectives, local(): lax.all_to_all(value, 'dp', 0, 0, axis_index_groups=groups, tiled=True)  17 us
    pallas_call x2, Pallas kernels, forward(): call(forward_kernel, ff // WIDE, [piece] * 4 + [whole((3, PART)), whole((...  16.2 us
    ppermute x9, waiting for transfers between devices, by_dp(): return lax.ppermute(value, 'dp', pairs)  12.9 us
    ppermute x9, starting transfers between devices, by_dp(): return lax.ppermute(value, 'dp', pairs)  9.45 us
    ppermute x6, starting transfers between devices, swap_x(): return lax.ppermute(value, 'mp', list(enumerate(other)))  9.44 us
  transfers between devices with their start and end apart: 31, of which 19 were waited for; matrix products, arithmetic and copies ran while one was open for 10% of the time, Pallas kernels for 12%

profile of v3, /device:TPU:0, one launch (start us, length us, event | category | flops | bytes accessed | tf_op | source)
XLA Modules:
  0.0 197.0 jit_solution(11419690265948037714)
XLA Ops:
  0.6 1.6 collective-permute-start
  2.3 1.7 collective-permute-start.1
  6.4 8.5 %all-to-all-start = ((f32[32,8,128]{2,1,0:T(8,128)}), f32[32,8,128]{2,1,0:T(8,128)}, u32[]{:S(2)}, u32[]{:S(2)}) async-start(f32[32,8,128]{2,1,0:T(8,128)} %broadcast_in_dim.31), calls=%async_computation | async-start | bytes 262144 | tf_op jit(solution)/shard_map/all_to_all | solution.py:419
  15.1 4.6 %constant_dynamic-slice_fusion = (bf16[384,1536]{1,0:T(8,128)(2,1)}, bf16[384,1536]{1,0:T(8,128)(2,1)}, bf16[384,1536]{1,0:T(8,128)(2,1)}, bf16[384,1536]{1,0:T(8,128)(2,1)}) fusion(bf16[1536,1536]{1,0:T(8,128)(2,1)} %out_w.3, s32[]{:T(128)S(6)} %select_n.114, s32[]{:T(128)S(6)} %select_n.113, s32[]{:T(128)S(6)} %select_n.112, s32[]{:T(128)S(6)} %select_n.111), kind=kLoop, calls=%fused_computation.59 | loop fusion | bytes 9437200 | tf_op jit(solution)/shard_map/dynamic_slice | solution.py:412
  19.7 3.0 %all-to-all-done = f32[32,8,128]{2,1,0:T(8,128)} async-done(((f32[32,8,128]{2,1,0:T(8,128)}), f32[32,8,128]{2,1,0:T(8,128)}, u32[]{:S(2)}, u32[]{:S(2)}) %all-to-all-start) | async-done | bytes 131104 | tf_op jit(solution)/shard_map/all_to_all | solution.py:419
  24.1 2.4 %fusion.34 = f32[1,1536]{1,0:T(1,128)S(1)} fusion(bf16[1024,1]{0,1:T(2,128)(2,1)S(1)} %reshape.95, bf16[1024,1536]{1,0:T(8,128)(2,1)} %param.18), kind=kOutput, calls=%fused_computation.68 | convolution fusion | flops 3145728 | bytes 3153920 | tf_op jit(solution)/shard_map/dot_general | solution.py:24
  26.5 1.5 collective-permute-start.2
  28.0 5.0 %collective-permute-done.2 = f32[1,1536]{1,0:T(1,128)S(1)} collective-permute-done((f32[1,1536]{1,0:T(1,128)S(1)}, f32[1,1536]{1,0:T(1,128)S(1)}, u32[]{:S(2)}, u32[]{:S(2)}) %collective-permute-start.2) | collective-permute-done | bytes 6176 | tf_op jit(solution)/shard_map/ppermute | solution.py:62
  33.0 3.9 %collective-permute-start.3 = (f32[1,1536]{1,0:T(1,128)S(1)}, f32[1,1536]{1,0:T(1,128)S(1)}, u32[]{:S(2)}, u32[]{:S(2)}) collective-permute-start(f32[1,1536]{1,0:T(1,128)S(1)} %add.193), channel_id=1, source_target_pairs={{0,3},{1,2},{2,1},{3,0},{4,7},{5,6},{6,5},{7,4},{8,11},{9,10},{10,... | collective-permute-start | bytes 18440 | tf_op jit(solution)/shard_map/ppermute | solution.py:62
  41.2 2.9 %collective-permute-done.5.m1 = f32[3,384]{1,0:T(4,128)S(1)} collective-permute-done((f32[3,384]{1,0:T(4,128)S(1)}, f32[3,384]{1,0:T(4,128)S(1)}, u32[]{:S(2)}, u32[]{:S(2)}) %collective-permute-start.5) | collective-permute-done | bytes 4640 | tf_op jit(solution)/shard_map/ppermute | solution.py:62
  44.1 3.3 %collective-permute-start.6 = (f32[6,384]{1,0:T(8,128)S(1)}, f32[6,384]{1,0:T(8,128)S(1)}, u32[]{:S(2)}, u32[]{:S(2)}) collective-permute-start(f32[6,384]{1,0:T(8,128)S(1)} %pad_maximum_fusion), channel_id=1, source_target_pairs={{0,3},{1,2},{2,1},{3,0},{4,7},{5,6},{6,5},{7,4},{8,11},{9,10},{10,... | collective-permute-start | bytes 27656 | tf_op jit(solution)/shard_map/ppermute | solution.py:62
  47.4 1.7 collective-permute-done.6.m2
  49.1 10.4 %forward.2 = (bf16[768,1536]{1,0:T(8,128)(2,1)S(1)}, bf16[768,1536]{1,0:T(8,128)(2,1)S(1)}, f32[768,1536]{1,0:T(8,128)S(1)}) custom-call(s32[16]{0:T(128)S(1)} %stack.59.at.refs_0_, bf16[1024,384]{1,0:T(8,128)(2,1)} %x0.3, bf16[1024,384]{1,0:T(8,128)(2,1)} %collective-permute-done.1.x1, bf16[1024,384]{1,0:T(8,128)(2,1)} %collective-permute-done.4.x2, ...), custom_call_target="tpu_custom_call" | custom-call | flops 3623878656 | bytes 12000000 | tf_op jit(solution)/shard_map/forward/pallas_call | solution.py:137
  59.6 1.4 convolution_convert_fusion
  61.1 1.4 convolution_convert_fusion.1
  62.5 3.5 %collective-permute-start.8 = (bf16[768,384]{1,0:T(8,128)(2,1)S(1)}, bf16[768,384]{1,0:T(8,128)(2,1)S(1)}, u32[]{:S(2)}, u32[]{:S(2)}) collective-permute-start(bf16[768,384]{1,0:T(8,128)(2,1)S(1)} %convolution_convert_fusion.1), channel_id=1, source_target_pairs={{0,3},{1,0},{2,1},{3,2},{4,5},{5,6},{6,7},{7,4},{8,11},{9,8},{10,9... | collective-permute-start | bytes 1769480 | tf_op jit(solution)/shard_map/ppermute | solution.py:36
  65.9 1.4 fusion.36
  67.4 1.4 fusion.35
  68.8 5.8 %forward.3 = (bf16[256,1536]{1,0:T(8,128)(2,1)S(1)}, bf16[256,1536]{1,0:T(8,128)(2,1)S(1)}, f32[256,1536]{1,0:T(8,128)S(1)}) custom-call(s32[16]{0:T(128)S(1)} %stack.59.at.refs_0_, bf16[1024,384]{1,0:T(8,128)(2,1)} %x0.3, bf16[1024,384]{1,0:T(8,128)(2,1)} %collective-permute-done.1.x1, bf16[1024,384]{1,0:T(8,128)(2,1)} %collective-permute-done.4.x2, ...), custom_call_target="tpu_custom_call" | custom-call | flops 1207959552 | bytes 12000000 | tf_op jit(solution)/shard_map/forward/pallas_call | solution.py:137
  74.6 2.4 %collective-permute-done.7 = bf16[768,384]{1,0:T(8,128)(2,1)S(1)} collective-permute-done((bf16[768,384]{1,0:T(8,128)(2,1)S(1)}, bf16[768,384]{1,0:T(8,128)(2,1)S(1)}, u32[]{:S(2)}, u32[]{:S(2)}) %collective-permute-start.7) | collective-permute-done | bytes 589856 | tf_op jit(solution)/shard_map/ppermute | solution.py:36
  78.5 3.1 %collective-permute-start.10 = (bf16[256,384]{1,0:T(8,128)(2,1)S(1)}, bf16[256,384]{1,0:T(8,128)(2,1)S(1)}, u32[]{:S(2)}, u32[]{:S(2)}) collective-permute-start(bf16[256,384]{1,0:T(8,128)(2,1)S(1)} %convolution_convert_fusion.3), channel_id=1, source_target_pairs={{0,3},{1,0},{2,1},{3,2},{4,5},{5,6},{6,7},{7,4},{8,11},{9,8},{10,9... | collective-permute-start | bytes 589832 | tf_op jit(solution)/shard_map/ppermute | solution.py:36
  81.6 2.4 %add_convert_fusion.slope = bf16[768,1536]{1,0:T(8,128)(2,1)S(1)} fusion(f32[768,1536]{1,0:T(8,128)S(1)} %get-tuple-element.91), kind=kLoop, calls=%fused_computation | loop fusion | flops 17694720 | bytes 7077888 | tf_op jit(solution)/shard_map/convert_element_type | solution.py:490
  84.0 5.5 %collective-permute-done.9 = bf16[768,384]{1,0:T(8,128)(2,1)S(1)} collective-permute-done((bf16[768,384]{1,0:T(8,128)(2,1)S(1)}, bf16[768,384]{1,0:T(8,128)(2,1)S(1)}, u32[]{:S(2)}, u32[]{:S(2)}) %collective-permute-start.9) | collective-permute-done | bytes 589856 | tf_op jit(solution)/shard_map/ppermute | solution.py:36
  90.2 3.0 %collective-permute-start.13 = (bf16[768,384]{1,0:T(8,128)(2,1)S(1)}, bf16[768,384]{1,0:T(8,128)(2,1)S(1)}, u32[]{:S(2)}, u32[]{:S(2)}) collective-permute-start(bf16[768,384]{1,0:T(8,128)(2,1)S(1)} %multiply_convert_fusion.b0.refs_1_), channel_id=1, source_target_pairs={{0,3},{1,0},{2,1},{3,2},{4,5},{5,6},{6,7},{7,4},{8,11},{9,8},{10,9... | collective-permute-start | bytes 1769480 | tf_op jit(solution)/shard_map/ppermute | solution.py:36
  94.7 2.2 %turn.1 = (bf16[768,1024]{1,0:T(8,128)(2,1)S(1)}, bf16[768,1024]{1,0:T(8,128)(2,1)S(1)}) custom-call(s32[16]{0:T(128)S(1)} %stack.59.at.refs_0_, bf16[768,1536]{1,0:T(8,128)(2,1)S(1)} %get-tuple-element.94.top, bf16[256,1536]{1,0:T(8,128)(2,1)S(1)} %get-tuple-element.95.low), custom_call_target="tpu_custom_call" | custom-call | flops 1572864 | bytes 6291456 | tf_op jit(solution)/shard_map/turn/pallas_call | solution.py:166
  96.9 8.9 %collective-permute-done.11 = bf16[256,384]{1,0:T(8,128)(2,1)S(1)} collective-permute-done((bf16[256,384]{1,0:T(8,128)(2,1)S(1)}, bf16[256,384]{1,0:T(8,128)(2,1)S(1)}, u32[]{:S(2)}, u32[]{:S(2)}) %collective-permute-start.11) | collective-permute-done | bytes 196640 | tf_op jit(solution)/shard_map/ppermute | solution.py:36
  105.9 1.3 collective-permute-done.12.b3.refs_2_
  108.3 2.9 %collective-permute-start.16 = (bf16[256,384]{1,0:T(8,128)(2,1)S(1)}, bf16[256,384]{1,0:T(8,128)(2,1)S(1)}, u32[]{:S(2)}, u32[]{:S(2)}) collective-permute-start(bf16[256,384]{1,0:T(8,128)(2,1)S(1)} %fusion.8.b0.refs_2_), channel_id=1, source_target_pairs={{0,3},{1,0},{2,1},{3,2},{4,5},{5,6},{6,7},{7,4},{8,11},{9,8},{10,9... | collective-permute-start | bytes 589832 | tf_op jit(solution)/shard_map/ppermute | solution.py:36
  111.2 2.0 rows_grad.3
  113.2 3.4 %collective-permute-done.16.b1.refs_3_ = bf16[256,384]{1,0:T(8,128)(2,1)S(1)} collective-permute-done((bf16[256,384]{1,0:T(8,128)(2,1)S(1)}, bf16[256,384]{1,0:T(8,128)(2,1)S(1)}, u32[]{:S(2)}, u32[]{:S(2)}) %collective-permute-start.16) | collective-permute-done | bytes 196640 | tf_op jit(solution)/shard_map/ppermute | solution.py:36
  116.5 3.7 %collective-permute-start.17 = (bf16[256,384]{1,0:T(8,128)(2,1)S(1)}, bf16[256,384]{1,0:T(8,128)(2,1)S(1)}, u32[]{:S(2)}, u32[]{:S(2)}) collective-permute-start(bf16[256,384]{1,0:T(8,128)(2,1)S(1)} %collective-permute-done.16.b1.refs_3_), channel_id=1, source_target_pairs={{0,3},{1,0},{2,1},{3,2},{4,5},{5,6},{6,7},{7,4},{8,11},{9,8},{10,9... | collective-permute-start | bytes 589832 | tf_op jit(solution)/shard_map/ppermute | solution.py:36
  120.4 5.6 %backward.2.right0 = bf16[768,1536]{1,0:T(8,128)(2,1)S(1)} custom-call(s32[16]{0:T(128)S(1)} %stack.59.at.refs_0_, bf16[768,384]{1,0:T(8,128)(2,1)S(1)} %multiply_convert_fusion.b0.refs_1_, bf16[768,384]{1,0:T(8,128)(2,1)S(1)} %collective-permute-done.13.b1.refs_1_, bf16[768,384]{1,0:T(8,128)(2,1)S(1)} %collective-permute-done.14.b2.refs_1_, ...), custom_call_target="tpu_custom_call" | custom-call | flops 3623878656 | bytes 14000000 | tf_op jit(solution)/shard_map/backward/pallas_call | solution.py:189
  126.0 4.8 %rows_grad.4 = (bf16[768,1536]{1,0:T(8,128)(2,1)S(1)}, bf16[768,1536]{1,0:T(8,128)(2,1)S(1)}, f32[1,1536]{1,0:T(1,128)S(1)}) custom-call(s32[16]{0:T(128)S(1)} %stack.59.at.refs_0_, bf16[768,384]{1,0:T(8,128)(2,1)S(1)} %collective-permute-done.13.b1.refs_1_, ...), custom_call_target="tpu_custom_call", output_to_operand_aliasing={{0}: (7, {}), {1}: (8, {})} | custom-call | flops 2415919104 | bytes 10000000 | tf_op jit(solution)/shard_map/rows_grad/pallas_call | solution.py:242
  130.8 2.8 %backward.3.right1 = bf16[256,1536]{1,0:T(8,128)(2,1)S(1)} custom-call(s32[16]{0:T(128)S(1)} %stack.59.at.refs_0_, bf16[256,384]{1,0:T(8,128)(2,1)S(1)} %fusion.8.b0.refs_2_, bf16[256,384]{1,0:T(8,128)(2,1)S(1)} %collective-permute-done.16.b1.refs_3_, bf16[256,384]{1,0:T(8,128)(2,1)S(1)} %collective-permute-done.17.b2.refs_2_, ...), custom_call_target="tpu_custom_call" | custom-call | flops 1207959552 | bytes 14000000 | tf_op jit(solution)/shard_map/backward/pallas_call | solution.py:189
  133.6 2.0 rows_grad.5
  135.6 6.7 %weight_grad.1 = (bf16[768,1536]{1,0:T(8,128)(2,1)S(1)}, bf16[768,1536]{1,0:T(8,128)(2,1)S(1)}, f32[1,128]{1,0:T(1,128)S(1)}) custom-call(s32[16]{0:T(128)S(1)} %stack.59.at.refs_0_, bf16[768,1024]{1,0:T(8,128)(2,1)S(1)} %get-tuple-element.99.keep_l, bf16[768,1024]{1,0:T(8,128)(2,1)S(1)} %get-tuple-element.100.send_l, bf16[768,1536]{1,0:T(8,128)(2,1)S(1)} %backward.2.right0, ...), custom_call_target="tpu_custom_call" | custom-call | flops 4831838208 | bytes 11000000 | tf_op jit(solution)/shard_map/weight_grad/pallas_call | solution.py:284
  142.8 3.5 %collective-permute-done.19 = f32[1,128]{1,0:T(1,128)S(1)} collective-permute-done((f32[1,128]{1,0:T(1,128)S(1)}, f32[1,128]{1,0:T(1,128)S(1)}, u32[]{:S(2)}, u32[]{:S(2)}) %collective-permute-start.19) | collective-permute-done | bytes 544 | tf_op jit(solution)/shard_map/ppermute | solution.py:62
  146.4 4.7 %collective-permute-done.20 = f32[1,128]{1,0:T(1,128)S(1)} collective-permute-done((f32[1,128]{1,0:T(1,128)S(1)}, f32[1,128]{1,0:T(1,128)S(1)}, u32[]{:S(2)}, u32[]{:S(2)}) %collective-permute-start.20) | collective-permute-done | bytes 544 | tf_op jit(solution)/shard_map/ppermute | solution.py:62
  152.4 1.4 far.1
  154.9 2.2 %collective-permute-start.25 = (bf16[4,48,1536]{2,1,0:T(8,128)(2,1)S(1)}, bf16[4,48,1536]{2,1,0:T(8,128)(2,1)S(1)}, u32[]{:S(2)}, u32[]{:S(2)}) collective-permute-start(bf16[4,48,1536]{2,1,0:T(8,128)(2,1)S(1)} %get-tuple-element.123), channel_id=1, source_target_pairs={{0,96},{4,28},{8,104},{12,4},{16,112},{20,12},{24,120},{28,20},{32... | collective-permute-start | bytes 1769480 | tf_op jit(solution)/shard_map/ppermute | solution.py:46
  157.1 1.9 near.1
  159.0 1.3 collective-permute-start.27
  161.1 3.8 %collective-permute-done.24.up = bf16[4,48,1536]{2,1,0:T(8,128)(2,1)S(1)} collective-permute-done((bf16[4,48,1536]{2,1,0:T(8,128)(2,1)S(1)}, bf16[4,48,1536]{2,1,0:T(8,128)(2,1)S(1)}, u32[]{:S(2)}, u32[]{:S(2)}) %collective-permute-start.24) | collective-permute-done | bytes 589856 | tf_op jit(solution)/shard_map/ppermute | solution.py:46
  164.9 1.6 relay.1
  166.6 1.5 collective-permute-start.26
  168.0 1.9 collective-permute-start.29
  171.4 6.3 %collective-permute-done.26.up1 = bf16[4,48,1536]{2,1,0:T(8,128)(2,1)S(1)} collective-permute-done((bf16[4,48,1536]{2,1,0:T(8,128)(2,1)S(1)}, bf16[4,48,1536]{2,1,0:T(8,128)(2,1)S(1)}, u32[]{:S(2)}, u32[]{:S(2)}) %collective-permute-start.26) | collective-permute-done | bytes 589856 | tf_op jit(solution)/shard_map/ppermute | solution.py:46
  178.9 17.0 %all_to_all.10 = bf16[4,2,48,1536]{3,2,1,0:T(8,128)(2,1)S(1)} all-to-all(bf16[4,2,48,1536]{3,2,1,0:T(8,128)(2,1)S(1)} %close.1), channel_id=1, replica_groups={{0,8,16,24},{32,40,48,56},{64,72,80,88},{96,104,112,120},{4,36,68,100},..., dimensions={0} | all-to-all | bytes 2359296 | tf_op jit(solution)/shard_map/all_to_all | solution.py:525
  (89 shorter events, 18.6 us)
Async XLA Ops:
  0.6 39.2 %copy-start = (bf16[1536,3,384]{2,0,1:T(8,128)(2,1)S(1)}, bf16[1536,3,384]{2,0,1:T(8,128)(2,1)}, u32[]{:S(2)}) copy-start(bf16[1536,3,384]{2,0,1:T(8,128)(2,1)} %param.19) | copy-start | bytes 10616836
  0.6 22.1 %collective-permute-start = (bf16[1024,384]{1,0:T(8,128)(2,1)}, bf16[1024,384]{1,0:T(8,128)(2,1)}, u32[]{:S(2)}, u32[]{:S(2)}) collective-permute-start(bf16[1024,384]{1,0:T(8,128)(2,1)} %x0.3), channel_id=1, source_target_pairs={{0,1},{1,2},{2,3},{3,0},{4,7},{5,4},{6,5},{7,6},{8,9},{9,10},{10,1... | collective-permute-start | bytes 2359304 | tf_op jit(solution)/shard_map/ppermute | solution.py:36
  2.3 20.5 %collective-permute-start.1 = (bf16[1024,384]{1,0:T(8,128)(2,1)}, bf16[1024,384]{1,0:T(8,128)(2,1)}, u32[]{:S(2)}, u32[]{:S(2)}) collective-permute-start(bf16[1024,384]{1,0:T(8,128)(2,1)} %x0.3), channel_id=1, source_target_pairs={{0,3},{1,0},{2,1},{3,2},{4,5},{5,6},{6,7},{7,4},{8,11},{9,8},{10,9... | collective-permute-start | bytes 2359304 | tf_op jit(solution)/shard_map/ppermute | solution.py:36
  6.4 16.4 %all-to-all-start = ((f32[32,8,128]{2,1,0:T(8,128)}), f32[32,8,128]{2,1,0:T(8,128)}, u32[]{:S(2)}, u32[]{:S(2)}) async-start(f32[32,8,128]{2,1,0:T(8,128)} %broadcast_in_dim.31), calls=%async_computation | async-start | bytes 262144 | tf_op jit(solution)/shard_map/all_to_all | solution.py:419
  15.0 8.0 %copy-start.10 = (s32[32]{0:T(128)S(1)}, s32[32]{0:T(128)}, u32[]{:S(2)}) copy-start(s32[32]{0:T(128)} %param.17) | copy-start | bytes 388
  22.8 15.7 %collective-permute-start.4 = (bf16[1024,384]{1,0:T(8,128)(2,1)}, bf16[1024,384]{1,0:T(8,128)(2,1)}, u32[]{:S(2)}, u32[]{:S(2)}) collective-permute-start(bf16[1024,384]{1,0:T(8,128)(2,1)} %collective-permute-done.x3), channel_id=1, source_target_pairs={{0,1},{1,2},{2,3},{3,0},{4,7},{5,4},{6,5},{7,6},{8,9},{9,10},{10,1... | collective-permute-start | bytes 2359304 | tf_op jit(solution)/shard_map/ppermute | solution.py:36
  26.5 6.5 %collective-permute-start.2 = (f32[1,1536]{1,0:T(1,128)S(1)}, f32[1,1536]{1,0:T(1,128)S(1)}, u32[]{:S(2)}, u32[]{:S(2)}) collective-permute-start(f32[1,1536]{1,0:T(1,128)S(1)} %fusion.34), channel_id=1, source_target_pairs={{0,1},{1,0},{2,3},{3,2},{4,5},{5,4},{6,7},{7,6},{8,9},{9,8},{10,11... | collective-permute-start | bytes 18440 | tf_op jit(solution)/shard_map/ppermute | solution.py:62
  33.0 5.5 %collective-permute-start.3 = (f32[1,1536]{1,0:T(1,128)S(1)}, f32[1,1536]{1,0:T(1,128)S(1)}, u32[]{:S(2)}, u32[]{:S(2)}) collective-permute-start(f32[1,1536]{1,0:T(1,128)S(1)} %add.193), channel_id=1, source_target_pairs={{0,3},{1,2},{2,1},{3,0},{4,7},{5,6},{6,5},{7,4},{8,11},{9,10},{10,... | collective-permute-start | bytes 18440 | tf_op jit(solution)/shard_map/ppermute | solution.py:62
  40.4 3.7 %collective-permute-start.5 = (f32[3,384]{1,0:T(4,128)S(1)}, f32[3,384]{1,0:T(4,128)S(1)}, u32[]{:S(2)}, u32[]{:S(2)}) collective-permute-start(f32[3,384]{1,0:T(4,128)S(1)} %bitcast.74), channel_id=1, source_target_pairs={{0,1},{1,0},{2,3},{3,2},{4,5},{5,4},{6,7},{7,6},{8,9},{9,8},{10,11... | collective-permute-start | bytes 13832 | tf_op jit(solution)/shard_map/ppermute | solution.py:62
  44.1 5.0 %collective-permute-start.6 = (f32[6,384]{1,0:T(8,128)S(1)}, f32[6,384]{1,0:T(8,128)S(1)}, u32[]{:S(2)}, u32[]{:S(2)}) collective-permute-start(f32[6,384]{1,0:T(8,128)S(1)} %pad_maximum_fusion), channel_id=1, source_target_pairs={{0,3},{1,2},{2,1},{3,0},{4,7},{5,6},{6,5},{7,4},{8,11},{9,10},{10,... | collective-permute-start | bytes 27656 | tf_op jit(solution)/shard_map/ppermute | solution.py:62
  47.4 12.1 %copy-start.5 = (bf16[384,1536]{1,0:T(8,128)(2,1)S(1)}, bf16[384,1536]{1,0:T(8,128)(2,1)}, u32[]{:S(2)}) copy-start(bf16[384,1536]{1,0:T(8,128)(2,1)} %get-tuple-element.78) | copy-start | bytes 3538948
  59.5 1.5 copy-start.4
  61.0 5.0 %copy-start.3 = (bf16[384,1536]{1,0:T(8,128)(2,1)S(1)}, bf16[384,1536]{1,0:T(8,128)(2,1)}, u32[]{:S(2)}) copy-start(bf16[384,1536]{1,0:T(8,128)(2,1)} %get-tuple-element.73) | copy-start | bytes 3538948
  61.0 16.0 %collective-permute-start.7 = (bf16[768,384]{1,0:T(8,128)(2,1)S(1)}, bf16[768,384]{1,0:T(8,128)(2,1)S(1)}, u32[]{:S(2)}, u32[]{:S(2)}) collective-permute-start(bf16[768,384]{1,0:T(8,128)(2,1)S(1)} %convolution_convert_fusion), channel_id=1, source_target_pairs={{0,1},{1,2},{2,3},{3,0},{4,7},{5,4},{6,5},{7,6},{8,9},{9,10},{10,1... | collective-permute-start | bytes 1769480 | tf_op jit(solution)/shard_map/ppermute | solution.py:36
  62.5 4.9 %copy-start.6 = (bf16[384,1536]{1,0:T(8,128)(2,1)S(1)}, bf16[384,1536]{1,0:T(8,128)(2,1)}, u32[]{:S(2)}) copy-start(bf16[384,1536]{1,0:T(8,128)(2,1)} %get-tuple-element.72) | copy-start | bytes 3538948
  62.5 14.5 %collective-permute-start.8 = (bf16[768,384]{1,0:T(8,128)(2,1)S(1)}, bf16[768,384]{1,0:T(8,128)(2,1)S(1)}, u32[]{:S(2)}, u32[]{:S(2)}) collective-permute-start(bf16[768,384]{1,0:T(8,128)(2,1)S(1)} %convolution_convert_fusion.1), channel_id=1, source_target_pairs={{0,3},{1,0},{2,1},{3,2},{4,5},{5,6},{6,7},{7,4},{8,11},{9,8},{10,9... | collective-permute-start | bytes 1769480 | tf_op jit(solution)/shard_map/ppermute | solution.py:36
  78.2 11.2 %copy-start.2 = (bf16[1024,384]{1,0:T(8,128)(2,1)S(1)}, bf16[1024,384]{1,0:T(8,128)(2,1)}, u32[]{:S(2)}) copy-start(bf16[1024,384]{1,0:T(8,128)(2,1)} %x0.3) | copy-start | bytes 2359300
  78.2 11.2 %copy-start.7 = (bf16[1024,384]{1,0:T(8,128)(2,1)S(1)}, bf16[1024,384]{1,0:T(8,128)(2,1)}, u32[]{:S(2)}) copy-start(bf16[1024,384]{1,0:T(8,128)(2,1)} %param.13) | copy-start | bytes 2359300
  78.3 11.2 %collective-permute-start.9 = (bf16[768,384]{1,0:T(8,128)(2,1)S(1)}, bf16[768,384]{1,0:T(8,128)(2,1)S(1)}, u32[]{:S(2)}, u32[]{:S(2)}) collective-permute-start(bf16[768,384]{1,0:T(8,128)(2,1)S(1)} %add_convert_fusion.2), channel_id=1, source_target_pairs={{0,1},{1,2},{2,3},{3,0},{4,7},{5,4},{6,5},{7,6},{8,9},{9,10},{10,1... | collective-permute-start | bytes 1769480 | tf_op jit(solution)/shard_map/ppermute | solution.py:36
  78.5 14.8 %collective-permute-start.10 = (bf16[256,384]{1,0:T(8,128)(2,1)S(1)}, bf16[256,384]{1,0:T(8,128)(2,1)S(1)}, u32[]{:S(2)}, u32[]{:S(2)}) collective-permute-start(bf16[256,384]{1,0:T(8,128)(2,1)S(1)} %convolution_convert_fusion.3), channel_id=1, source_target_pairs={{0,3},{1,0},{2,1},{3,2},{4,5},{5,6},{6,7},{7,4},{8,11},{9,8},{10,9... | collective-permute-start | bytes 589832 | tf_op jit(solution)/shard_map/ppermute | solution.py:36
  81.6 26.1 %collective-permute-start.15 = (bf16[256,384]{1,0:T(8,128)(2,1)S(1)}, bf16[256,384]{1,0:T(8,128)(2,1)S(1)}, u32[]{:S(2)}, u32[]{:S(2)}) collective-permute-start(bf16[256,384]{1,0:T(8,128)(2,1)S(1)} %convolution_convert_fusion.2), channel_id=1, source_target_pairs={{0,1},{1,2},{2,3},{3,0},{4,7},{5,4},{6,5},{7,6},{8,9},{9,10},{10,1... | collective-permute-start | bytes 589832 | tf_op jit(solution)/shard_map/ppermute | solution.py:36
  89.9 17.3 %collective-permute-start.12 = (bf16[768,384]{1,0:T(8,128)(2,1)S(1)}, bf16[768,384]{1,0:T(8,128)(2,1)S(1)}, u32[]{:S(2)}, u32[]{:S(2)}) collective-permute-start(bf16[768,384]{1,0:T(8,128)(2,1)S(1)} %multiply_convert_fusion.b0.refs_1_), channel_id=1, source_target_pairs={{0,1},{1,2},{2,3},{3,0},{4,7},{5,4},{6,5},{7,6},{8,9},{9,10},{10,1... | collective-permute-start | bytes 1769480 | tf_op jit(solution)/shard_map/ppermute | solution.py:36
  90.2 16.9 %collective-permute-start.13 = (bf16[768,384]{1,0:T(8,128)(2,1)S(1)}, bf16[768,384]{1,0:T(8,128)(2,1)S(1)}, u32[]{:S(2)}, u32[]{:S(2)}) collective-permute-start(bf16[768,384]{1,0:T(8,128)(2,1)S(1)} %multiply_convert_fusion.b0.refs_1_), channel_id=1, source_target_pairs={{0,3},{1,0},{2,1},{3,2},{4,5},{5,6},{6,7},{7,4},{8,11},{9,8},{10,9... | collective-permute-start | bytes 1769480 | tf_op jit(solution)/shard_map/ppermute | solution.py:36
  93.8 12.1 %collective-permute-start.11 = (bf16[256,384]{1,0:T(8,128)(2,1)S(1)}, bf16[256,384]{1,0:T(8,128)(2,1)S(1)}, u32[]{:S(2)}, u32[]{:S(2)}) collective-permute-start(bf16[256,384]{1,0:T(8,128)(2,1)S(1)} %fusion.7), channel_id=1, source_target_pairs={{0,3},{1,0},{2,1},{3,2},{4,5},{5,6},{6,7},{7,4},{8,11},{9,8},{10,9... | collective-permute-start | bytes 589832 | tf_op jit(solution)/shard_map/ppermute | solution.py:36
  94.7 25.7 %slice-start = ((s8[4718592]{0:T(1024)(128)(4,1)}), s8[4194304]{0:T(1024)(128)(4,1)S(1)}, s32[]{:S(2)}) async-start(s8[4718592]{0:T(1024)(128)(4,1)} %bitcast.72), calls=%async_computation.2 | async-start | bytes 8388608
  107.2 13.2 %collective-permute-start.14 = (bf16[768,384]{1,0:T(8,128)(2,1)S(1)}, bf16[768,384]{1,0:T(8,128)(2,1)S(1)}, u32[]{:S(2)}, u32[]{:S(2)}) collective-permute-start(bf16[768,384]{1,0:T(8,128)(2,1)S(1)} %collective-permute-done.12.b3.refs_2_), channel_id=1, source_target_pairs={{0,1},{1,2},{2,3},{3,0},{4,7},{5,4},{6,5},{7,6},{8,9},{9,10},{10,1... | collective-permute-start | bytes 1769480 | tf_op jit(solution)/shard_map/ppermute | solution.py:36
  107.6 12.8 %slice-start.1 = ((s8[4718592]{0:T(1024)(128)(4,1)}), s8[524288]{0:T(1024)(128)(4,1)S(1)}, s32[]{:S(2)}) async-start(s8[4718592]{0:T(1024)(128)(4,1)} %bitcast.72), calls=%async_computation.3 | async-start | bytes 1048576
  108.3 8.2 %collective-permute-start.16 = (bf16[256,384]{1,0:T(8,128)(2,1)S(1)}, bf16[256,384]{1,0:T(8,128)(2,1)S(1)}, u32[]{:S(2)}, u32[]{:S(2)}) collective-permute-start(bf16[256,384]{1,0:T(8,128)(2,1)S(1)} %fusion.8.b0.refs_2_), channel_id=1, source_target_pairs={{0,3},{1,0},{2,1},{3,2},{4,5},{5,6},{6,7},{7,4},{8,11},{9,8},{10,9... | collective-permute-start | bytes 589832 | tf_op jit(solution)/shard_map/ppermute | solution.py:36
  111.2 14.8 %collective-permute-start.18 = (bf16[256,384]{1,0:T(8,128)(2,1)S(1)}, bf16[256,384]{1,0:T(8,128)(2,1)S(1)}, u32[]{:S(2)}, u32[]{:S(2)}) collective-permute-start(bf16[256,384]{1,0:T(8,128)(2,1)S(1)} %fusion.8.b0.refs_2_), channel_id=1, source_target_pairs={{0,1},{1,2},{2,3},{3,0},{4,7},{5,4},{6,5},{7,6},{8,9},{9,10},{10,1... | collective-permute-start | bytes 589832 | tf_op jit(solution)/shard_map/ppermute | solution.py:36
  116.5 14.2 %collective-permute-start.17 = (bf16[256,384]{1,0:T(8,128)(2,1)S(1)}, bf16[256,384]{1,0:T(8,128)(2,1)S(1)}, u32[]{:S(2)}, u32[]{:S(2)}) collective-permute-start(bf16[256,384]{1,0:T(8,128)(2,1)S(1)} %collective-permute-done.16.b1.refs_3_), channel_id=1, source_target_pairs={{0,3},{1,0},{2,1},{3,2},{4,5},{5,6},{6,7},{7,4},{8,11},{9,8},{10,9... | collective-permute-start | bytes 589832 | tf_op jit(solution)/shard_map/ppermute | solution.py:36
  142.2 10.1 %collective-permute-start.22 = (bf16[768,1536]{1,0:T(8,128)(2,1)S(1)}, bf16[768,1536]{1,0:T(8,128)(2,1)S(1)}, u32[]{:S(2)}, u32[]{:S(2)}) collective-permute-start(bf16[768,1536]{1,0:T(8,128)(2,1)S(1)} %get-tuple-element.119), channel_id=1, source_target_pairs={{0,4},{4,0},{8,12},{12,8},{16,20},{20,16},{24,28},{28,24},{32,36},... | collective-permute-start | bytes 7077896 | tf_op jit(solution)/shard_map/ppermute | solution.py:46
  142.3 10.0 %collective-permute-start.23 = (bf16[768,1536]{1,0:T(8,128)(2,1)S(1)}, bf16[768,1536]{1,0:T(8,128)(2,1)S(1)}, u32[]{:S(2)}, u32[]{:S(2)}) collective-permute-start(bf16[768,1536]{1,0:T(8,128)(2,1)S(1)} %get-tuple-element.120), channel_id=1, source_target_pairs={{0,4},{4,0},{8,12},{12,8},{16,20},{20,16},{24,28},{28,24},{32,36},... | collective-permute-start | bytes 7077896 | tf_op jit(solution)/shard_map/ppermute | solution.py:46
  142.8 3.5 %collective-permute-start.19 = (f32[1,128]{1,0:T(1,128)S(1)}, f32[1,128]{1,0:T(1,128)S(1)}, u32[]{:S(2)}, u32[]{:S(2)}) collective-permute-start(f32[1,128]{1,0:T(1,128)S(1)} %get-tuple-element.116), channel_id=1, source_target_pairs={{0,1},{1,0},{2,3},{3,2},{4,5},{5,4},{6,7},{7,6},{8,9},{9,8},{10,11... | collective-permute-start | bytes 1544 | tf_op jit(solution)/shard_map/ppermute | solution.py:62
  146.4 4.8 %collective-permute-start.20 = (f32[1,128]{1,0:T(1,128)S(1)}, f32[1,128]{1,0:T(1,128)S(1)}, u32[]{:S(2)}, u32[]{:S(2)}) collective-permute-start(f32[1,128]{1,0:T(1,128)S(1)} %add.217), channel_id=1, source_target_pairs={{0,3},{1,2},{2,1},{3,0},{4,7},{5,6},{6,5},{7,4},{8,11},{9,10},{10,... | collective-permute-start | bytes 1544 | tf_op jit(solution)/shard_map/ppermute | solution.py:62
  151.1 1.2 collective-permute-start.21
  153.8 11.2 %collective-permute-start.24 = (bf16[4,48,1536]{2,1,0:T(8,128)(2,1)S(1)}, bf16[4,48,1536]{2,1,0:T(8,128)(2,1)S(1)}, u32[]{:S(2)}, u32[]{:S(2)}) collective-permute-start(bf16[4,48,1536]{2,1,0:T(8,128)(2,1)S(1)} %get-tuple-element.122), channel_id=1, source_target_pairs={{0,32},{4,12},{8,40},{12,20},{16,48},{20,28},{24,56},{28,4},{32,64... | collective-permute-start | bytes 1769480 | tf_op jit(solution)/shard_map/ppermute | solution.py:46
  154.9 10.1 %collective-permute-start.25 = (bf16[4,48,1536]{2,1,0:T(8,128)(2,1)S(1)}, bf16[4,48,1536]{2,1,0:T(8,128)(2,1)S(1)}, u32[]{:S(2)}, u32[]{:S(2)}) collective-permute-start(bf16[4,48,1536]{2,1,0:T(8,128)(2,1)S(1)} %get-tuple-element.123), channel_id=1, source_target_pairs={{0,96},{4,28},{8,104},{12,4},{16,112},{20,12},{24,120},{28,20},{32... | collective-permute-start | bytes 1769480 | tf_op jit(solution)/shard_map/ppermute | solution.py:46
  159.0 12.1 %collective-permute-start.27 = (bf16[4,48,1536]{2,1,0:T(8,128)(2,1)S(1)}, bf16[4,48,1536]{2,1,0:T(8,128)(2,1)S(1)}, u32[]{:S(2)}, u32[]{:S(2)}) collective-permute-start(bf16[4,48,1536]{2,1,0:T(8,128)(2,1)S(1)} %get-tuple-element.125), channel_id=1, source_target_pairs={{0,96},{4,28},{8,104},{12,4},{16,112},{20,12},{24,120},{28,20},{32... | collective-permute-start | bytes 1769480 | tf_op jit(solution)/shard_map/ppermute | solution.py:46
  160.3 11.1 %collective-permute-start.28 = (bf16[4,48,1536]{2,1,0:T(8,128)(2,1)S(1)}, bf16[4,48,1536]{2,1,0:T(8,128)(2,1)S(1)}, u32[]{:S(2)}, u32[]{:S(2)}) collective-permute-start(bf16[4,48,1536]{2,1,0:T(8,128)(2,1)S(1)} %get-tuple-element.126), channel_id=1, source_target_pairs={{0,32},{4,12},{8,40},{12,20},{16,48},{20,28},{24,56},{28,4},{32,64... | collective-permute-start | bytes 1769480 | tf_op jit(solution)/shard_map/ppermute | solution.py:46
  166.6 11.2 %collective-permute-start.26 = (bf16[4,48,1536]{2,1,0:T(8,128)(2,1)S(1)}, bf16[4,48,1536]{2,1,0:T(8,128)(2,1)S(1)}, u32[]{:S(2)}, u32[]{:S(2)}) collective-permute-start(bf16[4,48,1536]{2,1,0:T(8,128)(2,1)S(1)} %get-tuple-element.124), channel_id=1, source_target_pairs={{0,32},{4,12},{8,40},{12,20},{16,48},{20,28},{24,56},{28,4},{32,64... | collective-permute-start | bytes 1769480 | tf_op jit(solution)/shard_map/ppermute | solution.py:46
  168.0 9.9 %collective-permute-start.29 = (bf16[4,48,1536]{2,1,0:T(8,128)(2,1)S(1)}, bf16[4,48,1536]{2,1,0:T(8,128)(2,1)S(1)}, u32[]{:S(2)}, u32[]{:S(2)}) collective-permute-start(bf16[4,48,1536]{2,1,0:T(8,128)(2,1)S(1)} %get-tuple-element.127), channel_id=1, source_target_pairs={{0,96},{4,28},{8,104},{12,4},{16,112},{20,12},{24,120},{28,20},{32... | collective-permute-start | bytes 1769480 | tf_op jit(solution)/shard_map/ppermute | solution.py:46
  178.9 17.2 %copy-start.8 = (f32[48,1536]{1,0:T(8,128)S(1)}, f32[48,1536]{1,0:T(8,128)}, u32[]{:S(2)}) copy-start(f32[48,1536]{1,0:T(8,128)} %param.23) | copy-start | bytes 884740
  178.9 17.2 %copy-start.9 = (f32[48,1536]{1,0:T(8,128)S(1)}, f32[48,1536]{1,0:T(8,128)}, u32[]{:S(2)}) copy-start(f32[48,1536]{1,0:T(8,128)} %param.22) | copy-start | bytes 884740
  178.9 18.0 %copy-start.1 = (bf16[1536,3,384]{2,0,1:T(8,128)(2,1)S(1)}, bf16[1536,3,384]{2,0,1:T(8,128)(2,1)}, u32[]{:S(2)}) copy-start(bf16[1536,3,384]{2,0,1:T(8,128)(2,1)} %param.19) | copy-start | bytes 10616836

commit v4 on v1

--- a/solution.py
+++ b/solution.py
@@ -198,22 +198,66 @@
     )(at, *blocks, out_w, slope)
 
 
-def rows_kernel(count, at, *refs):
-    tops, lows = refs[:count], refs[count : 2 * count]
-    right0, right1 = refs[2 * count : 2 * count + 2]
-    keep, send, square, turned = refs[-4:]
-    rows = right0.shape[0]
-    for k in range(count):
+def turn_blocks(groups, turned):
+    for k in range(len(groups[0])):
 
         @pl.when(pl.program_id(0) == k)
         def _():
-            turned[:, :rows] = tops[k][...].T
-            turned[:, rows:] = lows[k][...].T
-
+            start = 0
+            for group in groups:
+                rows = group[k].shape[0]
+                turned[:, start : start + rows] = group[k][...].T
+                start += rows
+
+
+def cut_refs(refs, count, groups):
+    return [refs[g * count : (g + 1) * count] for g in range(groups)], refs[groups * count :]
+
+
+def product(turned, rights, cols):
+    start = 0
+    value = 0.0
+    for right in rights:
+        rows = right.shape[0]
+        value = value + dot(turned[:, start : start + rows], right[:, cols])
+        start += rows
+    return value
+
+
+def partial_kernel(count, at, *refs):
+    groups, (right, out, turned) = cut_refs(refs, count, 1)
+    turn_blocks(groups, turned)
+    for n in range(right.shape[1] // 512):
+        cols = slice(n * 512, (n + 1) * 512)
+        out[:, cols] = product(turned, [right], cols)
+
+
+def rows_partial(at, blocks, right):
+    rows, ff = right.shape
+    count = len(blocks)
+    return call(
+        lambda *refs: partial_kernel(count, *refs),
+        count,
+        [whole((rows, PART))] * count + [whole((rows, ff))],
+        pl.BlockSpec((PART, ff), lambda s, *_: (s, 0)),
+        shaped((count * PART, ff), F32),
+        [pltpu.VMEM((PART, rows), BF)],
+        cost(2 * rows * PART * ff * count, 4 * 10**6 * count),
+        "rows_partial",
+    )(at, *blocks, right)
+
+
+def rows_kernel(count, parts, partials, at, *refs):
+    groups, rest = cut_refs(refs, count, parts)
+    rights, rest = rest[:parts], rest[parts:]
+    keep, send, square, turned = refs[-4:]
+    turn_blocks(groups, turned)
     mine = at[4]
-    for n in range(right0.shape[1] // 512):
+    for n in range(rights[0].shape[1] // 512):
         cols = slice(n * 512, (n + 1) * 512)
-        value = dot(turned[:, :rows], right0[:, cols]) + dot(turned[:, rows:], right1[:, cols])
+        value = product(turned, rights, cols)
+        if partials:
+            value = value + rest[0][:, cols]
         piece = jnp.sum(value * value, 0, keepdims=True)
 
         @pl.when(pl.program_id(0) == 0)
@@ -232,25 +276,28 @@
             send[at_rows, cols] = jnp.where(mine == 0, high, low)
 
 
-def rows_grad(at, places, tops, lows, rights, before):
-    rows, ff = rights[0].shape
-    count = len(tops)
+def rows_grad(at, places, groups, rights, partials, before):
+    ff = rights[0].shape[1]
+    rows = sum(right.shape[0] for right in rights)
+    count, parts = len(places), len(groups)
     first = places[0]
     step = places[1] - first if count > 1 else 0
     out = pl.BlockSpec((PART // 2, ff), lambda s, a: (a[8 + first + s * step], 0))
-    return call(
-        lambda *refs: rows_kernel(count, *refs),
+    blocks = [block for group in groups for block in group]
+    operands = [*blocks, *rights, *partials, *before]
+    return call(
+        lambda *refs: rows_kernel(count, parts, len(partials), *refs),
         count,
-        [whole((rows, PART))] * (2 * count)
-        + [whole((rows, ff))] * 2
+        [whole(value.shape) for value in (*blocks, *rights)]
+        + [pl.BlockSpec((PART, ff), lambda s, *_: (s, 0))] * len(partials)
         + [pl.BlockSpec(memory_space=pl.ANY)] * len(before),
         [out, out, whole((1, ff))],
         [shaped((D // 2, ff))] * 2 + [shaped((1, ff), F32)],
-        [pltpu.VMEM((PART, 2 * rows), BF)],
-        cost(4 * rows * PART * ff * count, 5 * 10**6 * count),
+        [pltpu.VMEM((PART, rows), BF)],
+        cost(2 * rows * PART * ff * count, 5 * 10**6 * count),
         "rows_grad",
-        {2 * count + 3 + n: n for n in range(len(before))},
-    )(at, *tops, *lows, *rights, *before)
+        {len(operands) - len(before) + 1 + n: n for n in range(len(before))},
+    )(at, *operands)
 
 
 def weight_kernel(at, keep_l, send_l, right0, right1, q0, q1, q2, keep, send, square, sums):
@@ -466,17 +513,23 @@
     far0 = by_x(far0, 1)
     at_next, down0 = lax.optimization_barrier((at, down0))
     down0 = by_x(down0, -1)
-    up0, own0 = lax.optimization_barrier((project(hidden0, 1), project(hidden0, 0)))
+    up0 = lax.optimization_barrier(project(hidden0, 1))
     modded1, hidden1, pre1 = forward(1, at_next, latent_blocks, mods, in_w)
     hidden1, far0, down0 = lax.optimization_barrier((hidden1, far0, down0))
-    up0 = by_x((up0 + far0.astype(F32)).astype(BF), 1)
+    up0 = (up0 + far0.astype(F32)).astype(BF)
+    up0, hidden1 = lax.optimization_barrier((up0, hidden1))
+    up0 = by_x(up0, 1)
     far1, up1 = project(hidden1, 2).astype(BF), project(hidden1, 1).astype(BF)
-    far1, up1, hidden1, at_late, pre0, pre1 = lax.optimization_barrier(
-        (far1, up1, hidden1, at, pre0, pre1)
-    )
+    far1, up1, hidden0_late, at_late, pre0, pre1 = lax.optimization_barrier(
+        (far1, up1, hidden0, at, pre0, pre1)
+    )
+    own0 = lax.optimization_barrier(project(hidden0_late, 0))
     far1, up1 = by_x(far1, -1), by_x(up1, 1)
-    down1, own1 = lax.optimization_barrier((project(hidden1, 3), project(hidden1, 0)))
     back0 = leave(0, own0, up0, down0)
+    hidden1_late, back0 = lax.optimization_barrier((hidden1, back0))
+    down1, own1 = lax.optimization_barrier(
+        (project(hidden1_late, 3), project(hidden1_late, 0))
+    )
     behind0, ahead0 = by_x(back0, 1), by_x(back0, -1)
     down1 = by_x((down1 + far1.astype(F32)).astype(BF), -1)
     slope0, slope1 = slope_of(pre0).astype(BF), slope_of(pre1).astype(BF)
@@ -490,13 +543,14 @@
     far1 = by_x(ahead1, -1)
 
     rights = (hidden0, hidden1)
-    *second, square_a = rows_grad(at, (0,), (back0,), (back1,), rights, ())
+    *second, square_a = rows_grad(at, (0,), ((back0,), (back1,)), rights, (), ())
+    partial = rows_partial(at, (ahead0, behind0), hidden0)
     grad0 = backward(at, (back0, ahead0, far0, behind0), out_w, slope0)
     *second, square_b = rows_grad(
-        at, (1, 3), (ahead0, behind0), (ahead1, behind1), rights, tuple(second)
+        at, (1, 3), ((ahead1, behind1),), (hidden1,), (partial,), tuple(second)
     )
     grad1 = backward(at, (back1, ahead1, far1, behind1), out_w, slope1)
-    *second, square_c = rows_grad(at, (2,), (far0,), (far1,), rights, tuple(second))
+    *second, square_c = rows_grad(at, (2,), ((far0,), (far1,)), rights, (), tuple(second))
     keep2, send2 = second
     got2 = by_core(send2)
     keep1, send1, square = weight_grad(

time: 194 us -> 195 us (level)
    pallas_call x3 -> x4, Pallas kernels: 8.71 us -> 9.72 us  [the longest x3 7.28 us: rows_grad(): call(lambda *refs: rows_kernel(count, parts, len(partials), *refs), count...]
where the time goes in v4:
time: 195 us
  waiting for transfers between devices  54.5 us (28%)
  Pallas kernels  48.7 us (25%)
  starting transfers between devices  46.6 us (24%)
  blocking collectives  16.9 us (9%)
  matrix products  12 us (6%)
  other arithmetic  6.82 us (3%)
  local copies, waits for them, and re-layouts  6.09 us (3%)
  between operations  3.25 us (2%)
    ppermute x15, waiting for transfers between devices, by_x(): return lax.ppermute(value, ('dp', 'mp'), pairs)  19.5 us
    ppermute x15, starting transfers between devices, by_x(): return lax.ppermute(value, ('dp', 'mp'), pairs)  19.2 us
    ppermute x6, waiting for transfers between devices, swap_x(): return lax.ppermute(value, 'mp', list(enumerate(other)))  18.8 us
    all_to_all x1, blocking collectives, local(): lax.all_to_all(value, 'dp', 0, 0, axis_index_groups=groups, tiled=True)  16.9 us
    pallas_call x2, Pallas kernels, forward(): call(forward_kernel, ff // WIDE, [piece] * 4 + [whole((3, PART)), whole((...  15.8 us
    ppermute x9, waiting for transfers between devices, by_dp(): return lax.ppermute(value, 'dp', pairs)  13.3 us
    ppermute x6, starting transfers between devices, swap_x(): return lax.ppermute(value, 'mp', list(enumerate(other)))  9.43 us
    ppermute x9, starting transfers between devices, by_dp(): return lax.ppermute(value, 'dp', pairs)  9.37 us
  transfers between devices with their start and end apart: 31, of which 18 were waited for; matrix products, arithmetic and copies ran while one was open for 9% of the time, Pallas kernels for 13%

profile of v4, /device:TPU:0, one launch (start us, length us, event | category | flops | bytes accessed | tf_op | source)
XLA Modules:
  0.0 194.9 jit_solution(12432743134455944015)
XLA Ops:
  0.6 1.6 collective-permute-start
  2.3 1.7 collective-permute-start.1
  6.4 8.5 %all-to-all-start = ((f32[32,8,128]{2,1,0:T(8,128)}), f32[32,8,128]{2,1,0:T(8,128)}, u32[]{:S(2)}, u32[]{:S(2)}) async-start(f32[32,8,128]{2,1,0:T(8,128)} %broadcast_in_dim.31), calls=%async_computation | async-start | bytes 262144 | tf_op jit(solution)/shard_map/all_to_all | solution.py:463
  15.1 4.6 %constant_dynamic-slice_fusion = (bf16[384,1536]{1,0:T(8,128)(2,1)}, bf16[384,1536]{1,0:T(8,128)(2,1)}, bf16[384,1536]{1,0:T(8,128)(2,1)}, bf16[384,1536]{1,0:T(8,128)(2,1)}) fusion(bf16[1536,1536]{1,0:T(8,128)(2,1)} %out_w.3, s32[]{:T(128)S(6)} %select_n.112, s32[]{:T(128)S(6)} %select_n.111, s32[]{:T(128)S(6)} %select_n.110, s32[]{:T(128)S(6)} %select_n.109), kind=kLoop, calls=%fused_computation.51 | loop fusion | bytes 9437200 | tf_op jit(solution)/shard_map/dynamic_slice | solution.py:456
  19.8 3.0 %all-to-all-done = f32[32,8,128]{2,1,0:T(8,128)} async-done(((f32[32,8,128]{2,1,0:T(8,128)}), f32[32,8,128]{2,1,0:T(8,128)}, u32[]{:S(2)}, u32[]{:S(2)}) %all-to-all-start) | async-done | bytes 131104 | tf_op jit(solution)/shard_map/all_to_all | solution.py:463
  24.1 2.4 %fusion.27 = f32[1,1536]{1,0:T(1,128)S(1)} fusion(bf16[1024,1]{0,1:T(2,128)(2,1)S(1)} %reshape.95, bf16[1024,1536]{1,0:T(8,128)(2,1)} %param.18), kind=kOutput, calls=%fused_computation.60 | convolution fusion | flops 3145728 | bytes 3153920 | tf_op jit(solution)/shard_map/dot_general | solution.py:24
  26.5 1.5 collective-permute-start.2
  28.7 4.3 %collective-permute-done.2 = f32[1,1536]{1,0:T(1,128)S(1)} collective-permute-done((f32[1,1536]{1,0:T(1,128)S(1)}, f32[1,1536]{1,0:T(1,128)S(1)}, u32[]{:S(2)}, u32[]{:S(2)}) %collective-permute-start.2) | collective-permute-done | bytes 6176 | tf_op jit(solution)/shard_map/ppermute | solution.py:62
  33.0 3.9 %collective-permute-start.3 = (f32[1,1536]{1,0:T(1,128)S(1)}, f32[1,1536]{1,0:T(1,128)S(1)}, u32[]{:S(2)}, u32[]{:S(2)}) collective-permute-start(f32[1,1536]{1,0:T(1,128)S(1)} %add.191), channel_id=1, source_target_pairs={{0,3},{1,2},{2,1},{3,0},{4,7},{5,6},{6,5},{7,4},{8,11},{9,10},{10,... | collective-permute-start | bytes 18440 | tf_op jit(solution)/shard_map/ppermute | solution.py:62
  36.9 1.6 collective-permute-done.3
  41.4 2.9 %collective-permute-done.5.m1 = f32[3,384]{1,0:T(4,128)S(1)} collective-permute-done((f32[3,384]{1,0:T(4,128)S(1)}, f32[3,384]{1,0:T(4,128)S(1)}, u32[]{:S(2)}, u32[]{:S(2)}) %collective-permute-start.5) | collective-permute-done | bytes 4640 | tf_op jit(solution)/shard_map/ppermute | solution.py:62
  44.3 3.3 %collective-permute-start.6 = (f32[6,384]{1,0:T(8,128)S(1)}, f32[6,384]{1,0:T(8,128)S(1)}, u32[]{:S(2)}, u32[]{:S(2)}) collective-permute-start(f32[6,384]{1,0:T(8,128)S(1)} %pad_maximum_fusion), channel_id=1, source_target_pairs={{0,3},{1,2},{2,1},{3,0},{4,7},{5,6},{6,5},{7,4},{8,11},{9,10},{10,... | collective-permute-start | bytes 27656 | tf_op jit(solution)/shard_map/ppermute | solution.py:62
  47.7 1.6 collective-permute-done.6.m2
  49.3 7.9 %forward.2 = (bf16[512,1536]{1,0:T(8,128)(2,1)S(1)}, bf16[512,1536]{1,0:T(8,128)(2,1)S(1)}, f32[512,1536]{1,0:T(8,128)S(1)}) custom-call(s32[16]{0:T(128)S(1)} %stack.59.at.refs_0_, bf16[1024,384]{1,0:T(8,128)(2,1)} %x0.3, bf16[1024,384]{1,0:T(8,128)(2,1)} %collective-permute-done.1.x1, bf16[1024,384]{1,0:T(8,128)(2,1)} %copy-done.10, ...), custom_call_target="tpu_custom_call" | custom-call | flops 2415919104 | bytes 12000000 | tf_op jit(solution)/shard_map/forward/pallas_call | solution.py:137
  59.6 3.5 %collective-permute-start.8 = (bf16[512,384]{1,0:T(8,128)(2,1)S(1)}, bf16[512,384]{1,0:T(8,128)(2,1)S(1)}, u32[]{:S(2)}, u32[]{:S(2)}) collective-permute-start(bf16[512,384]{1,0:T(8,128)(2,1)S(1)} %convolution_convert_fusion.3), channel_id=1, source_target_pairs={{0,3},{1,0},{2,1},{3,2},{4,5},{5,6},{6,7},{7,4},{8,11},{9,8},{10,9... | collective-permute-start | bytes 1179656 | tf_op jit(solution)/shard_map/ppermute | solution.py:36
  64.0 7.9 %forward.3 = (bf16[512,1536]{1,0:T(8,128)(2,1)S(1)}, bf16[512,1536]{1,0:T(8,128)(2,1)S(1)}, f32[512,1536]{1,0:T(8,128)S(1)}) custom-call(s32[16]{0:T(128)S(1)} %stack.59.at.refs_0_, bf16[1024,384]{1,0:T(8,128)(2,1)} %x0.3, bf16[1024,384]{1,0:T(8,128)(2,1)} %collective-permute-done.1.x1, bf16[1024,384]{1,0:T(8,128)(2,1)} %copy-done.10, ...), custom_call_target="tpu_custom_call" | custom-call | flops 2415919104 | bytes 12000000 | tf_op jit(solution)/shard_map/forward/pallas_call | solution.py:137
  75.3 3.1 %collective-permute-start.10 = (bf16[512,384]{1,0:T(8,128)(2,1)S(1)}, bf16[512,384]{1,0:T(8,128)(2,1)S(1)}, u32[]{:S(2)}, u32[]{:S(2)}) collective-permute-start(bf16[512,384]{1,0:T(8,128)(2,1)S(1)} %convolution_convert_fusion.1), channel_id=1, source_target_pairs={{0,3},{1,0},{2,1},{3,2},{4,5},{5,6},{6,7},{7,4},{8,11},{9,8},{10,9... | collective-permute-start | bytes 1179656 | tf_op jit(solution)/shard_map/ppermute | solution.py:36
  78.4 7.9 %collective-permute-done.9 = bf16[512,384]{1,0:T(8,128)(2,1)S(1)} collective-permute-done((bf16[512,384]{1,0:T(8,128)(2,1)S(1)}, bf16[512,384]{1,0:T(8,128)(2,1)S(1)}, u32[]{:S(2)}, u32[]{:S(2)}) %collective-permute-start.9) | collective-permute-done | bytes 393248 | tf_op jit(solution)/shard_map/ppermute | solution.py:36
  86.8 3.2 %collective-permute-start.13 = (bf16[512,384]{1,0:T(8,128)(2,1)S(1)}, bf16[512,384]{1,0:T(8,128)(2,1)S(1)}, u32[]{:S(2)}, u32[]{:S(2)}) collective-permute-start(bf16[512,384]{1,0:T(8,128)(2,1)S(1)} %multiply_convert_fusion.1.b0.refs_1_), channel_id=1, source_target_pairs={{0,3},{1,0},{2,1},{3,2},{4,5},{5,6},{6,7},{7,4},{8,11},{9,8},{10,9... | collective-permute-start | bytes 1179656 | tf_op jit(solution)/shard_map/ppermute | solution.py:36
  92.2 3.2 %add_convert_fusion = (bf16[512,1536]{1,0:T(8,128)(2,1)S(1)}, bf16[512,1536]{1,0:T(8,128)(2,1)S(1)}) fusion(f32[512,1536]{1,0:T(8,128)S(1)} %get-tuple-element.89, f32[512,1536]{1,0:T(8,128)S(1)} %get-tuple-element.88), kind=kLoop, calls=%fused_computation | loop fusion | flops 23592960 | bytes 9437184 | tf_op jit(solution)/shard_map/convert_element_type | solution.py:535
  95.4 2.2 %turn.1 = (bf16[768,1024]{1,0:T(8,128)(2,1)S(1)}, bf16[768,1024]{1,0:T(8,128)(2,1)S(1)}) custom-call(s32[16]{0:T(128)S(1)} %stack.59.at.refs_0_, bf16[512,1536]{1,0:T(8,128)(2,1)S(1)} %get-tuple-element.91.top, bf16[512,1536]{1,0:T(8,128)(2,1)S(1)} %get-tuple-element.92.low), custom_call_target="tpu_custom_call" | custom-call | flops 1572864 | bytes 6291456 | tf_op jit(solution)/shard_map/turn/pallas_call | solution.py:166
  97.6 2.3 %collective-permute-done.11 = bf16[512,384]{1,0:T(8,128)(2,1)S(1)} collective-permute-done((bf16[512,384]{1,0:T(8,128)(2,1)S(1)}, bf16[512,384]{1,0:T(8,128)(2,1)S(1)}, u32[]{:S(2)}, u32[]{:S(2)}) %collective-permute-start.11) | collective-permute-done | bytes 393248 | tf_op jit(solution)/shard_map/ppermute | solution.py:36
  100.0 1.2 collective-permute-done.12.b3.refs_2_
  101.5 2.2 %collective-permute-start.16 = (bf16[512,384]{1,0:T(8,128)(2,1)S(1)}, bf16[512,384]{1,0:T(8,128)(2,1)S(1)}, u32[]{:S(2)}, u32[]{:S(2)}) collective-permute-start(bf16[512,384]{1,0:T(8,128)(2,1)S(1)} %multiply_convert_fusion.b0.refs_2_), channel_id=1, source_target_pairs={{0,3},{1,0},{2,1},{3,2},{4,5},{5,6},{6,7},{7,4},{8,11},{9,8},{10,9... | collective-permute-start | bytes 1179656 | tf_op jit(solution)/shard_map/ppermute | solution.py:36
  103.7 2.0 %rows_grad.3 = (bf16[768,1536]{1,0:T(8,128)(2,1)S(1)}, bf16[768,1536]{1,0:T(8,128)(2,1)S(1)}, f32[1,1536]{1,0:T(1,128)S(1)}) custom-call(s32[16]{0:T(128)S(1)} %stack.59.at.refs_0_, bf16[512,384]{1,0:T(8,128)(2,1)S(1)} %multiply_convert_fusion.1.b0.refs_1_, bf16[512,384]{1,0:T(8,128)(2,1)S(1)} %multiply_convert_fusion.b0.refs_2_, ...), custom_call_target="tpu_custom_call" | custom-call | flops 1207959552 | bytes 5000000 | tf_op jit(solution)/shard_map/rows_grad/pallas_call | solution.py:288
  105.6 8.0 %collective-permute-done.16.b1.refs_1_ = bf16[512,384]{1,0:T(8,128)(2,1)S(1)} collective-permute-done((bf16[512,384]{1,0:T(8,128)(2,1)S(1)}, bf16[512,384]{1,0:T(8,128)(2,1)S(1)}, u32[]{:S(2)}, u32[]{:S(2)}) %collective-permute-start.16) | collective-permute-done | bytes 393248 | tf_op jit(solution)/shard_map/ppermute | solution.py:36
  113.6 3.3 %collective-permute-start.17 = (bf16[512,384]{1,0:T(8,128)(2,1)S(1)}, bf16[512,384]{1,0:T(8,128)(2,1)S(1)}, u32[]{:S(2)}, u32[]{:S(2)}) collective-permute-start(bf16[512,384]{1,0:T(8,128)(2,1)S(1)} %collective-permute-done.16.b1.refs_1_), channel_id=1, source_target_pairs={{0,3},{1,0},{2,1},{3,2},{4,5},{5,6},{6,7},{7,4},{8,11},{9,8},{10,9... | collective-permute-start | bytes 1179656 | tf_op jit(solution)/shard_map/ppermute | solution.py:36
  116.9 2.4 %rows_partial.1.refs_4_ = f32[768,1536]{1,0:T(8,128)S(1)} custom-call(s32[16]{0:T(128)S(1)} %stack.59.at.refs_0_, bf16[512,384]{1,0:T(8,128)(2,1)S(1)} %collective-permute-done.13.b1.refs_1_, bf16[512,384]{1,0:T(8,128)(2,1)S(1)} %collective-permute-done.12.b3.refs_2_, bf16[512,1536]{1,0:T(8,128)(2,1)S(1)} %get-tuple-element.81.refs_3_), custom_call_target="tpu_custom_call" | custom-call | flops 1207959552 | bytes 8000000 | tf_op jit(solution)/shard_map/rows_partial/pallas_call | solution.py:238
  119.4 3.4 %rows_grad.4 = (bf16[768,1536]{1,0:T(8,128)(2,1)S(1)}, bf16[768,1536]{1,0:T(8,128)(2,1)S(1)}, f32[1,1536]{1,0:T(1,128)S(1)}) custom-call(s32[16]{0:T(128)S(1)} %stack.59.at.refs_0_, bf16[512,384]{1,0:T(8,128)(2,1)S(1)} %collective-permute-done.16.b1.refs_1_, ...), custom_call_target="tpu_custom_call", output_to_operand_aliasing={{0}: (5, {}), {1}: (6, {})} | custom-call | flops 1207959552 | bytes 10000000 | tf_op jit(solution)/shard_map/rows_grad/pallas_call | solution.py:288
  122.8 4.2 %backward.2.right0 = bf16[512,1536]{1,0:T(8,128)(2,1)S(1)} custom-call(s32[16]{0:T(128)S(1)} %stack.59.at.refs_0_, bf16[512,384]{1,0:T(8,128)(2,1)S(1)} %multiply_convert_fusion.1.b0.refs_1_, bf16[512,384]{1,0:T(8,128)(2,1)S(1)} %collective-permute-done.13.b1.refs_1_, bf16[512,384]{1,0:T(8,128)(2,1)S(1)} %collective-permute-done.14.b2.refs_1_, ...), custom_call_target="tpu_custom_call" | custom-call | flops 2415919104 | bytes 14000000 | tf_op jit(solution)/shard_map/backward/pallas_call | solution.py:189
  127.0 4.2 %backward.3.right1 = bf16[512,1536]{1,0:T(8,128)(2,1)S(1)} custom-call(s32[16]{0:T(128)S(1)} %stack.59.at.refs_0_, bf16[512,384]{1,0:T(8,128)(2,1)S(1)} %multiply_convert_fusion.b0.refs_2_, bf16[512,384]{1,0:T(8,128)(2,1)S(1)} %collective-permute-done.16.b1.refs_1_, bf16[512,384]{1,0:T(8,128)(2,1)S(1)} %collective-permute-done.17.b2.refs_2_, ...), custom_call_target="tpu_custom_call" | custom-call | flops 2415919104 | bytes 14000000 | tf_op jit(solution)/shard_map/backward/pallas_call | solution.py:189
  131.2 2.0 %rows_grad.5 = (bf16[768,1536]{1,0:T(8,128)(2,1)S(1)}, bf16[768,1536]{1,0:T(8,128)(2,1)S(1)}, f32[1,1536]{1,0:T(1,128)S(1)}) custom-call(s32[16]{0:T(128)S(1)} %stack.59.at.refs_0_, bf16[512,384]{1,0:T(8,128)(2,1)S(1)} %collective-permute-done.14.b2.refs_1_, ...), custom_call_target="tpu_custom_call", output_to_operand_aliasing={{0}: (5, {}), {1}: (6, {})} | custom-call | flops 1207959552 | bytes 5000000 | tf_op jit(solution)/shard_map/rows_grad/pallas_call | solution.py:288
  133.2 6.7 %weight_grad.1 = (bf16[768,1536]{1,0:T(8,128)(2,1)S(1)}, bf16[768,1536]{1,0:T(8,128)(2,1)S(1)}, f32[1,128]{1,0:T(1,128)S(1)}) custom-call(s32[16]{0:T(128)S(1)} %stack.59.at.refs_0_, bf16[768,1024]{1,0:T(8,128)(2,1)S(1)} %get-tuple-element.96.keep_l, bf16[768,1024]{1,0:T(8,128)(2,1)S(1)} %get-tuple-element.97.send_l, bf16[512,1536]{1,0:T(8,128)(2,1)S(1)} %backward.2.right0, ...), custom_call_target="tpu_custom_call" | custom-call | flops 4831838208 | bytes 11000000 | tf_op jit(solution)/shard_map/weight_grad/pallas_call | solution.py:330
  140.4 3.5 %collective-permute-done.19 = f32[1,128]{1,0:T(1,128)S(1)} collective-permute-done((f32[1,128]{1,0:T(1,128)S(1)}, f32[1,128]{1,0:T(1,128)S(1)}, u32[]{:S(2)}, u32[]{:S(2)}) %collective-permute-start.19) | collective-permute-done | bytes 544 | tf_op jit(solution)/shard_map/ppermute | solution.py:62
  144.0 4.7 %collective-permute-done.20 = f32[1,128]{1,0:T(1,128)S(1)} collective-permute-done((f32[1,128]{1,0:T(1,128)S(1)}, f32[1,128]{1,0:T(1,128)S(1)}, u32[]{:S(2)}, u32[]{:S(2)}) %collective-permute-start.20) | collective-permute-done | bytes 544 | tf_op jit(solution)/shard_map/ppermute | solution.py:62
  148.8 1.1 collective-permute-done.21.u1
  149.9 1.4 far.1
  151.4 1.4 collective-permute-start.24
  152.8 1.9 collective-permute-start.25
  154.7 1.9 near.1
  156.6 1.7 collective-permute-start.27
  158.7 3.8 %collective-permute-done.24.up = bf16[4,48,1536]{2,1,0:T(8,128)(2,1)S(1)} collective-permute-done((bf16[4,48,1536]{2,1,0:T(8,128)(2,1)S(1)}, bf16[4,48,1536]{2,1,0:T(8,128)(2,1)S(1)}, u32[]{:S(2)}, u32[]{:S(2)}) %collective-permute-start.24) | collective-permute-done | bytes 589856 | tf_op jit(solution)/shard_map/ppermute | solution.py:46
  162.6 1.6 relay.1
  164.3 1.7 collective-permute-start.26
  165.9 1.6 collective-permute-start.29
  167.6 1.4 collective-permute-done.27.down1
  169.3 6.3 %collective-permute-done.26.up1 = bf16[4,48,1536]{2,1,0:T(8,128)(2,1)S(1)} collective-permute-done((bf16[4,48,1536]{2,1,0:T(8,128)(2,1)S(1)}, bf16[4,48,1536]{2,1,0:T(8,128)(2,1)S(1)}, u32[]{:S(2)}, u32[]{:S(2)}) %collective-permute-start.26) | collective-permute-done | bytes 589856 | tf_op jit(solution)/shard_map/ppermute | solution.py:46
  176.8 16.9 %all_to_all.10 = bf16[4,2,48,1536]{3,2,1,0:T(8,128)(2,1)S(1)} all-to-all(bf16[4,2,48,1536]{3,2,1,0:T(8,128)(2,1)S(1)} %close.1), channel_id=1, replica_groups={{0,8,16,24},{32,40,48,56},{64,72,80,88},{96,104,112,120},{4,36,68,100},..., dimensions={0} | all-to-all | bytes 2359296 | tf_op jit(solution)/shard_map/all_to_all | solution.py:570
  (93 shorter events, 18.8 us)
Async XLA Ops:
  0.6 39.4 %copy-start = (bf16[1536,3,384]{2,0,1:T(8,128)(2,1)S(1)}, bf16[1536,3,384]{2,0,1:T(8,128)(2,1)}, u32[]{:S(2)}) copy-start(bf16[1536,3,384]{2,0,1:T(8,128)(2,1)} %param.19) | copy-start | bytes 10616836
  0.6 22.1 %collective-permute-start = (bf16[1024,384]{1,0:T(8,128)(2,1)}, bf16[1024,384]{1,0:T(8,128)(2,1)}, u32[]{:S(2)}, u32[]{:S(2)}) collective-permute-start(bf16[1024,384]{1,0:T(8,128)(2,1)} %x0.3), channel_id=1, source_target_pairs={{0,1},{1,2},{2,3},{3,0},{4,7},{5,4},{6,5},{7,6},{8,9},{9,10},{10,1... | collective-permute-start | bytes 2359304 | tf_op jit(solution)/shard_map/ppermute | solution.py:36
  2.3 20.5 %collective-permute-start.1 = (bf16[1024,384]{1,0:T(8,128)(2,1)}, bf16[1024,384]{1,0:T(8,128)(2,1)}, u32[]{:S(2)}, u32[]{:S(2)}) collective-permute-start(bf16[1024,384]{1,0:T(8,128)(2,1)} %x0.3), channel_id=1, source_target_pairs={{0,3},{1,0},{2,1},{3,2},{4,5},{5,6},{6,7},{7,4},{8,11},{9,8},{10,9... | collective-permute-start | bytes 2359304 | tf_op jit(solution)/shard_map/ppermute | solution.py:36
  6.4 16.4 %all-to-all-start = ((f32[32,8,128]{2,1,0:T(8,128)}), f32[32,8,128]{2,1,0:T(8,128)}, u32[]{:S(2)}, u32[]{:S(2)}) async-start(f32[32,8,128]{2,1,0:T(8,128)} %broadcast_in_dim.31), calls=%async_computation | async-start | bytes 262144 | tf_op jit(solution)/shard_map/all_to_all | solution.py:463
  15.0 8.0 %copy-start.11 = (s32[32]{0:T(128)S(1)}, s32[32]{0:T(128)}, u32[]{:S(2)}) copy-start(s32[32]{0:T(128)} %param.17) | copy-start | bytes 388
  22.8 15.7 %collective-permute-start.4 = (bf16[1024,384]{1,0:T(8,128)(2,1)}, bf16[1024,384]{1,0:T(8,128)(2,1)S(1)}, u32[]{:S(2)}, u32[]{:S(2)}) collective-permute-start(bf16[1024,384]{1,0:T(8,128)(2,1)} %collective-permute-done.x3), channel_id=1, source_target_pairs={{0,1},{1,2},{2,3},{3,0},{4,7},{5,4},{6,5},{7,6},{8,9},{9,10},{10,1... | collective-permute-start | bytes 2359304 | tf_op jit(solution)/shard_map/ppermute | solution.py:36
  26.5 6.5 %collective-permute-start.2 = (f32[1,1536]{1,0:T(1,128)S(1)}, f32[1,1536]{1,0:T(1,128)S(1)}, u32[]{:S(2)}, u32[]{:S(2)}) collective-permute-start(f32[1,1536]{1,0:T(1,128)S(1)} %fusion.27), channel_id=1, source_target_pairs={{0,1},{1,0},{2,3},{3,2},{4,5},{5,4},{6,7},{7,6},{8,9},{9,8},{10,11... | collective-permute-start | bytes 18440 | tf_op jit(solution)/shard_map/ppermute | solution.py:62
  33.0 5.5 %collective-permute-start.3 = (f32[1,1536]{1,0:T(1,128)S(1)}, f32[1,1536]{1,0:T(1,128)S(1)}, u32[]{:S(2)}, u32[]{:S(2)}) collective-permute-start(f32[1,1536]{1,0:T(1,128)S(1)} %add.191), channel_id=1, source_target_pairs={{0,3},{1,2},{2,1},{3,0},{4,7},{5,6},{6,5},{7,4},{8,11},{9,10},{10,... | collective-permute-start | bytes 18440 | tf_op jit(solution)/shard_map/ppermute | solution.py:62
  38.5 0.9 copy-start.10
  40.6 3.7 %collective-permute-start.5 = (f32[3,384]{1,0:T(4,128)S(1)}, f32[3,384]{1,0:T(4,128)S(1)}, u32[]{:S(2)}, u32[]{:S(2)}) collective-permute-start(f32[3,384]{1,0:T(4,128)S(1)} %bitcast.74), channel_id=1, source_target_pairs={{0,1},{1,0},{2,3},{3,2},{4,5},{5,4},{6,7},{7,6},{8,9},{9,8},{10,11... | collective-permute-start | bytes 13832 | tf_op jit(solution)/shard_map/ppermute | solution.py:62
  44.3 5.0 %collective-permute-start.6 = (f32[6,384]{1,0:T(8,128)S(1)}, f32[6,384]{1,0:T(8,128)S(1)}, u32[]{:S(2)}, u32[]{:S(2)}) collective-permute-start(f32[6,384]{1,0:T(8,128)S(1)} %pad_maximum_fusion), channel_id=1, source_target_pairs={{0,3},{1,2},{2,1},{3,0},{4,7},{5,6},{6,5},{7,4},{8,11},{9,10},{10,... | collective-permute-start | bytes 27656 | tf_op jit(solution)/shard_map/ppermute | solution.py:62
  47.6 9.6 %copy-start.3 = (bf16[384,1536]{1,0:T(8,128)(2,1)S(1)}, bf16[384,1536]{1,0:T(8,128)(2,1)}, u32[]{:S(2)}) copy-start(bf16[384,1536]{1,0:T(8,128)(2,1)} %get-tuple-element.71) | copy-start | bytes 3538948
  57.2 1.3 copy-start.5
  58.5 4.6 %copy-start.4 = (bf16[384,1536]{1,0:T(8,128)(2,1)S(1)}, bf16[384,1536]{1,0:T(8,128)(2,1)}, u32[]{:S(2)}) copy-start(bf16[384,1536]{1,0:T(8,128)(2,1)} %get-tuple-element.70) | copy-start | bytes 3538948
  59.5 12.4 %collective-permute-start.7 = (bf16[512,384]{1,0:T(8,128)(2,1)S(1)}, bf16[512,384]{1,0:T(8,128)(2,1)S(1)}, u32[]{:S(2)}, u32[]{:S(2)}) collective-permute-start(bf16[512,384]{1,0:T(8,128)(2,1)S(1)} %convolution_convert_fusion.2), channel_id=1, source_target_pairs={{0,1},{1,2},{2,3},{3,0},{4,7},{5,4},{6,5},{7,6},{8,9},{9,10},{10,1... | collective-permute-start | bytes 1179656 | tf_op jit(solution)/shard_map/ppermute | solution.py:36
  59.6 12.4 %collective-permute-start.8 = (bf16[512,384]{1,0:T(8,128)(2,1)S(1)}, bf16[512,384]{1,0:T(8,128)(2,1)S(1)}, u32[]{:S(2)}, u32[]{:S(2)}) collective-permute-start(bf16[512,384]{1,0:T(8,128)(2,1)S(1)} %convolution_convert_fusion.3), channel_id=1, source_target_pairs={{0,3},{1,0},{2,1},{3,2},{4,5},{5,6},{6,7},{7,4},{8,11},{9,8},{10,9... | collective-permute-start | bytes 1179656 | tf_op jit(solution)/shard_map/ppermute | solution.py:36
  73.0 1.3 copy-start.2
  73.0 13.3 %collective-permute-start.9 = (bf16[512,384]{1,0:T(8,128)(2,1)S(1)}, bf16[512,384]{1,0:T(8,128)(2,1)S(1)}, u32[]{:S(2)}, u32[]{:S(2)}) collective-permute-start(bf16[512,384]{1,0:T(8,128)(2,1)S(1)} %add_convert_fusion.3), channel_id=1, source_target_pairs={{0,1},{1,2},{2,3},{3,0},{4,7},{5,4},{6,5},{7,6},{8,9},{9,10},{10,1... | collective-permute-start | bytes 1179656 | tf_op jit(solution)/shard_map/ppermute | solution.py:36
  74.3 12.1 %copy-start.6 = (bf16[1024,384]{1,0:T(8,128)(2,1)S(1)}, bf16[1024,384]{1,0:T(8,128)(2,1)}, u32[]{:S(2)}) copy-start(bf16[1024,384]{1,0:T(8,128)(2,1)} %x0.3) | copy-start | bytes 2359300
  74.3 12.1 %copy-start.7 = (bf16[1024,384]{1,0:T(8,128)(2,1)S(1)}, bf16[1024,384]{1,0:T(8,128)(2,1)}, u32[]{:S(2)}) copy-start(bf16[1024,384]{1,0:T(8,128)(2,1)} %param.13) | copy-start | bytes 2359300
  75.3 16.7 %collective-permute-start.10 = (bf16[512,384]{1,0:T(8,128)(2,1)S(1)}, bf16[512,384]{1,0:T(8,128)(2,1)S(1)}, u32[]{:S(2)}, u32[]{:S(2)}) collective-permute-start(bf16[512,384]{1,0:T(8,128)(2,1)S(1)} %convolution_convert_fusion.1), channel_id=1, source_target_pairs={{0,3},{1,0},{2,1},{3,2},{4,5},{5,6},{6,7},{7,4},{8,11},{9,8},{10,9... | collective-permute-start | bytes 1179656 | tf_op jit(solution)/shard_map/ppermute | solution.py:36
  78.4 22.7 %collective-permute-start.15 = (bf16[512,384]{1,0:T(8,128)(2,1)S(1)}, bf16[512,384]{1,0:T(8,128)(2,1)S(1)}, u32[]{:S(2)}, u32[]{:S(2)}) collective-permute-start(bf16[512,384]{1,0:T(8,128)(2,1)S(1)} %convolution_convert_fusion), channel_id=1, source_target_pairs={{0,1},{1,2},{2,3},{3,0},{4,7},{5,4},{6,5},{7,6},{8,9},{9,10},{10,1... | collective-permute-start | bytes 1179656 | tf_op jit(solution)/shard_map/ppermute | solution.py:36
  86.7 14.4 %collective-permute-start.12 = (bf16[512,384]{1,0:T(8,128)(2,1)S(1)}, bf16[512,384]{1,0:T(8,128)(2,1)S(1)}, u32[]{:S(2)}, u32[]{:S(2)}) collective-permute-start(bf16[512,384]{1,0:T(8,128)(2,1)S(1)} %multiply_convert_fusion.1.b0.refs_1_), channel_id=1, source_target_pairs={{0,1},{1,2},{2,3},{3,0},{4,7},{5,4},{6,5},{7,6},{8,9},{9,10},{10,1... | collective-permute-start | bytes 1179656 | tf_op jit(solution)/shard_map/ppermute | solution.py:36
  86.8 14.3 %collective-permute-start.13 = (bf16[512,384]{1,0:T(8,128)(2,1)S(1)}, bf16[512,384]{1,0:T(8,128)(2,1)S(1)}, u32[]{:S(2)}, u32[]{:S(2)}) collective-permute-start(bf16[512,384]{1,0:T(8,128)(2,1)S(1)} %multiply_convert_fusion.1.b0.refs_1_), channel_id=1, source_target_pairs={{0,3},{1,0},{2,1},{3,2},{4,5},{5,6},{6,7},{7,4},{8,11},{9,8},{10,9... | collective-permute-start | bytes 1179656 | tf_op jit(solution)/shard_map/ppermute | solution.py:36
  92.1 7.8 %collective-permute-start.11 = (bf16[512,384]{1,0:T(8,128)(2,1)S(1)}, bf16[512,384]{1,0:T(8,128)(2,1)S(1)}, u32[]{:S(2)}, u32[]{:S(2)}) collective-permute-start(bf16[512,384]{1,0:T(8,128)(2,1)S(1)} %add_convert_fusion.2), channel_id=1, source_target_pairs={{0,3},{1,0},{2,1},{3,2},{4,5},{5,6},{6,7},{7,4},{8,11},{9,8},{10,9... | collective-permute-start | bytes 1179656 | tf_op jit(solution)/shard_map/ppermute | solution.py:36
  101.5 12.1 %collective-permute-start.16 = (bf16[512,384]{1,0:T(8,128)(2,1)S(1)}, bf16[512,384]{1,0:T(8,128)(2,1)S(1)}, u32[]{:S(2)}, u32[]{:S(2)}) collective-permute-start(bf16[512,384]{1,0:T(8,128)(2,1)S(1)} %multiply_convert_fusion.b0.refs_2_), channel_id=1, source_target_pairs={{0,3},{1,0},{2,1},{3,2},{4,5},{5,6},{6,7},{7,4},{8,11},{9,8},{10,9... | collective-permute-start | bytes 1179656 | tf_op jit(solution)/shard_map/ppermute | solution.py:36
  103.6 15.7 %collective-permute-start.18 = (bf16[512,384]{1,0:T(8,128)(2,1)S(1)}, bf16[512,384]{1,0:T(8,128)(2,1)S(1)}, u32[]{:S(2)}, u32[]{:S(2)}) collective-permute-start(bf16[512,384]{1,0:T(8,128)(2,1)S(1)} %multiply_convert_fusion.b0.refs_2_), channel_id=1, source_target_pairs={{0,1},{1,2},{2,3},{3,0},{4,7},{5,4},{6,5},{7,6},{8,9},{9,10},{10,1... | collective-permute-start | bytes 1179656 | tf_op jit(solution)/shard_map/ppermute | solution.py:36
  103.7 19.1 %collective-permute-start.14 = (bf16[512,384]{1,0:T(8,128)(2,1)S(1)}, bf16[512,384]{1,0:T(8,128)(2,1)S(1)}, u32[]{:S(2)}, u32[]{:S(2)}) collective-permute-start(bf16[512,384]{1,0:T(8,128)(2,1)S(1)} %collective-permute-done.12.b3.refs_2_), channel_id=1, source_target_pairs={{0,1},{1,2},{2,3},{3,0},{4,7},{5,4},{6,5},{7,6},{8,9},{9,10},{10,1... | collective-permute-start | bytes 1179656 | tf_op jit(solution)/shard_map/ppermute | solution.py:36
  113.6 13.4 %collective-permute-start.17 = (bf16[512,384]{1,0:T(8,128)(2,1)S(1)}, bf16[512,384]{1,0:T(8,128)(2,1)S(1)}, u32[]{:S(2)}, u32[]{:S(2)}) collective-permute-start(bf16[512,384]{1,0:T(8,128)(2,1)S(1)} %collective-permute-done.16.b1.refs_1_), channel_id=1, source_target_pairs={{0,3},{1,0},{2,1},{3,2},{4,5},{5,6},{6,7},{7,4},{8,11},{9,8},{10,9... | collective-permute-start | bytes 1179656 | tf_op jit(solution)/shard_map/ppermute | solution.py:36
  116.9 5.8 %slice-start = ((s8[4718592]{0:T(1024)(128)(4,1)}), s8[4194304]{0:T(1024)(128)(4,1)S(1)}, s32[]{:S(2)}) async-start(s8[4718592]{0:T(1024)(128)(4,1)} %bitcast.72), calls=%async_computation.2 | async-start | bytes 8388608
  119.4 3.4 %slice-start.1 = ((s8[4718592]{0:T(1024)(128)(4,1)}), s8[524288]{0:T(1024)(128)(4,1)S(1)}, s32[]{:S(2)}) async-start(s8[4718592]{0:T(1024)(128)(4,1)} %bitcast.72), calls=%async_computation.3 | async-start | bytes 1048576
  139.8 10.1 %collective-permute-start.22 = (bf16[768,1536]{1,0:T(8,128)(2,1)S(1)}, bf16[768,1536]{1,0:T(8,128)(2,1)S(1)}, u32[]{:S(2)}, u32[]{:S(2)}) collective-permute-start(bf16[768,1536]{1,0:T(8,128)(2,1)S(1)} %get-tuple-element.115), channel_id=1, source_target_pairs={{0,4},{4,0},{8,12},{12,8},{16,20},{20,16},{24,28},{28,24},{32,36},... | collective-permute-start | bytes 7077896 | tf_op jit(solution)/shard_map/ppermute | solution.py:46
  139.9 10.0 %collective-permute-start.23 = (bf16[768,1536]{1,0:T(8,128)(2,1)S(1)}, bf16[768,1536]{1,0:T(8,128)(2,1)S(1)}, u32[]{:S(2)}, u32[]{:S(2)}) collective-permute-start(bf16[768,1536]{1,0:T(8,128)(2,1)S(1)} %get-tuple-element.116), channel_id=1, source_target_pairs={{0,4},{4,0},{8,12},{12,8},{16,20},{20,16},{24,28},{28,24},{32,36},... | collective-permute-start | bytes 7077896 | tf_op jit(solution)/shard_map/ppermute | solution.py:46
  140.4 3.5 %collective-permute-start.19 = (f32[1,128]{1,0:T(1,128)S(1)}, f32[1,128]{1,0:T(1,128)S(1)}, u32[]{:S(2)}, u32[]{:S(2)}) collective-permute-start(f32[1,128]{1,0:T(1,128)S(1)} %get-tuple-element.112), channel_id=1, source_target_pairs={{0,1},{1,0},{2,3},{3,2},{4,5},{5,4},{6,7},{7,6},{8,9},{9,8},{10,11... | collective-permute-start | bytes 1544 | tf_op jit(solution)/shard_map/ppermute | solution.py:62
  144.0 4.8 %collective-permute-start.20 = (f32[1,128]{1,0:T(1,128)S(1)}, f32[1,128]{1,0:T(1,128)S(1)}, u32[]{:S(2)}, u32[]{:S(2)}) collective-permute-start(f32[1,128]{1,0:T(1,128)S(1)} %add.215), channel_id=1, source_target_pairs={{0,3},{1,2},{2,1},{3,0},{4,7},{5,6},{6,5},{7,4},{8,11},{9,10},{10,... | collective-permute-start | bytes 1544 | tf_op jit(solution)/shard_map/ppermute | solution.py:62
  148.7 1.2 collective-permute-start.21
  151.4 11.2 %collective-permute-start.24 = (bf16[4,48,1536]{2,1,0:T(8,128)(2,1)S(1)}, bf16[4,48,1536]{2,1,0:T(8,128)(2,1)S(1)}, u32[]{:S(2)}, u32[]{:S(2)}) collective-permute-start(bf16[4,48,1536]{2,1,0:T(8,128)(2,1)S(1)} %get-tuple-element.118), channel_id=1, source_target_pairs={{0,32},{4,12},{8,40},{12,20},{16,48},{20,28},{24,56},{28,4},{32,64... | collective-permute-start | bytes 1769480 | tf_op jit(solution)/shard_map/ppermute | solution.py:46
  152.8 9.9 %collective-permute-start.25 = (bf16[4,48,1536]{2,1,0:T(8,128)(2,1)S(1)}, bf16[4,48,1536]{2,1,0:T(8,128)(2,1)S(1)}, u32[]{:S(2)}, u32[]{:S(2)}) collective-permute-start(bf16[4,48,1536]{2,1,0:T(8,128)(2,1)S(1)} %get-tuple-element.119), channel_id=1, source_target_pairs={{0,96},{4,28},{8,104},{12,4},{16,112},{20,12},{24,120},{28,20},{32... | collective-permute-start | bytes 1769480 | tf_op jit(solution)/shard_map/ppermute | solution.py:46
  156.6 12.4 %collective-permute-start.27 = (bf16[4,48,1536]{2,1,0:T(8,128)(2,1)S(1)}, bf16[4,48,1536]{2,1,0:T(8,128)(2,1)S(1)}, u32[]{:S(2)}, u32[]{:S(2)}) collective-permute-start(bf16[4,48,1536]{2,1,0:T(8,128)(2,1)S(1)} %get-tuple-element.121), channel_id=1, source_target_pairs={{0,96},{4,28},{8,104},{12,4},{16,112},{20,12},{24,120},{28,20},{32... | collective-permute-start | bytes 1769480 | tf_op jit(solution)/shard_map/ppermute | solution.py:46
  158.2 11.1 %collective-permute-start.28 = (bf16[4,48,1536]{2,1,0:T(8,128)(2,1)S(1)}, bf16[4,48,1536]{2,1,0:T(8,128)(2,1)S(1)}, u32[]{:S(2)}, u32[]{:S(2)}) collective-permute-start(bf16[4,48,1536]{2,1,0:T(8,128)(2,1)S(1)} %get-tuple-element.122), channel_id=1, source_target_pairs={{0,32},{4,12},{8,40},{12,20},{16,48},{20,28},{24,56},{28,4},{32,64... | collective-permute-start | bytes 1769480 | tf_op jit(solution)/shard_map/ppermute | solution.py:46
  164.3 11.4 %collective-permute-start.26 = (bf16[4,48,1536]{2,1,0:T(8,128)(2,1)S(1)}, bf16[4,48,1536]{2,1,0:T(8,128)(2,1)S(1)}, u32[]{:S(2)}, u32[]{:S(2)}) collective-permute-start(bf16[4,48,1536]{2,1,0:T(8,128)(2,1)S(1)} %get-tuple-element.120), channel_id=1, source_target_pairs={{0,32},{4,12},{8,40},{12,20},{16,48},{20,28},{24,56},{28,4},{32,64... | collective-permute-start | bytes 1769480 | tf_op jit(solution)/shard_map/ppermute | solution.py:46
  165.9 9.9 %collective-permute-start.29 = (bf16[4,48,1536]{2,1,0:T(8,128)(2,1)S(1)}, bf16[4,48,1536]{2,1,0:T(8,128)(2,1)S(1)}, u32[]{:S(2)}, u32[]{:S(2)}) collective-permute-start(bf16[4,48,1536]{2,1,0:T(8,128)(2,1)S(1)} %get-tuple-element.123), channel_id=1, source_target_pairs={{0,96},{4,28},{8,104},{12,4},{16,112},{20,12},{24,120},{28,20},{32... | collective-permute-start | bytes 1769480 | tf_op jit(solution)/shard_map/ppermute | solution.py:46
  176.8 17.2 %copy-start.8 = (f32[48,1536]{1,0:T(8,128)S(1)}, f32[48,1536]{1,0:T(8,128)}, u32[]{:S(2)}) copy-start(f32[48,1536]{1,0:T(8,128)} %param.23) | copy-start | bytes 884740
  176.8 17.1 %copy-start.9 = (f32[48,1536]{1,0:T(8,128)S(1)}, f32[48,1536]{1,0:T(8,128)}, u32[]{:S(2)}) copy-start(f32[48,1536]{1,0:T(8,128)} %param.22) | copy-start | bytes 884740
  176.8 18.0 %copy-start.1 = (bf16[1536,3,384]{2,0,1:T(8,128)(2,1)S(1)}, bf16[1536,3,384]{2,0,1:T(8,128)(2,1)}, u32[]{:S(2)}) copy-start(bf16[1536,3,384]{2,0,1:T(8,128)(2,1)} %param.19) | copy-start | bytes 10616836

commit v5 on v4

--- a/solution.py
+++ b/solution.py
@@ -58,7 +58,7 @@
 
 
 def swap_x(value, kind):
-    other = [x ^ 1 for x in range(RING)] if kind == 0 else [3 - x for x in range(RING)]
+    other = [x ^ 1 for x in range(RING)] if kind == 0 else [x ^ 2 for x in range(RING)]
     return lax.ppermute(value, "mp", list(enumerate(other)))
 
 
@@ -343,16 +343,16 @@
     return kept[...].astype(F32) * u0[0:1, 0:1] + got[...].astype(F32) * u1[0:1, 0:1]
 
 
-def far_kernel(at, u0, u1, k1, k2, g1, g2, far1, far2):
+def spread_kernel(at, u0, u1, k1, k2, k3, k4, g1, g2, g3, g4, far1, far2, behind1, ahead2):
     far1[0] = scaled(k1, g1, u0, u1).astype(BF)
     far2[0] = scaled(k2, g2, u0, u1).astype(BF)
-
-
-def near_kernel(at, u0, u1, k1, k2, k3, k4, g1, g2, g3, g4, own, ahead2, behind1):
+    behind1[0] = scaled(k3, g3, u0, u1).astype(BF)
+    ahead2[0] = scaled(k4, g4, u0, u1).astype(BF)
+
+
+def own_kernel(at, u0, u1, k1, k2, g1, g2, own):
     own[0, 0] = scaled(k1, g1, u0, u1)
     own[0, 1] = scaled(k2, g2, u0, u1)
-    behind1[0] = scaled(k3, g3, u0, u1).astype(BF)
-    ahead2[0] = scaled(k4, g4, u0, u1).astype(BF)
 
 
 def relay_kernel(at, u0, u1, k1, k2, g1, g2, up, down, ahead1, behind2):
@@ -373,32 +373,33 @@
     single = shaped((RING, 48, ff))
     unit = [whole((1, 128))] * 2
     size = RING * 48 * ff
-    far1, far2 = call(
-        far_kernel,
-        RING,
-        unit + [block(2)] * 4,
-        [one, one],
-        [single] * 2,
-        [],
-        cost(6 * size, 12 * size),
-        "far",
-    )(at, u0, u1, first[0], second[0], first[1], second[1])
-    far1, far2 = move(far1, 1), move(far2, -1)
-    order = [block(0), block(0), block(3), block(1)]
-    own, ahead2, behind1 = call(
-        near_kernel,
+    order = [block(2), block(2), block(3), block(1)]
+    far1, far2, behind1, ahead2 = call(
+        spread_kernel,
         RING,
         unit + order * 2,
-        [both, one, one],
-        [shaped((RING, 2, 48, ff), F32), single, single],
+        [one] * 4,
+        [single] * 4,
         [],
-        cost(12 * size, 28 * size),
-        "near",
+        cost(12 * size, 24 * size),
+        "spread",
     )(
         at, u0, u1, first[0], second[0], first[0], second[0],
         first[1], second[1], first[1], second[1],
     )
+    far1, far2 = move(far1, 1), move(far2, -1)
     up2, down1 = move(ahead2, 1), move(behind1, -1)
+    own = call(
+        own_kernel,
+        RING,
+        unit + [block(0)] * 4,
+        both,
+        shaped((RING, 2, 48, ff), F32),
+        [],
+        cost(6 * size, 16 * size),
+        "own",
+    )(at, u0, u1, first[0], second[0], first[1], second[1])
+    own, far1, far2 = lax.optimization_barrier((own, far1, far2))
     ahead1, behind2 = call(
         relay_kernel,
         RING,
@@ -444,7 +445,7 @@
     way = 1 - 2 * me_c
 
     ahead = [(me_x + k * way) % RING for k in range(RING)]
-    swapped = [me_x, me_x ^ 1, 3 - me_x, (3 - me_x) ^ 1]
+    swapped = [me_x, me_x ^ 1, me_x ^ 2, me_x ^ 3]
     me_one = jnp.where(me_c == 0, me_y, me_z)
     stride = jnp.where(me_c == 0, 4, 1)
     at = jnp.stack(
@@ -540,11 +541,11 @@
     back1 = leave(1, own1, up1, down1)
     far0 = by_x(behind0, 1)
     behind1, ahead1 = by_x(back1, 1), by_x(back1, -1)
-    far1 = by_x(ahead1, -1)
-
     rights = (hidden0, hidden1)
     *second, square_a = rows_grad(at, (0,), ((back0,), (back1,)), rights, (), ())
     partial = rows_partial(at, (ahead0, behind0), hidden0)
+    ahead1, partial, square_a = lax.optimization_barrier((ahead1, partial, square_a))
+    far1 = by_x(ahead1, -1)
     grad0 = backward(at, (back0, ahead0, far0, behind0), out_w, slope0)
     *second, square_b = rows_grad(
         at, (1, 3), ((ahead1, behind1),), (hidden1,), (partial,), tuple(second)

time: 195 us -> 195 us (level)
  starting transfers between devices: 46.6 us -> 54.4 us
  waiting for transfers between devices: 54.5 us -> 46.8 us
    ppermute x15, waiting for transfers between devices: 19.5 us -> 12.8 us  [by_x(): return lax.ppermute(value, ('dp', 'mp'), pairs)]
    ppermute x15, starting transfers between devices: 19.2 us -> 24.9 us  [by_x(): return lax.ppermute(value, ('dp', 'mp'), pairs)]
    ppermute x6, starting transfers between devices: 9.43 us -> 11.6 us  [swap_x(): return lax.ppermute(value, 'mp', list(enumerate(other)))]
  transfers between devices with their start and end apart: 31 -> 31, of which waited for: 18 -> 17; matrix products, arithmetic and copies ran while one was open for 9% -> 9% of each run, Pallas kernels for 13% -> 13%
where the time goes in v5:
time: 195 us; the launch traced here: 194 us
  starting transfers between devices  54.4 us (28%)
  Pallas kernels  48.6 us (25%)
  waiting for transfers between devices  46.8 us (24%)
  blocking collectives  16.7 us (9%)
  matrix products  12 us (6%)
  other arithmetic  6.79 us (3%)
  local copies, waits for them, and re-layouts  5.9 us (3%)
  between operations  3.24 us (2%)
    ppermute x15, starting transfers between devices, by_x(): return lax.ppermute(value, ('dp', 'mp'), pairs)  24.9 us
    ppermute x6, waiting for transfers between devices, swap_x(): return lax.ppermute(value, 'mp', list(enumerate(other)))  17.7 us
    all_to_all x1, blocking collectives, local(): lax.all_to_all(value, 'dp', 0, 0, axis_index_groups=groups, tiled=True)  16.7 us
    pallas_call x2, Pallas kernels, forward(): call(forward_kernel, ff // WIDE, [piece] * 4 + [whole((3, PART)), whole((...  15.8 us
    ppermute x9, waiting for transfers between devices, by_dp(): return lax.ppermute(value, 'dp', pairs)  13.3 us
    ppermute x15, waiting for transfers between devices, by_x(): return lax.ppermute(value, ('dp', 'mp'), pairs)  12.8 us
    ppermute x6, starting transfers between devices, swap_x(): return lax.ppermute(value, 'mp', list(enumerate(other)))  11.6 us
    ppermute x9, starting transfers between devices, by_dp(): return lax.ppermute(value, 'dp', pairs)  9.38 us
  transfers between devices with their start and end apart: 31, of which 17 were waited for; matrix products, arithmetic and copies ran while one was open for 9% of the time, Pallas kernels for 13%

profile of v5, /device:TPU:0, one launch (start us, length us, event | category | flops | bytes accessed | tf_op | source)
XLA Modules:
  0.0 194.4 jit_solution(6711767814447356727)
XLA Ops:
  0.6 2.9 %collective-permute-start.1 = (bf16[1024,384]{1,0:T(8,128)(2,1)}, bf16[1024,384]{1,0:T(8,128)(2,1)}, u32[]{:S(2)}, u32[]{:S(2)}) collective-permute-start(bf16[1024,384]{1,0:T(8,128)(2,1)} %x0.3), channel_id=1, source_target_pairs={{0,3},{1,0},{2,1},{3,2},{4,5},{5,6},{6,7},{7,4},{8,11},{9,8},{10,9... | collective-permute-start | bytes 2359304 | tf_op jit(solution)/shard_map/ppermute | solution.py:36
  4.2 1.1 fusion.4
  6.0 8.5 %all-to-all-start = ((f32[32,8,128]{2,1,0:T(8,128)}), f32[32,8,128]{2,1,0:T(8,128)}, u32[]{:S(2)}, u32[]{:S(2)}) async-start(f32[32,8,128]{2,1,0:T(8,128)} %broadcast_in_dim.31), calls=%async_computation | async-start | bytes 262144 | tf_op jit(solution)/shard_map/all_to_all | solution.py:464
  14.6 4.6 %constant_dynamic-slice_fusion = (bf16[384,1536]{1,0:T(8,128)(2,1)}, bf16[384,1536]{1,0:T(8,128)(2,1)}, bf16[384,1536]{1,0:T(8,128)(2,1)}, bf16[384,1536]{1,0:T(8,128)(2,1)}) fusion(bf16[1536,1536]{1,0:T(8,128)(2,1)} %out_w.3, s32[]{:T(128)S(6)} %select_n.112, s32[]{:T(128)S(6)} %select_n.111, s32[]{:T(128)S(6)} %select_n.110, s32[]{:T(128)S(6)} %select_n.109), kind=kLoop, calls=%fused_computation.51 | loop fusion | bytes 9437200 | tf_op jit(solution)/shard_map/dynamic_slice | solution.py:457
  19.3 3.0 %all-to-all-done = f32[32,8,128]{2,1,0:T(8,128)} async-done(((f32[32,8,128]{2,1,0:T(8,128)}), f32[32,8,128]{2,1,0:T(8,128)}, u32[]{:S(2)}, u32[]{:S(2)}) %all-to-all-start) | async-done | bytes 131104 | tf_op jit(solution)/shard_map/all_to_all | solution.py:464
  23.1 1.0 select_reduce_fusion
  24.1 2.4 %fusion.27 = f32[1,1536]{1,0:T(1,128)S(1)} fusion(bf16[1024,1]{0,1:T(2,128)(2,1)S(1)} %reshape.95, bf16[1024,1536]{1,0:T(8,128)(2,1)} %param.18), kind=kOutput, calls=%fused_computation.60 | convolution fusion | flops 3145728 | bytes 3153920 | tf_op jit(solution)/shard_map/dot_general | solution.py:24
  26.5 1.5 collective-permute-start.2
  28.7 4.3 %collective-permute-done.2 = f32[1,1536]{1,0:T(1,128)S(1)} collective-permute-done((f32[1,1536]{1,0:T(1,128)S(1)}, f32[1,1536]{1,0:T(1,128)S(1)}, u32[]{:S(2)}, u32[]{:S(2)}) %collective-permute-start.2) | collective-permute-done | bytes 6176 | tf_op jit(solution)/shard_map/ppermute | solution.py:62
  33.0 4.0 %collective-permute-start.3 = (f32[1,1536]{1,0:T(1,128)S(1)}, f32[1,1536]{1,0:T(1,128)S(1)}, u32[]{:S(2)}, u32[]{:S(2)}) collective-permute-start(f32[1,1536]{1,0:T(1,128)S(1)} %add.191), channel_id=1, source_target_pairs={{0,2},{1,3},{2,0},{3,1},{4,6},{5,7},{6,4},{7,5},{8,10},{9,11},{10,... | collective-permute-start | bytes 18440 | tf_op jit(solution)/shard_map/ppermute | solution.py:62
  37.0 1.6 collective-permute-done.3
  40.7 2.1 %collective-permute-start.5 = (f32[3,384]{1,0:T(4,128)S(1)}, f32[3,384]{1,0:T(4,128)S(1)}, u32[]{:S(2)}, u32[]{:S(2)}) collective-permute-start(f32[3,384]{1,0:T(4,128)S(1)} %bitcast.74), channel_id=1, source_target_pairs={{0,1},{1,0},{2,3},{3,2},{4,5},{5,4},{6,7},{7,6},{8,9},{9,8},{10,11... | collective-permute-start | bytes 13832 | tf_op jit(solution)/shard_map/ppermute | solution.py:62
  42.9 1.6 collective-permute-done.5.m1
  44.5 4.0 %collective-permute-start.6 = (f32[6,384]{1,0:T(8,128)S(1)}, f32[6,384]{1,0:T(8,128)S(1)}, u32[]{:S(2)}, u32[]{:S(2)}) collective-permute-start(f32[6,384]{1,0:T(8,128)S(1)} %pad_maximum_fusion), channel_id=1, source_target_pairs={{0,2},{1,3},{2,0},{3,1},{4,6},{5,7},{6,4},{7,5},{8,10},{9,11},{10,... | collective-permute-start | bytes 27656 | tf_op jit(solution)/shard_map/ppermute | solution.py:62
  48.5 1.6 collective-permute-done.6.m2
  50.2 7.9 %forward.2 = (bf16[512,1536]{1,0:T(8,128)(2,1)S(1)}, bf16[512,1536]{1,0:T(8,128)(2,1)S(1)}, f32[512,1536]{1,0:T(8,128)S(1)}) custom-call(s32[16]{0:T(128)S(1)} %stack.59.at.refs_0_, bf16[1024,384]{1,0:T(8,128)(2,1)} %x0.3, bf16[1024,384]{1,0:T(8,128)(2,1)} %collective-permute-done.1.x1, bf16[1024,384]{1,0:T(8,128)(2,1)} %copy-done.10, ...), custom_call_target="tpu_custom_call" | custom-call | flops 2415919104 | bytes 12000000 | tf_op jit(solution)/shard_map/forward/pallas_call | solution.py:137
  60.3 4.2 %collective-permute-start.8 = (bf16[512,384]{1,0:T(8,128)(2,1)S(1)}, bf16[512,384]{1,0:T(8,128)(2,1)S(1)}, u32[]{:S(2)}, u32[]{:S(2)}) collective-permute-start(bf16[512,384]{1,0:T(8,128)(2,1)S(1)} %convolution_convert_fusion.3), channel_id=1, source_target_pairs={{0,3},{1,0},{2,1},{3,2},{4,5},{5,6},{6,7},{7,4},{8,11},{9,8},{10,9... | collective-permute-start | bytes 1179656 | tf_op jit(solution)/shard_map/ppermute | solution.py:36
  65.5 7.9 %forward.3 = (bf16[512,1536]{1,0:T(8,128)(2,1)S(1)}, bf16[512,1536]{1,0:T(8,128)(2,1)S(1)}, f32[512,1536]{1,0:T(8,128)S(1)}) custom-call(s32[16]{0:T(128)S(1)} %stack.59.at.refs_0_, bf16[1024,384]{1,0:T(8,128)(2,1)} %x0.3, bf16[1024,384]{1,0:T(8,128)(2,1)} %collective-permute-done.1.x1, bf16[1024,384]{1,0:T(8,128)(2,1)} %copy-done.10, ...), custom_call_target="tpu_custom_call" | custom-call | flops 2415919104 | bytes 12000000 | tf_op jit(solution)/shard_map/forward/pallas_call | solution.py:137
  75.7 3.3 %collective-permute-start.10 = (bf16[512,384]{1,0:T(8,128)(2,1)S(1)}, bf16[512,384]{1,0:T(8,128)(2,1)S(1)}, u32[]{:S(2)}, u32[]{:S(2)}) collective-permute-start(bf16[512,384]{1,0:T(8,128)(2,1)S(1)} %convolution_convert_fusion.1), channel_id=1, source_target_pairs={{0,3},{1,0},{2,1},{3,2},{4,5},{5,6},{6,7},{7,4},{8,11},{9,8},{10,9... | collective-permute-start | bytes 1179656 | tf_op jit(solution)/shard_map/ppermute | solution.py:36
  80.0 6.7 %collective-permute-done.9 = bf16[512,384]{1,0:T(8,128)(2,1)S(1)} collective-permute-done((bf16[512,384]{1,0:T(8,128)(2,1)S(1)}, bf16[512,384]{1,0:T(8,128)(2,1)S(1)}, u32[]{:S(2)}, u32[]{:S(2)}) %collective-permute-start.9) | collective-permute-done | bytes 393248 | tf_op jit(solution)/shard_map/ppermute | solution.py:36
  87.0 3.1 %collective-permute-start.13 = (bf16[512,384]{1,0:T(8,128)(2,1)S(1)}, bf16[512,384]{1,0:T(8,128)(2,1)S(1)}, u32[]{:S(2)}, u32[]{:S(2)}) collective-permute-start(bf16[512,384]{1,0:T(8,128)(2,1)S(1)} %multiply_convert_fusion.1.b0.refs_1_), channel_id=1, source_target_pairs={{0,3},{1,0},{2,1},{3,2},{4,5},{5,6},{6,7},{7,4},{8,11},{9,8},{10,9... | collective-permute-start | bytes 1179656 | tf_op jit(solution)/shard_map/ppermute | solution.py:36
  91.1 1.0 fusion.30
  92.1 3.3 %collective-permute-start.11 = (bf16[512,384]{1,0:T(8,128)(2,1)S(1)}, bf16[512,384]{1,0:T(8,128)(2,1)S(1)}, u32[]{:S(2)}, u32[]{:S(2)}) collective-permute-start(bf16[512,384]{1,0:T(8,128)(2,1)S(1)} %add_convert_fusion.2), channel_id=1, source_target_pairs={{0,3},{1,0},{2,1},{3,2},{4,5},{5,6},{6,7},{7,4},{8,11},{9,8},{10,9... | collective-permute-start | bytes 1179656 | tf_op jit(solution)/shard_map/ppermute | solution.py:36
  95.4 3.2 %add_convert_fusion = (bf16[512,1536]{1,0:T(8,128)(2,1)S(1)}, bf16[512,1536]{1,0:T(8,128)(2,1)S(1)}) fusion(f32[512,1536]{1,0:T(8,128)S(1)} %get-tuple-element.94, f32[512,1536]{1,0:T(8,128)S(1)} %get-tuple-element.93), kind=kLoop, calls=%fused_computation | loop fusion | flops 23592960 | bytes 9437184 | tf_op jit(solution)/shard_map/convert_element_type | solution.py:536
  98.6 2.2 %turn.1 = (bf16[768,1024]{1,0:T(8,128)(2,1)S(1)}, bf16[768,1024]{1,0:T(8,128)(2,1)S(1)}) custom-call(s32[16]{0:T(128)S(1)} %stack.59.at.refs_0_, bf16[512,1536]{1,0:T(8,128)(2,1)S(1)} %get-tuple-element.96.top, bf16[512,1536]{1,0:T(8,128)(2,1)S(1)} %get-tuple-element.97.low), custom_call_target="tpu_custom_call" | custom-call | flops 1572864 | bytes 6291456 | tf_op jit(solution)/shard_map/turn/pallas_call | solution.py:166
  101.2 3.6 %collective-permute-start.16 = (bf16[512,384]{1,0:T(8,128)(2,1)S(1)}, bf16[512,384]{1,0:T(8,128)(2,1)S(1)}, u32[]{:S(2)}, u32[]{:S(2)}) collective-permute-start(bf16[512,384]{1,0:T(8,128)(2,1)S(1)} %multiply_convert_fusion.refs_2_.b0), channel_id=1, source_target_pairs={{0,3},{1,0},{2,1},{3,2},{4,5},{5,6},{6,7},{7,4},{8,11},{9,8},{10,9... | collective-permute-start | bytes 1179656 | tf_op jit(solution)/shard_map/ppermute | solution.py:36
  104.9 2.0 %rows_grad.3 = (bf16[768,1536]{1,0:T(8,128)(2,1)S(1)}, bf16[768,1536]{1,0:T(8,128)(2,1)S(1)}, f32[1,1536]{1,0:T(1,128)S(1)}) custom-call(s32[16]{0:T(128)S(1)} %stack.59.at.refs_0_, bf16[512,384]{1,0:T(8,128)(2,1)S(1)} %multiply_convert_fusion.1.b0.refs_1_, bf16[512,384]{1,0:T(8,128)(2,1)S(1)} %multiply_convert_fusion.refs_2_.b0, ...), custom_call_target="tpu_custom_call" | custom-call | flops 1207959552 | bytes 5000000 | tf_op jit(solution)/shard_map/rows_grad/pallas_call | solution.py:288
  106.8 2.4 %rows_partial.1.refs_4_ = f32[768,1536]{1,0:T(8,128)S(1)} custom-call(s32[16]{0:T(128)S(1)} %stack.59.at.refs_0_, bf16[512,384]{1,0:T(8,128)(2,1)S(1)} %collective-permute-done.13.b1.refs_1_, bf16[512,384]{1,0:T(8,128)(2,1)S(1)} %collective-permute-done.12.b3.refs_2_, bf16[512,1536]{1,0:T(8,128)(2,1)S(1)} %get-tuple-element.86.refs_3_), custom_call_target="tpu_custom_call" | custom-call | flops 1207959552 | bytes 8000000 | tf_op jit(solution)/shard_map/rows_partial/pallas_call | solution.py:238
  109.3 4.5 %collective-permute-done.16.b1.refs_1_ = bf16[512,384]{1,0:T(8,128)(2,1)S(1)} collective-permute-done((bf16[512,384]{1,0:T(8,128)(2,1)S(1)}, bf16[512,384]{1,0:T(8,128)(2,1)S(1)}, u32[]{:S(2)}, u32[]{:S(2)}) %collective-permute-start.16) | collective-permute-done | bytes 393248 | tf_op jit(solution)/shard_map/ppermute | solution.py:36
  113.8 3.7 %collective-permute-start.17 = (bf16[512,384]{1,0:T(8,128)(2,1)S(1)}, bf16[512,384]{1,0:T(8,128)(2,1)S(1)}, u32[]{:S(2)}, u32[]{:S(2)}) collective-permute-start(bf16[512,384]{1,0:T(8,128)(2,1)S(1)} %collective-permute-done.16.b1.refs_1_), channel_id=1, source_target_pairs={{0,3},{1,0},{2,1},{3,2},{4,5},{5,6},{6,7},{7,4},{8,11},{9,8},{10,9... | collective-permute-start | bytes 1179656 | tf_op jit(solution)/shard_map/ppermute | solution.py:36
  118.0 3.4 %rows_grad.4 = (bf16[768,1536]{1,0:T(8,128)(2,1)S(1)}, bf16[768,1536]{1,0:T(8,128)(2,1)S(1)}, f32[1,1536]{1,0:T(1,128)S(1)}) custom-call(s32[16]{0:T(128)S(1)} %stack.59.at.refs_0_, bf16[512,384]{1,0:T(8,128)(2,1)S(1)} %collective-permute-done.16.b1.refs_1_, ...), custom_call_target="tpu_custom_call", output_to_operand_aliasing={{0}: (5, {}), {1}: (6, {})} | custom-call | flops 1207959552 | bytes 10000000 | tf_op jit(solution)/shard_map/rows_grad/pallas_call | solution.py:288
  122.3 4.2 %backward.2.right0 = bf16[512,1536]{1,0:T(8,128)(2,1)S(1)} custom-call(s32[16]{0:T(128)S(1)} %stack.59.at.refs_0_, bf16[512,384]{1,0:T(8,128)(2,1)S(1)} %multiply_convert_fusion.1.b0.refs_1_, bf16[512,384]{1,0:T(8,128)(2,1)S(1)} %collective-permute-done.13.b1.refs_1_, bf16[512,384]{1,0:T(8,128)(2,1)S(1)} %collective-permute-done.14.b2.refs_1_, ...), custom_call_target="tpu_custom_call" | custom-call | flops 2415919104 | bytes 14000000 | tf_op jit(solution)/shard_map/backward/pallas_call | solution.py:189
  126.5 4.2 %backward.3.right1 = bf16[512,1536]{1,0:T(8,128)(2,1)S(1)} custom-call(s32[16]{0:T(128)S(1)} %stack.59.at.refs_0_, bf16[512,384]{1,0:T(8,128)(2,1)S(1)} %multiply_convert_fusion.refs_2_.b0, bf16[512,384]{1,0:T(8,128)(2,1)S(1)} %collective-permute-done.16.b1.refs_1_, bf16[512,384]{1,0:T(8,128)(2,1)S(1)} %collective-permute-done.17.b2.refs_2_, ...), custom_call_target="tpu_custom_call" | custom-call | flops 2415919104 | bytes 14000000 | tf_op jit(solution)/shard_map/backward/pallas_call | solution.py:189
  130.7 2.0 %rows_grad.5 = (bf16[768,1536]{1,0:T(8,128)(2,1)S(1)}, bf16[768,1536]{1,0:T(8,128)(2,1)S(1)}, f32[1,1536]{1,0:T(1,128)S(1)}) custom-call(s32[16]{0:T(128)S(1)} %stack.59.at.refs_0_, bf16[512,384]{1,0:T(8,128)(2,1)S(1)} %collective-permute-done.14.b2.refs_1_, ...), custom_call_target="tpu_custom_call", output_to_operand_aliasing={{0}: (5, {}), {1}: (6, {})} | custom-call | flops 1207959552 | bytes 5000000 | tf_op jit(solution)/shard_map/rows_grad/pallas_call | solution.py:288
  132.7 6.7 %weight_grad.1 = (bf16[768,1536]{1,0:T(8,128)(2,1)S(1)}, bf16[768,1536]{1,0:T(8,128)(2,1)S(1)}, f32[1,128]{1,0:T(1,128)S(1)}) custom-call(s32[16]{0:T(128)S(1)} %stack.59.at.refs_0_, bf16[768,1024]{1,0:T(8,128)(2,1)S(1)} %get-tuple-element.101.keep_l, bf16[768,1024]{1,0:T(8,128)(2,1)S(1)} %get-tuple-element.102.send_l, ...), custom_call_target="tpu_custom_call" | custom-call | flops 4831838208 | bytes 11000000 | tf_op jit(solution)/shard_map/weight_grad/pallas_call | solution.py:330
  139.9 3.5 %collective-permute-done.19 = f32[1,128]{1,0:T(1,128)S(1)} collective-permute-done((f32[1,128]{1,0:T(1,128)S(1)}, f32[1,128]{1,0:T(1,128)S(1)}, u32[]{:S(2)}, u32[]{:S(2)}) %collective-permute-start.19) | collective-permute-done | bytes 544 | tf_op jit(solution)/shard_map/ppermute | solution.py:62
  143.5 5.0 %collective-permute-done.20 = f32[1,128]{1,0:T(1,128)S(1)} collective-permute-done((f32[1,128]{1,0:T(1,128)S(1)}, f32[1,128]{1,0:T(1,128)S(1)}, u32[]{:S(2)}, u32[]{:S(2)}) %collective-permute-start.20) | collective-permute-done | bytes 544 | tf_op jit(solution)/shard_map/ppermute | solution.py:62
  148.6 1.1 collective-permute-done.21.u1
  149.7 1.9 spread.1
  152.3 2.6 %collective-permute-start.25 = (bf16[4,48,1536]{2,1,0:T(8,128)(2,1)S(1)}, bf16[4,48,1536]{2,1,0:T(8,128)(2,1)S(1)}, u32[]{:S(2)}, u32[]{:S(2)}) collective-permute-start(bf16[4,48,1536]{2,1,0:T(8,128)(2,1)S(1)} %get-tuple-element.126), channel_id=1, source_target_pairs={{0,96},{4,28},{8,104},{12,4},{16,112},{20,12},{24,120},{28,20},{32... | collective-permute-start | bytes 1769480 | tf_op jit(solution)/shard_map/ppermute | solution.py:46
  155.8 1.2 collective-permute-start.28
  157.0 1.4 own.1
  158.4 4.4 %collective-permute-done.24.up = bf16[4,48,1536]{2,1,0:T(8,128)(2,1)S(1)} collective-permute-done((bf16[4,48,1536]{2,1,0:T(8,128)(2,1)S(1)}, bf16[4,48,1536]{2,1,0:T(8,128)(2,1)S(1)}, u32[]{:S(2)}, u32[]{:S(2)}) %collective-permute-start.24) | collective-permute-done | bytes 589856 | tf_op jit(solution)/shard_map/ppermute | solution.py:46
  162.8 1.6 relay.1
  164.4 1.1 collective-permute-start.26
  165.5 2.3 %collective-permute-start.29 = (bf16[4,48,1536]{2,1,0:T(8,128)(2,1)S(1)}, bf16[4,48,1536]{2,1,0:T(8,128)(2,1)S(1)}, u32[]{:S(2)}, u32[]{:S(2)}) collective-permute-start(bf16[4,48,1536]{2,1,0:T(8,128)(2,1)S(1)} %get-tuple-element.133), channel_id=1, source_target_pairs={{0,96},{4,28},{8,104},{12,4},{16,112},{20,12},{24,120},{28,20},{32... | collective-permute-start | bytes 1769480 | tf_op jit(solution)/shard_map/ppermute | solution.py:46
  169.1 6.5 %collective-permute-done.26.up1 = bf16[4,48,1536]{2,1,0:T(8,128)(2,1)S(1)} collective-permute-done((bf16[4,48,1536]{2,1,0:T(8,128)(2,1)S(1)}, bf16[4,48,1536]{2,1,0:T(8,128)(2,1)S(1)}, u32[]{:S(2)}, u32[]{:S(2)}) %collective-permute-start.26) | collective-permute-done | bytes 589856 | tf_op jit(solution)/shard_map/ppermute | solution.py:46
  176.6 16.7 %all_to_all.10 = bf16[4,2,48,1536]{3,2,1,0:T(8,128)(2,1)S(1)} all-to-all(bf16[4,2,48,1536]{3,2,1,0:T(8,128)(2,1)S(1)} %close.1), channel_id=1, replica_groups={{0,8,16,24},{32,40,48,56},{64,72,80,88},{96,104,112,120},{4,36,68,100},..., dimensions={0} | all-to-all | bytes 2359296 | tf_op jit(solution)/shard_map/all_to_all | solution.py:571
  (93 shorter events, 18.3 us)
Async XLA Ops:
  0.6 39.5 %copy-start = (bf16[1536,3,384]{2,0,1:T(8,128)(2,1)S(1)}, bf16[1536,3,384]{2,0,1:T(8,128)(2,1)}, u32[]{:S(2)}) copy-start(bf16[1536,3,384]{2,0,1:T(8,128)(2,1)} %param.19) | copy-start | bytes 10616836
  0.6 21.7 %collective-permute-start.1 = (bf16[1024,384]{1,0:T(8,128)(2,1)}, bf16[1024,384]{1,0:T(8,128)(2,1)}, u32[]{:S(2)}, u32[]{:S(2)}) collective-permute-start(bf16[1024,384]{1,0:T(8,128)(2,1)} %x0.3), channel_id=1, source_target_pairs={{0,3},{1,0},{2,1},{3,2},{4,5},{5,6},{6,7},{7,4},{8,11},{9,8},{10,9... | collective-permute-start | bytes 2359304 | tf_op jit(solution)/shard_map/ppermute | solution.py:36
  3.6 18.8 %collective-permute-start = (bf16[1024,384]{1,0:T(8,128)(2,1)}, bf16[1024,384]{1,0:T(8,128)(2,1)}, u32[]{:S(2)}, u32[]{:S(2)}) collective-permute-start(bf16[1024,384]{1,0:T(8,128)(2,1)} %x0.3), channel_id=1, source_target_pairs={{0,1},{1,2},{2,3},{3,0},{4,7},{5,4},{6,5},{7,6},{8,9},{9,10},{10,1... | collective-permute-start | bytes 2359304 | tf_op jit(solution)/shard_map/ppermute | solution.py:36
  6.0 16.3 %all-to-all-start = ((f32[32,8,128]{2,1,0:T(8,128)}), f32[32,8,128]{2,1,0:T(8,128)}, u32[]{:S(2)}, u32[]{:S(2)}) async-start(f32[32,8,128]{2,1,0:T(8,128)} %broadcast_in_dim.31), calls=%async_computation | async-start | bytes 262144 | tf_op jit(solution)/shard_map/all_to_all | solution.py:464
  14.6 8.5 %copy-start.11 = (s32[32]{0:T(128)S(1)}, s32[32]{0:T(128)}, u32[]{:S(2)}) copy-start(s32[32]{0:T(128)} %param.17) | copy-start | bytes 388
  22.3 16.3 %collective-permute-start.4 = (bf16[1024,384]{1,0:T(8,128)(2,1)}, bf16[1024,384]{1,0:T(8,128)(2,1)S(1)}, u32[]{:S(2)}, u32[]{:S(2)}) collective-permute-start(bf16[1024,384]{1,0:T(8,128)(2,1)} %collective-permute-done.x3), channel_id=1, source_target_pairs={{0,1},{1,2},{2,3},{3,0},{4,7},{5,4},{6,5},{7,6},{8,9},{9,10},{10,1... | collective-permute-start | bytes 2359304 | tf_op jit(solution)/shard_map/ppermute | solution.py:36
  26.5 6.5 %collective-permute-start.2 = (f32[1,1536]{1,0:T(1,128)S(1)}, f32[1,1536]{1,0:T(1,128)S(1)}, u32[]{:S(2)}, u32[]{:S(2)}) collective-permute-start(f32[1,1536]{1,0:T(1,128)S(1)} %fusion.27), channel_id=1, source_target_pairs={{0,1},{1,0},{2,3},{3,2},{4,5},{5,4},{6,7},{7,6},{8,9},{9,8},{10,11... | collective-permute-start | bytes 18440 | tf_op jit(solution)/shard_map/ppermute | solution.py:62
  33.0 5.6 %collective-permute-start.3 = (f32[1,1536]{1,0:T(1,128)S(1)}, f32[1,1536]{1,0:T(1,128)S(1)}, u32[]{:S(2)}, u32[]{:S(2)}) collective-permute-start(f32[1,1536]{1,0:T(1,128)S(1)} %add.191), channel_id=1, source_target_pairs={{0,2},{1,3},{2,0},{3,1},{4,6},{5,7},{6,4},{7,5},{8,10},{9,11},{10,... | collective-permute-start | bytes 18440 | tf_op jit(solution)/shard_map/ppermute | solution.py:62
  38.6 0.9 copy-start.10
  40.7 3.7 %collective-permute-start.5 = (f32[3,384]{1,0:T(4,128)S(1)}, f32[3,384]{1,0:T(4,128)S(1)}, u32[]{:S(2)}, u32[]{:S(2)}) collective-permute-start(f32[3,384]{1,0:T(4,128)S(1)} %bitcast.74), channel_id=1, source_target_pairs={{0,1},{1,0},{2,3},{3,2},{4,5},{5,4},{6,7},{7,6},{8,9},{9,8},{10,11... | collective-permute-start | bytes 13832 | tf_op jit(solution)/shard_map/ppermute | solution.py:62
  44.5 5.7 %collective-permute-start.6 = (f32[6,384]{1,0:T(8,128)S(1)}, f32[6,384]{1,0:T(8,128)S(1)}, u32[]{:S(2)}, u32[]{:S(2)}) collective-permute-start(f32[6,384]{1,0:T(8,128)S(1)} %pad_maximum_fusion), channel_id=1, source_target_pairs={{0,2},{1,3},{2,0},{3,1},{4,6},{5,7},{6,4},{7,5},{8,10},{9,11},{10,... | collective-permute-start | bytes 27656 | tf_op jit(solution)/shard_map/ppermute | solution.py:62
  48.5 9.6 %copy-start.4 = (bf16[384,1536]{1,0:T(8,128)(2,1)S(1)}, bf16[384,1536]{1,0:T(8,128)(2,1)}, u32[]{:S(2)}) copy-start(bf16[384,1536]{1,0:T(8,128)(2,1)} %get-tuple-element.79) | copy-start | bytes 3538948
  58.1 1.3 copy-start.2
  59.3 5.2 %copy-start.5 = (bf16[384,1536]{1,0:T(8,128)(2,1)S(1)}, bf16[384,1536]{1,0:T(8,128)(2,1)}, u32[]{:S(2)}) copy-start(bf16[384,1536]{1,0:T(8,128)(2,1)} %get-tuple-element.75) | copy-start | bytes 3538948
  60.3 13.0 %collective-permute-start.8 = (bf16[512,384]{1,0:T(8,128)(2,1)S(1)}, bf16[512,384]{1,0:T(8,128)(2,1)S(1)}, u32[]{:S(2)}, u32[]{:S(2)}) collective-permute-start(bf16[512,384]{1,0:T(8,128)(2,1)S(1)} %convolution_convert_fusion.3), channel_id=1, source_target_pairs={{0,3},{1,0},{2,1},{3,2},{4,5},{5,6},{6,7},{7,4},{8,11},{9,8},{10,9... | collective-permute-start | bytes 1179656 | tf_op jit(solution)/shard_map/ppermute | solution.py:36
  64.5 9.0 %collective-permute-start.7 = (bf16[512,384]{1,0:T(8,128)(2,1)S(1)}, bf16[512,384]{1,0:T(8,128)(2,1)S(1)}, u32[]{:S(2)}, u32[]{:S(2)}) collective-permute-start(bf16[512,384]{1,0:T(8,128)(2,1)S(1)} %convolution_convert_fusion.2), channel_id=1, source_target_pairs={{0,1},{1,2},{2,3},{3,0},{4,7},{5,4},{6,5},{7,6},{8,9},{9,10},{10,1... | collective-permute-start | bytes 1179656 | tf_op jit(solution)/shard_map/ppermute | solution.py:36
  74.5 4.4 %copy-start.3 = (bf16[384,1536]{1,0:T(8,128)(2,1)S(1)}, bf16[384,1536]{1,0:T(8,128)(2,1)}, u32[]{:S(2)}) copy-start(bf16[384,1536]{1,0:T(8,128)(2,1)} %get-tuple-element.87) | copy-start | bytes 3538948
  74.6 12.1 %collective-permute-start.9 = (bf16[512,384]{1,0:T(8,128)(2,1)S(1)}, bf16[512,384]{1,0:T(8,128)(2,1)S(1)}, u32[]{:S(2)}, u32[]{:S(2)}) collective-permute-start(bf16[512,384]{1,0:T(8,128)(2,1)S(1)} %add_convert_fusion.3), channel_id=1, source_target_pairs={{0,1},{1,2},{2,3},{3,0},{4,7},{5,4},{6,5},{7,6},{8,9},{9,10},{10,1... | collective-permute-start | bytes 1179656 | tf_op jit(solution)/shard_map/ppermute | solution.py:36
  75.6 11.0 %copy-start.6 = (bf16[1024,384]{1,0:T(8,128)(2,1)S(1)}, bf16[1024,384]{1,0:T(8,128)(2,1)}, u32[]{:S(2)}) copy-start(bf16[1024,384]{1,0:T(8,128)(2,1)} %x0.3) | copy-start | bytes 2359300
  75.7 11.0 %copy-start.7 = (bf16[1024,384]{1,0:T(8,128)(2,1)S(1)}, bf16[1024,384]{1,0:T(8,128)(2,1)}, u32[]{:S(2)}) copy-start(bf16[1024,384]{1,0:T(8,128)(2,1)} %param.13) | copy-start | bytes 2359300
  75.7 16.4 %collective-permute-start.10 = (bf16[512,384]{1,0:T(8,128)(2,1)S(1)}, bf16[512,384]{1,0:T(8,128)(2,1)S(1)}, u32[]{:S(2)}, u32[]{:S(2)}) collective-permute-start(bf16[512,384]{1,0:T(8,128)(2,1)S(1)} %convolution_convert_fusion.1), channel_id=1, source_target_pairs={{0,3},{1,0},{2,1},{3,2},{4,5},{5,6},{6,7},{7,4},{8,11},{9,8},{10,9... | collective-permute-start | bytes 1179656 | tf_op jit(solution)/shard_map/ppermute | solution.py:36
  78.9 21.9 %collective-permute-start.15 = (bf16[512,384]{1,0:T(8,128)(2,1)S(1)}, bf16[512,384]{1,0:T(8,128)(2,1)S(1)}, u32[]{:S(2)}, u32[]{:S(2)}) collective-permute-start(bf16[512,384]{1,0:T(8,128)(2,1)S(1)} %convolution_convert_fusion), channel_id=1, source_target_pairs={{0,1},{1,2},{2,3},{3,0},{4,7},{5,4},{6,5},{7,6},{8,9},{9,10},{10,1... | collective-permute-start | bytes 1179656 | tf_op jit(solution)/shard_map/ppermute | solution.py:36
  87.0 13.9 %collective-permute-start.13 = (bf16[512,384]{1,0:T(8,128)(2,1)S(1)}, bf16[512,384]{1,0:T(8,128)(2,1)S(1)}, u32[]{:S(2)}, u32[]{:S(2)}) collective-permute-start(bf16[512,384]{1,0:T(8,128)(2,1)S(1)} %multiply_convert_fusion.1.b0.refs_1_), channel_id=1, source_target_pairs={{0,3},{1,0},{2,1},{3,2},{4,5},{5,6},{6,7},{7,4},{8,11},{9,8},{10,9... | collective-permute-start | bytes 1179656 | tf_op jit(solution)/shard_map/ppermute | solution.py:36
  90.1 10.8 %collective-permute-start.12 = (bf16[512,384]{1,0:T(8,128)(2,1)S(1)}, bf16[512,384]{1,0:T(8,128)(2,1)S(1)}, u32[]{:S(2)}, u32[]{:S(2)}) collective-permute-start(bf16[512,384]{1,0:T(8,128)(2,1)S(1)} %multiply_convert_fusion.1.b0.refs_1_), channel_id=1, source_target_pairs={{0,1},{1,2},{2,3},{3,0},{4,7},{5,4},{6,5},{7,6},{8,9},{9,10},{10,1... | collective-permute-start | bytes 1179656 | tf_op jit(solution)/shard_map/ppermute | solution.py:36
  92.1 8.7 %collective-permute-start.11 = (bf16[512,384]{1,0:T(8,128)(2,1)S(1)}, bf16[512,384]{1,0:T(8,128)(2,1)S(1)}, u32[]{:S(2)}, u32[]{:S(2)}) collective-permute-start(bf16[512,384]{1,0:T(8,128)(2,1)S(1)} %add_convert_fusion.2), channel_id=1, source_target_pairs={{0,3},{1,0},{2,1},{3,2},{4,5},{5,6},{6,7},{7,4},{8,11},{9,8},{10,9... | collective-permute-start | bytes 1179656 | tf_op jit(solution)/shard_map/ppermute | solution.py:36
  101.2 12.5 %collective-permute-start.16 = (bf16[512,384]{1,0:T(8,128)(2,1)S(1)}, bf16[512,384]{1,0:T(8,128)(2,1)S(1)}, u32[]{:S(2)}, u32[]{:S(2)}) collective-permute-start(bf16[512,384]{1,0:T(8,128)(2,1)S(1)} %multiply_convert_fusion.refs_2_.b0), channel_id=1, source_target_pairs={{0,3},{1,0},{2,1},{3,2},{4,5},{5,6},{6,7},{7,4},{8,11},{9,8},{10,9... | collective-permute-start | bytes 1179656 | tf_op jit(solution)/shard_map/ppermute | solution.py:36
  104.9 13.1 %collective-permute-start.18 = (bf16[512,384]{1,0:T(8,128)(2,1)S(1)}, bf16[512,384]{1,0:T(8,128)(2,1)S(1)}, u32[]{:S(2)}, u32[]{:S(2)}) collective-permute-start(bf16[512,384]{1,0:T(8,128)(2,1)S(1)} %multiply_convert_fusion.refs_2_.b0), channel_id=1, source_target_pairs={{0,1},{1,2},{2,3},{3,0},{4,7},{5,4},{6,5},{7,6},{8,9},{9,10},{10,1... | collective-permute-start | bytes 1179656 | tf_op jit(solution)/shard_map/ppermute | solution.py:36
  104.9 17.4 %collective-permute-start.14 = (bf16[512,384]{1,0:T(8,128)(2,1)S(1)}, bf16[512,384]{1,0:T(8,128)(2,1)S(1)}, u32[]{:S(2)}, u32[]{:S(2)}) collective-permute-start(bf16[512,384]{1,0:T(8,128)(2,1)S(1)} %collective-permute-done.12.b3.refs_2_), channel_id=1, source_target_pairs={{0,1},{1,2},{2,3},{3,0},{4,7},{5,4},{6,5},{7,6},{8,9},{9,10},{10,1... | collective-permute-start | bytes 1179656 | tf_op jit(solution)/shard_map/ppermute | solution.py:36
  106.8 15.4 %slice-start = ((s8[4718592]{0:T(1024)(128)(4,1)}), s8[4194304]{0:T(1024)(128)(4,1)S(1)}, s32[]{:S(2)}) async-start(s8[4718592]{0:T(1024)(128)(4,1)} %bitcast.72), calls=%async_computation.2 | async-start | bytes 8388608
  113.8 12.7 %collective-permute-start.17 = (bf16[512,384]{1,0:T(8,128)(2,1)S(1)}, bf16[512,384]{1,0:T(8,128)(2,1)S(1)}, u32[]{:S(2)}, u32[]{:S(2)}) collective-permute-start(bf16[512,384]{1,0:T(8,128)(2,1)S(1)} %collective-permute-done.16.b1.refs_1_), channel_id=1, source_target_pairs={{0,3},{1,0},{2,1},{3,2},{4,5},{5,6},{6,7},{7,4},{8,11},{9,8},{10,9... | collective-permute-start | bytes 1179656 | tf_op jit(solution)/shard_map/ppermute | solution.py:36
  118.0 4.3 %slice-start.1 = ((s8[4718592]{0:T(1024)(128)(4,1)}), s8[524288]{0:T(1024)(128)(4,1)S(1)}, s32[]{:S(2)}) async-start(s8[4718592]{0:T(1024)(128)(4,1)} %bitcast.72), calls=%async_computation.3 | async-start | bytes 1048576
  139.3 10.4 %collective-permute-start.22 = (bf16[768,1536]{1,0:T(8,128)(2,1)S(1)}, bf16[768,1536]{1,0:T(8,128)(2,1)S(1)}, u32[]{:S(2)}, u32[]{:S(2)}) collective-permute-start(bf16[768,1536]{1,0:T(8,128)(2,1)S(1)} %get-tuple-element.123), channel_id=1, source_target_pairs={{0,4},{4,0},{8,12},{12,8},{16,20},{20,16},{24,28},{28,24},{32,36},... | collective-permute-start | bytes 7077896 | tf_op jit(solution)/shard_map/ppermute | solution.py:46
  139.4 10.3 %collective-permute-start.23 = (bf16[768,1536]{1,0:T(8,128)(2,1)S(1)}, bf16[768,1536]{1,0:T(8,128)(2,1)S(1)}, u32[]{:S(2)}, u32[]{:S(2)}) collective-permute-start(bf16[768,1536]{1,0:T(8,128)(2,1)S(1)} %get-tuple-element.124), channel_id=1, source_target_pairs={{0,4},{4,0},{8,12},{12,8},{16,20},{20,16},{24,28},{28,24},{32,36},... | collective-permute-start | bytes 7077896 | tf_op jit(solution)/shard_map/ppermute | solution.py:46
  139.9 3.5 %collective-permute-start.19 = (f32[1,128]{1,0:T(1,128)S(1)}, f32[1,128]{1,0:T(1,128)S(1)}, u32[]{:S(2)}, u32[]{:S(2)}) collective-permute-start(f32[1,128]{1,0:T(1,128)S(1)} %get-tuple-element.120), channel_id=1, source_target_pairs={{0,1},{1,0},{2,3},{3,2},{4,5},{5,4},{6,7},{7,6},{8,9},{9,8},{10,11... | collective-permute-start | bytes 1544 | tf_op jit(solution)/shard_map/ppermute | solution.py:62
  143.5 5.0 %collective-permute-start.20 = (f32[1,128]{1,0:T(1,128)S(1)}, f32[1,128]{1,0:T(1,128)S(1)}, u32[]{:S(2)}, u32[]{:S(2)}) collective-permute-start(f32[1,128]{1,0:T(1,128)S(1)} %add.215), channel_id=1, source_target_pairs={{0,2},{1,3},{2,0},{3,1},{4,6},{5,7},{6,4},{7,5},{8,10},{9,11},{10,... | collective-permute-start | bytes 1544 | tf_op jit(solution)/shard_map/ppermute | solution.py:62
  148.5 1.2 collective-permute-start.21
  151.6 11.2 %collective-permute-start.24 = (bf16[4,48,1536]{2,1,0:T(8,128)(2,1)S(1)}, bf16[4,48,1536]{2,1,0:T(8,128)(2,1)S(1)}, u32[]{:S(2)}, u32[]{:S(2)}) collective-permute-start(bf16[4,48,1536]{2,1,0:T(8,128)(2,1)S(1)} %get-tuple-element.125), channel_id=1, source_target_pairs={{0,32},{4,12},{8,40},{12,20},{16,48},{20,28},{24,56},{28,4},{32,64... | collective-permute-start | bytes 1769480 | tf_op jit(solution)/shard_map/ppermute | solution.py:46
  152.3 10.5 %collective-permute-start.25 = (bf16[4,48,1536]{2,1,0:T(8,128)(2,1)S(1)}, bf16[4,48,1536]{2,1,0:T(8,128)(2,1)S(1)}, u32[]{:S(2)}, u32[]{:S(2)}) collective-permute-start(bf16[4,48,1536]{2,1,0:T(8,128)(2,1)S(1)} %get-tuple-element.126), channel_id=1, source_target_pairs={{0,96},{4,28},{8,104},{12,4},{16,112},{20,12},{24,120},{28,20},{32... | collective-permute-start | bytes 1769480 | tf_op jit(solution)/shard_map/ppermute | solution.py:46
  155.0 13.7 %collective-permute-start.27 = (bf16[4,48,1536]{2,1,0:T(8,128)(2,1)S(1)}, bf16[4,48,1536]{2,1,0:T(8,128)(2,1)S(1)}, u32[]{:S(2)}, u32[]{:S(2)}) collective-permute-start(bf16[4,48,1536]{2,1,0:T(8,128)(2,1)S(1)} %get-tuple-element.131), channel_id=1, source_target_pairs={{0,96},{4,28},{8,104},{12,4},{16,112},{20,12},{24,120},{28,20},{32... | collective-permute-start | bytes 1769480 | tf_op jit(solution)/shard_map/ppermute | solution.py:46
  155.8 13.3 %collective-permute-start.28 = (bf16[4,48,1536]{2,1,0:T(8,128)(2,1)S(1)}, bf16[4,48,1536]{2,1,0:T(8,128)(2,1)S(1)}, u32[]{:S(2)}, u32[]{:S(2)}) collective-permute-start(bf16[4,48,1536]{2,1,0:T(8,128)(2,1)S(1)} %get-tuple-element.132), channel_id=1, source_target_pairs={{0,32},{4,12},{8,40},{12,20},{16,48},{20,28},{24,56},{28,4},{32,64... | collective-permute-start | bytes 1769480 | tf_op jit(solution)/shard_map/ppermute | solution.py:46
  164.4 11.2 %collective-permute-start.26 = (bf16[4,48,1536]{2,1,0:T(8,128)(2,1)S(1)}, bf16[4,48,1536]{2,1,0:T(8,128)(2,1)S(1)}, u32[]{:S(2)}, u32[]{:S(2)}) collective-permute-start(bf16[4,48,1536]{2,1,0:T(8,128)(2,1)S(1)} %get-tuple-element.130), channel_id=1, source_target_pairs={{0,32},{4,12},{8,40},{12,20},{16,48},{20,28},{24,56},{28,4},{32,64... | collective-permute-start | bytes 1769480 | tf_op jit(solution)/shard_map/ppermute | solution.py:46
  165.5 10.1 %collective-permute-start.29 = (bf16[4,48,1536]{2,1,0:T(8,128)(2,1)S(1)}, bf16[4,48,1536]{2,1,0:T(8,128)(2,1)S(1)}, u32[]{:S(2)}, u32[]{:S(2)}) collective-permute-start(bf16[4,48,1536]{2,1,0:T(8,128)(2,1)S(1)} %get-tuple-element.133), channel_id=1, source_target_pairs={{0,96},{4,28},{8,104},{12,4},{16,112},{20,12},{24,120},{28,20},{32... | collective-permute-start | bytes 1769480 | tf_op jit(solution)/shard_map/ppermute | solution.py:46
  176.6 17.0 %copy-start.8 = (f32[48,1536]{1,0:T(8,128)S(1)}, f32[48,1536]{1,0:T(8,128)}, u32[]{:S(2)}) copy-start(f32[48,1536]{1,0:T(8,128)} %param.23) | copy-start | bytes 884740
  176.6 17.0 %copy-start.9 = (f32[48,1536]{1,0:T(8,128)S(1)}, f32[48,1536]{1,0:T(8,128)}, u32[]{:S(2)}) copy-start(f32[48,1536]{1,0:T(8,128)} %param.22) | copy-start | bytes 884740
  176.6 17.8 %copy-start.1 = (bf16[1536,3,384]{2,0,1:T(8,128)(2,1)S(1)}, bf16[1536,3,384]{2,0,1:T(8,128)(2,1)}, u32[]{:S(2)}) copy-start(bf16[1536,3,384]{2,0,1:T(8,128)(2,1)} %param.19) | copy-start | bytes 10616836

commit v6 on v5

--- a/solution.py
+++ b/solution.py
@@ -58,7 +58,7 @@
 
 
 def swap_x(value, kind):
-    other = [x ^ 1 for x in range(RING)] if kind == 0 else [x ^ 2 for x in range(RING)]
+    other = [x ^ 1 for x in range(RING)] if kind == 0 else [3 - x for x in range(RING)]
     return lax.ppermute(value, "mp", list(enumerate(other)))
 
 
@@ -276,20 +276,19 @@
             send[at_rows, cols] = jnp.where(mine == 0, high, low)
 
 
-def rows_grad(at, places, groups, rights, partials, before):
+def rows_grad(at, place, groups, rights, partials, before):
     ff = rights[0].shape[1]
     rows = sum(right.shape[0] for right in rights)
-    count, parts = len(places), len(groups)
-    first = places[0]
-    step = places[1] - first if count > 1 else 0
-    out = pl.BlockSpec((PART // 2, ff), lambda s, a: (a[8 + first + s * step], 0))
+    count, parts = 1, len(groups)
+    out = pl.BlockSpec((PART // 2, ff), lambda s, a: (a[8 + place], 0))
+    offset = place // 2
     blocks = [block for group in groups for block in group]
     operands = [*blocks, *rights, *partials, *before]
     return call(
         lambda *refs: rows_kernel(count, parts, len(partials), *refs),
         count,
         [whole(value.shape) for value in (*blocks, *rights)]
-        + [pl.BlockSpec((PART, ff), lambda s, *_: (s, 0))] * len(partials)
+        + [pl.BlockSpec((PART, ff), lambda s, *_: (offset, 0))] * len(partials)
         + [pl.BlockSpec(memory_space=pl.ANY)] * len(before),
         [out, out, whole((1, ff))],
         [shaped((D // 2, ff))] * 2 + [shaped((1, ff), F32)],
@@ -300,7 +299,7 @@
     )(at, *operands)
 
 
-def weight_kernel(at, keep_l, send_l, right0, right1, q0, q1, q2, keep, send, square, sums):
+def weight_kernel(at, keep_l, send_l, right0, right1, q0, q1, q2, q3, keep, send, square, sums):
     rows = right0.shape[0]
     keep_v = dot(keep_l[:, :rows], right0[...]) + dot(keep_l[:, rows:], right1[...])
     send_v = dot(send_l[:, :rows], right0[...]) + dot(send_l[:, rows:], right1[...])
@@ -319,7 +318,7 @@
 
     @pl.when(step == pl.num_programs(0) - 1)
     def _():
-        rest = q0[...] + q1[...] + q2[...]
+        rest = q0[...] + q1[...] + q2[...] + q3[...]
         total = jnp.sum(sums[...], 1, keepdims=True) + jnp.sum(rest, 1, keepdims=True)
         square[...] = jnp.broadcast_to(total, square.shape)
 
@@ -330,7 +329,7 @@
     return call(
         weight_kernel,
         ff // width,
-        [whole((D // 2, 2 * rows))] * 2 + [columns(rows, width)] * 2 + [whole((1, ff))] * 3,
+        [whole((D // 2, 2 * rows))] * 2 + [columns(rows, width)] * 2 + [whole((1, ff))] * 4,
         [columns(D // 2, width)] * 2 + [whole((1, 128))],
         [shaped((D // 2, ff))] * 2 + [shaped((1, 128), F32)],
         [pltpu.VMEM((1, width), F32)],
@@ -445,7 +444,7 @@
     way = 1 - 2 * me_c
 
     ahead = [(me_x + k * way) % RING for k in range(RING)]
-    swapped = [me_x, me_x ^ 1, me_x ^ 2, me_x ^ 3]
+    swapped = [me_x, me_x ^ 1, 3 - me_x, (3 - me_x) ^ 1]
     me_one = jnp.where(me_c == 0, me_y, me_z)
     stride = jnp.where(me_c == 0, 4, 1)
     at = jnp.stack(
@@ -540,22 +539,23 @@
     )
     back1 = leave(1, own1, up1, down1)
     far0 = by_x(behind0, 1)
-    behind1, ahead1 = by_x(back1, 1), by_x(back1, -1)
+    ahead1 = by_x(back1, -1)
+    back1_late, far0 = lax.optimization_barrier((back1, far0))
+    behind1 = by_x(back1_late, 1)
     rights = (hidden0, hidden1)
-    *second, square_a = rows_grad(at, (0,), ((back0,), (back1,)), rights, (), ())
+    *second, square_a = rows_grad(at, 0, ((back0,), (back1,)), rights, (), ())
     partial = rows_partial(at, (ahead0, behind0), hidden0)
     ahead1, partial, square_a = lax.optimization_barrier((ahead1, partial, square_a))
     far1 = by_x(ahead1, -1)
     grad0 = backward(at, (back0, ahead0, far0, behind0), out_w, slope0)
-    *second, square_b = rows_grad(
-        at, (1, 3), ((ahead1, behind1),), (hidden1,), (partial,), tuple(second)
-    )
+    *second, square_b = rows_grad(at, 1, ((ahead1,),), (hidden1,), (partial,), tuple(second))
+    *second, square_d = rows_grad(at, 3, ((behind1,),), (hidden1,), (partial,), tuple(second))
     grad1 = backward(at, (back1, ahead1, far1, behind1), out_w, slope1)
-    *second, square_c = rows_grad(at, (2,), ((far0,), (far1,)), rights, (), tuple(second))
+    *second, square_c = rows_grad(at, 2, ((far0,), (far1,)), rights, (), tuple(second))
     keep2, send2 = second
     got2 = by_core(send2)
     keep1, send1, square = weight_grad(
-        at, mod_keep, mod_send, (grad0, grad1), (square_a, square_b, square_c)
+        at, mod_keep, mod_send, (grad0, grad1), (square_a, square_b, square_c, square_d)
     )
     got1 = by_core(send1)
     square = square + swap_x(square, 0)

time: 195 us -> 193 us (0.990)
  starting transfers between devices: 54.4 us -> 48.8 us
  waiting for transfers between devices: 46.8 us -> 50.7 us
    ppermute x15, starting transfers between devices: 24.9 us -> 19.3 us  [by_x(): return lax.ppermute(value, ('dp', 'mp'), pairs)]
    ppermute x15, waiting for transfers between devices: 12.8 us -> 17.4 us  [by_x(): return lax.ppermute(value, ('dp', 'mp'), pairs)]
    pallas_call x3 -> x4, Pallas kernels: 7.28 us -> 6.7 us  [rows_grad(): call(lambda *refs: rows_kernel(count, parts, len(partials), *refs), count...]
  transfers between devices with their start and end apart: 31 -> 31, of which waited for: 17 -> 18; matrix products, arithmetic and copies ran while one was open for 9% -> 10% of each run, Pallas kernels for 13% -> 12%
where the time goes in v6:
time: 193 us
  waiting for transfers between devices  50.7 us (26%)
  starting transfers between devices  48.8 us (25%)
  Pallas kernels  48 us (25%)
  blocking collectives  16.9 us (9%)
  matrix products  12 us (6%)
  other arithmetic  6.82 us (4%)
  local copies, waits for them, and re-layouts  6.09 us (3%)
  between operations  3.24 us (2%)
    ppermute x15, starting transfers between devices, by_x(): return lax.ppermute(value, ('dp', 'mp'), pairs)  19.3 us
    ppermute x15, waiting for transfers between devices, by_x(): return lax.ppermute(value, ('dp', 'mp'), pairs)  17.4 us
    all_to_all x1, blocking collectives, local(): lax.all_to_all(value, 'dp', 0, 0, axis_index_groups=groups, tiled=True)  16.9 us
    ppermute x6, waiting for transfers between devices, swap_x(): return lax.ppermute(value, 'mp', list(enumerate(other)))  16.6 us
    pallas_call x2, Pallas kernels, forward(): call(forward_kernel, ff // WIDE, [piece] * 4 + [whole((3, PART)), whole((...  15.8 us
    ppermute x9, waiting for transfers between devices, by_dp(): return lax.ppermute(value, 'dp', pairs)  13.8 us
    ppermute x6, starting transfers between devices, swap_x(): return lax.ppermute(value, 'mp', list(enumerate(other)))  11.6 us
    ppermute x9, starting transfers between devices, by_dp(): return lax.ppermute(value, 'dp', pairs)  9.36 us
  transfers between devices with their start and end apart: 31, of which 18 were waited for; matrix products, arithmetic and copies ran while one was open for 10% of the time, Pallas kernels for 12%

profile of v6, /device:TPU:0, one launch (start us, length us, event | category | flops | bytes accessed | tf_op | source)
XLA Modules:
  0.0 192.6 jit_solution(16235049329445990346)
XLA Ops:
  0.6 1.6 collective-permute-start
  2.3 1.7 collective-permute-start.1
  6.4 8.5 %all-to-all-start = ((f32[32,8,128]{2,1,0:T(8,128)}), f32[32,8,128]{2,1,0:T(8,128)}, u32[]{:S(2)}, u32[]{:S(2)}) async-start(f32[32,8,128]{2,1,0:T(8,128)} %broadcast_in_dim.31), calls=%async_computation | async-start | bytes 262144 | tf_op jit(solution)/shard_map/all_to_all | solution.py:463
  15.1 4.6 %constant_dynamic-slice_fusion = (bf16[384,1536]{1,0:T(8,128)(2,1)}, bf16[384,1536]{1,0:T(8,128)(2,1)}, bf16[384,1536]{1,0:T(8,128)(2,1)}, bf16[384,1536]{1,0:T(8,128)(2,1)}) fusion(bf16[1536,1536]{1,0:T(8,128)(2,1)} %out_w.3, s32[]{:T(128)S(6)} %select_n.112, s32[]{:T(128)S(6)} %select_n.111, s32[]{:T(128)S(6)} %select_n.110, s32[]{:T(128)S(6)} %select_n.109), kind=kLoop, calls=%fused_computation.51 | loop fusion | bytes 9437200 | tf_op jit(solution)/shard_map/dynamic_slice | solution.py:456
  19.8 3.0 %all-to-all-done = f32[32,8,128]{2,1,0:T(8,128)} async-done(((f32[32,8,128]{2,1,0:T(8,128)}), f32[32,8,128]{2,1,0:T(8,128)}, u32[]{:S(2)}, u32[]{:S(2)}) %all-to-all-start) | async-done | bytes 131104 | tf_op jit(solution)/shard_map/all_to_all | solution.py:463
  24.1 2.4 %fusion.27 = f32[1,1536]{1,0:T(1,128)S(1)} fusion(bf16[1024,1]{0,1:T(2,128)(2,1)S(1)} %reshape.95, bf16[1024,1536]{1,0:T(8,128)(2,1)} %param.18), kind=kOutput, calls=%fused_computation.60 | convolution fusion | flops 3145728 | bytes 3153920 | tf_op jit(solution)/shard_map/dot_general | solution.py:24
  26.5 1.5 collective-permute-start.2
  28.7 4.3 %collective-permute-done.2 = f32[1,1536]{1,0:T(1,128)S(1)} collective-permute-done((f32[1,1536]{1,0:T(1,128)S(1)}, f32[1,1536]{1,0:T(1,128)S(1)}, u32[]{:S(2)}, u32[]{:S(2)}) %collective-permute-start.2) | collective-permute-done | bytes 6176 | tf_op jit(solution)/shard_map/ppermute | solution.py:62
  33.0 3.9 %collective-permute-start.3 = (f32[1,1536]{1,0:T(1,128)S(1)}, f32[1,1536]{1,0:T(1,128)S(1)}, u32[]{:S(2)}, u32[]{:S(2)}) collective-permute-start(f32[1,1536]{1,0:T(1,128)S(1)} %add.191), channel_id=1, source_target_pairs={{0,3},{1,2},{2,1},{3,0},{4,7},{5,6},{6,5},{7,4},{8,11},{9,10},{10,... | collective-permute-start | bytes 18440 | tf_op jit(solution)/shard_map/ppermute | solution.py:62
  36.9 1.6 collective-permute-done.3
  41.4 2.9 %collective-permute-done.5.m1 = f32[3,384]{1,0:T(4,128)S(1)} collective-permute-done((f32[3,384]{1,0:T(4,128)S(1)}, f32[3,384]{1,0:T(4,128)S(1)}, u32[]{:S(2)}, u32[]{:S(2)}) %collective-permute-start.5) | collective-permute-done | bytes 4640 | tf_op jit(solution)/shard_map/ppermute | solution.py:62
  44.3 3.3 %collective-permute-start.6 = (f32[6,384]{1,0:T(8,128)S(1)}, f32[6,384]{1,0:T(8,128)S(1)}, u32[]{:S(2)}, u32[]{:S(2)}) collective-permute-start(f32[6,384]{1,0:T(8,128)S(1)} %pad_maximum_fusion), channel_id=1, source_target_pairs={{0,3},{1,2},{2,1},{3,0},{4,7},{5,6},{6,5},{7,4},{8,11},{9,10},{10,... | collective-permute-start | bytes 27656 | tf_op jit(solution)/shard_map/ppermute | solution.py:62
  47.7 1.6 collective-permute-done.6.m2
  49.3 7.9 %forward.2 = (bf16[512,1536]{1,0:T(8,128)(2,1)S(1)}, bf16[512,1536]{1,0:T(8,128)(2,1)S(1)}, f32[512,1536]{1,0:T(8,128)S(1)}) custom-call(s32[16]{0:T(128)S(1)} %stack.59.at.refs_0_, bf16[1024,384]{1,0:T(8,128)(2,1)} %x0.3, bf16[1024,384]{1,0:T(8,128)(2,1)} %collective-permute-done.1.x1, bf16[1024,384]{1,0:T(8,128)(2,1)} %copy-done.10, ...), custom_call_target="tpu_custom_call" | custom-call | flops 2415919104 | bytes 12000000 | tf_op jit(solution)/shard_map/forward/pallas_call | solution.py:137
  59.6 3.5 %collective-permute-start.8 = (bf16[512,384]{1,0:T(8,128)(2,1)S(1)}, bf16[512,384]{1,0:T(8,128)(2,1)S(1)}, u32[]{:S(2)}, u32[]{:S(2)}) collective-permute-start(bf16[512,384]{1,0:T(8,128)(2,1)S(1)} %convolution_convert_fusion.3), channel_id=1, source_target_pairs={{0,3},{1,0},{2,1},{3,2},{4,5},{5,6},{6,7},{7,4},{8,11},{9,8},{10,9... | collective-permute-start | bytes 1179656 | tf_op jit(solution)/shard_map/ppermute | solution.py:36
  64.0 7.9 %forward.3 = (bf16[512,1536]{1,0:T(8,128)(2,1)S(1)}, bf16[512,1536]{1,0:T(8,128)(2,1)S(1)}, f32[512,1536]{1,0:T(8,128)S(1)}) custom-call(s32[16]{0:T(128)S(1)} %stack.59.at.refs_0_, bf16[1024,384]{1,0:T(8,128)(2,1)} %x0.3, bf16[1024,384]{1,0:T(8,128)(2,1)} %collective-permute-done.1.x1, bf16[1024,384]{1,0:T(8,128)(2,1)} %copy-done.10, ...), custom_call_target="tpu_custom_call" | custom-call | flops 2415919104 | bytes 12000000 | tf_op jit(solution)/shard_map/forward/pallas_call | solution.py:137
  75.3 3.1 %collective-permute-start.10 = (bf16[512,384]{1,0:T(8,128)(2,1)S(1)}, bf16[512,384]{1,0:T(8,128)(2,1)S(1)}, u32[]{:S(2)}, u32[]{:S(2)}) collective-permute-start(bf16[512,384]{1,0:T(8,128)(2,1)S(1)} %convolution_convert_fusion.1), channel_id=1, source_target_pairs={{0,3},{1,0},{2,1},{3,2},{4,5},{5,6},{6,7},{7,4},{8,11},{9,8},{10,9... | collective-permute-start | bytes 1179656 | tf_op jit(solution)/shard_map/ppermute | solution.py:36
  78.4 7.9 %collective-permute-done.9 = bf16[512,384]{1,0:T(8,128)(2,1)S(1)} collective-permute-done((bf16[512,384]{1,0:T(8,128)(2,1)S(1)}, bf16[512,384]{1,0:T(8,128)(2,1)S(1)}, u32[]{:S(2)}, u32[]{:S(2)}) %collective-permute-start.9) | collective-permute-done | bytes 393248 | tf_op jit(solution)/shard_map/ppermute | solution.py:36
  86.8 3.2 %collective-permute-start.13 = (bf16[512,384]{1,0:T(8,128)(2,1)S(1)}, bf16[512,384]{1,0:T(8,128)(2,1)S(1)}, u32[]{:S(2)}, u32[]{:S(2)}) collective-permute-start(bf16[512,384]{1,0:T(8,128)(2,1)S(1)} %multiply_convert_fusion.1.b0.refs_1_), channel_id=1, source_target_pairs={{0,3},{1,0},{2,1},{3,2},{4,5},{5,6},{6,7},{7,4},{8,11},{9,8},{10,9... | collective-permute-start | bytes 1179656 | tf_op jit(solution)/shard_map/ppermute | solution.py:36
  92.2 3.2 %add_convert_fusion = (bf16[512,1536]{1,0:T(8,128)(2,1)S(1)}, bf16[512,1536]{1,0:T(8,128)(2,1)S(1)}) fusion(f32[512,1536]{1,0:T(8,128)S(1)} %get-tuple-element.99, f32[512,1536]{1,0:T(8,128)S(1)} %get-tuple-element.98), kind=kLoop, calls=%fused_computation | loop fusion | flops 23592960 | bytes 9437184 | tf_op jit(solution)/shard_map/convert_element_type | solution.py:535
  95.4 2.2 %turn.1 = (bf16[768,1024]{1,0:T(8,128)(2,1)S(1)}, bf16[768,1024]{1,0:T(8,128)(2,1)S(1)}) custom-call(s32[16]{0:T(128)S(1)} %stack.59.at.refs_0_, bf16[512,1536]{1,0:T(8,128)(2,1)S(1)} %get-tuple-element.101.top, bf16[512,1536]{1,0:T(8,128)(2,1)S(1)} %get-tuple-element.102.low), custom_call_target="tpu_custom_call" | custom-call | flops 1572864 | bytes 6291456 | tf_op jit(solution)/shard_map/turn/pallas_call | solution.py:166
  97.6 2.3 %collective-permute-done.11 = bf16[512,384]{1,0:T(8,128)(2,1)S(1)} collective-permute-done((bf16[512,384]{1,0:T(8,128)(2,1)S(1)}, bf16[512,384]{1,0:T(8,128)(2,1)S(1)}, u32[]{:S(2)}, u32[]{:S(2)}) %collective-permute-start.11) | collective-permute-done | bytes 393248 | tf_op jit(solution)/shard_map/ppermute | solution.py:36
  101.5 3.5 %collective-permute-start.16 = (bf16[512,384]{1,0:T(8,128)(2,1)S(1)}, bf16[512,384]{1,0:T(8,128)(2,1)S(1)}, u32[]{:S(2)}, u32[]{:S(2)}) collective-permute-start(bf16[512,384]{1,0:T(8,128)(2,1)S(1)} %multiply_convert_fusion.refs_2_.b0), channel_id=1, source_target_pairs={{0,3},{1,0},{2,1},{3,2},{4,5},{5,6},{6,7},{7,4},{8,11},{9,8},{10,9... | collective-permute-start | bytes 1179656 | tf_op jit(solution)/shard_map/ppermute | solution.py:36
  105.0 2.0 %rows_grad.4 = (bf16[768,1536]{1,0:T(8,128)(2,1)S(1)}, bf16[768,1536]{1,0:T(8,128)(2,1)S(1)}, f32[1,1536]{1,0:T(1,128)S(1)}) custom-call(s32[16]{0:T(128)S(1)} %stack.59.at.refs_0_, bf16[512,384]{1,0:T(8,128)(2,1)S(1)} %multiply_convert_fusion.1.b0.refs_1_, bf16[512,384]{1,0:T(8,128)(2,1)S(1)} %multiply_convert_fusion.refs_2_.b0, ...), custom_call_target="tpu_custom_call" | custom-call | flops 1207959552 | bytes 5000000 | tf_op jit(solution)/shard_map/rows_grad/pallas_call | solution.py:287
  107.0 2.4 %rows_partial.1.refs_3_ = f32[768,1536]{1,0:T(8,128)S(1)} custom-call(s32[16]{0:T(128)S(1)} %stack.59.at.refs_0_, bf16[512,384]{1,0:T(8,128)(2,1)S(1)} %collective-permute-done.13.b1.refs_1_, bf16[512,384]{1,0:T(8,128)(2,1)S(1)} %collective-permute-done.12.b3.refs_2_, bf16[512,1536]{1,0:T(8,128)(2,1)S(1)} %get-tuple-element.91.refs_3_), custom_call_target="tpu_custom_call" | custom-call | flops 1207959552 | bytes 8000000 | tf_op jit(solution)/shard_map/rows_partial/pallas_call | solution.py:238
  109.4 2.6 %collective-permute-done.15.b2.refs_1_ = bf16[512,384]{1,0:T(8,128)(2,1)S(1)} collective-permute-done((bf16[512,384]{1,0:T(8,128)(2,1)S(1)}, bf16[512,384]{1,0:T(8,128)(2,1)S(1)}, u32[]{:S(2)}, u32[]{:S(2)}) %collective-permute-start.15) | collective-permute-done | bytes 393248 | tf_op jit(solution)/shard_map/ppermute | solution.py:36
  112.0 1.9 %collective-permute-start.17 = (bf16[512,384]{1,0:T(8,128)(2,1)S(1)}, bf16[512,384]{1,0:T(8,128)(2,1)S(1)}, u32[]{:S(2)}, u32[]{:S(2)}) collective-permute-start(bf16[512,384]{1,0:T(8,128)(2,1)S(1)} %collective-permute-done.16.b1.refs_1_), channel_id=1, source_target_pairs={{0,3},{1,0},{2,1},{3,2},{4,5},{5,6},{6,7},{7,4},{8,11},{9,8},{10,9... | collective-permute-start | bytes 1179656 | tf_op jit(solution)/shard_map/ppermute | solution.py:36
  114.1 1.4 rows_grad.5
  115.5 4.2 %backward.2.right0 = bf16[512,1536]{1,0:T(8,128)(2,1)S(1)} custom-call(s32[16]{0:T(128)S(1)} %stack.59.at.refs_0_, bf16[512,384]{1,0:T(8,128)(2,1)S(1)} %multiply_convert_fusion.1.b0.refs_1_, bf16[512,384]{1,0:T(8,128)(2,1)S(1)} %collective-permute-done.13.b1.refs_1_, bf16[512,384]{1,0:T(8,128)(2,1)S(1)} %collective-permute-done.15.b2.refs_1_, ...), custom_call_target="tpu_custom_call" | custom-call | flops 2415919104 | bytes 14000000 | tf_op jit(solution)/shard_map/backward/pallas_call | solution.py:189
  119.7 3.2 %collective-permute-done.17.b2.refs_2_ = bf16[512,384]{1,0:T(8,128)(2,1)S(1)} collective-permute-done((bf16[512,384]{1,0:T(8,128)(2,1)S(1)}, bf16[512,384]{1,0:T(8,128)(2,1)S(1)}, u32[]{:S(2)}, u32[]{:S(2)}) %collective-permute-start.17) | collective-permute-done | bytes 393248 | tf_op jit(solution)/shard_map/ppermute | solution.py:36
  123.0 4.2 %backward.3.right1 = bf16[512,1536]{1,0:T(8,128)(2,1)S(1)} custom-call(s32[16]{0:T(128)S(1)} %stack.59.at.refs_0_, bf16[512,384]{1,0:T(8,128)(2,1)S(1)} %multiply_convert_fusion.refs_2_.b0, bf16[512,384]{1,0:T(8,128)(2,1)S(1)} %collective-permute-done.16.b1.refs_1_, bf16[512,384]{1,0:T(8,128)(2,1)S(1)} %collective-permute-done.17.b2.refs_2_, ...), custom_call_target="tpu_custom_call" | custom-call | flops 2415919104 | bytes 14000000 | tf_op jit(solution)/shard_map/backward/pallas_call | solution.py:189
  127.2 1.4 rows_grad.6
  128.6 2.0 %rows_grad.7 = (bf16[768,1536]{1,0:T(8,128)(2,1)S(1)}, bf16[768,1536]{1,0:T(8,128)(2,1)S(1)}, f32[1,1536]{1,0:T(1,128)S(1)}) custom-call(s32[16]{0:T(128)S(1)} %stack.59.at.refs_0_, bf16[512,384]{1,0:T(8,128)(2,1)S(1)} %collective-permute-done.15.b2.refs_1_, ...), custom_call_target="tpu_custom_call", output_to_operand_aliasing={{0}: (5, {}), {1}: (6, {})} | custom-call | flops 1207959552 | bytes 5000000 | tf_op jit(solution)/shard_map/rows_grad/pallas_call | solution.py:287
  130.5 6.7 %weight_grad.1 = (bf16[768,1536]{1,0:T(8,128)(2,1)S(1)}, bf16[768,1536]{1,0:T(8,128)(2,1)S(1)}, f32[1,128]{1,0:T(1,128)S(1)}) custom-call(s32[16]{0:T(128)S(1)} %stack.59.at.refs_0_, bf16[768,1024]{1,0:T(8,128)(2,1)S(1)} %get-tuple-element.106.keep_l, bf16[768,1024]{1,0:T(8,128)(2,1)S(1)} %get-tuple-element.107.send_l, ...), custom_call_target="tpu_custom_call" | custom-call | flops 4831838208 | bytes 11000000 | tf_op jit(solution)/shard_map/weight_grad/pallas_call | solution.py:329
  138.0 3.3 %collective-permute-done.19 = f32[1,128]{1,0:T(1,128)S(1)} collective-permute-done((f32[1,128]{1,0:T(1,128)S(1)}, f32[1,128]{1,0:T(1,128)S(1)}, u32[]{:S(2)}, u32[]{:S(2)}) %collective-permute-start.19) | collective-permute-done | bytes 544 | tf_op jit(solution)/shard_map/ppermute | solution.py:62
  141.3 2.0 %collective-permute-start.20 = (f32[1,128]{1,0:T(1,128)S(1)}, f32[1,128]{1,0:T(1,128)S(1)}, u32[]{:S(2)}, u32[]{:S(2)}) collective-permute-start(f32[1,128]{1,0:T(1,128)S(1)} %add.215), channel_id=1, source_target_pairs={{0,3},{1,2},{2,1},{3,0},{4,7},{5,6},{6,5},{7,4},{8,11},{9,10},{10,... | collective-permute-start | bytes 1544 | tf_op jit(solution)/shard_map/ppermute | solution.py:62
  143.3 2.8 %collective-permute-done.20 = f32[1,128]{1,0:T(1,128)S(1)} collective-permute-done((f32[1,128]{1,0:T(1,128)S(1)}, f32[1,128]{1,0:T(1,128)S(1)}, u32[]{:S(2)}, u32[]{:S(2)}) %collective-permute-start.20) | collective-permute-done | bytes 544 | tf_op jit(solution)/shard_map/ppermute | solution.py:62
  147.3 1.9 spread.1
  150.5 2.0 %collective-permute-start.25 = (bf16[4,48,1536]{2,1,0:T(8,128)(2,1)S(1)}, bf16[4,48,1536]{2,1,0:T(8,128)(2,1)S(1)}, u32[]{:S(2)}, u32[]{:S(2)}) collective-permute-start(bf16[4,48,1536]{2,1,0:T(8,128)(2,1)S(1)} %get-tuple-element.136), channel_id=1, source_target_pairs={{0,96},{4,28},{8,104},{12,4},{16,112},{20,12},{24,120},{28,20},{32... | collective-permute-start | bytes 1769480 | tf_op jit(solution)/shard_map/ppermute | solution.py:46
  152.5 1.5 collective-permute-start.27
  154.6 1.4 own.1
  156.0 4.4 %collective-permute-done.24.up = bf16[4,48,1536]{2,1,0:T(8,128)(2,1)S(1)} collective-permute-done((bf16[4,48,1536]{2,1,0:T(8,128)(2,1)S(1)}, bf16[4,48,1536]{2,1,0:T(8,128)(2,1)S(1)}, u32[]{:S(2)}, u32[]{:S(2)}) %collective-permute-start.24) | collective-permute-done | bytes 589856 | tf_op jit(solution)/shard_map/ppermute | solution.py:46
  160.4 1.6 relay.1
  162.1 1.7 collective-permute-start.26
  163.7 1.7 collective-permute-start.29
  165.4 1.3 collective-permute-done.27.down1
  166.8 6.5 %collective-permute-done.26.up1 = bf16[4,48,1536]{2,1,0:T(8,128)(2,1)S(1)} collective-permute-done((bf16[4,48,1536]{2,1,0:T(8,128)(2,1)S(1)}, bf16[4,48,1536]{2,1,0:T(8,128)(2,1)S(1)}, u32[]{:S(2)}, u32[]{:S(2)}) %collective-permute-start.26) | collective-permute-done | bytes 589856 | tf_op jit(solution)/shard_map/ppermute | solution.py:46
  174.6 16.9 %all_to_all.10 = bf16[4,2,48,1536]{3,2,1,0:T(8,128)(2,1)S(1)} all-to-all(bf16[4,2,48,1536]{3,2,1,0:T(8,128)(2,1)S(1)} %close.1), channel_id=1, replica_groups={{0,8,16,24},{32,40,48,56},{64,72,80,88},{96,104,112,120},{4,36,68,100},..., dimensions={0} | all-to-all | bytes 2359296 | tf_op jit(solution)/shard_map/all_to_all | solution.py:571
  (94 shorter events, 22.6 us)
Async XLA Ops:
  0.6 39.4 %copy-start = (bf16[1536,3,384]{2,0,1:T(8,128)(2,1)S(1)}, bf16[1536,3,384]{2,0,1:T(8,128)(2,1)}, u32[]{:S(2)}) copy-start(bf16[1536,3,384]{2,0,1:T(8,128)(2,1)} %param.19) | copy-start | bytes 10616836
  0.6 22.1 %collective-permute-start = (bf16[1024,384]{1,0:T(8,128)(2,1)}, bf16[1024,384]{1,0:T(8,128)(2,1)}, u32[]{:S(2)}, u32[]{:S(2)}) collective-permute-start(bf16[1024,384]{1,0:T(8,128)(2,1)} %x0.3), channel_id=1, source_target_pairs={{0,1},{1,2},{2,3},{3,0},{4,7},{5,4},{6,5},{7,6},{8,9},{9,10},{10,1... | collective-permute-start | bytes 2359304 | tf_op jit(solution)/shard_map/ppermute | solution.py:36
  2.3 20.5 %collective-permute-start.1 = (bf16[1024,384]{1,0:T(8,128)(2,1)}, bf16[1024,384]{1,0:T(8,128)(2,1)}, u32[]{:S(2)}, u32[]{:S(2)}) collective-permute-start(bf16[1024,384]{1,0:T(8,128)(2,1)} %x0.3), channel_id=1, source_target_pairs={{0,3},{1,0},{2,1},{3,2},{4,5},{5,6},{6,7},{7,4},{8,11},{9,8},{10,9... | collective-permute-start | bytes 2359304 | tf_op jit(solution)/shard_map/ppermute | solution.py:36
  6.4 16.4 %all-to-all-start = ((f32[32,8,128]{2,1,0:T(8,128)}), f32[32,8,128]{2,1,0:T(8,128)}, u32[]{:S(2)}, u32[]{:S(2)}) async-start(f32[32,8,128]{2,1,0:T(8,128)} %broadcast_in_dim.31), calls=%async_computation | async-start | bytes 262144 | tf_op jit(solution)/shard_map/all_to_all | solution.py:463
  15.0 8.0 %copy-start.11 = (s32[32]{0:T(128)S(1)}, s32[32]{0:T(128)}, u32[]{:S(2)}) copy-start(s32[32]{0:T(128)} %param.17) | copy-start | bytes 388
  22.8 15.7 %collective-permute-start.4 = (bf16[1024,384]{1,0:T(8,128)(2,1)}, bf16[1024,384]{1,0:T(8,128)(2,1)S(1)}, u32[]{:S(2)}, u32[]{:S(2)}) collective-permute-start(bf16[1024,384]{1,0:T(8,128)(2,1)} %collective-permute-done.x3), channel_id=1, source_target_pairs={{0,1},{1,2},{2,3},{3,0},{4,7},{5,4},{6,5},{7,6},{8,9},{9,10},{10,1... | collective-permute-start | bytes 2359304 | tf_op jit(solution)/shard_map/ppermute | solution.py:36
  26.5 6.5 %collective-permute-start.2 = (f32[1,1536]{1,0:T(1,128)S(1)}, f32[1,1536]{1,0:T(1,128)S(1)}, u32[]{:S(2)}, u32[]{:S(2)}) collective-permute-start(f32[1,1536]{1,0:T(1,128)S(1)} %fusion.27), channel_id=1, source_target_pairs={{0,1},{1,0},{2,3},{3,2},{4,5},{5,4},{6,7},{7,6},{8,9},{9,8},{10,11... | collective-permute-start | bytes 18440 | tf_op jit(solution)/shard_map/ppermute | solution.py:62
  33.0 5.5 %collective-permute-start.3 = (f32[1,1536]{1,0:T(1,128)S(1)}, f32[1,1536]{1,0:T(1,128)S(1)}, u32[]{:S(2)}, u32[]{:S(2)}) collective-permute-start(f32[1,1536]{1,0:T(1,128)S(1)} %add.191), channel_id=1, source_target_pairs={{0,3},{1,2},{2,1},{3,0},{4,7},{5,6},{6,5},{7,4},{8,11},{9,10},{10,... | collective-permute-start | bytes 18440 | tf_op jit(solution)/shard_map/ppermute | solution.py:62
  38.5 0.9 copy-start.10
  40.6 3.7 %collective-permute-start.5 = (f32[3,384]{1,0:T(4,128)S(1)}, f32[3,384]{1,0:T(4,128)S(1)}, u32[]{:S(2)}, u32[]{:S(2)}) collective-permute-start(f32[3,384]{1,0:T(4,128)S(1)} %bitcast.74), channel_id=1, source_target_pairs={{0,1},{1,0},{2,3},{3,2},{4,5},{5,4},{6,7},{7,6},{8,9},{9,8},{10,11... | collective-permute-start | bytes 13832 | tf_op jit(solution)/shard_map/ppermute | solution.py:62
  44.3 5.0 %collective-permute-start.6 = (f32[6,384]{1,0:T(8,128)S(1)}, f32[6,384]{1,0:T(8,128)S(1)}, u32[]{:S(2)}, u32[]{:S(2)}) collective-permute-start(f32[6,384]{1,0:T(8,128)S(1)} %pad_maximum_fusion), channel_id=1, source_target_pairs={{0,3},{1,2},{2,1},{3,0},{4,7},{5,6},{6,5},{7,4},{8,11},{9,10},{10,... | collective-permute-start | bytes 27656 | tf_op jit(solution)/shard_map/ppermute | solution.py:62
  47.6 9.6 %copy-start.3 = (bf16[384,1536]{1,0:T(8,128)(2,1)S(1)}, bf16[384,1536]{1,0:T(8,128)(2,1)}, u32[]{:S(2)}) copy-start(bf16[384,1536]{1,0:T(8,128)(2,1)} %get-tuple-element.81) | copy-start | bytes 3538948
  57.2 1.3 copy-start.5
  58.5 4.6 %copy-start.4 = (bf16[384,1536]{1,0:T(8,128)(2,1)S(1)}, bf16[384,1536]{1,0:T(8,128)(2,1)}, u32[]{:S(2)}) copy-start(bf16[384,1536]{1,0:T(8,128)(2,1)} %get-tuple-element.80) | copy-start | bytes 3538948
  59.5 12.4 %collective-permute-start.7 = (bf16[512,384]{1,0:T(8,128)(2,1)S(1)}, bf16[512,384]{1,0:T(8,128)(2,1)S(1)}, u32[]{:S(2)}, u32[]{:S(2)}) collective-permute-start(bf16[512,384]{1,0:T(8,128)(2,1)S(1)} %convolution_convert_fusion.2), channel_id=1, source_target_pairs={{0,1},{1,2},{2,3},{3,0},{4,7},{5,4},{6,5},{7,6},{8,9},{9,10},{10,1... | collective-permute-start | bytes 1179656 | tf_op jit(solution)/shard_map/ppermute | solution.py:36
  59.6 12.4 %collective-permute-start.8 = (bf16[512,384]{1,0:T(8,128)(2,1)S(1)}, bf16[512,384]{1,0:T(8,128)(2,1)S(1)}, u32[]{:S(2)}, u32[]{:S(2)}) collective-permute-start(bf16[512,384]{1,0:T(8,128)(2,1)S(1)} %convolution_convert_fusion.3), channel_id=1, source_target_pairs={{0,3},{1,0},{2,1},{3,2},{4,5},{5,6},{6,7},{7,4},{8,11},{9,8},{10,9... | collective-permute-start | bytes 1179656 | tf_op jit(solution)/shard_map/ppermute | solution.py:36
  73.0 1.3 copy-start.2
  73.0 13.3 %collective-permute-start.9 = (bf16[512,384]{1,0:T(8,128)(2,1)S(1)}, bf16[512,384]{1,0:T(8,128)(2,1)S(1)}, u32[]{:S(2)}, u32[]{:S(2)}) collective-permute-start(bf16[512,384]{1,0:T(8,128)(2,1)S(1)} %add_convert_fusion.3), channel_id=1, source_target_pairs={{0,1},{1,2},{2,3},{3,0},{4,7},{5,4},{6,5},{7,6},{8,9},{9,10},{10,1... | collective-permute-start | bytes 1179656 | tf_op jit(solution)/shard_map/ppermute | solution.py:36
  74.3 12.1 %copy-start.6 = (bf16[1024,384]{1,0:T(8,128)(2,1)S(1)}, bf16[1024,384]{1,0:T(8,128)(2,1)}, u32[]{:S(2)}) copy-start(bf16[1024,384]{1,0:T(8,128)(2,1)} %x0.3) | copy-start | bytes 2359300
  74.3 12.1 %copy-start.7 = (bf16[1024,384]{1,0:T(8,128)(2,1)S(1)}, bf16[1024,384]{1,0:T(8,128)(2,1)}, u32[]{:S(2)}) copy-start(bf16[1024,384]{1,0:T(8,128)(2,1)} %param.13) | copy-start | bytes 2359300
  75.3 16.7 %collective-permute-start.10 = (bf16[512,384]{1,0:T(8,128)(2,1)S(1)}, bf16[512,384]{1,0:T(8,128)(2,1)S(1)}, u32[]{:S(2)}, u32[]{:S(2)}) collective-permute-start(bf16[512,384]{1,0:T(8,128)(2,1)S(1)} %convolution_convert_fusion.1), channel_id=1, source_target_pairs={{0,3},{1,0},{2,1},{3,2},{4,5},{5,6},{6,7},{7,4},{8,11},{9,8},{10,9... | collective-permute-start | bytes 1179656 | tf_op jit(solution)/shard_map/ppermute | solution.py:36
  78.4 22.7 %collective-permute-start.14 = (bf16[512,384]{1,0:T(8,128)(2,1)S(1)}, bf16[512,384]{1,0:T(8,128)(2,1)S(1)}, u32[]{:S(2)}, u32[]{:S(2)}) collective-permute-start(bf16[512,384]{1,0:T(8,128)(2,1)S(1)} %convolution_convert_fusion), channel_id=1, source_target_pairs={{0,1},{1,2},{2,3},{3,0},{4,7},{5,4},{6,5},{7,6},{8,9},{9,10},{10,1... | collective-permute-start | bytes 1179656 | tf_op jit(solution)/shard_map/ppermute | solution.py:36
  86.7 14.4 %collective-permute-start.12 = (bf16[512,384]{1,0:T(8,128)(2,1)S(1)}, bf16[512,384]{1,0:T(8,128)(2,1)S(1)}, u32[]{:S(2)}, u32[]{:S(2)}) collective-permute-start(bf16[512,384]{1,0:T(8,128)(2,1)S(1)} %multiply_convert_fusion.1.b0.refs_1_), channel_id=1, source_target_pairs={{0,1},{1,2},{2,3},{3,0},{4,7},{5,4},{6,5},{7,6},{8,9},{9,10},{10,1... | collective-permute-start | bytes 1179656 | tf_op jit(solution)/shard_map/ppermute | solution.py:36
  86.8 14.3 %collective-permute-start.13 = (bf16[512,384]{1,0:T(8,128)(2,1)S(1)}, bf16[512,384]{1,0:T(8,128)(2,1)S(1)}, u32[]{:S(2)}, u32[]{:S(2)}) collective-permute-start(bf16[512,384]{1,0:T(8,128)(2,1)S(1)} %multiply_convert_fusion.1.b0.refs_1_), channel_id=1, source_target_pairs={{0,3},{1,0},{2,1},{3,2},{4,5},{5,6},{6,7},{7,4},{8,11},{9,8},{10,9... | collective-permute-start | bytes 1179656 | tf_op jit(solution)/shard_map/ppermute | solution.py:36
  92.1 7.8 %collective-permute-start.11 = (bf16[512,384]{1,0:T(8,128)(2,1)S(1)}, bf16[512,384]{1,0:T(8,128)(2,1)S(1)}, u32[]{:S(2)}, u32[]{:S(2)}) collective-permute-start(bf16[512,384]{1,0:T(8,128)(2,1)S(1)} %add_convert_fusion.2), channel_id=1, source_target_pairs={{0,3},{1,0},{2,1},{3,2},{4,5},{5,6},{6,7},{7,4},{8,11},{9,8},{10,9... | collective-permute-start | bytes 1179656 | tf_op jit(solution)/shard_map/ppermute | solution.py:36
  101.1 10.9 %collective-permute-start.15 = (bf16[512,384]{1,0:T(8,128)(2,1)S(1)}, bf16[512,384]{1,0:T(8,128)(2,1)S(1)}, u32[]{:S(2)}, u32[]{:S(2)}) collective-permute-start(bf16[512,384]{1,0:T(8,128)(2,1)S(1)} %collective-permute-done.12.b3.refs_2_), channel_id=1, source_target_pairs={{0,1},{1,2},{2,3},{3,0},{4,7},{5,4},{6,5},{7,6},{8,9},{9,10},{10,1... | collective-permute-start | bytes 1179656 | tf_op jit(solution)/shard_map/ppermute | solution.py:36
  101.5 10.6 %collective-permute-start.16 = (bf16[512,384]{1,0:T(8,128)(2,1)S(1)}, bf16[512,384]{1,0:T(8,128)(2,1)S(1)}, u32[]{:S(2)}, u32[]{:S(2)}) collective-permute-start(bf16[512,384]{1,0:T(8,128)(2,1)S(1)} %multiply_convert_fusion.refs_2_.b0), channel_id=1, source_target_pairs={{0,3},{1,0},{2,1},{3,2},{4,5},{5,6},{6,7},{7,4},{8,11},{9,8},{10,9... | collective-permute-start | bytes 1179656 | tf_op jit(solution)/shard_map/ppermute | solution.py:36
  107.0 8.5 %slice-start = ((s8[4718592]{0:T(1024)(128)(4,1)}), s8[4194304]{0:T(1024)(128)(4,1)S(1)}, s32[]{:S(2)}) async-start(s8[4718592]{0:T(1024)(128)(4,1)} %bitcast.72), calls=%async_computation.2 | async-start | bytes 8388608
  112.0 10.8 %collective-permute-start.17 = (bf16[512,384]{1,0:T(8,128)(2,1)S(1)}, bf16[512,384]{1,0:T(8,128)(2,1)S(1)}, u32[]{:S(2)}, u32[]{:S(2)}) collective-permute-start(bf16[512,384]{1,0:T(8,128)(2,1)S(1)} %collective-permute-done.16.b1.refs_1_), channel_id=1, source_target_pairs={{0,3},{1,0},{2,1},{3,2},{4,5},{5,6},{6,7},{7,4},{8,11},{9,8},{10,9... | collective-permute-start | bytes 1179656 | tf_op jit(solution)/shard_map/ppermute | solution.py:36
  114.0 9.0 %collective-permute-start.18 = (bf16[512,384]{1,0:T(8,128)(2,1)S(1)}, bf16[512,384]{1,0:T(8,128)(2,1)S(1)}, u32[]{:S(2)}, u32[]{:S(2)}) collective-permute-start(bf16[512,384]{1,0:T(8,128)(2,1)S(1)} %multiply_convert_fusion.refs_2_.b0), channel_id=1, source_target_pairs={{0,1},{1,2},{2,3},{3,0},{4,7},{5,4},{6,5},{7,6},{8,9},{9,10},{10,1... | collective-permute-start | bytes 1179656 | tf_op jit(solution)/shard_map/ppermute | solution.py:36
  114.1 1.4 slice-start.1
  137.2 10.1 %collective-permute-start.22 = (bf16[768,1536]{1,0:T(8,128)(2,1)S(1)}, bf16[768,1536]{1,0:T(8,128)(2,1)S(1)}, u32[]{:S(2)}, u32[]{:S(2)}) collective-permute-start(bf16[768,1536]{1,0:T(8,128)(2,1)S(1)} %get-tuple-element.133), channel_id=1, source_target_pairs={{0,4},{4,0},{8,12},{12,8},{16,20},{20,16},{24,28},{28,24},{32,36},... | collective-permute-start | bytes 7077896 | tf_op jit(solution)/shard_map/ppermute | solution.py:46
  137.3 10.0 %collective-permute-start.23 = (bf16[768,1536]{1,0:T(8,128)(2,1)S(1)}, bf16[768,1536]{1,0:T(8,128)(2,1)S(1)}, u32[]{:S(2)}, u32[]{:S(2)}) collective-permute-start(bf16[768,1536]{1,0:T(8,128)(2,1)S(1)} %get-tuple-element.134), channel_id=1, source_target_pairs={{0,4},{4,0},{8,12},{12,8},{16,20},{20,16},{24,28},{28,24},{32,36},... | collective-permute-start | bytes 7077896 | tf_op jit(solution)/shard_map/ppermute | solution.py:46
  137.8 3.5 %collective-permute-start.19 = (f32[1,128]{1,0:T(1,128)S(1)}, f32[1,128]{1,0:T(1,128)S(1)}, u32[]{:S(2)}, u32[]{:S(2)}) collective-permute-start(f32[1,128]{1,0:T(1,128)S(1)} %get-tuple-element.130), channel_id=1, source_target_pairs={{0,1},{1,0},{2,3},{3,2},{4,5},{5,4},{6,7},{7,6},{8,9},{9,8},{10,11... | collective-permute-start | bytes 1544 | tf_op jit(solution)/shard_map/ppermute | solution.py:62
  141.3 4.8 %collective-permute-start.20 = (f32[1,128]{1,0:T(1,128)S(1)}, f32[1,128]{1,0:T(1,128)S(1)}, u32[]{:S(2)}, u32[]{:S(2)}) collective-permute-start(f32[1,128]{1,0:T(1,128)S(1)} %add.215), channel_id=1, source_target_pairs={{0,3},{1,2},{2,1},{3,0},{4,7},{5,6},{6,5},{7,4},{8,11},{9,10},{10,... | collective-permute-start | bytes 1544 | tf_op jit(solution)/shard_map/ppermute | solution.py:62
  146.1 1.2 collective-permute-start.21
  149.2 11.2 %collective-permute-start.24 = (bf16[4,48,1536]{2,1,0:T(8,128)(2,1)S(1)}, bf16[4,48,1536]{2,1,0:T(8,128)(2,1)S(1)}, u32[]{:S(2)}, u32[]{:S(2)}) collective-permute-start(bf16[4,48,1536]{2,1,0:T(8,128)(2,1)S(1)} %get-tuple-element.135), channel_id=1, source_target_pairs={{0,32},{4,12},{8,40},{12,20},{16,48},{20,28},{24,56},{28,4},{32,64... | collective-permute-start | bytes 1769480 | tf_op jit(solution)/shard_map/ppermute | solution.py:46
  150.5 9.9 %collective-permute-start.25 = (bf16[4,48,1536]{2,1,0:T(8,128)(2,1)S(1)}, bf16[4,48,1536]{2,1,0:T(8,128)(2,1)S(1)}, u32[]{:S(2)}, u32[]{:S(2)}) collective-permute-start(bf16[4,48,1536]{2,1,0:T(8,128)(2,1)S(1)} %get-tuple-element.136), channel_id=1, source_target_pairs={{0,96},{4,28},{8,104},{12,4},{16,112},{20,12},{24,120},{28,20},{32... | collective-permute-start | bytes 1769480 | tf_op jit(solution)/shard_map/ppermute | solution.py:46
  152.5 14.2 %collective-permute-start.27 = (bf16[4,48,1536]{2,1,0:T(8,128)(2,1)S(1)}, bf16[4,48,1536]{2,1,0:T(8,128)(2,1)S(1)}, u32[]{:S(2)}, u32[]{:S(2)}) collective-permute-start(bf16[4,48,1536]{2,1,0:T(8,128)(2,1)S(1)} %get-tuple-element.141), channel_id=1, source_target_pairs={{0,96},{4,28},{8,104},{12,4},{16,112},{20,12},{24,120},{28,20},{32... | collective-permute-start | bytes 1769480 | tf_op jit(solution)/shard_map/ppermute | solution.py:46
  154.0 12.7 %collective-permute-start.28 = (bf16[4,48,1536]{2,1,0:T(8,128)(2,1)S(1)}, bf16[4,48,1536]{2,1,0:T(8,128)(2,1)S(1)}, u32[]{:S(2)}, u32[]{:S(2)}) collective-permute-start(bf16[4,48,1536]{2,1,0:T(8,128)(2,1)S(1)} %get-tuple-element.142), channel_id=1, source_target_pairs={{0,32},{4,12},{8,40},{12,20},{16,48},{20,28},{24,56},{28,4},{32,64... | collective-permute-start | bytes 1769480 | tf_op jit(solution)/shard_map/ppermute | solution.py:46
  162.1 11.2 %collective-permute-start.26 = (bf16[4,48,1536]{2,1,0:T(8,128)(2,1)S(1)}, bf16[4,48,1536]{2,1,0:T(8,128)(2,1)S(1)}, u32[]{:S(2)}, u32[]{:S(2)}) collective-permute-start(bf16[4,48,1536]{2,1,0:T(8,128)(2,1)S(1)} %get-tuple-element.140), channel_id=1, source_target_pairs={{0,32},{4,12},{8,40},{12,20},{16,48},{20,28},{24,56},{28,4},{32,64... | collective-permute-start | bytes 1769480 | tf_op jit(solution)/shard_map/ppermute | solution.py:46
  163.7 9.9 %collective-permute-start.29 = (bf16[4,48,1536]{2,1,0:T(8,128)(2,1)S(1)}, bf16[4,48,1536]{2,1,0:T(8,128)(2,1)S(1)}, u32[]{:S(2)}, u32[]{:S(2)}) collective-permute-start(bf16[4,48,1536]{2,1,0:T(8,128)(2,1)S(1)} %get-tuple-element.143), channel_id=1, source_target_pairs={{0,96},{4,28},{8,104},{12,4},{16,112},{20,12},{24,120},{28,20},{32... | collective-permute-start | bytes 1769480 | tf_op jit(solution)/shard_map/ppermute | solution.py:46
  174.6 17.2 %copy-start.8 = (f32[48,1536]{1,0:T(8,128)S(1)}, f32[48,1536]{1,0:T(8,128)}, u32[]{:S(2)}) copy-start(f32[48,1536]{1,0:T(8,128)} %param.23) | copy-start | bytes 884740
  174.6 17.2 %copy-start.9 = (f32[48,1536]{1,0:T(8,128)S(1)}, f32[48,1536]{1,0:T(8,128)}, u32[]{:S(2)}) copy-start(f32[48,1536]{1,0:T(8,128)} %param.22) | copy-start | bytes 884740
  174.6 18.0 %copy-start.1 = (bf16[1536,3,384]{2,0,1:T(8,128)(2,1)S(1)}, bf16[1536,3,384]{2,0,1:T(8,128)(2,1)}, u32[]{:S(2)}) copy-start(bf16[1536,3,384]{2,0,1:T(8,128)(2,1)} %param.19) | copy-start | bytes 10616836

commit v7 on v6

--- a/solution.py
+++ b/solution.py
@@ -104,24 +104,47 @@
     )
 
 
-def forward_kernel(at, x0, x1, x2, x3, m0, m1, m2, in_w, modded_o, hidden, pre, mods, modded):
+def statistics_kernel(at, x0, x1, x2, x3, center_o, scale_o):
+    total = 0.0
+    squares = 0.0
+    for ref in (x0, x1, x2, x3):
+        value = ref[...].astype(F32)
+        total = total + jnp.sum(value, 1, keepdims=True)
+        squares = squares + jnp.sum(value * value, 1, keepdims=True)
+    center = total / D
+    scale = lax.rsqrt(squares / D - center * center + 1e-06)
+    center_o[...] = jnp.broadcast_to(center, center_o.shape)
+    scale_o[...] = jnp.broadcast_to(scale, scale_o.shape)
+
+
+def statistics(chunk, at, blocks):
+    rows = blocks[0].shape[0] // 2
+    steps = 2
+    out = pl.BlockSpec((rows // steps, 128), lambda s, *_: (s, 0))
+    return call(
+        statistics_kernel,
+        steps,
+        [pl.BlockSpec((rows // steps, PART), lambda s, *_: (chunk * steps + s, 0))] * 4,
+        [out] * 2,
+        [shaped((rows, 128), F32)] * 2,
+        [],
+        cost(4 * rows * D, 3 * rows * D),
+        "statistics",
+    )(at, *[in_hbm(b) for b in blocks])
+
+
+def forward_kernel(
+    at, x0, x1, x2, x3, center, scale, m0, m1, m2, in_w, modded_o, hidden, pre, mods, modded
+):
     step = pl.program_id(0)
 
     @pl.when(step == 0)
     def _():
         for place, ref, row in ((0, m0, 0), (1, m1, 0), (2, m2, 0), (3, m2, 3)):
             mods[:, pl.ds(pl.multiple_of(at[place], 128), PART)] = ref[row : row + 2]
-        total = 0.0
-        squares = 0.0
-        for ref in (x0, x1, x2, x3):
-            value = ref[...].astype(F32)
-            total = total + jnp.sum(value, 1, keepdims=True)
-            squares = squares + jnp.sum(value * value, 1, keepdims=True)
-        center = total / D
-        scale = lax.rsqrt(squares / D - center * center + 1e-06)
         for k, ref in enumerate((x0, x1, x2, x3)):
             cols = pl.ds(pl.multiple_of(at[8 + k] * PART, 128), PART)
-            normed = (ref[...].astype(F32) - center) * scale
+            normed = (ref[...].astype(F32) - center[:, 0:1]) * scale[:, 0:1]
             modded[:, cols] = (normed * (1.0 + mods[1:2, cols]) + mods[0:1, cols]).astype(BF)
 
     modded_o[...] = modded[:, pl.ds(pl.multiple_of(step * WIDE, 128), WIDE)]
@@ -131,20 +154,21 @@
     hidden[...] = ((0.5 * value) * (1.0 + bent)).astype(BF)
 
 
-def forward(chunk, at, blocks, mods, in_w):
+def forward(chunk, at, blocks, stats, mods, in_w):
     rows, ff = blocks[0].shape[0] // 2, in_w.shape[1]
     piece = pl.BlockSpec((rows, PART), lambda s, *_: (chunk, 0))
     return call(
         forward_kernel,
         ff // WIDE,
         [piece] * 4
+        + [whole((rows, 128))] * 2
         + [whole((3, PART)), whole((3, PART)), whole((6, PART)), columns(D, WIDE)],
         [columns(rows, WIDE)] * 3,
         [shaped((rows, D)), shaped((rows, ff)), shaped((rows, ff), F32)],
         [pltpu.VMEM((2, D), F32), pltpu.VMEM((rows, D), BF)],
         cost(2 * rows * D * ff, 12 * 10**6, rows * ff),
         "forward",
-    )(at, *[in_hbm(b) for b in blocks], *mods, in_hbm(in_w))
+    )(at, *[in_hbm(b) for b in blocks], *stats, *mods, in_hbm(in_w))
 
 
 def split_rows(at, turned, keep, send):
@@ -480,8 +504,14 @@
     modulation = jnp.einsum("ed,dkf->ekf", chosen, mod_w, preferred_element_type=F32)[0]
     gate = modulation[2:3]
     own_mods = modulation
-    pair_mods = swap_x(own_mods, 0)
+    latent_blocks = (latents, next_ahead, far, behind)
+    pair_mods, *stats0 = lax.optimization_barrier(
+        (swap_x(own_mods, 0), *statistics(0, at, latent_blocks))
+    )
     far_mods = swap_x(jnp.concatenate([own_mods, pair_mods], 0), 1)
+    far_mods, *stats1 = lax.optimization_barrier(
+        (far_mods, *statistics(1, at, latent_blocks))
+    )
     mods = (own_mods, pair_mods, far_mods)
 
     count = tok_count[0]
@@ -507,14 +537,13 @@
         delta = (output - targets[at_rows].astype(F32)) * live * factor
         return (gate * delta).astype(BF)
 
-    latent_blocks = (latents, next_ahead, far, behind)
-    modded0, hidden0, pre0 = forward(0, at, latent_blocks, mods, in_w)
+    modded0, hidden0, pre0 = forward(0, at, latent_blocks, stats0, mods, in_w)
     far0, down0 = project(hidden0, 2).astype(BF), project(hidden0, 3).astype(BF)
     far0 = by_x(far0, 1)
     at_next, down0 = lax.optimization_barrier((at, down0))
     down0 = by_x(down0, -1)
     up0 = lax.optimization_barrier(project(hidden0, 1))
-    modded1, hidden1, pre1 = forward(1, at_next, latent_blocks, mods, in_w)
+    modded1, hidden1, pre1 = forward(1, at_next, latent_blocks, stats1, mods, in_w)
     hidden1, far0, down0 = lax.optimization_barrier((hidden1, far0, down0))
     up0 = (up0 + far0.astype(F32)).astype(BF)
     up0, hidden1 = lax.optimization_barrier((up0, hidden1))

time: 193 us -> 194 us (level)
  Pallas kernels: 48 us -> 51.7 us
  waiting for transfers between devices: 50.7 us -> 47.7 us
    ppermute x6, waiting for transfers between devices: 16.6 us -> 11.6 us  [swap_x(): return lax.ppermute(value, 'mp', list(enumerate(other)))]
    pallas_call x2 -> x4, Pallas kernels: 15.8 us -> 19.5 us  [the longest x2 14.4 us: forward(): call(forward_kernel, ff // WIDE, [piece] * 4 + [whole((rows, 128))] * 2 +...]
    ppermute x15, waiting for transfers between devices: 17.4 us -> 19.7 us  [by_x(): return lax.ppermute(value, ('dp', 'mp'), pairs)]
  transfers between devices with their start and end apart: 31 -> 31, of which waited for: 18 -> 17; matrix products, arithmetic and copies ran while one was open for 10% -> 10% of each run, Pallas kernels for 12% -> 14%
where the time goes in v7:
time: 194 us; the launch traced here: 193 us
  Pallas kernels  51.7 us (27%)
  starting transfers between devices  49.5 us (26%)
  waiting for transfers between devices  47.7 us (25%)
  blocking collectives  16.5 us (9%)
  matrix products  12 us (6%)
  other arithmetic  6.73 us (3%)
  local copies, waits for them, and re-layouts  5.74 us (3%)
  between operations  3.28 us (2%)
    ppermute x15, waiting for transfers between devices, by_x(): return lax.ppermute(value, ('dp', 'mp'), pairs)  19.7 us
    ppermute x15, starting transfers between devices, by_x(): return lax.ppermute(value, ('dp', 'mp'), pairs)  19.1 us
    all_to_all x1, blocking collectives, local(): lax.all_to_all(value, 'dp', 0, 0, axis_index_groups=groups, tiled=True)  16.5 us
    pallas_call x2, Pallas kernels, forward(): call(forward_kernel, ff // WIDE, [piece] * 4 + [whole((rows, 128))] * 2 +...  14.4 us
    ppermute x9, waiting for transfers between devices, by_dp(): return lax.ppermute(value, 'dp', pairs)  13.3 us
    ppermute x6, starting transfers between devices, swap_x(): return lax.ppermute(value, 'mp', list(enumerate(other)))  12.4 us
    ppermute x6, waiting for transfers between devices, swap_x(): return lax.ppermute(value, 'mp', list(enumerate(other)))  11.6 us
    ppermute x9, starting transfers between devices, by_dp(): return lax.ppermute(value, 'dp', pairs)  9.38 us
  transfers between devices with their start and end apart: 31, of which 17 were waited for; matrix products, arithmetic and copies ran while one was open for 10% of the time, Pallas kernels for 14%

profile of v7, /device:TPU:0, one launch (start us, length us, event | category | flops | bytes accessed | tf_op | source)
XLA Modules:
  0.0 193.1 jit_solution(2189426407225862677)
XLA Ops:
  0.6 1.6 collective-permute-start
  2.3 1.7 collective-permute-start.1
  6.4 8.5 %all-to-all-start = ((f32[32,8,128]{2,1,0:T(8,128)}), f32[32,8,128]{2,1,0:T(8,128)}, u32[]{:S(2)}, u32[]{:S(2)}) async-start(f32[32,8,128]{2,1,0:T(8,128)} %broadcast_in_dim.31), calls=%async_computation | async-start | bytes 262144 | tf_op jit(solution)/shard_map/all_to_all | solution.py:487
  15.1 4.6 %constant_dynamic-slice_fusion = (bf16[384,1536]{1,0:T(8,128)(2,1)}, bf16[384,1536]{1,0:T(8,128)(2,1)}, bf16[384,1536]{1,0:T(8,128)(2,1)}, bf16[384,1536]{1,0:T(8,128)(2,1)}) fusion(bf16[1536,1536]{1,0:T(8,128)(2,1)} %out_w.3, s32[]{:T(128)S(6)} %select_n.112, s32[]{:T(128)S(6)} %select_n.111, s32[]{:T(128)S(6)} %select_n.110, s32[]{:T(128)S(6)} %select_n.109), kind=kLoop, calls=%fused_computation.51 | loop fusion | bytes 9437200 | tf_op jit(solution)/shard_map/dynamic_slice | solution.py:480
  19.8 3.0 %all-to-all-done = f32[32,8,128]{2,1,0:T(8,128)} async-done(((f32[32,8,128]{2,1,0:T(8,128)}), f32[32,8,128]{2,1,0:T(8,128)}, u32[]{:S(2)}, u32[]{:S(2)}) %all-to-all-start) | async-done | bytes 131104 | tf_op jit(solution)/shard_map/all_to_all | solution.py:487
  24.1 2.4 %fusion.27 = f32[1,1536]{1,0:T(1,128)S(1)} fusion(bf16[1024,1]{0,1:T(2,128)(2,1)S(1)} %reshape.95, bf16[1024,1536]{1,0:T(8,128)(2,1)} %param.18), kind=kOutput, calls=%fused_computation.60 | convolution fusion | flops 3145728 | bytes 3153920 | tf_op jit(solution)/shard_map/dot_general | solution.py:24
  26.5 1.5 collective-permute-start.2
  28.7 4.3 %collective-permute-done.2 = f32[1,1536]{1,0:T(1,128)S(1)} collective-permute-done((f32[1,1536]{1,0:T(1,128)S(1)}, f32[1,1536]{1,0:T(1,128)S(1)}, u32[]{:S(2)}, u32[]{:S(2)}) %collective-permute-start.2) | collective-permute-done | bytes 6176 | tf_op jit(solution)/shard_map/ppermute | solution.py:62
  33.0 3.9 %collective-permute-start.3 = (f32[1,1536]{1,0:T(1,128)S(1)}, f32[1,1536]{1,0:T(1,128)S(1)}, u32[]{:S(2)}, u32[]{:S(2)}) collective-permute-start(f32[1,1536]{1,0:T(1,128)S(1)} %add.191), channel_id=1, source_target_pairs={{0,3},{1,2},{2,1},{3,0},{4,7},{5,6},{6,5},{7,4},{8,11},{9,10},{10,... | collective-permute-start | bytes 18440 | tf_op jit(solution)/shard_map/ppermute | solution.py:62
  36.9 1.6 collective-permute-done.3
  41.2 2.5 %statistics.2 = (f32[512,128]{1,0:T(8,128)S(1)}, f32[512,128]{1,0:T(8,128)S(1)}) custom-call(s32[16]{0:T(128)S(1)} %stack.59.at.refs_0_, bf16[1024,384]{1,0:T(8,128)(2,1)} %x0.7, bf16[1024,384]{1,0:T(8,128)(2,1)} %collective-permute-done.1.x1, bf16[1024,384]{1,0:T(8,128)(2,1)} %collective-permute-done.4.x2, bf16[1024,384]{1,0:T(8,128)(2,1)} %collective-permute-done.x3), custom_call_target="tpu_custom_call" | custom-call | flops 3145728 | bytes 2359296 | tf_op jit(solution)/shard_map/statistics/pallas_call | solution.py:124
  44.1 3.3 %collective-permute-start.6 = (f32[6,384]{1,0:T(8,128)S(1)}, f32[6,384]{1,0:T(8,128)S(1)}, u32[]{:S(2)}, u32[]{:S(2)}) collective-permute-start(f32[6,384]{1,0:T(8,128)S(1)} %pad_maximum_fusion), channel_id=1, source_target_pairs={{0,3},{1,2},{2,1},{3,0},{4,7},{5,6},{6,5},{7,4},{8,11},{9,10},{10,... | collective-permute-start | bytes 27656 | tf_op jit(solution)/shard_map/ppermute | solution.py:62
  47.4 2.5 %statistics.3 = (f32[512,128]{1,0:T(8,128)S(1)}, f32[512,128]{1,0:T(8,128)S(1)}) custom-call(s32[16]{0:T(128)S(1)} %stack.59.at.refs_0_, bf16[1024,384]{1,0:T(8,128)(2,1)} %x0.7, bf16[1024,384]{1,0:T(8,128)(2,1)} %collective-permute-done.1.x1, bf16[1024,384]{1,0:T(8,128)(2,1)} %collective-permute-done.4.x2, bf16[1024,384]{1,0:T(8,128)(2,1)} %collective-permute-done.x3), custom_call_target="tpu_custom_call" | custom-call | flops 3145728 | bytes 2359296 | tf_op jit(solution)/shard_map/statistics/pallas_call | solution.py:124
  50.0 7.2 %forward.2 = (bf16[512,1536]{1,0:T(8,128)(2,1)S(1)}, bf16[512,1536]{1,0:T(8,128)(2,1)S(1)}, f32[512,1536]{1,0:T(8,128)S(1)}) custom-call(s32[16]{0:T(128)S(1)} %stack.59.at.refs_0_, bf16[1024,384]{1,0:T(8,128)(2,1)} %x0.7, bf16[1024,384]{1,0:T(8,128)(2,1)} %collective-permute-done.1.x1, bf16[1024,384]{1,0:T(8,128)(2,1)} %collective-permute-done.4.x2, ...), custom_call_target="tpu_custom_call" | custom-call | flops 2415919104 | bytes 12000000 | tf_op jit(solution)/shard_map/forward/pallas_call | solution.py:160
  60.0 2.8 %collective-permute-start.8 = (bf16[512,384]{1,0:T(8,128)(2,1)S(1)}, bf16[512,384]{1,0:T(8,128)(2,1)S(1)}, u32[]{:S(2)}, u32[]{:S(2)}) collective-permute-start(bf16[512,384]{1,0:T(8,128)(2,1)S(1)} %convolution_convert_fusion.3), channel_id=1, source_target_pairs={{0,3},{1,0},{2,1},{3,2},{4,5},{5,6},{6,7},{7,4},{8,11},{9,8},{10,9... | collective-permute-start | bytes 1179656 | tf_op jit(solution)/shard_map/ppermute | solution.py:36
  63.8 7.2 %forward.3 = (bf16[512,1536]{1,0:T(8,128)(2,1)S(1)}, bf16[512,1536]{1,0:T(8,128)(2,1)S(1)}, f32[512,1536]{1,0:T(8,128)S(1)}) custom-call(s32[16]{0:T(128)S(1)} %stack.59.at.refs_0_, bf16[1024,384]{1,0:T(8,128)(2,1)} %x0.7, bf16[1024,384]{1,0:T(8,128)(2,1)} %collective-permute-done.1.x1, bf16[1024,384]{1,0:T(8,128)(2,1)} %collective-permute-done.4.x2, ...), custom_call_target="tpu_custom_call" | custom-call | flops 2415919104 | bytes 12000000 | tf_op jit(solution)/shard_map/forward/pallas_call | solution.py:160
  74.4 3.3 %collective-permute-start.10 = (bf16[512,384]{1,0:T(8,128)(2,1)S(1)}, bf16[512,384]{1,0:T(8,128)(2,1)S(1)}, u32[]{:S(2)}, u32[]{:S(2)}) collective-permute-start(bf16[512,384]{1,0:T(8,128)(2,1)S(1)} %convolution_convert_fusion.1), channel_id=1, source_target_pairs={{0,3},{1,0},{2,1},{3,2},{4,5},{5,6},{6,7},{7,4},{8,11},{9,8},{10,9... | collective-permute-start | bytes 1179656 | tf_op jit(solution)/shard_map/ppermute | solution.py:36
  77.7 7.8 %collective-permute-done.9 = bf16[512,384]{1,0:T(8,128)(2,1)S(1)} collective-permute-done((bf16[512,384]{1,0:T(8,128)(2,1)S(1)}, bf16[512,384]{1,0:T(8,128)(2,1)S(1)}, u32[]{:S(2)}, u32[]{:S(2)}) %collective-permute-start.9) | collective-permute-done | bytes 393248 | tf_op jit(solution)/shard_map/ppermute | solution.py:36
  86.0 3.2 %collective-permute-start.13 = (bf16[512,384]{1,0:T(8,128)(2,1)S(1)}, bf16[512,384]{1,0:T(8,128)(2,1)S(1)}, u32[]{:S(2)}, u32[]{:S(2)}) collective-permute-start(bf16[512,384]{1,0:T(8,128)(2,1)S(1)} %multiply_convert_fusion.1.b0.refs_1_), channel_id=1, source_target_pairs={{0,3},{1,0},{2,1},{3,2},{4,5},{5,6},{6,7},{7,4},{8,11},{9,8},{10,9... | collective-permute-start | bytes 1179656 | tf_op jit(solution)/shard_map/ppermute | solution.py:36
  91.3 3.2 %add_convert_fusion = (bf16[512,1536]{1,0:T(8,128)(2,1)S(1)}, bf16[512,1536]{1,0:T(8,128)(2,1)S(1)}) fusion(f32[512,1536]{1,0:T(8,128)S(1)} %get-tuple-element.119, f32[512,1536]{1,0:T(8,128)S(1)} %get-tuple-element.118), kind=kLoop, calls=%fused_computation | loop fusion | flops 23592960 | bytes 9437184 | tf_op jit(solution)/shard_map/convert_element_type | solution.py:564
  94.5 2.2 %turn.1 = (bf16[768,1024]{1,0:T(8,128)(2,1)S(1)}, bf16[768,1024]{1,0:T(8,128)(2,1)S(1)}) custom-call(s32[16]{0:T(128)S(1)} %stack.59.at.refs_0_, bf16[512,1536]{1,0:T(8,128)(2,1)S(1)} %get-tuple-element.121.top, bf16[512,1536]{1,0:T(8,128)(2,1)S(1)} %get-tuple-element.122.low), custom_call_target="tpu_custom_call" | custom-call | flops 1572864 | bytes 6291456 | tf_op jit(solution)/shard_map/turn/pallas_call | solution.py:190
  96.8 2.3 %collective-permute-done.11 = bf16[512,384]{1,0:T(8,128)(2,1)S(1)} collective-permute-done((bf16[512,384]{1,0:T(8,128)(2,1)S(1)}, bf16[512,384]{1,0:T(8,128)(2,1)S(1)}, u32[]{:S(2)}, u32[]{:S(2)}) %collective-permute-start.11) | collective-permute-done | bytes 393248 | tf_op jit(solution)/shard_map/ppermute | solution.py:36
  99.1 2.4 %collective-permute-done.12.b3.refs_2_ = bf16[512,384]{1,0:T(8,128)(2,1)S(1)} collective-permute-done((bf16[512,384]{1,0:T(8,128)(2,1)S(1)}, bf16[512,384]{1,0:T(8,128)(2,1)S(1)}, u32[]{:S(2)}, u32[]{:S(2)}) %collective-permute-start.12) | collective-permute-done | bytes 393248 | tf_op jit(solution)/shard_map/ppermute | solution.py:36
  101.9 3.3 %collective-permute-start.16 = (bf16[512,384]{1,0:T(8,128)(2,1)S(1)}, bf16[512,384]{1,0:T(8,128)(2,1)S(1)}, u32[]{:S(2)}, u32[]{:S(2)}) collective-permute-start(bf16[512,384]{1,0:T(8,128)(2,1)S(1)} %multiply_convert_fusion.refs_2_.b0), channel_id=1, source_target_pairs={{0,3},{1,0},{2,1},{3,2},{4,5},{5,6},{6,7},{7,4},{8,11},{9,8},{10,9... | collective-permute-start | bytes 1179656 | tf_op jit(solution)/shard_map/ppermute | solution.py:36
  105.1 2.0 %rows_grad.4 = (bf16[768,1536]{1,0:T(8,128)(2,1)S(1)}, bf16[768,1536]{1,0:T(8,128)(2,1)S(1)}, f32[1,1536]{1,0:T(1,128)S(1)}) custom-call(s32[16]{0:T(128)S(1)} %stack.59.at.refs_0_, bf16[512,384]{1,0:T(8,128)(2,1)S(1)} %multiply_convert_fusion.1.b0.refs_1_, bf16[512,384]{1,0:T(8,128)(2,1)S(1)} %multiply_convert_fusion.refs_2_.b0, ...), custom_call_target="tpu_custom_call" | custom-call | flops 1207959552 | bytes 5000000 | tf_op jit(solution)/shard_map/rows_grad/pallas_call | solution.py:311
  107.1 2.4 %rows_partial.1.refs_3_ = f32[768,1536]{1,0:T(8,128)S(1)} custom-call(s32[16]{0:T(128)S(1)} %stack.59.at.refs_0_, bf16[512,384]{1,0:T(8,128)(2,1)S(1)} %collective-permute-done.13.b1.refs_1_, bf16[512,384]{1,0:T(8,128)(2,1)S(1)} %collective-permute-done.12.b3.refs_2_, bf16[512,1536]{1,0:T(8,128)(2,1)S(1)} %get-tuple-element.111.refs_3_), custom_call_target="tpu_custom_call" | custom-call | flops 1207959552 | bytes 8000000 | tf_op jit(solution)/shard_map/rows_partial/pallas_call | solution.py:262
  109.6 3.8 %collective-permute-done.15.b2.refs_1_ = bf16[512,384]{1,0:T(8,128)(2,1)S(1)} collective-permute-done((bf16[512,384]{1,0:T(8,128)(2,1)S(1)}, bf16[512,384]{1,0:T(8,128)(2,1)S(1)}, u32[]{:S(2)}, u32[]{:S(2)}) %collective-permute-start.15) | collective-permute-done | bytes 393248 | tf_op jit(solution)/shard_map/ppermute | solution.py:36
  114.1 1.3 collective-permute-start.18
  115.4 1.4 rows_grad.5
  116.8 4.2 %backward.2.right0 = bf16[512,1536]{1,0:T(8,128)(2,1)S(1)} custom-call(s32[16]{0:T(128)S(1)} %stack.59.at.refs_0_, bf16[512,384]{1,0:T(8,128)(2,1)S(1)} %multiply_convert_fusion.1.b0.refs_1_, bf16[512,384]{1,0:T(8,128)(2,1)S(1)} %collective-permute-done.13.b1.refs_1_, bf16[512,384]{1,0:T(8,128)(2,1)S(1)} %collective-permute-done.15.b2.refs_1_, ...), custom_call_target="tpu_custom_call" | custom-call | flops 2415919104 | bytes 14000000 | tf_op jit(solution)/shard_map/backward/pallas_call | solution.py:213
  121.0 3.0 %collective-permute-done.17.b2.refs_2_ = bf16[512,384]{1,0:T(8,128)(2,1)S(1)} collective-permute-done((bf16[512,384]{1,0:T(8,128)(2,1)S(1)}, bf16[512,384]{1,0:T(8,128)(2,1)S(1)}, u32[]{:S(2)}, u32[]{:S(2)}) %collective-permute-start.17) | collective-permute-done | bytes 393248 | tf_op jit(solution)/shard_map/ppermute | solution.py:36
  124.4 4.2 %backward.3.right1 = bf16[512,1536]{1,0:T(8,128)(2,1)S(1)} custom-call(s32[16]{0:T(128)S(1)} %stack.59.at.refs_0_, bf16[512,384]{1,0:T(8,128)(2,1)S(1)} %multiply_convert_fusion.refs_2_.b0, bf16[512,384]{1,0:T(8,128)(2,1)S(1)} %collective-permute-done.16.b1.refs_1_, bf16[512,384]{1,0:T(8,128)(2,1)S(1)} %collective-permute-done.17.b2.refs_2_, ...), custom_call_target="tpu_custom_call" | custom-call | flops 2415919104 | bytes 14000000 | tf_op jit(solution)/shard_map/backward/pallas_call | solution.py:213
  128.6 1.4 rows_grad.6
  130.0 2.0 %rows_grad.7 = (bf16[768,1536]{1,0:T(8,128)(2,1)S(1)}, bf16[768,1536]{1,0:T(8,128)(2,1)S(1)}, f32[1,1536]{1,0:T(1,128)S(1)}) custom-call(s32[16]{0:T(128)S(1)} %stack.59.at.refs_0_, bf16[512,384]{1,0:T(8,128)(2,1)S(1)} %collective-permute-done.15.b2.refs_1_, ...), custom_call_target="tpu_custom_call", output_to_operand_aliasing={{0}: (5, {}), {1}: (6, {})} | custom-call | flops 1207959552 | bytes 5000000 | tf_op jit(solution)/shard_map/rows_grad/pallas_call | solution.py:311
  131.9 6.7 %weight_grad.1 = (bf16[768,1536]{1,0:T(8,128)(2,1)S(1)}, bf16[768,1536]{1,0:T(8,128)(2,1)S(1)}, f32[1,128]{1,0:T(1,128)S(1)}) custom-call(s32[16]{0:T(128)S(1)} %stack.59.at.refs_0_, bf16[768,1024]{1,0:T(8,128)(2,1)S(1)} %get-tuple-element.126.keep_l, bf16[768,1024]{1,0:T(8,128)(2,1)S(1)} %get-tuple-element.127.send_l, ...), custom_call_target="tpu_custom_call" | custom-call | flops 4831838208 | bytes 11000000 | tf_op jit(solution)/shard_map/weight_grad/pallas_call | solution.py:353
  139.2 3.5 %collective-permute-done.19 = f32[1,128]{1,0:T(1,128)S(1)} collective-permute-done((f32[1,128]{1,0:T(1,128)S(1)}, f32[1,128]{1,0:T(1,128)S(1)}, u32[]{:S(2)}, u32[]{:S(2)}) %collective-permute-start.19) | collective-permute-done | bytes 544 | tf_op jit(solution)/shard_map/ppermute | solution.py:62
  142.7 3.0 %collective-permute-start.20 = (f32[1,128]{1,0:T(1,128)S(1)}, f32[1,128]{1,0:T(1,128)S(1)}, u32[]{:S(2)}, u32[]{:S(2)}) collective-permute-start(f32[1,128]{1,0:T(1,128)S(1)} %add.215), channel_id=1, source_target_pairs={{0,3},{1,2},{2,1},{3,0},{4,7},{5,6},{6,5},{7,4},{8,11},{9,10},{10,... | collective-permute-start | bytes 1544 | tf_op jit(solution)/shard_map/ppermute | solution.py:62
  145.7 1.8 collective-permute-done.20
  147.6 1.1 collective-permute-done.21.u1
  148.7 1.9 spread.1
  151.1 2.9 %collective-permute-start.25 = (bf16[4,48,1536]{2,1,0:T(8,128)(2,1)S(1)}, bf16[4,48,1536]{2,1,0:T(8,128)(2,1)S(1)}, u32[]{:S(2)}, u32[]{:S(2)}) collective-permute-start(bf16[4,48,1536]{2,1,0:T(8,128)(2,1)S(1)} %get-tuple-element.156), channel_id=1, source_target_pairs={{0,96},{4,28},{8,104},{12,4},{16,112},{20,12},{24,120},{28,20},{32... | collective-permute-start | bytes 1769480 | tf_op jit(solution)/shard_map/ppermute | solution.py:46
  154.5 1.4 collective-permute-start.28
  156.0 1.4 own.1
  157.3 4.4 %collective-permute-done.24.up = bf16[4,48,1536]{2,1,0:T(8,128)(2,1)S(1)} collective-permute-done((bf16[4,48,1536]{2,1,0:T(8,128)(2,1)S(1)}, bf16[4,48,1536]{2,1,0:T(8,128)(2,1)S(1)}, u32[]{:S(2)}, u32[]{:S(2)}) %collective-permute-start.24) | collective-permute-done | bytes 589856 | tf_op jit(solution)/shard_map/ppermute | solution.py:46
  161.8 1.6 relay.1
  164.2 2.6 %collective-permute-start.29 = (bf16[4,48,1536]{2,1,0:T(8,128)(2,1)S(1)}, bf16[4,48,1536]{2,1,0:T(8,128)(2,1)S(1)}, u32[]{:S(2)}, u32[]{:S(2)}) collective-permute-start(bf16[4,48,1536]{2,1,0:T(8,128)(2,1)S(1)} %get-tuple-element.163), channel_id=1, source_target_pairs={{0,96},{4,28},{8,104},{12,4},{16,112},{20,12},{24,120},{28,20},{32... | collective-permute-start | bytes 1769480 | tf_op jit(solution)/shard_map/ppermute | solution.py:46
  168.1 6.5 %collective-permute-done.26.up1 = bf16[4,48,1536]{2,1,0:T(8,128)(2,1)S(1)} collective-permute-done((bf16[4,48,1536]{2,1,0:T(8,128)(2,1)S(1)}, bf16[4,48,1536]{2,1,0:T(8,128)(2,1)S(1)}, u32[]{:S(2)}, u32[]{:S(2)}) %collective-permute-start.26) | collective-permute-done | bytes 589856 | tf_op jit(solution)/shard_map/ppermute | solution.py:46
  175.6 16.5 %all_to_all.10 = bf16[4,2,48,1536]{3,2,1,0:T(8,128)(2,1)S(1)} all-to-all(bf16[4,2,48,1536]{3,2,1,0:T(8,128)(2,1)S(1)} %close.1), channel_id=1, replica_groups={{0,8,16,24},{32,40,48,56},{64,72,80,88},{96,104,112,120},{4,36,68,100},..., dimensions={0} | all-to-all | bytes 2359296 | tf_op jit(solution)/shard_map/all_to_all | solution.py:600
  (94 shorter events, 22.4 us)
Async XLA Ops:
  0.6 39.2 %copy-start = (bf16[1536,3,384]{2,0,1:T(8,128)(2,1)S(1)}, bf16[1536,3,384]{2,0,1:T(8,128)(2,1)}, u32[]{:S(2)}) copy-start(bf16[1536,3,384]{2,0,1:T(8,128)(2,1)} %param.19) | copy-start | bytes 10616836
  0.6 22.1 %collective-permute-start = (bf16[1024,384]{1,0:T(8,128)(2,1)}, bf16[1024,384]{1,0:T(8,128)(2,1)}, u32[]{:S(2)}, u32[]{:S(2)}) collective-permute-start(bf16[1024,384]{1,0:T(8,128)(2,1)} %x0.7), channel_id=1, source_target_pairs={{0,1},{1,2},{2,3},{3,0},{4,7},{5,4},{6,5},{7,6},{8,9},{9,10},{10,1... | collective-permute-start | bytes 2359304 | tf_op jit(solution)/shard_map/ppermute | solution.py:36
  2.3 20.5 %collective-permute-start.1 = (bf16[1024,384]{1,0:T(8,128)(2,1)}, bf16[1024,384]{1,0:T(8,128)(2,1)}, u32[]{:S(2)}, u32[]{:S(2)}) collective-permute-start(bf16[1024,384]{1,0:T(8,128)(2,1)} %x0.7), channel_id=1, source_target_pairs={{0,3},{1,0},{2,1},{3,2},{4,5},{5,6},{6,7},{7,4},{8,11},{9,8},{10,9... | collective-permute-start | bytes 2359304 | tf_op jit(solution)/shard_map/ppermute | solution.py:36
  6.4 16.4 %all-to-all-start = ((f32[32,8,128]{2,1,0:T(8,128)}), f32[32,8,128]{2,1,0:T(8,128)}, u32[]{:S(2)}, u32[]{:S(2)}) async-start(f32[32,8,128]{2,1,0:T(8,128)} %broadcast_in_dim.31), calls=%async_computation | async-start | bytes 262144 | tf_op jit(solution)/shard_map/all_to_all | solution.py:487
  15.0 8.0 %copy-start.10 = (s32[32]{0:T(128)S(1)}, s32[32]{0:T(128)}, u32[]{:S(2)}) copy-start(s32[32]{0:T(128)} %param.17) | copy-start | bytes 388
  22.8 15.7 %collective-permute-start.4 = (bf16[1024,384]{1,0:T(8,128)(2,1)}, bf16[1024,384]{1,0:T(8,128)(2,1)}, u32[]{:S(2)}, u32[]{:S(2)}) collective-permute-start(bf16[1024,384]{1,0:T(8,128)(2,1)} %collective-permute-done.x3), channel_id=1, source_target_pairs={{0,1},{1,2},{2,3},{3,0},{4,7},{5,4},{6,5},{7,6},{8,9},{9,10},{10,1... | collective-permute-start | bytes 2359304 | tf_op jit(solution)/shard_map/ppermute | solution.py:36
  26.5 6.5 %collective-permute-start.2 = (f32[1,1536]{1,0:T(1,128)S(1)}, f32[1,1536]{1,0:T(1,128)S(1)}, u32[]{:S(2)}, u32[]{:S(2)}) collective-permute-start(f32[1,1536]{1,0:T(1,128)S(1)} %fusion.27), channel_id=1, source_target_pairs={{0,1},{1,0},{2,3},{3,2},{4,5},{5,4},{6,7},{7,6},{8,9},{9,8},{10,11... | collective-permute-start | bytes 18440 | tf_op jit(solution)/shard_map/ppermute | solution.py:62
  33.0 5.5 %collective-permute-start.3 = (f32[1,1536]{1,0:T(1,128)S(1)}, f32[1,1536]{1,0:T(1,128)S(1)}, u32[]{:S(2)}, u32[]{:S(2)}) collective-permute-start(f32[1,1536]{1,0:T(1,128)S(1)} %add.191), channel_id=1, source_target_pairs={{0,3},{1,2},{2,1},{3,0},{4,7},{5,6},{6,5},{7,4},{8,11},{9,10},{10,... | collective-permute-start | bytes 18440 | tf_op jit(solution)/shard_map/ppermute | solution.py:62
  40.4 3.7 %collective-permute-start.5 = (f32[3,384]{1,0:T(4,128)S(1)}, f32[3,384]{1,0:T(4,128)S(1)}, u32[]{:S(2)}, u32[]{:S(2)}) collective-permute-start(f32[3,384]{1,0:T(4,128)S(1)} %bitcast.74), channel_id=1, source_target_pairs={{0,1},{1,0},{2,3},{3,2},{4,5},{5,4},{6,7},{7,6},{8,9},{9,8},{10,11... | collective-permute-start | bytes 13832 | tf_op jit(solution)/shard_map/ppermute | solution.py:62
  44.1 5.9 %collective-permute-start.6 = (f32[6,384]{1,0:T(8,128)S(1)}, f32[6,384]{1,0:T(8,128)S(1)}, u32[]{:S(2)}, u32[]{:S(2)}) collective-permute-start(f32[6,384]{1,0:T(8,128)S(1)} %pad_maximum_fusion), channel_id=1, source_target_pairs={{0,3},{1,2},{2,1},{3,0},{4,7},{5,6},{6,5},{7,4},{8,11},{9,10},{10,... | collective-permute-start | bytes 27656 | tf_op jit(solution)/shard_map/ppermute | solution.py:62
  50.0 7.2 %copy-start.4 = (bf16[384,1536]{1,0:T(8,128)(2,1)S(1)}, bf16[384,1536]{1,0:T(8,128)(2,1)}, u32[]{:S(2)}) copy-start(bf16[384,1536]{1,0:T(8,128)(2,1)} %get-tuple-element.99) | copy-start | bytes 3538948
  57.2 1.3 copy-start.6
  58.5 4.3 %copy-start.5 = (bf16[384,1536]{1,0:T(8,128)(2,1)S(1)}, bf16[384,1536]{1,0:T(8,128)(2,1)}, u32[]{:S(2)}) copy-start(bf16[384,1536]{1,0:T(8,128)(2,1)} %get-tuple-element.98) | copy-start | bytes 3538948
  59.5 11.5 %collective-permute-start.7 = (bf16[512,384]{1,0:T(8,128)(2,1)S(1)}, bf16[512,384]{1,0:T(8,128)(2,1)S(1)}, u32[]{:S(2)}, u32[]{:S(2)}) collective-permute-start(bf16[512,384]{1,0:T(8,128)(2,1)S(1)} %convolution_convert_fusion.2), channel_id=1, source_target_pairs={{0,1},{1,2},{2,3},{3,0},{4,7},{5,4},{6,5},{7,6},{8,9},{9,10},{10,1... | collective-permute-start | bytes 1179656 | tf_op jit(solution)/shard_map/ppermute | solution.py:36
  60.0 11.0 %collective-permute-start.8 = (bf16[512,384]{1,0:T(8,128)(2,1)S(1)}, bf16[512,384]{1,0:T(8,128)(2,1)S(1)}, u32[]{:S(2)}, u32[]{:S(2)}) collective-permute-start(bf16[512,384]{1,0:T(8,128)(2,1)S(1)} %convolution_convert_fusion.3), channel_id=1, source_target_pairs={{0,3},{1,0},{2,1},{3,2},{4,5},{5,6},{6,7},{7,4},{8,11},{9,8},{10,9... | collective-permute-start | bytes 1179656 | tf_op jit(solution)/shard_map/ppermute | solution.py:36
  72.1 1.3 copy-start.3
  72.1 13.4 %collective-permute-start.9 = (bf16[512,384]{1,0:T(8,128)(2,1)S(1)}, bf16[512,384]{1,0:T(8,128)(2,1)S(1)}, u32[]{:S(2)}, u32[]{:S(2)}) collective-permute-start(bf16[512,384]{1,0:T(8,128)(2,1)S(1)} %add_convert_fusion.3), channel_id=1, source_target_pairs={{0,1},{1,2},{2,3},{3,0},{4,7},{5,4},{6,5},{7,6},{8,9},{9,10},{10,1... | collective-permute-start | bytes 1179656 | tf_op jit(solution)/shard_map/ppermute | solution.py:36
  73.4 12.2 %copy-start.2 = (bf16[1024,384]{1,0:T(8,128)(2,1)S(1)}, bf16[1024,384]{1,0:T(8,128)(2,1)}, u32[]{:S(2)}) copy-start(bf16[1024,384]{1,0:T(8,128)(2,1)} %x0.7) | copy-start | bytes 2359300
  73.4 12.2 %copy-start.7 = (bf16[1024,384]{1,0:T(8,128)(2,1)S(1)}, bf16[1024,384]{1,0:T(8,128)(2,1)}, u32[]{:S(2)}) copy-start(bf16[1024,384]{1,0:T(8,128)(2,1)} %param.13) | copy-start | bytes 2359300
  74.4 16.8 %collective-permute-start.10 = (bf16[512,384]{1,0:T(8,128)(2,1)S(1)}, bf16[512,384]{1,0:T(8,128)(2,1)S(1)}, u32[]{:S(2)}, u32[]{:S(2)}) collective-permute-start(bf16[512,384]{1,0:T(8,128)(2,1)S(1)} %convolution_convert_fusion.1), channel_id=1, source_target_pairs={{0,3},{1,0},{2,1},{3,2},{4,5},{5,6},{6,7},{7,4},{8,11},{9,8},{10,9... | collective-permute-start | bytes 1179656 | tf_op jit(solution)/shard_map/ppermute | solution.py:36
  77.7 23.8 %collective-permute-start.14 = (bf16[512,384]{1,0:T(8,128)(2,1)S(1)}, bf16[512,384]{1,0:T(8,128)(2,1)S(1)}, u32[]{:S(2)}, u32[]{:S(2)}) collective-permute-start(bf16[512,384]{1,0:T(8,128)(2,1)S(1)} %convolution_convert_fusion), channel_id=1, source_target_pairs={{0,1},{1,2},{2,3},{3,0},{4,7},{5,4},{6,5},{7,6},{8,9},{9,10},{10,1... | collective-permute-start | bytes 1179656 | tf_op jit(solution)/shard_map/ppermute | solution.py:36
  85.9 15.6 %collective-permute-start.12 = (bf16[512,384]{1,0:T(8,128)(2,1)S(1)}, bf16[512,384]{1,0:T(8,128)(2,1)S(1)}, u32[]{:S(2)}, u32[]{:S(2)}) collective-permute-start(bf16[512,384]{1,0:T(8,128)(2,1)S(1)} %multiply_convert_fusion.1.b0.refs_1_), channel_id=1, source_target_pairs={{0,1},{1,2},{2,3},{3,0},{4,7},{5,4},{6,5},{7,6},{8,9},{9,10},{10,1... | collective-permute-start | bytes 1179656 | tf_op jit(solution)/shard_map/ppermute | solution.py:36
  86.0 15.5 %collective-permute-start.13 = (bf16[512,384]{1,0:T(8,128)(2,1)S(1)}, bf16[512,384]{1,0:T(8,128)(2,1)S(1)}, u32[]{:S(2)}, u32[]{:S(2)}) collective-permute-start(bf16[512,384]{1,0:T(8,128)(2,1)S(1)} %multiply_convert_fusion.1.b0.refs_1_), channel_id=1, source_target_pairs={{0,3},{1,0},{2,1},{3,2},{4,5},{5,6},{6,7},{7,4},{8,11},{9,8},{10,9... | collective-permute-start | bytes 1179656 | tf_op jit(solution)/shard_map/ppermute | solution.py:36
  91.3 7.8 %collective-permute-start.11 = (bf16[512,384]{1,0:T(8,128)(2,1)S(1)}, bf16[512,384]{1,0:T(8,128)(2,1)S(1)}, u32[]{:S(2)}, u32[]{:S(2)}) collective-permute-start(bf16[512,384]{1,0:T(8,128)(2,1)S(1)} %add_convert_fusion.2), channel_id=1, source_target_pairs={{0,3},{1,0},{2,1},{3,2},{4,5},{5,6},{6,7},{7,4},{8,11},{9,8},{10,9... | collective-permute-start | bytes 1179656 | tf_op jit(solution)/shard_map/ppermute | solution.py:36
  101.5 11.9 %collective-permute-start.15 = (bf16[512,384]{1,0:T(8,128)(2,1)S(1)}, bf16[512,384]{1,0:T(8,128)(2,1)S(1)}, u32[]{:S(2)}, u32[]{:S(2)}) collective-permute-start(bf16[512,384]{1,0:T(8,128)(2,1)S(1)} %collective-permute-done.12.b3.refs_2_), channel_id=1, source_target_pairs={{0,1},{1,2},{2,3},{3,0},{4,7},{5,4},{6,5},{7,6},{8,9},{9,10},{10,1... | collective-permute-start | bytes 1179656 | tf_op jit(solution)/shard_map/ppermute | solution.py:36
  101.9 11.5 %collective-permute-start.16 = (bf16[512,384]{1,0:T(8,128)(2,1)S(1)}, bf16[512,384]{1,0:T(8,128)(2,1)S(1)}, u32[]{:S(2)}, u32[]{:S(2)}) collective-permute-start(bf16[512,384]{1,0:T(8,128)(2,1)S(1)} %multiply_convert_fusion.refs_2_.b0), channel_id=1, source_target_pairs={{0,3},{1,0},{2,1},{3,2},{4,5},{5,6},{6,7},{7,4},{8,11},{9,8},{10,9... | collective-permute-start | bytes 1179656 | tf_op jit(solution)/shard_map/ppermute | solution.py:36
  107.1 9.7 %slice-start = ((s8[4718592]{0:T(1024)(128)(4,1)}), s8[4194304]{0:T(1024)(128)(4,1)S(1)}, s32[]{:S(2)}) async-start(s8[4718592]{0:T(1024)(128)(4,1)} %bitcast.72), calls=%async_computation.2 | async-start | bytes 8388608
  113.4 10.7 %collective-permute-start.17 = (bf16[512,384]{1,0:T(8,128)(2,1)S(1)}, bf16[512,384]{1,0:T(8,128)(2,1)S(1)}, u32[]{:S(2)}, u32[]{:S(2)}) collective-permute-start(bf16[512,384]{1,0:T(8,128)(2,1)S(1)} %collective-permute-done.16.b1.refs_1_), channel_id=1, source_target_pairs={{0,3},{1,0},{2,1},{3,2},{4,5},{5,6},{6,7},{7,4},{8,11},{9,8},{10,9... | collective-permute-start | bytes 1179656 | tf_op jit(solution)/shard_map/ppermute | solution.py:36
  114.1 10.2 %collective-permute-start.18 = (bf16[512,384]{1,0:T(8,128)(2,1)S(1)}, bf16[512,384]{1,0:T(8,128)(2,1)S(1)}, u32[]{:S(2)}, u32[]{:S(2)}) collective-permute-start(bf16[512,384]{1,0:T(8,128)(2,1)S(1)} %multiply_convert_fusion.refs_2_.b0), channel_id=1, source_target_pairs={{0,1},{1,2},{2,3},{3,0},{4,7},{5,4},{6,5},{7,6},{8,9},{9,10},{10,1... | collective-permute-start | bytes 1179656 | tf_op jit(solution)/shard_map/ppermute | solution.py:36
  115.4 1.4 slice-start.1
  138.6 10.1 %collective-permute-start.22 = (bf16[768,1536]{1,0:T(8,128)(2,1)S(1)}, bf16[768,1536]{1,0:T(8,128)(2,1)S(1)}, u32[]{:S(2)}, u32[]{:S(2)}) collective-permute-start(bf16[768,1536]{1,0:T(8,128)(2,1)S(1)} %get-tuple-element.153), channel_id=1, source_target_pairs={{0,4},{4,0},{8,12},{12,8},{16,20},{20,16},{24,28},{28,24},{32,36},... | collective-permute-start | bytes 7077896 | tf_op jit(solution)/shard_map/ppermute | solution.py:46
  138.7 10.0 %collective-permute-start.23 = (bf16[768,1536]{1,0:T(8,128)(2,1)S(1)}, bf16[768,1536]{1,0:T(8,128)(2,1)S(1)}, u32[]{:S(2)}, u32[]{:S(2)}) collective-permute-start(bf16[768,1536]{1,0:T(8,128)(2,1)S(1)} %get-tuple-element.154), channel_id=1, source_target_pairs={{0,4},{4,0},{8,12},{12,8},{16,20},{20,16},{24,28},{28,24},{32,36},... | collective-permute-start | bytes 7077896 | tf_op jit(solution)/shard_map/ppermute | solution.py:46
  139.2 3.5 %collective-permute-start.19 = (f32[1,128]{1,0:T(1,128)S(1)}, f32[1,128]{1,0:T(1,128)S(1)}, u32[]{:S(2)}, u32[]{:S(2)}) collective-permute-start(f32[1,128]{1,0:T(1,128)S(1)} %get-tuple-element.150), channel_id=1, source_target_pairs={{0,1},{1,0},{2,3},{3,2},{4,5},{5,4},{6,7},{7,6},{8,9},{9,8},{10,11... | collective-permute-start | bytes 1544 | tf_op jit(solution)/shard_map/ppermute | solution.py:62
  142.7 4.8 %collective-permute-start.20 = (f32[1,128]{1,0:T(1,128)S(1)}, f32[1,128]{1,0:T(1,128)S(1)}, u32[]{:S(2)}, u32[]{:S(2)}) collective-permute-start(f32[1,128]{1,0:T(1,128)S(1)} %add.215), channel_id=1, source_target_pairs={{0,3},{1,2},{2,1},{3,0},{4,7},{5,6},{6,5},{7,4},{8,11},{9,10},{10,... | collective-permute-start | bytes 1544 | tf_op jit(solution)/shard_map/ppermute | solution.py:62
  147.5 1.2 collective-permute-start.21
  150.6 11.2 %collective-permute-start.24 = (bf16[4,48,1536]{2,1,0:T(8,128)(2,1)S(1)}, bf16[4,48,1536]{2,1,0:T(8,128)(2,1)S(1)}, u32[]{:S(2)}, u32[]{:S(2)}) collective-permute-start(bf16[4,48,1536]{2,1,0:T(8,128)(2,1)S(1)} %get-tuple-element.155), channel_id=1, source_target_pairs={{0,32},{4,12},{8,40},{12,20},{16,48},{20,28},{24,56},{28,4},{32,64... | collective-permute-start | bytes 1769480 | tf_op jit(solution)/shard_map/ppermute | solution.py:46
  151.1 10.7 %collective-permute-start.25 = (bf16[4,48,1536]{2,1,0:T(8,128)(2,1)S(1)}, bf16[4,48,1536]{2,1,0:T(8,128)(2,1)S(1)}, u32[]{:S(2)}, u32[]{:S(2)}) collective-permute-start(bf16[4,48,1536]{2,1,0:T(8,128)(2,1)S(1)} %get-tuple-element.156), channel_id=1, source_target_pairs={{0,96},{4,28},{8,104},{12,4},{16,112},{20,12},{24,120},{28,20},{32... | collective-permute-start | bytes 1769480 | tf_op jit(solution)/shard_map/ppermute | solution.py:46
  153.9 13.7 %collective-permute-start.27 = (bf16[4,48,1536]{2,1,0:T(8,128)(2,1)S(1)}, bf16[4,48,1536]{2,1,0:T(8,128)(2,1)S(1)}, u32[]{:S(2)}, u32[]{:S(2)}) collective-permute-start(bf16[4,48,1536]{2,1,0:T(8,128)(2,1)S(1)} %get-tuple-element.161), channel_id=1, source_target_pairs={{0,96},{4,28},{8,104},{12,4},{16,112},{20,12},{24,120},{28,20},{32... | collective-permute-start | bytes 1769480 | tf_op jit(solution)/shard_map/ppermute | solution.py:46
  154.5 13.6 %collective-permute-start.28 = (bf16[4,48,1536]{2,1,0:T(8,128)(2,1)S(1)}, bf16[4,48,1536]{2,1,0:T(8,128)(2,1)S(1)}, u32[]{:S(2)}, u32[]{:S(2)}) collective-permute-start(bf16[4,48,1536]{2,1,0:T(8,128)(2,1)S(1)} %get-tuple-element.162), channel_id=1, source_target_pairs={{0,32},{4,12},{8,40},{12,20},{16,48},{20,28},{24,56},{28,4},{32,64... | collective-permute-start | bytes 1769480 | tf_op jit(solution)/shard_map/ppermute | solution.py:46
  163.4 11.2 %collective-permute-start.26 = (bf16[4,48,1536]{2,1,0:T(8,128)(2,1)S(1)}, bf16[4,48,1536]{2,1,0:T(8,128)(2,1)S(1)}, u32[]{:S(2)}, u32[]{:S(2)}) collective-permute-start(bf16[4,48,1536]{2,1,0:T(8,128)(2,1)S(1)} %get-tuple-element.160), channel_id=1, source_target_pairs={{0,32},{4,12},{8,40},{12,20},{16,48},{20,28},{24,56},{28,4},{32,64... | collective-permute-start | bytes 1769480 | tf_op jit(solution)/shard_map/ppermute | solution.py:46
  164.2 10.3 %collective-permute-start.29 = (bf16[4,48,1536]{2,1,0:T(8,128)(2,1)S(1)}, bf16[4,48,1536]{2,1,0:T(8,128)(2,1)S(1)}, u32[]{:S(2)}, u32[]{:S(2)}) collective-permute-start(bf16[4,48,1536]{2,1,0:T(8,128)(2,1)S(1)} %get-tuple-element.163), channel_id=1, source_target_pairs={{0,96},{4,28},{8,104},{12,4},{16,112},{20,12},{24,120},{28,20},{32... | collective-permute-start | bytes 1769480 | tf_op jit(solution)/shard_map/ppermute | solution.py:46
  175.6 16.7 %copy-start.8 = (f32[48,1536]{1,0:T(8,128)S(1)}, f32[48,1536]{1,0:T(8,128)}, u32[]{:S(2)}) copy-start(f32[48,1536]{1,0:T(8,128)} %param.23) | copy-start | bytes 884740
  175.6 16.7 %copy-start.9 = (f32[48,1536]{1,0:T(8,128)S(1)}, f32[48,1536]{1,0:T(8,128)}, u32[]{:S(2)}) copy-start(f32[48,1536]{1,0:T(8,128)} %param.22) | copy-start | bytes 884740
  175.6 17.6 %copy-start.1 = (bf16[1536,3,384]{2,0,1:T(8,128)(2,1)S(1)}, bf16[1536,3,384]{2,0,1:T(8,128)(2,1)}, u32[]{:S(2)}) copy-start(bf16[1536,3,384]{2,0,1:T(8,128)(2,1)} %param.19) | copy-start | bytes 10616836

commit v8 on v6

--- a/solution.py
+++ b/solution.py
@@ -359,9 +359,16 @@
     behind2[0] = (scaled(k2, g2, u0, u1) + down[0].astype(F32)).astype(BF)
 
 
-def close_kernel(at, own, up1, down1, up2, down2, out):
-    out[0, 0] = (own[0, 0] + up1[0].astype(F32) + down1[0].astype(F32)).astype(BF)
-    out[0, 1] = (own[0, 1] + up2[0].astype(F32) + down2[0].astype(F32)).astype(BF)
+def close_kernel(at, own, up1, down1, up2, down2, own_o, ahead, far, behind):
+    first = own[0, 0] + up1[0].astype(F32) + down1[0].astype(F32)
+    second = own[0, 1] + up2[0].astype(F32) + down2[0].astype(F32)
+    step = pl.program_id(0)
+    for k, out in enumerate((far, ahead, behind, own_o)):
+
+        @pl.when(step == k)
+        def _():
+            out[0] = first.astype(out.dtype)
+            out[1] = second.astype(out.dtype)
 
 
 def ring_stage(at, u0, u1, first, second, move):
@@ -410,12 +417,14 @@
         "relay",
     )(at, u0, u1, first[0], second[0], first[1], second[1], far1, far2)
     up1, down2 = move(ahead1, 1), move(behind2, -1)
+    place = lambda s, a: a[16 + s]
     return call(
         close_kernel,
         RING,
-        [both] + [one] * 4,
-        both,
-        shaped((RING, 2, 48, ff)),
+        [pl.BlockSpec((1, 2, 48, ff), lambda s, a: (place(s, a), 0, 0, 0))]
+        + [pl.BlockSpec((1, 48, ff), lambda s, a: (place(s, a), 0, 0))] * 4,
+        [pl.BlockSpec((2, 48, ff), lambda s, *_: (0, 0, 0))] * 4,
+        [shaped((2, 48, ff), k) for k in (F32, BF, BF, BF)],
         [],
         cost(4 * size, 20 * size),
         "close",
@@ -446,12 +455,14 @@
     ahead = [(me_x + k * way) % RING for k in range(RING)]
     swapped = [me_x, me_x ^ 1, 3 - me_x, (3 - me_x) ^ 1]
     me_one = jnp.where(me_c == 0, me_y, me_z)
+    me_two = jnp.where(me_c == 0, me_z, me_y)
     stride = jnp.where(me_c == 0, 4, 1)
     at = jnp.stack(
         [b * PART for b in swapped]
         + [me_c * 48, jnp.where(me_c == 0, 1, 4), me_c * 0, me_c * 0]
         + ahead
         + [((me_one + k) % RING) * stride for k in range(RING)]
+        + [(me_two + k) % RING for k in (2, 1, 3, 0)]
     ).astype(jnp.int32)
     outs = [lax.dynamic_slice_in_dim(out_w, b * PART, PART, 0) for b in ahead]
 
@@ -563,13 +574,14 @@
     root = math.sqrt(2.0 * D * FF)
     unit = root / (jnp.sqrt(square) + 0.01)
 
-    value = ring_stage(
+    own, ahead, far, behind = ring_stage(
         at, unit, by_core(unit), (keep1, got1), (keep2, got2), lambda v, w: by_turns(v, w, True)
     )
-    groups = [[(y * RING + z) * 2 for z in range(RING)] for y in range(RING)]
-    groups += [[(y * RING + z) * 2 + 1 for y in range(RING)] for z in range(RING)]
-    got = lax.all_to_all(value, "dp", 0, 0, axis_index_groups=groups, tiled=True)
-    value = jnp.sum(got.astype(F32), 0)
+    value = own + (
+        by_turns(far, 2, False).astype(F32)
+        + by_turns(ahead, 1, False).astype(F32)
+        + by_turns(behind, -1, False).astype(F32)
+    )
     return (value[0] + noise_in) / 32.0, (value[1] + noise_out) / 32.0
 
 

time: 193 us -> 193 us (level)
  blocking collectives: 16.9 us -> 0 us
  waiting for transfers between devices: 50.7 us -> 59.9 us
  starting transfers between devices: 48.8 us -> 54.8 us
    all_to_all x1 -> x0, blocking collectives: 16.9 us -> none  [local(): lax.all_to_all(value, 'dp', 0, 0, axis_index_groups=groups, tiled=True)]
    ppermute x9 -> x12, waiting for transfers between devices: 13.8 us -> 23 us  [by_dp(): return lax.ppermute(value, 'dp', pairs)]
    ppermute x9 -> x12, starting transfers between devices: 9.36 us -> 15.3 us  [by_dp(): return lax.ppermute(value, 'dp', pairs)]
  transfers between devices with their start and end apart: 31 -> 34, of which waited for: 18 -> 20; matrix products, arithmetic and copies ran while one was open for 10% -> 10% of each run, Pallas kernels for 12% -> 12%
where the time goes in v8:
time: 193 us; the launch traced here: 192 us
  waiting for transfers between devices  59.9 us (31%)
  starting transfers between devices  54.8 us (28%)
  Pallas kernels  48.3 us (25%)
  matrix products  12 us (6%)
  local copies, waits for them, and re-layouts  7.24 us (4%)
  other arithmetic  6.78 us (4%)
  between operations  3.24 us (2%)
    ppermute x12, waiting for transfers between devices, by_dp(): return lax.ppermute(value, 'dp', pairs)  23 us
    ppermute x15, starting transfers between devices, by_x(): return lax.ppermute(value, ('dp', 'mp'), pairs)  19.3 us
    ppermute x15, waiting for transfers between devices, by_x(): return lax.ppermute(value, ('dp', 'mp'), pairs)  17.4 us
    ppermute x6, waiting for transfers between devices, swap_x(): return lax.ppermute(value, 'mp', list(enumerate(other)))  16.5 us
    pallas_call x2, Pallas kernels, forward(): call(forward_kernel, ff // WIDE, [piece] * 4 + [whole((3, PART)), whole((...  15.8 us
    ppermute x12, starting transfers between devices, by_dp(): return lax.ppermute(value, 'dp', pairs)  15.3 us
    ppermute x6, starting transfers between devices, swap_x(): return lax.ppermute(value, 'mp', list(enumerate(other)))  11.7 us
    all_to_all x1, starting transfers between devices, local(): received = lax.all_to_all(everywhere, 'dp', 0, 0, tiled=True)  8.54 us
  transfers between devices with their start and end apart: 34, of which 20 were waited for; matrix products, arithmetic and copies ran while one was open for 10% of the time, Pallas kernels for 12%

profile of v8, /device:TPU:0, one launch (start us, length us, event | category | flops | bytes accessed | tf_op | source)
XLA Modules:
  0.0 192.2 jit_solution(6841624173379400287)
XLA Ops:
  0.6 1.6 collective-permute-start
  2.3 1.7 collective-permute-start.1
  6.4 8.5 %all-to-all-start = ((f32[32,8,128]{2,1,0:T(8,128)}), f32[32,8,128]{2,1,0:T(8,128)}, u32[]{:S(2)}, u32[]{:S(2)}) async-start(f32[32,8,128]{2,1,0:T(8,128)} %broadcast_in_dim.31), calls=%async_computation | async-start | bytes 262144 | tf_op jit(solution)/shard_map/all_to_all | solution.py:474
  15.1 4.6 %constant_dynamic-slice_fusion = (bf16[384,1536]{1,0:T(8,128)(2,1)}, bf16[384,1536]{1,0:T(8,128)(2,1)}, bf16[384,1536]{1,0:T(8,128)(2,1)}, bf16[384,1536]{1,0:T(8,128)(2,1)}) fusion(bf16[1536,1536]{1,0:T(8,128)(2,1)} %out_w.3, s32[]{:T(128)S(6)} %select_n.136, s32[]{:T(128)S(6)} %select_n.135, s32[]{:T(128)S(6)} %select_n.134, s32[]{:T(128)S(6)} %select_n.133), kind=kLoop, calls=%fused_computation.51 | loop fusion | bytes 9437200 | tf_op jit(solution)/shard_map/dynamic_slice | solution.py:467
  19.7 3.0 %all-to-all-done = f32[32,8,128]{2,1,0:T(8,128)} async-done(((f32[32,8,128]{2,1,0:T(8,128)}), f32[32,8,128]{2,1,0:T(8,128)}, u32[]{:S(2)}, u32[]{:S(2)}) %all-to-all-start) | async-done | bytes 131104 | tf_op jit(solution)/shard_map/all_to_all | solution.py:474
  24.1 2.4 %fusion.27 = f32[1,1536]{1,0:T(1,128)S(1)} fusion(bf16[1024,1]{0,1:T(2,128)(2,1)S(1)} %reshape.95, bf16[1024,1536]{1,0:T(8,128)(2,1)} %param.18), kind=kOutput, calls=%fused_computation.60 | convolution fusion | flops 3145728 | bytes 3153920 | tf_op jit(solution)/shard_map/dot_general | solution.py:24
  26.5 1.5 collective-permute-start.2
  28.7 4.3 %collective-permute-done.2 = f32[1,1536]{1,0:T(1,128)S(1)} collective-permute-done((f32[1,1536]{1,0:T(1,128)S(1)}, f32[1,1536]{1,0:T(1,128)S(1)}, u32[]{:S(2)}, u32[]{:S(2)}) %collective-permute-start.2) | collective-permute-done | bytes 6176 | tf_op jit(solution)/shard_map/ppermute | solution.py:62
  33.0 3.9 %collective-permute-start.3 = (f32[1,1536]{1,0:T(1,128)S(1)}, f32[1,1536]{1,0:T(1,128)S(1)}, u32[]{:S(2)}, u32[]{:S(2)}) collective-permute-start(f32[1,1536]{1,0:T(1,128)S(1)} %add.228), channel_id=1, source_target_pairs={{0,3},{1,2},{2,1},{3,0},{4,7},{5,6},{6,5},{7,4},{8,11},{9,10},{10,... | collective-permute-start | bytes 18440 | tf_op jit(solution)/shard_map/ppermute | solution.py:62
  36.9 1.6 collective-permute-done.3
  41.4 2.9 %collective-permute-done.5.m1 = f32[3,384]{1,0:T(4,128)S(1)} collective-permute-done((f32[3,384]{1,0:T(4,128)S(1)}, f32[3,384]{1,0:T(4,128)S(1)}, u32[]{:S(2)}, u32[]{:S(2)}) %collective-permute-start.5) | collective-permute-done | bytes 4640 | tf_op jit(solution)/shard_map/ppermute | solution.py:62
  44.3 3.3 %collective-permute-start.6 = (f32[6,384]{1,0:T(8,128)S(1)}, f32[6,384]{1,0:T(8,128)S(1)}, u32[]{:S(2)}, u32[]{:S(2)}) collective-permute-start(f32[6,384]{1,0:T(8,128)S(1)} %pad_maximum_fusion), channel_id=1, source_target_pairs={{0,3},{1,2},{2,1},{3,0},{4,7},{5,6},{6,5},{7,4},{8,11},{9,10},{10,... | collective-permute-start | bytes 27656 | tf_op jit(solution)/shard_map/ppermute | solution.py:62
  47.7 1.6 collective-permute-done.6.m2
  49.3 7.9 %forward.2 = (bf16[512,1536]{1,0:T(8,128)(2,1)S(1)}, bf16[512,1536]{1,0:T(8,128)(2,1)S(1)}, f32[512,1536]{1,0:T(8,128)S(1)}) custom-call(s32[20]{0:T(128)S(1)} %stack.75.at.refs_0_, bf16[1024,384]{1,0:T(8,128)(2,1)} %x0.3, bf16[1024,384]{1,0:T(8,128)(2,1)} %collective-permute-done.1.x1, bf16[1024,384]{1,0:T(8,128)(2,1)} %copy-done.10, ...), custom_call_target="tpu_custom_call" | custom-call | flops 2415919104 | bytes 12000000 | tf_op jit(solution)/shard_map/forward/pallas_call | solution.py:137
  59.6 3.5 %collective-permute-start.8 = (bf16[512,384]{1,0:T(8,128)(2,1)S(1)}, bf16[512,384]{1,0:T(8,128)(2,1)S(1)}, u32[]{:S(2)}, u32[]{:S(2)}) collective-permute-start(bf16[512,384]{1,0:T(8,128)(2,1)S(1)} %convolution_convert_fusion.3), channel_id=1, source_target_pairs={{0,3},{1,0},{2,1},{3,2},{4,5},{5,6},{6,7},{7,4},{8,11},{9,8},{10,9... | collective-permute-start | bytes 1179656 | tf_op jit(solution)/shard_map/ppermute | solution.py:36
  64.0 7.9 %forward.3 = (bf16[512,1536]{1,0:T(8,128)(2,1)S(1)}, bf16[512,1536]{1,0:T(8,128)(2,1)S(1)}, f32[512,1536]{1,0:T(8,128)S(1)}) custom-call(s32[20]{0:T(128)S(1)} %stack.75.at.refs_0_, bf16[1024,384]{1,0:T(8,128)(2,1)} %x0.3, bf16[1024,384]{1,0:T(8,128)(2,1)} %collective-permute-done.1.x1, bf16[1024,384]{1,0:T(8,128)(2,1)} %copy-done.10, ...), custom_call_target="tpu_custom_call" | custom-call | flops 2415919104 | bytes 12000000 | tf_op jit(solution)/shard_map/forward/pallas_call | solution.py:137
  75.3 3.1 %collective-permute-start.10 = (bf16[512,384]{1,0:T(8,128)(2,1)S(1)}, bf16[512,384]{1,0:T(8,128)(2,1)S(1)}, u32[]{:S(2)}, u32[]{:S(2)}) collective-permute-start(bf16[512,384]{1,0:T(8,128)(2,1)S(1)} %convolution_convert_fusion.1), channel_id=1, source_target_pairs={{0,3},{1,0},{2,1},{3,2},{4,5},{5,6},{6,7},{7,4},{8,11},{9,8},{10,9... | collective-permute-start | bytes 1179656 | tf_op jit(solution)/shard_map/ppermute | solution.py:36
  78.4 7.9 %collective-permute-done.9 = bf16[512,384]{1,0:T(8,128)(2,1)S(1)} collective-permute-done((bf16[512,384]{1,0:T(8,128)(2,1)S(1)}, bf16[512,384]{1,0:T(8,128)(2,1)S(1)}, u32[]{:S(2)}, u32[]{:S(2)}) %collective-permute-start.9) | collective-permute-done | bytes 393248 | tf_op jit(solution)/shard_map/ppermute | solution.py:36
  86.8 3.2 %collective-permute-start.13 = (bf16[512,384]{1,0:T(8,128)(2,1)S(1)}, bf16[512,384]{1,0:T(8,128)(2,1)S(1)}, u32[]{:S(2)}, u32[]{:S(2)}) collective-permute-start(bf16[512,384]{1,0:T(8,128)(2,1)S(1)} %multiply_convert_fusion.1.b0.refs_1_), channel_id=1, source_target_pairs={{0,3},{1,0},{2,1},{3,2},{4,5},{5,6},{6,7},{7,4},{8,11},{9,8},{10,9... | collective-permute-start | bytes 1179656 | tf_op jit(solution)/shard_map/ppermute | solution.py:36
  92.2 3.2 %add_convert_fusion = (bf16[512,1536]{1,0:T(8,128)(2,1)S(1)}, bf16[512,1536]{1,0:T(8,128)(2,1)S(1)}) fusion(f32[512,1536]{1,0:T(8,128)S(1)} %get-tuple-element.103, f32[512,1536]{1,0:T(8,128)S(1)} %get-tuple-element.102), kind=kLoop, calls=%fused_computation | loop fusion | flops 23592960 | bytes 9437184 | tf_op jit(solution)/shard_map/convert_element_type | solution.py:546
  95.4 2.2 %turn.1 = (bf16[768,1024]{1,0:T(8,128)(2,1)S(1)}, bf16[768,1024]{1,0:T(8,128)(2,1)S(1)}) custom-call(s32[20]{0:T(128)S(1)} %stack.75.at.refs_0_, bf16[512,1536]{1,0:T(8,128)(2,1)S(1)} %get-tuple-element.105.top, bf16[512,1536]{1,0:T(8,128)(2,1)S(1)} %get-tuple-element.106.low), custom_call_target="tpu_custom_call" | custom-call | flops 1572864 | bytes 6291456 | tf_op jit(solution)/shard_map/turn/pallas_call | solution.py:166
  97.6 2.3 %collective-permute-done.11 = bf16[512,384]{1,0:T(8,128)(2,1)S(1)} collective-permute-done((bf16[512,384]{1,0:T(8,128)(2,1)S(1)}, bf16[512,384]{1,0:T(8,128)(2,1)S(1)}, u32[]{:S(2)}, u32[]{:S(2)}) %collective-permute-start.11) | collective-permute-done | bytes 393248 | tf_op jit(solution)/shard_map/ppermute | solution.py:36
  101.5 3.5 %collective-permute-start.16 = (bf16[512,384]{1,0:T(8,128)(2,1)S(1)}, bf16[512,384]{1,0:T(8,128)(2,1)S(1)}, u32[]{:S(2)}, u32[]{:S(2)}) collective-permute-start(bf16[512,384]{1,0:T(8,128)(2,1)S(1)} %multiply_convert_fusion.refs_2_.b0), channel_id=1, source_target_pairs={{0,3},{1,0},{2,1},{3,2},{4,5},{5,6},{6,7},{7,4},{8,11},{9,8},{10,9... | collective-permute-start | bytes 1179656 | tf_op jit(solution)/shard_map/ppermute | solution.py:36
  105.0 2.0 %rows_grad.4 = (bf16[768,1536]{1,0:T(8,128)(2,1)S(1)}, bf16[768,1536]{1,0:T(8,128)(2,1)S(1)}, f32[1,1536]{1,0:T(1,128)S(1)}) custom-call(s32[20]{0:T(128)S(1)} %stack.75.at.refs_0_, bf16[512,384]{1,0:T(8,128)(2,1)S(1)} %multiply_convert_fusion.1.b0.refs_1_, bf16[512,384]{1,0:T(8,128)(2,1)S(1)} %multiply_convert_fusion.refs_2_.b0, ...), custom_call_target="tpu_custom_call" | custom-call | flops 1207959552 | bytes 5000000 | tf_op jit(solution)/shard_map/rows_grad/pallas_call | solution.py:287
  107.0 2.4 %rows_partial.1.refs_3_ = f32[768,1536]{1,0:T(8,128)S(1)} custom-call(s32[20]{0:T(128)S(1)} %stack.75.at.refs_0_, bf16[512,384]{1,0:T(8,128)(2,1)S(1)} %collective-permute-done.13.b1.refs_1_, bf16[512,384]{1,0:T(8,128)(2,1)S(1)} %collective-permute-done.12.b3.refs_2_, bf16[512,1536]{1,0:T(8,128)(2,1)S(1)} %get-tuple-element.95.refs_3_), custom_call_target="tpu_custom_call" | custom-call | flops 1207959552 | bytes 8000000 | tf_op jit(solution)/shard_map/rows_partial/pallas_call | solution.py:238
  109.4 2.6 %collective-permute-done.15.b2.refs_1_ = bf16[512,384]{1,0:T(8,128)(2,1)S(1)} collective-permute-done((bf16[512,384]{1,0:T(8,128)(2,1)S(1)}, bf16[512,384]{1,0:T(8,128)(2,1)S(1)}, u32[]{:S(2)}, u32[]{:S(2)}) %collective-permute-start.15) | collective-permute-done | bytes 393248 | tf_op jit(solution)/shard_map/ppermute | solution.py:36
  112.1 1.9 %collective-permute-start.17 = (bf16[512,384]{1,0:T(8,128)(2,1)S(1)}, bf16[512,384]{1,0:T(8,128)(2,1)S(1)}, u32[]{:S(2)}, u32[]{:S(2)}) collective-permute-start(bf16[512,384]{1,0:T(8,128)(2,1)S(1)} %collective-permute-done.16.b1.refs_1_), channel_id=1, source_target_pairs={{0,3},{1,0},{2,1},{3,2},{4,5},{5,6},{6,7},{7,4},{8,11},{9,8},{10,9... | collective-permute-start | bytes 1179656 | tf_op jit(solution)/shard_map/ppermute | solution.py:36
  114.1 1.4 rows_grad.5
  115.5 4.2 %backward.2.right0 = bf16[512,1536]{1,0:T(8,128)(2,1)S(1)} custom-call(s32[20]{0:T(128)S(1)} %stack.75.at.refs_0_, bf16[512,384]{1,0:T(8,128)(2,1)S(1)} %multiply_convert_fusion.1.b0.refs_1_, bf16[512,384]{1,0:T(8,128)(2,1)S(1)} %collective-permute-done.13.b1.refs_1_, bf16[512,384]{1,0:T(8,128)(2,1)S(1)} %collective-permute-done.15.b2.refs_1_, ...), custom_call_target="tpu_custom_call" | custom-call | flops 2415919104 | bytes 14000000 | tf_op jit(solution)/shard_map/backward/pallas_call | solution.py:189
  119.7 3.2 %collective-permute-done.17.b2.refs_2_ = bf16[512,384]{1,0:T(8,128)(2,1)S(1)} collective-permute-done((bf16[512,384]{1,0:T(8,128)(2,1)S(1)}, bf16[512,384]{1,0:T(8,128)(2,1)S(1)}, u32[]{:S(2)}, u32[]{:S(2)}) %collective-permute-start.17) | collective-permute-done | bytes 393248 | tf_op jit(solution)/shard_map/ppermute | solution.py:36
  123.0 4.2 %backward.3.right1 = bf16[512,1536]{1,0:T(8,128)(2,1)S(1)} custom-call(s32[20]{0:T(128)S(1)} %stack.75.at.refs_0_, bf16[512,384]{1,0:T(8,128)(2,1)S(1)} %multiply_convert_fusion.refs_2_.b0, bf16[512,384]{1,0:T(8,128)(2,1)S(1)} %collective-permute-done.16.b1.refs_1_, bf16[512,384]{1,0:T(8,128)(2,1)S(1)} %collective-permute-done.17.b2.refs_2_, ...), custom_call_target="tpu_custom_call" | custom-call | flops 2415919104 | bytes 14000000 | tf_op jit(solution)/shard_map/backward/pallas_call | solution.py:189
  128.6 2.0 %rows_grad.7 = (bf16[768,1536]{1,0:T(8,128)(2,1)S(1)}, bf16[768,1536]{1,0:T(8,128)(2,1)S(1)}, f32[1,1536]{1,0:T(1,128)S(1)}) custom-call(s32[20]{0:T(128)S(1)} %stack.75.at.refs_0_, bf16[512,384]{1,0:T(8,128)(2,1)S(1)} %collective-permute-done.15.b2.refs_1_, ...), custom_call_target="tpu_custom_call", output_to_operand_aliasing={{0}: (5, {}), {1}: (6, {})} | custom-call | flops 1207959552 | bytes 5000000 | tf_op jit(solution)/shard_map/rows_grad/pallas_call | solution.py:287
  130.5 6.7 %weight_grad.1 = (bf16[768,1536]{1,0:T(8,128)(2,1)S(1)}, bf16[768,1536]{1,0:T(8,128)(2,1)S(1)}, f32[1,128]{1,0:T(1,128)S(1)}) custom-call(s32[20]{0:T(128)S(1)} %stack.75.at.refs_0_, bf16[768,1024]{1,0:T(8,128)(2,1)S(1)} %get-tuple-element.110.keep_l, bf16[768,1024]{1,0:T(8,128)(2,1)S(1)} %get-tuple-element.111.send_l, ...), custom_call_target="tpu_custom_call" | custom-call | flops 4831838208 | bytes 11000000 | tf_op jit(solution)/shard_map/weight_grad/pallas_call | solution.py:329
  138.0 3.3 %collective-permute-done.19 = f32[1,128]{1,0:T(1,128)S(1)} collective-permute-done((f32[1,128]{1,0:T(1,128)S(1)}, f32[1,128]{1,0:T(1,128)S(1)}, u32[]{:S(2)}, u32[]{:S(2)}) %collective-permute-start.19) | collective-permute-done | bytes 544 | tf_op jit(solution)/shard_map/ppermute | solution.py:62
  141.4 2.0 %collective-permute-start.20 = (f32[1,128]{1,0:T(1,128)S(1)}, f32[1,128]{1,0:T(1,128)S(1)}, u32[]{:S(2)}, u32[]{:S(2)}) collective-permute-start(f32[1,128]{1,0:T(1,128)S(1)} %add.252), channel_id=1, source_target_pairs={{0,3},{1,2},{2,1},{3,0},{4,7},{5,6},{6,5},{7,4},{8,11},{9,10},{10,... | collective-permute-start | bytes 1544 | tf_op jit(solution)/shard_map/ppermute | solution.py:62
  143.4 2.7 %collective-permute-done.20 = f32[1,128]{1,0:T(1,128)S(1)} collective-permute-done((f32[1,128]{1,0:T(1,128)S(1)}, f32[1,128]{1,0:T(1,128)S(1)}, u32[]{:S(2)}, u32[]{:S(2)}) %collective-permute-start.20) | collective-permute-done | bytes 544 | tf_op jit(solution)/shard_map/ppermute | solution.py:62
  147.3 1.9 spread.1
  150.5 2.0 %collective-permute-start.25 = (bf16[4,48,1536]{2,1,0:T(8,128)(2,1)S(1)}, bf16[4,48,1536]{2,1,0:T(8,128)(2,1)S(1)}, u32[]{:S(2)}, u32[]{:S(2)}) collective-permute-start(bf16[4,48,1536]{2,1,0:T(8,128)(2,1)S(1)} %get-tuple-element.140), channel_id=1, source_target_pairs={{0,96},{4,28},{8,104},{12,4},{16,112},{20,12},{24,120},{28,20},{32... | collective-permute-start | bytes 1769480 | tf_op jit(solution)/shard_map/ppermute | solution.py:46
  152.6 1.5 collective-permute-start.27
  156.0 4.4 %collective-permute-done.24.up = bf16[4,48,1536]{2,1,0:T(8,128)(2,1)S(1)} collective-permute-done((bf16[4,48,1536]{2,1,0:T(8,128)(2,1)S(1)}, bf16[4,48,1536]{2,1,0:T(8,128)(2,1)S(1)}, u32[]{:S(2)}, u32[]{:S(2)}) %collective-permute-start.24) | collective-permute-done | bytes 589856 | tf_op jit(solution)/shard_map/ppermute | solution.py:46
  160.4 1.6 relay.1
  162.1 1.6 collective-permute-start.26
  163.7 1.7 collective-permute-start.29
  166.8 6.5 %collective-permute-done.26.up1 = bf16[4,48,1536]{2,1,0:T(8,128)(2,1)S(1)} collective-permute-done((bf16[4,48,1536]{2,1,0:T(8,128)(2,1)S(1)}, bf16[4,48,1536]{2,1,0:T(8,128)(2,1)S(1)}, u32[]{:S(2)}, u32[]{:S(2)}) %collective-permute-start.26) | collective-permute-done | bytes 589856 | tf_op jit(solution)/shard_map/ppermute | solution.py:46
  174.8 4.1 %collective-permute-start.32 = (bf16[2,48,1536]{2,1,0:T(8,128)(2,1)S(1)}, bf16[2,48,1536]{2,1,0:T(8,128)(2,1)S(1)}, u32[]{:S(2)}, u32[]{:S(2)}) collective-permute-start(bf16[2,48,1536]{2,1,0:T(8,128)(2,1)S(1)} %get-tuple-element.151), channel_id=1, source_target_pairs={{0,24},{4,100},{8,0},{12,108},{16,8},{20,116},{24,16},{28,124},{32... | collective-permute-start | bytes 884744 | tf_op jit(solution)/shard_map/ppermute | solution.py:46
  178.9 1.9 collective-permute-start.30
  180.8 2.4 %collective-permute-done.32 = bf16[2,48,1536]{2,1,0:T(8,128)(2,1)S(1)} collective-permute-done((bf16[2,48,1536]{2,1,0:T(8,128)(2,1)S(1)}, bf16[2,48,1536]{2,1,0:T(8,128)(2,1)S(1)}, u32[]{:S(2)}, u32[]{:S(2)}) %collective-permute-start.32) | collective-permute-done | bytes 294944 | tf_op jit(solution)/shard_map/ppermute | solution.py:46
  183.2 6.9 %collective-permute-done.31 = bf16[2,48,1536]{2,1,0:T(8,128)(2,1)S(1)} collective-permute-done((bf16[2,48,1536]{2,1,0:T(8,128)(2,1)S(1)}, bf16[2,48,1536]{2,1,0:T(8,128)(2,1)S(1)}, u32[]{:S(2)}, u32[]{:S(2)}) %collective-permute-start.31) | collective-permute-done | bytes 294944 | tf_op jit(solution)/shard_map/ppermute | solution.py:46
  (99 shorter events, 28.1 us)
Async XLA Ops:
  0.6 39.4 %copy-start = (bf16[1536,3,384]{2,0,1:T(8,128)(2,1)S(1)}, bf16[1536,3,384]{2,0,1:T(8,128)(2,1)}, u32[]{:S(2)}) copy-start(bf16[1536,3,384]{2,0,1:T(8,128)(2,1)} %param.19) | copy-start | bytes 10616836
  0.6 22.1 %collective-permute-start = (bf16[1024,384]{1,0:T(8,128)(2,1)}, bf16[1024,384]{1,0:T(8,128)(2,1)}, u32[]{:S(2)}, u32[]{:S(2)}) collective-permute-start(bf16[1024,384]{1,0:T(8,128)(2,1)} %x0.3), channel_id=1, source_target_pairs={{0,1},{1,2},{2,3},{3,0},{4,7},{5,4},{6,5},{7,6},{8,9},{9,10},{10,1... | collective-permute-start | bytes 2359304 | tf_op jit(solution)/shard_map/ppermute | solution.py:36
  2.3 20.5 %collective-permute-start.1 = (bf16[1024,384]{1,0:T(8,128)(2,1)}, bf16[1024,384]{1,0:T(8,128)(2,1)}, u32[]{:S(2)}, u32[]{:S(2)}) collective-permute-start(bf16[1024,384]{1,0:T(8,128)(2,1)} %x0.3), channel_id=1, source_target_pairs={{0,3},{1,0},{2,1},{3,2},{4,5},{5,6},{6,7},{7,4},{8,11},{9,8},{10,9... | collective-permute-start | bytes 2359304 | tf_op jit(solution)/shard_map/ppermute | solution.py:36
  6.4 16.4 %all-to-all-start = ((f32[32,8,128]{2,1,0:T(8,128)}), f32[32,8,128]{2,1,0:T(8,128)}, u32[]{:S(2)}, u32[]{:S(2)}) async-start(f32[32,8,128]{2,1,0:T(8,128)} %broadcast_in_dim.31), calls=%async_computation | async-start | bytes 262144 | tf_op jit(solution)/shard_map/all_to_all | solution.py:474
  15.0 8.0 %copy-start.11 = (s32[32]{0:T(128)S(1)}, s32[32]{0:T(128)}, u32[]{:S(2)}) copy-start(s32[32]{0:T(128)} %param.17) | copy-start | bytes 388
  22.8 15.7 %collective-permute-start.4 = (bf16[1024,384]{1,0:T(8,128)(2,1)}, bf16[1024,384]{1,0:T(8,128)(2,1)S(1)}, u32[]{:S(2)}, u32[]{:S(2)}) collective-permute-start(bf16[1024,384]{1,0:T(8,128)(2,1)} %collective-permute-done.x3), channel_id=1, source_target_pairs={{0,1},{1,2},{2,3},{3,0},{4,7},{5,4},{6,5},{7,6},{8,9},{9,10},{10,1... | collective-permute-start | bytes 2359304 | tf_op jit(solution)/shard_map/ppermute | solution.py:36
  26.5 6.5 %collective-permute-start.2 = (f32[1,1536]{1,0:T(1,128)S(1)}, f32[1,1536]{1,0:T(1,128)S(1)}, u32[]{:S(2)}, u32[]{:S(2)}) collective-permute-start(f32[1,1536]{1,0:T(1,128)S(1)} %fusion.27), channel_id=1, source_target_pairs={{0,1},{1,0},{2,3},{3,2},{4,5},{5,4},{6,7},{7,6},{8,9},{9,8},{10,11... | collective-permute-start | bytes 18440 | tf_op jit(solution)/shard_map/ppermute | solution.py:62
  33.0 5.5 %collective-permute-start.3 = (f32[1,1536]{1,0:T(1,128)S(1)}, f32[1,1536]{1,0:T(1,128)S(1)}, u32[]{:S(2)}, u32[]{:S(2)}) collective-permute-start(f32[1,1536]{1,0:T(1,128)S(1)} %add.228), channel_id=1, source_target_pairs={{0,3},{1,2},{2,1},{3,0},{4,7},{5,6},{6,5},{7,4},{8,11},{9,10},{10,... | collective-permute-start | bytes 18440 | tf_op jit(solution)/shard_map/ppermute | solution.py:62
  38.5 0.9 copy-start.10
  40.6 3.7 %collective-permute-start.5 = (f32[3,384]{1,0:T(4,128)S(1)}, f32[3,384]{1,0:T(4,128)S(1)}, u32[]{:S(2)}, u32[]{:S(2)}) collective-permute-start(f32[3,384]{1,0:T(4,128)S(1)} %bitcast.78), channel_id=1, source_target_pairs={{0,1},{1,0},{2,3},{3,2},{4,5},{5,4},{6,7},{7,6},{8,9},{9,8},{10,11... | collective-permute-start | bytes 13832 | tf_op jit(solution)/shard_map/ppermute | solution.py:62
  44.3 5.0 %collective-permute-start.6 = (f32[6,384]{1,0:T(8,128)S(1)}, f32[6,384]{1,0:T(8,128)S(1)}, u32[]{:S(2)}, u32[]{:S(2)}) collective-permute-start(f32[6,384]{1,0:T(8,128)S(1)} %pad_maximum_fusion), channel_id=1, source_target_pairs={{0,3},{1,2},{2,1},{3,0},{4,7},{5,6},{6,5},{7,4},{8,11},{9,10},{10,... | collective-permute-start | bytes 27656 | tf_op jit(solution)/shard_map/ppermute | solution.py:62
  47.7 9.6 %copy-start.3 = (bf16[384,1536]{1,0:T(8,128)(2,1)S(1)}, bf16[384,1536]{1,0:T(8,128)(2,1)}, u32[]{:S(2)}) copy-start(bf16[384,1536]{1,0:T(8,128)(2,1)} %get-tuple-element.85) | copy-start | bytes 3538948
  57.2 1.3 copy-start.5
  58.5 4.6 %copy-start.4 = (bf16[384,1536]{1,0:T(8,128)(2,1)S(1)}, bf16[384,1536]{1,0:T(8,128)(2,1)}, u32[]{:S(2)}) copy-start(bf16[384,1536]{1,0:T(8,128)(2,1)} %get-tuple-element.84) | copy-start | bytes 3538948
  59.5 12.4 %collective-permute-start.7 = (bf16[512,384]{1,0:T(8,128)(2,1)S(1)}, bf16[512,384]{1,0:T(8,128)(2,1)S(1)}, u32[]{:S(2)}, u32[]{:S(2)}) collective-permute-start(bf16[512,384]{1,0:T(8,128)(2,1)S(1)} %convolution_convert_fusion.2), channel_id=1, source_target_pairs={{0,1},{1,2},{2,3},{3,0},{4,7},{5,4},{6,5},{7,6},{8,9},{9,10},{10,1... | collective-permute-start | bytes 1179656 | tf_op jit(solution)/shard_map/ppermute | solution.py:36
  59.6 12.4 %collective-permute-start.8 = (bf16[512,384]{1,0:T(8,128)(2,1)S(1)}, bf16[512,384]{1,0:T(8,128)(2,1)S(1)}, u32[]{:S(2)}, u32[]{:S(2)}) collective-permute-start(bf16[512,384]{1,0:T(8,128)(2,1)S(1)} %convolution_convert_fusion.3), channel_id=1, source_target_pairs={{0,3},{1,0},{2,1},{3,2},{4,5},{5,6},{6,7},{7,4},{8,11},{9,8},{10,9... | collective-permute-start | bytes 1179656 | tf_op jit(solution)/shard_map/ppermute | solution.py:36
  73.0 1.3 copy-start.2
  73.0 13.3 %collective-permute-start.9 = (bf16[512,384]{1,0:T(8,128)(2,1)S(1)}, bf16[512,384]{1,0:T(8,128)(2,1)S(1)}, u32[]{:S(2)}, u32[]{:S(2)}) collective-permute-start(bf16[512,384]{1,0:T(8,128)(2,1)S(1)} %add_convert_fusion.3), channel_id=1, source_target_pairs={{0,1},{1,2},{2,3},{3,0},{4,7},{5,4},{6,5},{7,6},{8,9},{9,10},{10,1... | collective-permute-start | bytes 1179656 | tf_op jit(solution)/shard_map/ppermute | solution.py:36
  74.3 12.1 %copy-start.6 = (bf16[1024,384]{1,0:T(8,128)(2,1)S(1)}, bf16[1024,384]{1,0:T(8,128)(2,1)}, u32[]{:S(2)}) copy-start(bf16[1024,384]{1,0:T(8,128)(2,1)} %x0.3) | copy-start | bytes 2359300
  74.3 12.1 %copy-start.7 = (bf16[1024,384]{1,0:T(8,128)(2,1)S(1)}, bf16[1024,384]{1,0:T(8,128)(2,1)}, u32[]{:S(2)}) copy-start(bf16[1024,384]{1,0:T(8,128)(2,1)} %param.13) | copy-start | bytes 2359300
  75.3 16.7 %collective-permute-start.10 = (bf16[512,384]{1,0:T(8,128)(2,1)S(1)}, bf16[512,384]{1,0:T(8,128)(2,1)S(1)}, u32[]{:S(2)}, u32[]{:S(2)}) collective-permute-start(bf16[512,384]{1,0:T(8,128)(2,1)S(1)} %convolution_convert_fusion.1), channel_id=1, source_target_pairs={{0,3},{1,0},{2,1},{3,2},{4,5},{5,6},{6,7},{7,4},{8,11},{9,8},{10,9... | collective-permute-start | bytes 1179656 | tf_op jit(solution)/shard_map/ppermute | solution.py:36
  78.4 22.7 %collective-permute-start.14 = (bf16[512,384]{1,0:T(8,128)(2,1)S(1)}, bf16[512,384]{1,0:T(8,128)(2,1)S(1)}, u32[]{:S(2)}, u32[]{:S(2)}) collective-permute-start(bf16[512,384]{1,0:T(8,128)(2,1)S(1)} %convolution_convert_fusion), channel_id=1, source_target_pairs={{0,1},{1,2},{2,3},{3,0},{4,7},{5,4},{6,5},{7,6},{8,9},{9,10},{10,1... | collective-permute-start | bytes 1179656 | tf_op jit(solution)/shard_map/ppermute | solution.py:36
  86.7 14.4 %collective-permute-start.12 = (bf16[512,384]{1,0:T(8,128)(2,1)S(1)}, bf16[512,384]{1,0:T(8,128)(2,1)S(1)}, u32[]{:S(2)}, u32[]{:S(2)}) collective-permute-start(bf16[512,384]{1,0:T(8,128)(2,1)S(1)} %multiply_convert_fusion.1.b0.refs_1_), channel_id=1, source_target_pairs={{0,1},{1,2},{2,3},{3,0},{4,7},{5,4},{6,5},{7,6},{8,9},{9,10},{10,1... | collective-permute-start | bytes 1179656 | tf_op jit(solution)/shard_map/ppermute | solution.py:36
  86.8 14.3 %collective-permute-start.13 = (bf16[512,384]{1,0:T(8,128)(2,1)S(1)}, bf16[512,384]{1,0:T(8,128)(2,1)S(1)}, u32[]{:S(2)}, u32[]{:S(2)}) collective-permute-start(bf16[512,384]{1,0:T(8,128)(2,1)S(1)} %multiply_convert_fusion.1.b0.refs_1_), channel_id=1, source_target_pairs={{0,3},{1,0},{2,1},{3,2},{4,5},{5,6},{6,7},{7,4},{8,11},{9,8},{10,9... | collective-permute-start | bytes 1179656 | tf_op jit(solution)/shard_map/ppermute | solution.py:36
  92.1 7.8 %collective-permute-start.11 = (bf16[512,384]{1,0:T(8,128)(2,1)S(1)}, bf16[512,384]{1,0:T(8,128)(2,1)S(1)}, u32[]{:S(2)}, u32[]{:S(2)}) collective-permute-start(bf16[512,384]{1,0:T(8,128)(2,1)S(1)} %add_convert_fusion.2), channel_id=1, source_target_pairs={{0,3},{1,0},{2,1},{3,2},{4,5},{5,6},{6,7},{7,4},{8,11},{9,8},{10,9... | collective-permute-start | bytes 1179656 | tf_op jit(solution)/shard_map/ppermute | solution.py:36
  101.1 10.9 %collective-permute-start.15 = (bf16[512,384]{1,0:T(8,128)(2,1)S(1)}, bf16[512,384]{1,0:T(8,128)(2,1)S(1)}, u32[]{:S(2)}, u32[]{:S(2)}) collective-permute-start(bf16[512,384]{1,0:T(8,128)(2,1)S(1)} %collective-permute-done.12.b3.refs_2_), channel_id=1, source_target_pairs={{0,1},{1,2},{2,3},{3,0},{4,7},{5,4},{6,5},{7,6},{8,9},{9,10},{10,1... | collective-permute-start | bytes 1179656 | tf_op jit(solution)/shard_map/ppermute | solution.py:36
  101.5 10.6 %collective-permute-start.16 = (bf16[512,384]{1,0:T(8,128)(2,1)S(1)}, bf16[512,384]{1,0:T(8,128)(2,1)S(1)}, u32[]{:S(2)}, u32[]{:S(2)}) collective-permute-start(bf16[512,384]{1,0:T(8,128)(2,1)S(1)} %multiply_convert_fusion.refs_2_.b0), channel_id=1, source_target_pairs={{0,3},{1,0},{2,1},{3,2},{4,5},{5,6},{6,7},{7,4},{8,11},{9,8},{10,9... | collective-permute-start | bytes 1179656 | tf_op jit(solution)/shard_map/ppermute | solution.py:36
  107.0 8.5 %slice-start = ((s8[4718592]{0:T(1024)(128)(4,1)}), s8[4194304]{0:T(1024)(128)(4,1)S(1)}, s32[]{:S(2)}) async-start(s8[4718592]{0:T(1024)(128)(4,1)} %bitcast.76), calls=%async_computation.1 | async-start | bytes 8388608
  112.1 10.8 %collective-permute-start.17 = (bf16[512,384]{1,0:T(8,128)(2,1)S(1)}, bf16[512,384]{1,0:T(8,128)(2,1)S(1)}, u32[]{:S(2)}, u32[]{:S(2)}) collective-permute-start(bf16[512,384]{1,0:T(8,128)(2,1)S(1)} %collective-permute-done.16.b1.refs_1_), channel_id=1, source_target_pairs={{0,3},{1,0},{2,1},{3,2},{4,5},{5,6},{6,7},{7,4},{8,11},{9,8},{10,9... | collective-permute-start | bytes 1179656 | tf_op jit(solution)/shard_map/ppermute | solution.py:36
  114.0 9.0 %collective-permute-start.18 = (bf16[512,384]{1,0:T(8,128)(2,1)S(1)}, bf16[512,384]{1,0:T(8,128)(2,1)S(1)}, u32[]{:S(2)}, u32[]{:S(2)}) collective-permute-start(bf16[512,384]{1,0:T(8,128)(2,1)S(1)} %multiply_convert_fusion.refs_2_.b0), channel_id=1, source_target_pairs={{0,1},{1,2},{2,3},{3,0},{4,7},{5,4},{6,5},{7,6},{8,9},{9,10},{10,1... | collective-permute-start | bytes 1179656 | tf_op jit(solution)/shard_map/ppermute | solution.py:36
  114.1 1.4 slice-start.1
  137.2 10.1 %collective-permute-start.22 = (bf16[768,1536]{1,0:T(8,128)(2,1)S(1)}, bf16[768,1536]{1,0:T(8,128)(2,1)S(1)}, u32[]{:S(2)}, u32[]{:S(2)}) collective-permute-start(bf16[768,1536]{1,0:T(8,128)(2,1)S(1)} %get-tuple-element.137), channel_id=1, source_target_pairs={{0,4},{4,0},{8,12},{12,8},{16,20},{20,16},{24,28},{28,24},{32,36},... | collective-permute-start | bytes 7077896 | tf_op jit(solution)/shard_map/ppermute | solution.py:46
  137.3 10.0 %collective-permute-start.23 = (bf16[768,1536]{1,0:T(8,128)(2,1)S(1)}, bf16[768,1536]{1,0:T(8,128)(2,1)S(1)}, u32[]{:S(2)}, u32[]{:S(2)}) collective-permute-start(bf16[768,1536]{1,0:T(8,128)(2,1)S(1)} %get-tuple-element.138), channel_id=1, source_target_pairs={{0,4},{4,0},{8,12},{12,8},{16,20},{20,16},{24,28},{28,24},{32,36},... | collective-permute-start | bytes 7077896 | tf_op jit(solution)/shard_map/ppermute | solution.py:46
  137.8 3.5 %collective-permute-start.19 = (f32[1,128]{1,0:T(1,128)S(1)}, f32[1,128]{1,0:T(1,128)S(1)}, u32[]{:S(2)}, u32[]{:S(2)}) collective-permute-start(f32[1,128]{1,0:T(1,128)S(1)} %get-tuple-element.134), channel_id=1, source_target_pairs={{0,1},{1,0},{2,3},{3,2},{4,5},{5,4},{6,7},{7,6},{8,9},{9,8},{10,11... | collective-permute-start | bytes 1544 | tf_op jit(solution)/shard_map/ppermute | solution.py:62
  141.4 4.8 %collective-permute-start.20 = (f32[1,128]{1,0:T(1,128)S(1)}, f32[1,128]{1,0:T(1,128)S(1)}, u32[]{:S(2)}, u32[]{:S(2)}) collective-permute-start(f32[1,128]{1,0:T(1,128)S(1)} %add.252), channel_id=1, source_target_pairs={{0,3},{1,2},{2,1},{3,0},{4,7},{5,6},{6,5},{7,4},{8,11},{9,10},{10,... | collective-permute-start | bytes 1544 | tf_op jit(solution)/shard_map/ppermute | solution.py:62
  146.1 1.2 collective-permute-start.21
  149.2 11.2 %collective-permute-start.24 = (bf16[4,48,1536]{2,1,0:T(8,128)(2,1)S(1)}, bf16[4,48,1536]{2,1,0:T(8,128)(2,1)S(1)}, u32[]{:S(2)}, u32[]{:S(2)}) collective-permute-start(bf16[4,48,1536]{2,1,0:T(8,128)(2,1)S(1)} %get-tuple-element.139), channel_id=1, source_target_pairs={{0,32},{4,12},{8,40},{12,20},{16,48},{20,28},{24,56},{28,4},{32,64... | collective-permute-start | bytes 1769480 | tf_op jit(solution)/shard_map/ppermute | solution.py:46
  150.5 9.9 %collective-permute-start.25 = (bf16[4,48,1536]{2,1,0:T(8,128)(2,1)S(1)}, bf16[4,48,1536]{2,1,0:T(8,128)(2,1)S(1)}, u32[]{:S(2)}, u32[]{:S(2)}) collective-permute-start(bf16[4,48,1536]{2,1,0:T(8,128)(2,1)S(1)} %get-tuple-element.140), channel_id=1, source_target_pairs={{0,96},{4,28},{8,104},{12,4},{16,112},{20,12},{24,120},{28,20},{32... | collective-permute-start | bytes 1769480 | tf_op jit(solution)/shard_map/ppermute | solution.py:46
  152.6 14.2 %collective-permute-start.27 = (bf16[4,48,1536]{2,1,0:T(8,128)(2,1)S(1)}, bf16[4,48,1536]{2,1,0:T(8,128)(2,1)S(1)}, u32[]{:S(2)}, u32[]{:S(2)}) collective-permute-start(bf16[4,48,1536]{2,1,0:T(8,128)(2,1)S(1)} %get-tuple-element.145), channel_id=1, source_target_pairs={{0,96},{4,28},{8,104},{12,4},{16,112},{20,12},{24,120},{28,20},{32... | collective-permute-start | bytes 1769480 | tf_op jit(solution)/shard_map/ppermute | solution.py:46
  154.0 12.7 %collective-permute-start.28 = (bf16[4,48,1536]{2,1,0:T(8,128)(2,1)S(1)}, bf16[4,48,1536]{2,1,0:T(8,128)(2,1)S(1)}, u32[]{:S(2)}, u32[]{:S(2)}) collective-permute-start(bf16[4,48,1536]{2,1,0:T(8,128)(2,1)S(1)} %get-tuple-element.146), channel_id=1, source_target_pairs={{0,32},{4,12},{8,40},{12,20},{16,48},{20,28},{24,56},{28,4},{32,64... | collective-permute-start | bytes 1769480 | tf_op jit(solution)/shard_map/ppermute | solution.py:46
  162.1 11.2 %collective-permute-start.26 = (bf16[4,48,1536]{2,1,0:T(8,128)(2,1)S(1)}, bf16[4,48,1536]{2,1,0:T(8,128)(2,1)S(1)}, u32[]{:S(2)}, u32[]{:S(2)}) collective-permute-start(bf16[4,48,1536]{2,1,0:T(8,128)(2,1)S(1)} %get-tuple-element.144), channel_id=1, source_target_pairs={{0,32},{4,12},{8,40},{12,20},{16,48},{20,28},{24,56},{28,4},{32,64... | collective-permute-start | bytes 1769480 | tf_op jit(solution)/shard_map/ppermute | solution.py:46
  163.7 9.9 %collective-permute-start.29 = (bf16[4,48,1536]{2,1,0:T(8,128)(2,1)S(1)}, bf16[4,48,1536]{2,1,0:T(8,128)(2,1)S(1)}, u32[]{:S(2)}, u32[]{:S(2)}) collective-permute-start(bf16[4,48,1536]{2,1,0:T(8,128)(2,1)S(1)} %get-tuple-element.147), channel_id=1, source_target_pairs={{0,96},{4,28},{8,104},{12,4},{16,112},{20,12},{24,120},{28,20},{32... | collective-permute-start | bytes 1769480 | tf_op jit(solution)/shard_map/ppermute | solution.py:46
  174.8 15.4 %copy-start.8 = (f32[48,1536]{1,0:T(8,128)S(1)}, f32[48,1536]{1,0:T(8,128)}, u32[]{:S(2)}) copy-start(f32[48,1536]{1,0:T(8,128)} %param.23) | copy-start | bytes 884740
  174.8 15.4 %copy-start.9 = (f32[48,1536]{1,0:T(8,128)S(1)}, f32[48,1536]{1,0:T(8,128)}, u32[]{:S(2)}) copy-start(f32[48,1536]{1,0:T(8,128)} %param.22) | copy-start | bytes 884740
  174.8 8.3 %collective-permute-start.32 = (bf16[2,48,1536]{2,1,0:T(8,128)(2,1)S(1)}, bf16[2,48,1536]{2,1,0:T(8,128)(2,1)S(1)}, u32[]{:S(2)}, u32[]{:S(2)}) collective-permute-start(bf16[2,48,1536]{2,1,0:T(8,128)(2,1)S(1)} %get-tuple-element.151), channel_id=1, source_target_pairs={{0,24},{4,100},{8,0},{12,108},{16,8},{20,116},{24,16},{28,124},{32... | collective-permute-start | bytes 884744 | tf_op jit(solution)/shard_map/ppermute | solution.py:46
  178.9 11.1 %collective-permute-start.31 = (bf16[2,48,1536]{2,1,0:T(8,128)(2,1)S(1)}, bf16[2,48,1536]{2,1,0:T(8,128)(2,1)S(1)}, u32[]{:S(2)}, u32[]{:S(2)}) collective-permute-start(bf16[2,48,1536]{2,1,0:T(8,128)(2,1)S(1)} %get-tuple-element.150), channel_id=1, source_target_pairs={{0,8},{4,36},{8,16},{12,44},{16,24},{20,52},{24,0},{28,60},{32,40}... | collective-permute-start | bytes 884744 | tf_op jit(solution)/shard_map/ppermute | solution.py:46
  178.9 11.1 %collective-permute-start.30 = (bf16[2,48,1536]{2,1,0:T(8,128)(2,1)S(1)}, bf16[2,48,1536]{2,1,0:T(8,128)(2,1)S(1)}, u32[]{:S(2)}, u32[]{:S(2)}) collective-permute-start(bf16[2,48,1536]{2,1,0:T(8,128)(2,1)S(1)} %get-tuple-element.149), channel_id=1, source_target_pairs={{0,16},{4,68},{8,24},{12,76},{16,0},{20,84},{24,8},{28,92},{32,48}... | collective-permute-start | bytes 884744 | tf_op jit(solution)/shard_map/ppermute | solution.py:46
  190.0 2.2 %copy-start.1 = (bf16[1536,3,384]{2,0,1:T(8,128)(2,1)S(1)}, bf16[1536,3,384]{2,0,1:T(8,128)(2,1)}, u32[]{:S(2)}) copy-start(bf16[1536,3,384]{2,0,1:T(8,128)(2,1)} %param.19) | copy-start | bytes 10616836

commit v9 on v8

--- a/solution.py
+++ b/solution.py
@@ -578,9 +578,9 @@
         at, unit, by_core(unit), (keep1, got1), (keep2, got2), lambda v, w: by_turns(v, w, True)
     )
     value = own + (
-        by_turns(far, 2, False).astype(F32)
+        by_turns(behind, -1, False).astype(F32)
         + by_turns(ahead, 1, False).astype(F32)
-        + by_turns(behind, -1, False).astype(F32)
+        + by_turns(far, 2, False).astype(F32)
     )
     return (value[0] + noise_in) / 32.0, (value[1] + noise_out) / 32.0
 

time: 193 us -> 190 us (0.984)
  waiting for transfers between devices: 59.9 us -> 56.3 us
    ppermute x12, waiting for transfers between devices: 23 us -> 19.4 us  [by_dp(): return lax.ppermute(value, 'dp', pairs)]
  transfers between devices with their start and end apart: 34 -> 34, of which waited for: 20 -> 21; matrix products, arithmetic and copies ran while one was open for 10% -> 10% of each run, Pallas kernels for 12% -> 12%
where the time goes in v9:
time: 190 us
  waiting for transfers between devices  56.3 us (30%)
  starting transfers between devices  56 us (29%)
  Pallas kernels  48.3 us (25%)
  matrix products  12 us (6%)
  local copies, waits for them, and re-layouts  7.24 us (4%)
  other arithmetic  6.78 us (4%)
  between operations  3.24 us (2%)
    ppermute x12, waiting for transfers between devices, by_dp(): return lax.ppermute(value, 'dp', pairs)  19.4 us
    ppermute x15, starting transfers between devices, by_x(): return lax.ppermute(value, ('dp', 'mp'), pairs)  19.3 us
    ppermute x15, waiting for transfers between devices, by_x(): return lax.ppermute(value, ('dp', 'mp'), pairs)  17.4 us
    ppermute x12, starting transfers between devices, by_dp(): return lax.ppermute(value, 'dp', pairs)  16.6 us
    ppermute x6, waiting for transfers between devices, swap_x(): return lax.ppermute(value, 'mp', list(enumerate(other)))  16.5 us
    pallas_call x2, Pallas kernels, forward(): call(forward_kernel, ff // WIDE, [piece] * 4 + [whole((3, PART)), whole((...  15.8 us
    ppermute x6, starting transfers between devices, swap_x(): return lax.ppermute(value, 'mp', list(enumerate(other)))  11.7 us
    all_to_all x1, starting transfers between devices, local(): received = lax.all_to_all(everywhere, 'dp', 0, 0, tiled=True)  8.54 us
  transfers between devices with their start and end apart: 34, of which 21 were waited for; matrix products, arithmetic and copies ran while one was open for 10% of the time, Pallas kernels for 12%

profile of v9, /device:TPU:0, one launch (start us, length us, event | category | flops | bytes accessed | tf_op | source)
XLA Modules:
  0.0 189.9 jit_solution(7378895190939843385)
XLA Ops:
  0.6 1.6 collective-permute-start
  2.3 1.7 collective-permute-start.1
  6.4 8.5 %all-to-all-start = ((f32[32,8,128]{2,1,0:T(8,128)}), f32[32,8,128]{2,1,0:T(8,128)}, u32[]{:S(2)}, u32[]{:S(2)}) async-start(f32[32,8,128]{2,1,0:T(8,128)} %broadcast_in_dim.31), calls=%async_computation | async-start | bytes 262144 | tf_op jit(solution)/shard_map/all_to_all | solution.py:474
  15.1 4.6 %constant_dynamic-slice_fusion = (bf16[384,1536]{1,0:T(8,128)(2,1)}, bf16[384,1536]{1,0:T(8,128)(2,1)}, bf16[384,1536]{1,0:T(8,128)(2,1)}, bf16[384,1536]{1,0:T(8,128)(2,1)}) fusion(bf16[1536,1536]{1,0:T(8,128)(2,1)} %out_w.3, s32[]{:T(128)S(6)} %select_n.136, s32[]{:T(128)S(6)} %select_n.135, s32[]{:T(128)S(6)} %select_n.134, s32[]{:T(128)S(6)} %select_n.133), kind=kLoop, calls=%fused_computation.51 | loop fusion | bytes 9437200 | tf_op jit(solution)/shard_map/dynamic_slice | solution.py:467
  19.7 3.0 %all-to-all-done = f32[32,8,128]{2,1,0:T(8,128)} async-done(((f32[32,8,128]{2,1,0:T(8,128)}), f32[32,8,128]{2,1,0:T(8,128)}, u32[]{:S(2)}, u32[]{:S(2)}) %all-to-all-start) | async-done | bytes 131104 | tf_op jit(solution)/shard_map/all_to_all | solution.py:474
  24.1 2.4 %fusion.27 = f32[1,1536]{1,0:T(1,128)S(1)} fusion(bf16[1024,1]{0,1:T(2,128)(2,1)S(1)} %reshape.95, bf16[1024,1536]{1,0:T(8,128)(2,1)} %param.18), kind=kOutput, calls=%fused_computation.60 | convolution fusion | flops 3145728 | bytes 3153920 | tf_op jit(solution)/shard_map/dot_general | solution.py:24
  26.5 1.5 collective-permute-start.2
  28.7 4.3 %collective-permute-done.2 = f32[1,1536]{1,0:T(1,128)S(1)} collective-permute-done((f32[1,1536]{1,0:T(1,128)S(1)}, f32[1,1536]{1,0:T(1,128)S(1)}, u32[]{:S(2)}, u32[]{:S(2)}) %collective-permute-start.2) | collective-permute-done | bytes 6176 | tf_op jit(solution)/shard_map/ppermute | solution.py:62
  33.0 3.9 %collective-permute-start.3 = (f32[1,1536]{1,0:T(1,128)S(1)}, f32[1,1536]{1,0:T(1,128)S(1)}, u32[]{:S(2)}, u32[]{:S(2)}) collective-permute-start(f32[1,1536]{1,0:T(1,128)S(1)} %add.228), channel_id=1, source_target_pairs={{0,3},{1,2},{2,1},{3,0},{4,7},{5,6},{6,5},{7,4},{8,11},{9,10},{10,... | collective-permute-start | bytes 18440 | tf_op jit(solution)/shard_map/ppermute | solution.py:62
  36.9 1.6 collective-permute-done.3
  41.4 2.9 %collective-permute-done.5.m1 = f32[3,384]{1,0:T(4,128)S(1)} collective-permute-done((f32[3,384]{1,0:T(4,128)S(1)}, f32[3,384]{1,0:T(4,128)S(1)}, u32[]{:S(2)}, u32[]{:S(2)}) %collective-permute-start.5) | collective-permute-done | bytes 4640 | tf_op jit(solution)/shard_map/ppermute | solution.py:62
  44.3 3.3 %collective-permute-start.6 = (f32[6,384]{1,0:T(8,128)S(1)}, f32[6,384]{1,0:T(8,128)S(1)}, u32[]{:S(2)}, u32[]{:S(2)}) collective-permute-start(f32[6,384]{1,0:T(8,128)S(1)} %pad_maximum_fusion), channel_id=1, source_target_pairs={{0,3},{1,2},{2,1},{3,0},{4,7},{5,6},{6,5},{7,4},{8,11},{9,10},{10,... | collective-permute-start | bytes 27656 | tf_op jit(solution)/shard_map/ppermute | solution.py:62
  47.7 1.6 collective-permute-done.6.m2
  49.3 7.9 %forward.2 = (bf16[512,1536]{1,0:T(8,128)(2,1)S(1)}, bf16[512,1536]{1,0:T(8,128)(2,1)S(1)}, f32[512,1536]{1,0:T(8,128)S(1)}) custom-call(s32[20]{0:T(128)S(1)} %stack.75.at.refs_0_, bf16[1024,384]{1,0:T(8,128)(2,1)} %x0.3, bf16[1024,384]{1,0:T(8,128)(2,1)} %collective-permute-done.1.x1, bf16[1024,384]{1,0:T(8,128)(2,1)} %copy-done.10, ...), custom_call_target="tpu_custom_call" | custom-call | flops 2415919104 | bytes 12000000 | tf_op jit(solution)/shard_map/forward/pallas_call | solution.py:137
  59.6 3.5 %collective-permute-start.8 = (bf16[512,384]{1,0:T(8,128)(2,1)S(1)}, bf16[512,384]{1,0:T(8,128)(2,1)S(1)}, u32[]{:S(2)}, u32[]{:S(2)}) collective-permute-start(bf16[512,384]{1,0:T(8,128)(2,1)S(1)} %convolution_convert_fusion.3), channel_id=1, source_target_pairs={{0,3},{1,0},{2,1},{3,2},{4,5},{5,6},{6,7},{7,4},{8,11},{9,8},{10,9... | collective-permute-start | bytes 1179656 | tf_op jit(solution)/shard_map/ppermute | solution.py:36
  64.0 7.9 %forward.3 = (bf16[512,1536]{1,0:T(8,128)(2,1)S(1)}, bf16[512,1536]{1,0:T(8,128)(2,1)S(1)}, f32[512,1536]{1,0:T(8,128)S(1)}) custom-call(s32[20]{0:T(128)S(1)} %stack.75.at.refs_0_, bf16[1024,384]{1,0:T(8,128)(2,1)} %x0.3, bf16[1024,384]{1,0:T(8,128)(2,1)} %collective-permute-done.1.x1, bf16[1024,384]{1,0:T(8,128)(2,1)} %copy-done.10, ...), custom_call_target="tpu_custom_call" | custom-call | flops 2415919104 | bytes 12000000 | tf_op jit(solution)/shard_map/forward/pallas_call | solution.py:137
  75.3 3.1 %collective-permute-start.10 = (bf16[512,384]{1,0:T(8,128)(2,1)S(1)}, bf16[512,384]{1,0:T(8,128)(2,1)S(1)}, u32[]{:S(2)}, u32[]{:S(2)}) collective-permute-start(bf16[512,384]{1,0:T(8,128)(2,1)S(1)} %convolution_convert_fusion.1), channel_id=1, source_target_pairs={{0,3},{1,0},{2,1},{3,2},{4,5},{5,6},{6,7},{7,4},{8,11},{9,8},{10,9... | collective-permute-start | bytes 1179656 | tf_op jit(solution)/shard_map/ppermute | solution.py:36
  78.4 7.9 %collective-permute-done.9 = bf16[512,384]{1,0:T(8,128)(2,1)S(1)} collective-permute-done((bf16[512,384]{1,0:T(8,128)(2,1)S(1)}, bf16[512,384]{1,0:T(8,128)(2,1)S(1)}, u32[]{:S(2)}, u32[]{:S(2)}) %collective-permute-start.9) | collective-permute-done | bytes 393248 | tf_op jit(solution)/shard_map/ppermute | solution.py:36
  86.8 3.2 %collective-permute-start.13 = (bf16[512,384]{1,0:T(8,128)(2,1)S(1)}, bf16[512,384]{1,0:T(8,128)(2,1)S(1)}, u32[]{:S(2)}, u32[]{:S(2)}) collective-permute-start(bf16[512,384]{1,0:T(8,128)(2,1)S(1)} %multiply_convert_fusion.1.b0.refs_1_), channel_id=1, source_target_pairs={{0,3},{1,0},{2,1},{3,2},{4,5},{5,6},{6,7},{7,4},{8,11},{9,8},{10,9... | collective-permute-start | bytes 1179656 | tf_op jit(solution)/shard_map/ppermute | solution.py:36
  92.2 3.2 %add_convert_fusion = (bf16[512,1536]{1,0:T(8,128)(2,1)S(1)}, bf16[512,1536]{1,0:T(8,128)(2,1)S(1)}) fusion(f32[512,1536]{1,0:T(8,128)S(1)} %get-tuple-element.103, f32[512,1536]{1,0:T(8,128)S(1)} %get-tuple-element.102), kind=kLoop, calls=%fused_computation | loop fusion | flops 23592960 | bytes 9437184 | tf_op jit(solution)/shard_map/convert_element_type | solution.py:546
  95.4 2.2 %turn.1 = (bf16[768,1024]{1,0:T(8,128)(2,1)S(1)}, bf16[768,1024]{1,0:T(8,128)(2,1)S(1)}) custom-call(s32[20]{0:T(128)S(1)} %stack.75.at.refs_0_, bf16[512,1536]{1,0:T(8,128)(2,1)S(1)} %get-tuple-element.105.top, bf16[512,1536]{1,0:T(8,128)(2,1)S(1)} %get-tuple-element.106.low), custom_call_target="tpu_custom_call" | custom-call | flops 1572864 | bytes 6291456 | tf_op jit(solution)/shard_map/turn/pallas_call | solution.py:166
  97.6 2.3 %collective-permute-done.11 = bf16[512,384]{1,0:T(8,128)(2,1)S(1)} collective-permute-done((bf16[512,384]{1,0:T(8,128)(2,1)S(1)}, bf16[512,384]{1,0:T(8,128)(2,1)S(1)}, u32[]{:S(2)}, u32[]{:S(2)}) %collective-permute-start.11) | collective-permute-done | bytes 393248 | tf_op jit(solution)/shard_map/ppermute | solution.py:36
  101.5 3.5 %collective-permute-start.16 = (bf16[512,384]{1,0:T(8,128)(2,1)S(1)}, bf16[512,384]{1,0:T(8,128)(2,1)S(1)}, u32[]{:S(2)}, u32[]{:S(2)}) collective-permute-start(bf16[512,384]{1,0:T(8,128)(2,1)S(1)} %multiply_convert_fusion.refs_2_.b0), channel_id=1, source_target_pairs={{0,3},{1,0},{2,1},{3,2},{4,5},{5,6},{6,7},{7,4},{8,11},{9,8},{10,9... | collective-permute-start | bytes 1179656 | tf_op jit(solution)/shard_map/ppermute | solution.py:36
  105.0 2.0 %rows_grad.4 = (bf16[768,1536]{1,0:T(8,128)(2,1)S(1)}, bf16[768,1536]{1,0:T(8,128)(2,1)S(1)}, f32[1,1536]{1,0:T(1,128)S(1)}) custom-call(s32[20]{0:T(128)S(1)} %stack.75.at.refs_0_, bf16[512,384]{1,0:T(8,128)(2,1)S(1)} %multiply_convert_fusion.1.b0.refs_1_, bf16[512,384]{1,0:T(8,128)(2,1)S(1)} %multiply_convert_fusion.refs_2_.b0, ...), custom_call_target="tpu_custom_call" | custom-call | flops 1207959552 | bytes 5000000 | tf_op jit(solution)/shard_map/rows_grad/pallas_call | solution.py:287
  107.0 2.4 %rows_partial.1.refs_3_ = f32[768,1536]{1,0:T(8,128)S(1)} custom-call(s32[20]{0:T(128)S(1)} %stack.75.at.refs_0_, bf16[512,384]{1,0:T(8,128)(2,1)S(1)} %collective-permute-done.13.b1.refs_1_, bf16[512,384]{1,0:T(8,128)(2,1)S(1)} %collective-permute-done.12.b3.refs_2_, bf16[512,1536]{1,0:T(8,128)(2,1)S(1)} %get-tuple-element.95.refs_3_), custom_call_target="tpu_custom_call" | custom-call | flops 1207959552 | bytes 8000000 | tf_op jit(solution)/shard_map/rows_partial/pallas_call | solution.py:238
  109.4 2.6 %collective-permute-done.15.b2.refs_1_ = bf16[512,384]{1,0:T(8,128)(2,1)S(1)} collective-permute-done((bf16[512,384]{1,0:T(8,128)(2,1)S(1)}, bf16[512,384]{1,0:T(8,128)(2,1)S(1)}, u32[]{:S(2)}, u32[]{:S(2)}) %collective-permute-start.15) | collective-permute-done | bytes 393248 | tf_op jit(solution)/shard_map/ppermute | solution.py:36
  112.1 1.9 %collective-permute-start.17 = (bf16[512,384]{1,0:T(8,128)(2,1)S(1)}, bf16[512,384]{1,0:T(8,128)(2,1)S(1)}, u32[]{:S(2)}, u32[]{:S(2)}) collective-permute-start(bf16[512,384]{1,0:T(8,128)(2,1)S(1)} %collective-permute-done.16.b1.refs_1_), channel_id=1, source_target_pairs={{0,3},{1,0},{2,1},{3,2},{4,5},{5,6},{6,7},{7,4},{8,11},{9,8},{10,9... | collective-permute-start | bytes 1179656 | tf_op jit(solution)/shard_map/ppermute | solution.py:36
  114.1 1.4 rows_grad.5
  115.5 4.2 %backward.2.right0 = bf16[512,1536]{1,0:T(8,128)(2,1)S(1)} custom-call(s32[20]{0:T(128)S(1)} %stack.75.at.refs_0_, bf16[512,384]{1,0:T(8,128)(2,1)S(1)} %multiply_convert_fusion.1.b0.refs_1_, bf16[512,384]{1,0:T(8,128)(2,1)S(1)} %collective-permute-done.13.b1.refs_1_, bf16[512,384]{1,0:T(8,128)(2,1)S(1)} %collective-permute-done.15.b2.refs_1_, ...), custom_call_target="tpu_custom_call" | custom-call | flops 2415919104 | bytes 14000000 | tf_op jit(solution)/shard_map/backward/pallas_call | solution.py:189
  119.7 3.2 %collective-permute-done.17.b2.refs_2_ = bf16[512,384]{1,0:T(8,128)(2,1)S(1)} collective-permute-done((bf16[512,384]{1,0:T(8,128)(2,1)S(1)}, bf16[512,384]{1,0:T(8,128)(2,1)S(1)}, u32[]{:S(2)}, u32[]{:S(2)}) %collective-permute-start.17) | collective-permute-done | bytes 393248 | tf_op jit(solution)/shard_map/ppermute | solution.py:36
  123.0 4.2 %backward.3.right1 = bf16[512,1536]{1,0:T(8,128)(2,1)S(1)} custom-call(s32[20]{0:T(128)S(1)} %stack.75.at.refs_0_, bf16[512,384]{1,0:T(8,128)(2,1)S(1)} %multiply_convert_fusion.refs_2_.b0, bf16[512,384]{1,0:T(8,128)(2,1)S(1)} %collective-permute-done.16.b1.refs_1_, bf16[512,384]{1,0:T(8,128)(2,1)S(1)} %collective-permute-done.17.b2.refs_2_, ...), custom_call_target="tpu_custom_call" | custom-call | flops 2415919104 | bytes 14000000 | tf_op jit(solution)/shard_map/backward/pallas_call | solution.py:189
  128.6 2.0 %rows_grad.7 = (bf16[768,1536]{1,0:T(8,128)(2,1)S(1)}, bf16[768,1536]{1,0:T(8,128)(2,1)S(1)}, f32[1,1536]{1,0:T(1,128)S(1)}) custom-call(s32[20]{0:T(128)S(1)} %stack.75.at.refs_0_, bf16[512,384]{1,0:T(8,128)(2,1)S(1)} %collective-permute-done.15.b2.refs_1_, ...), custom_call_target="tpu_custom_call", output_to_operand_aliasing={{0}: (5, {}), {1}: (6, {})} | custom-call | flops 1207959552 | bytes 5000000 | tf_op jit(solution)/shard_map/rows_grad/pallas_call | solution.py:287
  130.5 6.7 %weight_grad.1 = (bf16[768,1536]{1,0:T(8,128)(2,1)S(1)}, bf16[768,1536]{1,0:T(8,128)(2,1)S(1)}, f32[1,128]{1,0:T(1,128)S(1)}) custom-call(s32[20]{0:T(128)S(1)} %stack.75.at.refs_0_, bf16[768,1024]{1,0:T(8,128)(2,1)S(1)} %get-tuple-element.110.keep_l, bf16[768,1024]{1,0:T(8,128)(2,1)S(1)} %get-tuple-element.111.send_l, ...), custom_call_target="tpu_custom_call" | custom-call | flops 4831838208 | bytes 11000000 | tf_op jit(solution)/shard_map/weight_grad/pallas_call | solution.py:329
  138.0 3.3 %collective-permute-done.19 = f32[1,128]{1,0:T(1,128)S(1)} collective-permute-done((f32[1,128]{1,0:T(1,128)S(1)}, f32[1,128]{1,0:T(1,128)S(1)}, u32[]{:S(2)}, u32[]{:S(2)}) %collective-permute-start.19) | collective-permute-done | bytes 544 | tf_op jit(solution)/shard_map/ppermute | solution.py:62
  141.4 2.0 %collective-permute-start.20 = (f32[1,128]{1,0:T(1,128)S(1)}, f32[1,128]{1,0:T(1,128)S(1)}, u32[]{:S(2)}, u32[]{:S(2)}) collective-permute-start(f32[1,128]{1,0:T(1,128)S(1)} %add.252), channel_id=1, source_target_pairs={{0,3},{1,2},{2,1},{3,0},{4,7},{5,6},{6,5},{7,4},{8,11},{9,10},{10,... | collective-permute-start | bytes 1544 | tf_op jit(solution)/shard_map/ppermute | solution.py:62
  143.4 2.7 %collective-permute-done.20 = f32[1,128]{1,0:T(1,128)S(1)} collective-permute-done((f32[1,128]{1,0:T(1,128)S(1)}, f32[1,128]{1,0:T(1,128)S(1)}, u32[]{:S(2)}, u32[]{:S(2)}) %collective-permute-start.20) | collective-permute-done | bytes 544 | tf_op jit(solution)/shard_map/ppermute | solution.py:62
  147.3 1.9 %spread.1 = (bf16[4,48,1536]{2,1,0:T(8,128)(2,1)S(1)}, bf16[4,48,1536]{2,1,0:T(8,128)(2,1)S(1)}, bf16[4,48,1536]{2,1,0:T(8,128)(2,1)S(1)}, bf16[4,48,1536]{2,1,0:T(8,128)(2,1)S(1)}) custom-call(s32[20]{0:T(128)S(1)} %stack.75.at.refs_0_, f32[1,128]{1,0:T(1,128)S(1)} %add_divide_fusion.u0, f32[1,128]{1,0:T(1,128)S(1)} %collective-permute-done.21.u1, ...), custom_call_target="tpu_custom_call" | custom-call | flops 3538944 | bytes 7077888 | tf_op jit(solution)/shard_map/spread/pallas_call | solution.py:383
  150.5 2.0 %collective-permute-start.25 = (bf16[4,48,1536]{2,1,0:T(8,128)(2,1)S(1)}, bf16[4,48,1536]{2,1,0:T(8,128)(2,1)S(1)}, u32[]{:S(2)}, u32[]{:S(2)}) collective-permute-start(bf16[4,48,1536]{2,1,0:T(8,128)(2,1)S(1)} %get-tuple-element.140), channel_id=1, source_target_pairs={{0,96},{4,28},{8,104},{12,4},{16,112},{20,12},{24,120},{28,20},{32... | collective-permute-start | bytes 1769480 | tf_op jit(solution)/shard_map/ppermute | solution.py:46
  152.6 1.5 collective-permute-start.27
  156.0 4.4 %collective-permute-done.24.up = bf16[4,48,1536]{2,1,0:T(8,128)(2,1)S(1)} collective-permute-done((bf16[4,48,1536]{2,1,0:T(8,128)(2,1)S(1)}, bf16[4,48,1536]{2,1,0:T(8,128)(2,1)S(1)}, u32[]{:S(2)}, u32[]{:S(2)}) %collective-permute-start.24) | collective-permute-done | bytes 589856 | tf_op jit(solution)/shard_map/ppermute | solution.py:46
  160.4 1.6 relay.1
  162.1 1.6 collective-permute-start.26
  163.7 1.7 collective-permute-start.29
  166.8 6.5 %collective-permute-done.26.up1 = bf16[4,48,1536]{2,1,0:T(8,128)(2,1)S(1)} collective-permute-done((bf16[4,48,1536]{2,1,0:T(8,128)(2,1)S(1)}, bf16[4,48,1536]{2,1,0:T(8,128)(2,1)S(1)}, u32[]{:S(2)}, u32[]{:S(2)}) %collective-permute-start.26) | collective-permute-done | bytes 589856 | tf_op jit(solution)/shard_map/ppermute | solution.py:46
  174.8 4.0 %collective-permute-start.32 = (bf16[2,48,1536]{2,1,0:T(8,128)(2,1)S(1)}, bf16[2,48,1536]{2,1,0:T(8,128)(2,1)S(1)}, u32[]{:S(2)}, u32[]{:S(2)}) collective-permute-start(bf16[2,48,1536]{2,1,0:T(8,128)(2,1)S(1)} %get-tuple-element.151), channel_id=1, source_target_pairs={{0,16},{4,68},{8,24},{12,76},{16,0},{20,84},{24,8},{28,92},{32,48}... | collective-permute-start | bytes 884744 | tf_op jit(solution)/shard_map/ppermute | solution.py:46
  179.8 2.2 %collective-permute-start.30 = (bf16[2,48,1536]{2,1,0:T(8,128)(2,1)S(1)}, bf16[2,48,1536]{2,1,0:T(8,128)(2,1)S(1)}, u32[]{:S(2)}, u32[]{:S(2)}) collective-permute-start(bf16[2,48,1536]{2,1,0:T(8,128)(2,1)S(1)} %get-tuple-element.149), channel_id=1, source_target_pairs={{0,24},{4,100},{8,0},{12,108},{16,8},{20,116},{24,16},{28,124},{32... | collective-permute-start | bytes 884744 | tf_op jit(solution)/shard_map/ppermute | solution.py:46
  182.0 1.5 collective-permute-done.32
  183.5 3.2 %collective-permute-done.31 = bf16[2,48,1536]{2,1,0:T(8,128)(2,1)S(1)} collective-permute-done((bf16[2,48,1536]{2,1,0:T(8,128)(2,1)S(1)}, bf16[2,48,1536]{2,1,0:T(8,128)(2,1)S(1)}, u32[]{:S(2)}, u32[]{:S(2)}) %collective-permute-start.31) | collective-permute-done | bytes 294944 | tf_op jit(solution)/shard_map/ppermute | solution.py:46
  (99 shorter events, 30.0 us)
Async XLA Ops:
  0.6 39.4 %copy-start = (bf16[1536,3,384]{2,0,1:T(8,128)(2,1)S(1)}, bf16[1536,3,384]{2,0,1:T(8,128)(2,1)}, u32[]{:S(2)}) copy-start(bf16[1536,3,384]{2,0,1:T(8,128)(2,1)} %param.19) | copy-start | bytes 10616836
  0.6 22.1 %collective-permute-start = (bf16[1024,384]{1,0:T(8,128)(2,1)}, bf16[1024,384]{1,0:T(8,128)(2,1)}, u32[]{:S(2)}, u32[]{:S(2)}) collective-permute-start(bf16[1024,384]{1,0:T(8,128)(2,1)} %x0.3), channel_id=1, source_target_pairs={{0,1},{1,2},{2,3},{3,0},{4,7},{5,4},{6,5},{7,6},{8,9},{9,10},{10,1... | collective-permute-start | bytes 2359304 | tf_op jit(solution)/shard_map/ppermute | solution.py:36
  2.3 20.5 %collective-permute-start.1 = (bf16[1024,384]{1,0:T(8,128)(2,1)}, bf16[1024,384]{1,0:T(8,128)(2,1)}, u32[]{:S(2)}, u32[]{:S(2)}) collective-permute-start(bf16[1024,384]{1,0:T(8,128)(2,1)} %x0.3), channel_id=1, source_target_pairs={{0,3},{1,0},{2,1},{3,2},{4,5},{5,6},{6,7},{7,4},{8,11},{9,8},{10,9... | collective-permute-start | bytes 2359304 | tf_op jit(solution)/shard_map/ppermute | solution.py:36
  6.4 16.4 %all-to-all-start = ((f32[32,8,128]{2,1,0:T(8,128)}), f32[32,8,128]{2,1,0:T(8,128)}, u32[]{:S(2)}, u32[]{:S(2)}) async-start(f32[32,8,128]{2,1,0:T(8,128)} %broadcast_in_dim.31), calls=%async_computation | async-start | bytes 262144 | tf_op jit(solution)/shard_map/all_to_all | solution.py:474
  15.0 8.0 %copy-start.11 = (s32[32]{0:T(128)S(1)}, s32[32]{0:T(128)}, u32[]{:S(2)}) copy-start(s32[32]{0:T(128)} %param.17) | copy-start | bytes 388
  22.8 15.7 %collective-permute-start.4 = (bf16[1024,384]{1,0:T(8,128)(2,1)}, bf16[1024,384]{1,0:T(8,128)(2,1)S(1)}, u32[]{:S(2)}, u32[]{:S(2)}) collective-permute-start(bf16[1024,384]{1,0:T(8,128)(2,1)} %collective-permute-done.x3), channel_id=1, source_target_pairs={{0,1},{1,2},{2,3},{3,0},{4,7},{5,4},{6,5},{7,6},{8,9},{9,10},{10,1... | collective-permute-start | bytes 2359304 | tf_op jit(solution)/shard_map/ppermute | solution.py:36
  26.5 6.5 %collective-permute-start.2 = (f32[1,1536]{1,0:T(1,128)S(1)}, f32[1,1536]{1,0:T(1,128)S(1)}, u32[]{:S(2)}, u32[]{:S(2)}) collective-permute-start(f32[1,1536]{1,0:T(1,128)S(1)} %fusion.27), channel_id=1, source_target_pairs={{0,1},{1,0},{2,3},{3,2},{4,5},{5,4},{6,7},{7,6},{8,9},{9,8},{10,11... | collective-permute-start | bytes 18440 | tf_op jit(solution)/shard_map/ppermute | solution.py:62
  33.0 5.5 %collective-permute-start.3 = (f32[1,1536]{1,0:T(1,128)S(1)}, f32[1,1536]{1,0:T(1,128)S(1)}, u32[]{:S(2)}, u32[]{:S(2)}) collective-permute-start(f32[1,1536]{1,0:T(1,128)S(1)} %add.228), channel_id=1, source_target_pairs={{0,3},{1,2},{2,1},{3,0},{4,7},{5,6},{6,5},{7,4},{8,11},{9,10},{10,... | collective-permute-start | bytes 18440 | tf_op jit(solution)/shard_map/ppermute | solution.py:62
  38.5 0.9 copy-start.10
  40.6 3.7 %collective-permute-start.5 = (f32[3,384]{1,0:T(4,128)S(1)}, f32[3,384]{1,0:T(4,128)S(1)}, u32[]{:S(2)}, u32[]{:S(2)}) collective-permute-start(f32[3,384]{1,0:T(4,128)S(1)} %bitcast.78), channel_id=1, source_target_pairs={{0,1},{1,0},{2,3},{3,2},{4,5},{5,4},{6,7},{7,6},{8,9},{9,8},{10,11... | collective-permute-start | bytes 13832 | tf_op jit(solution)/shard_map/ppermute | solution.py:62
  44.3 5.0 %collective-permute-start.6 = (f32[6,384]{1,0:T(8,128)S(1)}, f32[6,384]{1,0:T(8,128)S(1)}, u32[]{:S(2)}, u32[]{:S(2)}) collective-permute-start(f32[6,384]{1,0:T(8,128)S(1)} %pad_maximum_fusion), channel_id=1, source_target_pairs={{0,3},{1,2},{2,1},{3,0},{4,7},{5,6},{6,5},{7,4},{8,11},{9,10},{10,... | collective-permute-start | bytes 27656 | tf_op jit(solution)/shard_map/ppermute | solution.py:62
  47.7 9.6 %copy-start.3 = (bf16[384,1536]{1,0:T(8,128)(2,1)S(1)}, bf16[384,1536]{1,0:T(8,128)(2,1)}, u32[]{:S(2)}) copy-start(bf16[384,1536]{1,0:T(8,128)(2,1)} %get-tuple-element.85) | copy-start | bytes 3538948
  57.2 1.3 copy-start.5
  58.5 4.6 %copy-start.4 = (bf16[384,1536]{1,0:T(8,128)(2,1)S(1)}, bf16[384,1536]{1,0:T(8,128)(2,1)}, u32[]{:S(2)}) copy-start(bf16[384,1536]{1,0:T(8,128)(2,1)} %get-tuple-element.84) | copy-start | bytes 3538948
  59.5 12.4 %collective-permute-start.7 = (bf16[512,384]{1,0:T(8,128)(2,1)S(1)}, bf16[512,384]{1,0:T(8,128)(2,1)S(1)}, u32[]{:S(2)}, u32[]{:S(2)}) collective-permute-start(bf16[512,384]{1,0:T(8,128)(2,1)S(1)} %convolution_convert_fusion.2), channel_id=1, source_target_pairs={{0,1},{1,2},{2,3},{3,0},{4,7},{5,4},{6,5},{7,6},{8,9},{9,10},{10,1... | collective-permute-start | bytes 1179656 | tf_op jit(solution)/shard_map/ppermute | solution.py:36
  59.6 12.4 %collective-permute-start.8 = (bf16[512,384]{1,0:T(8,128)(2,1)S(1)}, bf16[512,384]{1,0:T(8,128)(2,1)S(1)}, u32[]{:S(2)}, u32[]{:S(2)}) collective-permute-start(bf16[512,384]{1,0:T(8,128)(2,1)S(1)} %convolution_convert_fusion.3), channel_id=1, source_target_pairs={{0,3},{1,0},{2,1},{3,2},{4,5},{5,6},{6,7},{7,4},{8,11},{9,8},{10,9... | collective-permute-start | bytes 1179656 | tf_op jit(solution)/shard_map/ppermute | solution.py:36
  73.0 1.3 copy-start.2
  73.0 13.3 %collective-permute-start.9 = (bf16[512,384]{1,0:T(8,128)(2,1)S(1)}, bf16[512,384]{1,0:T(8,128)(2,1)S(1)}, u32[]{:S(2)}, u32[]{:S(2)}) collective-permute-start(bf16[512,384]{1,0:T(8,128)(2,1)S(1)} %add_convert_fusion.3), channel_id=1, source_target_pairs={{0,1},{1,2},{2,3},{3,0},{4,7},{5,4},{6,5},{7,6},{8,9},{9,10},{10,1... | collective-permute-start | bytes 1179656 | tf_op jit(solution)/shard_map/ppermute | solution.py:36
  74.3 12.1 %copy-start.6 = (bf16[1024,384]{1,0:T(8,128)(2,1)S(1)}, bf16[1024,384]{1,0:T(8,128)(2,1)}, u32[]{:S(2)}) copy-start(bf16[1024,384]{1,0:T(8,128)(2,1)} %x0.3) | copy-start | bytes 2359300
  74.3 12.1 %copy-start.7 = (bf16[1024,384]{1,0:T(8,128)(2,1)S(1)}, bf16[1024,384]{1,0:T(8,128)(2,1)}, u32[]{:S(2)}) copy-start(bf16[1024,384]{1,0:T(8,128)(2,1)} %param.13) | copy-start | bytes 2359300
  75.3 16.7 %collective-permute-start.10 = (bf16[512,384]{1,0:T(8,128)(2,1)S(1)}, bf16[512,384]{1,0:T(8,128)(2,1)S(1)}, u32[]{:S(2)}, u32[]{:S(2)}) collective-permute-start(bf16[512,384]{1,0:T(8,128)(2,1)S(1)} %convolution_convert_fusion.1), channel_id=1, source_target_pairs={{0,3},{1,0},{2,1},{3,2},{4,5},{5,6},{6,7},{7,4},{8,11},{9,8},{10,9... | collective-permute-start | bytes 1179656 | tf_op jit(solution)/shard_map/ppermute | solution.py:36
  78.4 22.7 %collective-permute-start.14 = (bf16[512,384]{1,0:T(8,128)(2,1)S(1)}, bf16[512,384]{1,0:T(8,128)(2,1)S(1)}, u32[]{:S(2)}, u32[]{:S(2)}) collective-permute-start(bf16[512,384]{1,0:T(8,128)(2,1)S(1)} %convolution_convert_fusion), channel_id=1, source_target_pairs={{0,1},{1,2},{2,3},{3,0},{4,7},{5,4},{6,5},{7,6},{8,9},{9,10},{10,1... | collective-permute-start | bytes 1179656 | tf_op jit(solution)/shard_map/ppermute | solution.py:36
  86.7 14.4 %collective-permute-start.12 = (bf16[512,384]{1,0:T(8,128)(2,1)S(1)}, bf16[512,384]{1,0:T(8,128)(2,1)S(1)}, u32[]{:S(2)}, u32[]{:S(2)}) collective-permute-start(bf16[512,384]{1,0:T(8,128)(2,1)S(1)} %multiply_convert_fusion.1.b0.refs_1_), channel_id=1, source_target_pairs={{0,1},{1,2},{2,3},{3,0},{4,7},{5,4},{6,5},{7,6},{8,9},{9,10},{10,1... | collective-permute-start | bytes 1179656 | tf_op jit(solution)/shard_map/ppermute | solution.py:36
  86.8 14.3 %collective-permute-start.13 = (bf16[512,384]{1,0:T(8,128)(2,1)S(1)}, bf16[512,384]{1,0:T(8,128)(2,1)S(1)}, u32[]{:S(2)}, u32[]{:S(2)}) collective-permute-start(bf16[512,384]{1,0:T(8,128)(2,1)S(1)} %multiply_convert_fusion.1.b0.refs_1_), channel_id=1, source_target_pairs={{0,3},{1,0},{2,1},{3,2},{4,5},{5,6},{6,7},{7,4},{8,11},{9,8},{10,9... | collective-permute-start | bytes 1179656 | tf_op jit(solution)/shard_map/ppermute | solution.py:36
  92.1 7.8 %collective-permute-start.11 = (bf16[512,384]{1,0:T(8,128)(2,1)S(1)}, bf16[512,384]{1,0:T(8,128)(2,1)S(1)}, u32[]{:S(2)}, u32[]{:S(2)}) collective-permute-start(bf16[512,384]{1,0:T(8,128)(2,1)S(1)} %add_convert_fusion.2), channel_id=1, source_target_pairs={{0,3},{1,0},{2,1},{3,2},{4,5},{5,6},{6,7},{7,4},{8,11},{9,8},{10,9... | collective-permute-start | bytes 1179656 | tf_op jit(solution)/shard_map/ppermute | solution.py:36
  101.1 10.9 %collective-permute-start.15 = (bf16[512,384]{1,0:T(8,128)(2,1)S(1)}, bf16[512,384]{1,0:T(8,128)(2,1)S(1)}, u32[]{:S(2)}, u32[]{:S(2)}) collective-permute-start(bf16[512,384]{1,0:T(8,128)(2,1)S(1)} %collective-permute-done.12.b3.refs_2_), channel_id=1, source_target_pairs={{0,1},{1,2},{2,3},{3,0},{4,7},{5,4},{6,5},{7,6},{8,9},{9,10},{10,1... | collective-permute-start | bytes 1179656 | tf_op jit(solution)/shard_map/ppermute | solution.py:36
  101.5 10.6 %collective-permute-start.16 = (bf16[512,384]{1,0:T(8,128)(2,1)S(1)}, bf16[512,384]{1,0:T(8,128)(2,1)S(1)}, u32[]{:S(2)}, u32[]{:S(2)}) collective-permute-start(bf16[512,384]{1,0:T(8,128)(2,1)S(1)} %multiply_convert_fusion.refs_2_.b0), channel_id=1, source_target_pairs={{0,3},{1,0},{2,1},{3,2},{4,5},{5,6},{6,7},{7,4},{8,11},{9,8},{10,9... | collective-permute-start | bytes 1179656 | tf_op jit(solution)/shard_map/ppermute | solution.py:36
  107.0 8.5 %slice-start = ((s8[4718592]{0:T(1024)(128)(4,1)}), s8[4194304]{0:T(1024)(128)(4,1)S(1)}, s32[]{:S(2)}) async-start(s8[4718592]{0:T(1024)(128)(4,1)} %bitcast.76), calls=%async_computation.1 | async-start | bytes 8388608
  112.1 10.8 %collective-permute-start.17 = (bf16[512,384]{1,0:T(8,128)(2,1)S(1)}, bf16[512,384]{1,0:T(8,128)(2,1)S(1)}, u32[]{:S(2)}, u32[]{:S(2)}) collective-permute-start(bf16[512,384]{1,0:T(8,128)(2,1)S(1)} %collective-permute-done.16.b1.refs_1_), channel_id=1, source_target_pairs={{0,3},{1,0},{2,1},{3,2},{4,5},{5,6},{6,7},{7,4},{8,11},{9,8},{10,9... | collective-permute-start | bytes 1179656 | tf_op jit(solution)/shard_map/ppermute | solution.py:36
  114.0 9.0 %collective-permute-start.18 = (bf16[512,384]{1,0:T(8,128)(2,1)S(1)}, bf16[512,384]{1,0:T(8,128)(2,1)S(1)}, u32[]{:S(2)}, u32[]{:S(2)}) collective-permute-start(bf16[512,384]{1,0:T(8,128)(2,1)S(1)} %multiply_convert_fusion.refs_2_.b0), channel_id=1, source_target_pairs={{0,1},{1,2},{2,3},{3,0},{4,7},{5,4},{6,5},{7,6},{8,9},{9,10},{10,1... | collective-permute-start | bytes 1179656 | tf_op jit(solution)/shard_map/ppermute | solution.py:36
  114.1 1.4 slice-start.1
  137.2 10.1 %collective-permute-start.22 = (bf16[768,1536]{1,0:T(8,128)(2,1)S(1)}, bf16[768,1536]{1,0:T(8,128)(2,1)S(1)}, u32[]{:S(2)}, u32[]{:S(2)}) collective-permute-start(bf16[768,1536]{1,0:T(8,128)(2,1)S(1)} %get-tuple-element.137), channel_id=1, source_target_pairs={{0,4},{4,0},{8,12},{12,8},{16,20},{20,16},{24,28},{28,24},{32,36},... | collective-permute-start | bytes 7077896 | tf_op jit(solution)/shard_map/ppermute | solution.py:46
  137.3 10.0 %collective-permute-start.23 = (bf16[768,1536]{1,0:T(8,128)(2,1)S(1)}, bf16[768,1536]{1,0:T(8,128)(2,1)S(1)}, u32[]{:S(2)}, u32[]{:S(2)}) collective-permute-start(bf16[768,1536]{1,0:T(8,128)(2,1)S(1)} %get-tuple-element.138), channel_id=1, source_target_pairs={{0,4},{4,0},{8,12},{12,8},{16,20},{20,16},{24,28},{28,24},{32,36},... | collective-permute-start | bytes 7077896 | tf_op jit(solution)/shard_map/ppermute | solution.py:46
  137.8 3.5 %collective-permute-start.19 = (f32[1,128]{1,0:T(1,128)S(1)}, f32[1,128]{1,0:T(1,128)S(1)}, u32[]{:S(2)}, u32[]{:S(2)}) collective-permute-start(f32[1,128]{1,0:T(1,128)S(1)} %get-tuple-element.134), channel_id=1, source_target_pairs={{0,1},{1,0},{2,3},{3,2},{4,5},{5,4},{6,7},{7,6},{8,9},{9,8},{10,11... | collective-permute-start | bytes 1544 | tf_op jit(solution)/shard_map/ppermute | solution.py:62
  141.4 4.8 %collective-permute-start.20 = (f32[1,128]{1,0:T(1,128)S(1)}, f32[1,128]{1,0:T(1,128)S(1)}, u32[]{:S(2)}, u32[]{:S(2)}) collective-permute-start(f32[1,128]{1,0:T(1,128)S(1)} %add.252), channel_id=1, source_target_pairs={{0,3},{1,2},{2,1},{3,0},{4,7},{5,6},{6,5},{7,4},{8,11},{9,10},{10,... | collective-permute-start | bytes 1544 | tf_op jit(solution)/shard_map/ppermute | solution.py:62
  146.1 1.2 collective-permute-start.21
  149.2 11.2 %collective-permute-start.24 = (bf16[4,48,1536]{2,1,0:T(8,128)(2,1)S(1)}, bf16[4,48,1536]{2,1,0:T(8,128)(2,1)S(1)}, u32[]{:S(2)}, u32[]{:S(2)}) collective-permute-start(bf16[4,48,1536]{2,1,0:T(8,128)(2,1)S(1)} %get-tuple-element.139), channel_id=1, source_target_pairs={{0,32},{4,12},{8,40},{12,20},{16,48},{20,28},{24,56},{28,4},{32,64... | collective-permute-start | bytes 1769480 | tf_op jit(solution)/shard_map/ppermute | solution.py:46
  150.5 9.9 %collective-permute-start.25 = (bf16[4,48,1536]{2,1,0:T(8,128)(2,1)S(1)}, bf16[4,48,1536]{2,1,0:T(8,128)(2,1)S(1)}, u32[]{:S(2)}, u32[]{:S(2)}) collective-permute-start(bf16[4,48,1536]{2,1,0:T(8,128)(2,1)S(1)} %get-tuple-element.140), channel_id=1, source_target_pairs={{0,96},{4,28},{8,104},{12,4},{16,112},{20,12},{24,120},{28,20},{32... | collective-permute-start | bytes 1769480 | tf_op jit(solution)/shard_map/ppermute | solution.py:46
  152.6 14.2 %collective-permute-start.27 = (bf16[4,48,1536]{2,1,0:T(8,128)(2,1)S(1)}, bf16[4,48,1536]{2,1,0:T(8,128)(2,1)S(1)}, u32[]{:S(2)}, u32[]{:S(2)}) collective-permute-start(bf16[4,48,1536]{2,1,0:T(8,128)(2,1)S(1)} %get-tuple-element.145), channel_id=1, source_target_pairs={{0,96},{4,28},{8,104},{12,4},{16,112},{20,12},{24,120},{28,20},{32... | collective-permute-start | bytes 1769480 | tf_op jit(solution)/shard_map/ppermute | solution.py:46
  154.0 12.7 %collective-permute-start.28 = (bf16[4,48,1536]{2,1,0:T(8,128)(2,1)S(1)}, bf16[4,48,1536]{2,1,0:T(8,128)(2,1)S(1)}, u32[]{:S(2)}, u32[]{:S(2)}) collective-permute-start(bf16[4,48,1536]{2,1,0:T(8,128)(2,1)S(1)} %get-tuple-element.146), channel_id=1, source_target_pairs={{0,32},{4,12},{8,40},{12,20},{16,48},{20,28},{24,56},{28,4},{32,64... | collective-permute-start | bytes 1769480 | tf_op jit(solution)/shard_map/ppermute | solution.py:46
  162.1 11.2 %collective-permute-start.26 = (bf16[4,48,1536]{2,1,0:T(8,128)(2,1)S(1)}, bf16[4,48,1536]{2,1,0:T(8,128)(2,1)S(1)}, u32[]{:S(2)}, u32[]{:S(2)}) collective-permute-start(bf16[4,48,1536]{2,1,0:T(8,128)(2,1)S(1)} %get-tuple-element.144), channel_id=1, source_target_pairs={{0,32},{4,12},{8,40},{12,20},{16,48},{20,28},{24,56},{28,4},{32,64... | collective-permute-start | bytes 1769480 | tf_op jit(solution)/shard_map/ppermute | solution.py:46
  163.7 9.9 %collective-permute-start.29 = (bf16[4,48,1536]{2,1,0:T(8,128)(2,1)S(1)}, bf16[4,48,1536]{2,1,0:T(8,128)(2,1)S(1)}, u32[]{:S(2)}, u32[]{:S(2)}) collective-permute-start(bf16[4,48,1536]{2,1,0:T(8,128)(2,1)S(1)} %get-tuple-element.147), channel_id=1, source_target_pairs={{0,96},{4,28},{8,104},{12,4},{16,112},{20,12},{24,120},{28,20},{32... | collective-permute-start | bytes 1769480 | tf_op jit(solution)/shard_map/ppermute | solution.py:46
  174.8 13.0 %copy-start.8 = (f32[48,1536]{1,0:T(8,128)S(1)}, f32[48,1536]{1,0:T(8,128)}, u32[]{:S(2)}) copy-start(f32[48,1536]{1,0:T(8,128)} %param.23) | copy-start | bytes 884740
  174.8 13.0 %copy-start.9 = (f32[48,1536]{1,0:T(8,128)S(1)}, f32[48,1536]{1,0:T(8,128)}, u32[]{:S(2)}) copy-start(f32[48,1536]{1,0:T(8,128)} %param.22) | copy-start | bytes 884740
  174.8 8.7 %collective-permute-start.32 = (bf16[2,48,1536]{2,1,0:T(8,128)(2,1)S(1)}, bf16[2,48,1536]{2,1,0:T(8,128)(2,1)S(1)}, u32[]{:S(2)}, u32[]{:S(2)}) collective-permute-start(bf16[2,48,1536]{2,1,0:T(8,128)(2,1)S(1)} %get-tuple-element.151), channel_id=1, source_target_pairs={{0,16},{4,68},{8,24},{12,76},{16,0},{20,84},{24,8},{28,92},{32,48}... | collective-permute-start | bytes 884744 | tf_op jit(solution)/shard_map/ppermute | solution.py:46
  178.8 7.9 %collective-permute-start.31 = (bf16[2,48,1536]{2,1,0:T(8,128)(2,1)S(1)}, bf16[2,48,1536]{2,1,0:T(8,128)(2,1)S(1)}, u32[]{:S(2)}, u32[]{:S(2)}) collective-permute-start(bf16[2,48,1536]{2,1,0:T(8,128)(2,1)S(1)} %get-tuple-element.150), channel_id=1, source_target_pairs={{0,8},{4,36},{8,16},{12,44},{16,24},{20,52},{24,0},{28,60},{32,40}... | collective-permute-start | bytes 884744 | tf_op jit(solution)/shard_map/ppermute | solution.py:46
  179.8 7.9 %collective-permute-start.30 = (bf16[2,48,1536]{2,1,0:T(8,128)(2,1)S(1)}, bf16[2,48,1536]{2,1,0:T(8,128)(2,1)S(1)}, u32[]{:S(2)}, u32[]{:S(2)}) collective-permute-start(bf16[2,48,1536]{2,1,0:T(8,128)(2,1)S(1)} %get-tuple-element.149), channel_id=1, source_target_pairs={{0,24},{4,100},{8,0},{12,108},{16,8},{20,116},{24,16},{28,124},{32... | collective-permute-start | bytes 884744 | tf_op jit(solution)/shard_map/ppermute | solution.py:46
  187.7 2.2 %copy-start.1 = (bf16[1536,3,384]{2,0,1:T(8,128)(2,1)S(1)}, bf16[1536,3,384]{2,0,1:T(8,128)(2,1)}, u32[]{:S(2)}) copy-start(bf16[1536,3,384]{2,0,1:T(8,128)(2,1)} %param.19) | copy-start | bytes 10616836
